TPU v7x, 256 devices: a whole 4x4x8 slice. The times are simulated.
256 devices in a mesh: dp: 16 (over y, x), seq: 16 (over z, core).
Axes of the slice: x: 4, y: 4, z: 8, core: 2. Of those that a mesh axis runs over, the one named last changes fastest.
Arguments:
- x_in: float32 [16, 4096, 2560], P('dp', 'seq'), may hold values from -45 to 45
- a_log: float32 [16, 40, 4096], P('dp', None, 'seq'), may hold values from -0.6 to 0, as said below
- b_in: float32 [16, 4096, 128], P('dp', 'seq'), may hold values from -0.03125 to 0.03125
- c_in: float32 [16, 4096, 128], P('dp', 'seq'), may hold values from -6 to 6
- g_out: bfloat16 [16, 4096, 2560], P('dp', 'seq'), may hold values from -6 to 6
- w_out: bfloat16 [2560, 2560], P('dp'), may hold values from -0.125 to 0.125
- d_skip: float32 [40], replicated, may hold values from 0.5 to 2
- group_ids: int32 [40], replicated, may hold values from 0 to 3, as said below
Outputs:
- grad_x: float32 [16, 4096, 2560], P('dp', 'seq')
- grad_a: float32 [16, 40, 4096], P('dp', None, 'seq')
- grad_b: float32 [16, 4096, 128], P('dp', 'seq')
- grad_c: float32 [16, 4096, 128], P('dp', 'seq')
- clipped_w: float32 [2560, 2560], P('dp')
- clipped_d: float32 [40], replicated
Inputs may be any that keep to these rules, and one draw needn't show every extreme that they name: `group_ids`: values 0 to 3, each named by at least one head. `a_log`: log decays, negative.
All inputs are finite; a program needn't handle non-finite values.
Results may differ from a plain program's by a relative error of at most 0.015.
Values may be sent and summed in bfloat16 or wider, within the bound.
No kernel may reach another device: no remote copies, remote signals or barrier semaphores. Data moves between devices by JAX's collectives and lax.ppermute only.
A program may use at most 128 MiB of HBM per device.

v0:
```python
import jax
import jax.numpy as jnp
from jax import lax
from jax.sharding import PartitionSpec as P

D = 2560
P_SIZE = 64
SPAN = 256
GROUPS = 4


def prefix(x, axis, combine, identity, reverse):
    length, mine = (lax.axis_size(axis), lax.axis_index(axis))
    everything = jax.tree.map(lambda part: lax.all_gather(part, axis), x)
    start = jax.tree.map(
        lambda part, zero: jnp.broadcast_to(jnp.asarray(zero, part.dtype), part.shape), x, identity
    )

    def hop(k, before):
        at = length - 1 - k if reverse else k
        reached = at > mine if reverse else at < mine
        new = combine(before, jax.tree.map(lambda part: part[at], everything))
        return jax.tree.map(lambda a, b: jnp.where(reached, a, b), new, before)

    return lax.fori_loop(0, length, hop, start)


def ssd_block(xs, decay, b_rows, c_rows, skip, start_state):
    length = xs.shape[0]
    heads = decay.shape[0]
    width = xs.shape[1] // heads
    blocks = length // SPAN
    xs_b = xs.reshape(blocks, SPAN, heads, width)
    dec_b = decay.reshape(heads, blocks, SPAN).transpose(1, 0, 2)
    b_b = b_rows.reshape(blocks, SPAN, b_rows.shape[1])
    c_b = c_rows.reshape(blocks, SPAN, c_rows.shape[1])
    lower = jnp.arange(SPAN)[:, None] >= jnp.arange(SPAN)[None, :]
    high = lax.Precision.HIGHEST

    def step(state, item):
        xq, dq, bq, cq = item
        cum = jnp.cumsum(dq, axis=1)
        diff = cum[:, :, None] - cum[:, None, :]
        weights = jnp.where(lower[None], jnp.exp(jnp.where(lower[None], diff, 0.0)), 0.0)
        scores = jnp.dot(cq, bq.T, precision=high)
        mixed = weights * scores[None]
        intra = jnp.einsum("hij,jhp->ihp", mixed, xq, precision=high)
        inter = jnp.einsum("in,hpn->ihp", cq, state, precision=high) * jnp.exp(cum).T[:, :, None]
        tail = jnp.exp(cum[:, -1:] - cum)
        new_state = jnp.exp(cum[:, -1])[:, None, None] * state + jnp.einsum(
            "jhp,jn,hj->hpn", xq, bq, tail, precision=high
        )
        out = intra + inter + skip[None, :, None] * xq
        return (new_state, out)

    final, outs = lax.scan(step, start_state, (xs_b, dec_b, b_b, c_b))
    return (outs.reshape(length, heads * width), final)


def chain(earlier, later):
    return (earlier[0] + later[0], jnp.exp(later[0])[:, None, None] * earlier[1] + later[1])


def group_tables(group_ids, first_row, row_count, heads, width):
    head_onehot = (group_ids[:, None] == jnp.arange(GROUPS, dtype=jnp.int32)[None, :]).astype(
        jnp.float32
    )
    row_heads = (first_row + jnp.arange(row_count, dtype=jnp.int32)) // width
    row_onehot = (row_heads[:, None] == jnp.arange(heads, dtype=jnp.int32)[None, :]).astype(
        jnp.float32
    )
    row_groups = jnp.dot(row_onehot, head_onehot, precision=lax.Precision.HIGHEST)
    return (head_onehot, row_groups)


def clip_factor(sumsq, head_onehot, tokens_all):
    counts = jnp.sum(head_onehot, axis=0)
    return jnp.minimum(
        1.0, 7.0 * jnp.sqrt(counts * (P_SIZE * D + 1.0) * tokens_all) / jnp.sqrt(sumsq + 1e-06)
    )


def per_device(x_in, a_log, b_in, c_in, g_out, w_out, d_skip, group_ids):
    high = lax.Precision.HIGHEST
    inputs = x_in[0]
    decay = a_log[0]
    b_rows = b_in[0]
    c_rows = c_in[0]
    grads_out = g_out[0]
    heads = decay.shape[0]
    width = inputs.shape[1] // heads
    dp_count = lax.axis_size("dp")
    seq_count = lax.axis_size("seq")
    tokens_all = float(inputs.shape[0] * seq_count * dp_count)
    cum = jnp.cumsum(decay, axis=1)
    total = cum[:, -1]
    tail = jnp.exp(total[:, None] - cum)
    stacked = inputs.reshape(-1, heads, width)
    local_end = jnp.einsum("jhp,jn,hj->hpn", stacked, b_rows, tail, precision=high)
    empty = (jnp.zeros_like(total), jnp.zeros_like(local_end))
    _, start_state = prefix((total, local_end), "seq", chain, empty, False)

    def forward(xs, dec, b_part, c_part, skip, start):
        return ssd_block(xs, dec, b_part, c_part, skip, start)

    (y_full, _), pull = jax.vjp(forward, inputs, decay, b_rows, c_rows, d_skip, start_state)
    y_low = y_full.astype(jnp.bfloat16)
    g_y = lax.dot_general(
        grads_out,
        lax.all_gather(w_out, "dp", axis=0, tiled=True),
        (((1,), (1,)), ((), ())),
        preferred_element_type=jnp.float32,
    )
    entry = jnp.einsum(
        "hi,in,ihp->hpn", jnp.exp(cum), c_rows, g_y.reshape(-1, heads, width), precision=high
    )
    _, end_grad = prefix((total, entry), "seq", chain, empty, True)
    gx, ga, gb, gc, gd, _ = pull((g_y, end_grad))
    owned = lax.psum_scatter(
        lax.dot_general(
            y_low, grads_out, (((0,), (0,)), ((), ())), preferred_element_type=jnp.float32
        ).astype(jnp.bfloat16),
        "dp",
        scatter_dimension=0,
        tiled=True,
    ).astype(jnp.float32)
    grad_w = lax.psum(owned, "seq")
    grad_d = lax.psum(gd, ("dp", "seq"))
    first_row = lax.axis_index("dp") * grad_w.shape[0]
    head_onehot, row_groups = group_tables(group_ids, first_row, grad_w.shape[0], heads, width)
    partial_sq = jnp.dot(jnp.sum(grad_w * grad_w, axis=1), row_groups, precision=high)
    sumsq = lax.psum(partial_sq, "dp")
    sumsq = sumsq + jnp.dot(grad_d * grad_d, head_onehot, precision=high)
    factor = clip_factor(sumsq, head_onehot, tokens_all)
    clipped_w = grad_w * jnp.dot(row_groups, factor, precision=high)[:, None]
    clipped_d = grad_d * jnp.dot(head_onehot, factor, precision=high)
    return (gx[None], ga[None], gb[None], gc[None], clipped_w, clipped_d)


def solution(mesh):
    return jax.shard_map(
        per_device,
        mesh=mesh,
        in_specs=(
            P("dp", "seq", None),
            P("dp", None, "seq"),
            P("dp", "seq", None),
            P("dp", "seq", None),
            P("dp", "seq", None),
            P("dp", None),
            P(),
            P(),
        ),
        out_specs=(
            P("dp", "seq", None),
            P("dp", None, "seq"),
            P("dp", "seq", None),
            P("dp", "seq", None),
            P("dp", None),
            P(),
        ),
        check_vma=False,
    )
```

profile of v0, /device:TPU:2, one launch (start us, length us, event | category | flops | bytes accessed | tf_op | source)
XLA Modules:
  0.0 720.2 jit_solution(15672095264673269281)
XLA Ops:
  14.8 96.2 %all-gather.7.cloned.1.call-done = bf16[2560,2560]{1,0:T(8,128)(2,1)} async-done(((bf16[160,2560]{1,0:T(8,128)(2,1)}), bf16[2560,2560]{1,0:T(8,128)(2,1)}) %all-gather.7.cloned.1.call-update) | async-done | bytes 13107216 | tf_op jit(solution)/shard_map/all_gather | solution.py:110
  111.0 15.7 %fusion.20 = (f32[2560]{0:T(1024)S(1)}, f32[256,2560]{1,0:T(8,128)}, f32[256,2560]{1,0:T(8,128)}) fusion(f32[1,256,2560]{2,1,0:T(8,128)} %param.12, f32[256,2560]{1,0:T(8,128)} %copy.103, bf16[2560,2560]{1,0:T(8,128)(2,1)} %all-gather.7.cloned.1.call-done, bf16[1,256,2560]{2,1,0:T(8,128)(2,1)S(1)} %copy-done), kind=kOutput, calls=%fused_computation.27 | convolution fusion | flops 3357406720 | bytes 24913920 | tf_op jit(solution)/shard_map/dot_general | solution.py:108
  126.7 3.3 copy.88
  129.9 5.0 fusion.26
  135.1 3.2 copy.97
  139.6 27.8 %all-reduce.2 = f32[640]{0:T(1024)S(1)} all-reduce(f32[640]{0:T(1024)S(1)} %fusion.76), channel_id=2, replica_groups=mesh['dp'=16,'seq'=16] {'seq'}, use_global_device_ids=true, to_apply=%add.2 | all-reduce | flops 640 | bytes 5120
  167.5 82.8 %all-gather.9.cloned.1.call-done = f32[640,64,128]{2,1,0:T(8,128)} async-done(((f32[40,64,128]{2,1,0:T(8,128)}), f32[640,64,128]{2,1,0:T(8,128)}) %all-gather.9.cloned.1.call-update) | async-done | bytes 20971536 | tf_op jit(solution)/shard_map/all_gather | solution.py:14
  250.3 26.8 %while.24 = (s32[]{:T(128)}, f32[40,64,128]{2,1,0:T(8,128)S(1)}, s32[]{:T(128)}, f32[16,40]{1,0:T(8,128)S(1)}, f32[16,40,64,128]{3,2,1,0:T(8,128)}, /*index=5*/s32[]{:T(128)}, s32[]{:T(128)}, s32[]{:T(128)}, s32[]{:T(128)}) while((s32[]{:T(128)}, f32[40,64,128]{2,1,0:T(8,128)S(1)}, s32[]{:T(128)}, f32[16,40]{1,0:T(8,128)S(1)}, ...), condition=%wide.region_3.4_spmd.clone, body=%wide.region_2.3_spmd.clone.sunk | while | flops 1310728 | bytes 3932807 | solution.py:25
  277.2 5.5 fusion.24
  282.9 5.1 fusion.30
  288.0 11.0 %reduce-scatter.2.cloned.1.call-start = ((), (), s32[]{:S(2)}) async-start(), calls=%async_computation.2 | async-start | bytes 13926400 | tf_op jit(solution)/shard_map/reduce_scatter | solution.py:119
  300.2 101.7 %all-gather.11.cloned.1.call-done = f32[640,64,128]{2,1,0:T(8,128)} async-done(((f32[40,64,128]{2,1,0:T(8,128)}), f32[640,64,128]{2,1,0:T(8,128)}) %all-gather.11.cloned.1.call-update) | async-done | bytes 20971536 | tf_op jit(solution)/shard_map/all_gather | solution.py:14
  401.9 47.7 %while.25 = (s32[]{:T(128)}, f32[40,64,128]{2,1,0:T(8,128)}, s32[]{:T(128)}, f32[16,40]{1,0:T(8,128)S(1)}, f32[16,40,64,128]{3,2,1,0:T(8,128)}, /*index=5*/s32[]{:T(128)}, s32[]{:T(128)}) while((s32[]{:T(128)}, f32[40,64,128]{2,1,0:T(8,128)}, s32[]{:T(128)}, f32[16,40]{1,0:T(8,128)S(1)}, f32[16,40,64,128]{3,2,1,0:T(8,128)}, ...), condition=%wide.region_5.6_spmd.clone, body=%wide.region_4.5_spmd.clone.sunk | while | flops 1310724 | bytes 3932745 | solution.py:25
  449.6 5.2 fusion.23
  454.8 13.3 %fusion.22 = bf16[256,40,64]{0,2,1:T(8,128)(2,1)S(1)} fusion(f32[40,64,256]{2,1,0:T(8,128)S(1)} %get-tuple-element.659, f32[256,40,64]{0,2,1:T(8,128)S(1)} %bitcast.179, f32[256,256]{1,0:T(8,128)S(1)} %copy-done.10, f32[40,256]{1,0:T(8,128)S(1)} %copy_bitcast_fusion, pred[256,256]{1,0:T(8,128)(4,1)S(1)} %iota_compare_fusion, f32[256,40]{0,1:T(8,128)S(1)} %copy.95, ...), kind=kOutput, calls=%fused_computation.30 | convolution fusion | flops 2027028480 | bytes 6963360 | tf_op jit(solution)/shard_map/jvp()/while/body/eval_jaxpr/hij,jhp->ihp/dot_general | solution.py:47
  468.1 6.6 convolution_convert_fusion
  477.1 16.6 %fusion.9 = (f32[40,256]{1,0:T(8,128)S(1)}, f32[40,256]{1,0:T(8,128)S(1)}, f32[256,256]{1,0:T(8,128)S(1)}) fusion(f32[256,256]{1,0:T(8,128)S(1)} %copy-done.11, f32[40,256]{1,0:T(8,128)S(1)} %copy_bitcast_fusion, pred[256,256]{1,0:T(8,128)(4,1)S(1)} %iota_compare_fusion, f32[40,64,256]{2,1,0:T(8,128)} %bitcast.182, f32[256,40,64]{0,2,1:T(8,128)} %bitcast.177), kind=kOutput, calls=%fused_computation.15 | convolution fusion | flops 2042015744 | bytes 5955584 | tf_op jit(solution)/shard_map/transpose(jvp())/while/body/eval_jaxpr/hij,jhp->ihp/dot_general | solution.py:47
  497.8 77.5 %psum.23 = f32[40]{0:T(128)} all-reduce(f32[40]{0:T(128)S(1)} %reduce_sum.145), channel_id=1, replica_groups=mesh['dp'=16,'seq'=16] {'dp','seq'}, use_global_device_ids=true, to_apply=%region_21.22 | all-reduce | flops 40 | bytes 320 | tf_op jit(solution)/shard_map/psum | solution.py:128
  575.2 6.0 fusion.44
  589.5 6.1 convolution_bitcast_fusion
  596.6 11.8 %bitcast_add_fusion.3 = f32[256,40,64]{0,2,1:T(8,128)} fusion(f32[40,64,256]{2,1,0:T(8,128)} %get-tuple-element.657, f32[256,40,64]{0,2,1:T(8,128)S(1)} %bitcast.183, f32[40,64,256]{2,1,0:T(8,128)S(1)} %bitcast.184, f32[256,256]{1,0:T(8,128)S(1)} %copy-done.12, f32[40,256]{1,0:T(8,128)S(1)} %copy-done.14, pred[256,256]{1,0:T(8,128)(4,1)S(1)} %copy-done.16, ...), kind=kOutput, calls=%fused_computation.36 | convolution fusion | flops 2026373120 | bytes 10895520 | tf_op jit(solution)/shard_map/transpose(jvp())/while/body/eval_jaxpr/hij,jhp->ihp/dot_general | solution.py:47
  608.4 58.5 %all-reduce.4 = f32[160,2560]{1,0:T(8,128)S(1)} all-reduce(bf16[160,2560]{1,0:T(8,128)(2,1)} %reduce-scatter.2.cloned.1.call-done), channel_id=1, replica_groups=mesh['dp'=16,'seq'=16] {'seq'}, use_global_device_ids=true, to_apply=%region_15.16 | all-reduce | flops 409600 | bytes 2457600 | tf_op jit(solution)/shard_map/psum | solution.py:127
  668.4 3.3 copy.105
  671.7 37.8 %psum.22 = f32[4]{0:T(128)S(1)} all-reduce(f32[4]{0:T(128)S(1)} %convolution_bitcast_fusion.3), channel_id=1, replica_groups=mesh['dp'=16,'seq'=16] {'dp'}, use_global_device_ids=true, to_apply=%region_18.19 | all-reduce | flops 4 | bytes 32 | tf_op jit(solution)/shard_map/psum | solution.py:132
  (173 shorter events, 104.5 us)
Async XLA Ops:
  7.2 103.8 %copy-start = (bf16[1,256,2560]{2,1,0:T(8,128)(2,1)S(1)}, bf16[1,256,2560]{2,1,0:T(8,128)(2,1)}, u32[]{:S(2)}) copy-start(bf16[1,256,2560]{2,1,0:T(8,128)(2,1)} %param.16) | copy-start | bytes 3932164
  7.2 103.8 %all-gather.7.cloned.1.call-start = ((), (), s32[]{:S(2)}) async-start(), calls=%async_computation.1 | async-start | bytes 13926400 | tf_op jit(solution)/shard_map/all_gather | solution.py:110
  7.9 242.4 %all-gather.9.cloned.1.call-start = ((), (), s32[]{:S(2)}) async-start(), calls=%async_computation.3 | async-start | bytes 22282240 | tf_op jit(solution)/shard_map/all_gather | solution.py:14
  9.7 467.4 %copy-start.13 = (f32[40,256]{1,0:T(8,128)}, f32[40,256]{1,0:T(8,128)S(1)}, u32[]{:S(2)}) copy-start(f32[40,256]{1,0:T(8,128)S(1)} %copy_bitcast_fusion) | copy-start | bytes 122884
  126.7 3.3 copy-start.6
  135.0 266.9 %all-gather.11.cloned.1.call-start = ((), (), s32[]{:S(2)}) async-start(), calls=%async_computation.4 | async-start | bytes 22282240 | tf_op jit(solution)/shard_map/all_gather | solution.py:14
  135.0 3.2 copy-start.21
  250.3 26.8 %copy-start.7 = (f32[1,256,128]{2,1,0:T(8,128)S(1)}, f32[1,256,128]{2,1,0:T(8,128)}, u32[]{:S(2)}) copy-start(f32[1,256,128]{2,1,0:T(8,128)} %param.14) | copy-start | bytes 393220
  282.9 5.1 copy-start.9
  288.0 320.4 %reduce-scatter.2.cloned.1.call-start = ((), (), s32[]{:S(2)}) async-start(), calls=%async_computation.2 | async-start | bytes 13926400 | tf_op jit(solution)/shard_map/reduce_scatter | solution.py:119
  299.1 178.0 %copy-start.15 = (pred[256,256]{1,0:T(8,128)(4,1)}, pred[256,256]{1,0:T(8,128)(4,1)S(1)}, u32[]{:S(2)}) copy-start(pred[256,256]{1,0:T(8,128)(4,1)S(1)} %iota_compare_fusion) | copy-start | bytes 196612
  449.6 5.2 copy-start.3
  449.6 5.2 copy-start.10
  449.6 5.2 copy-start.17
  497.7 86.2 %copy-start.2 = (f32[40,64,128]{2,1,0:T(8,128)S(1)}, f32[40,64,128]{2,1,0:T(8,128)}, u32[]{:S(2)}) copy-start(f32[40,64,128]{2,1,0:T(8,128)} %get-tuple-element.548) | copy-start | bytes 3932164
  585.9 10.7 %copy-start.12 = (f32[256,256]{1,0:T(8,128)S(1)}, f32[256,256]{1,0:T(8,128)}, u32[]{:S(2)}) copy-start(f32[256,256]{1,0:T(8,128)} %fusion.60) | copy-start | bytes 786436
  585.9 10.7 %copy-start.14 = (f32[40,256]{1,0:T(8,128)S(1)}, f32[40,256]{1,0:T(8,128)}, u32[]{:S(2)}) copy-start(f32[40,256]{1,0:T(8,128)} %copy-done.13) | copy-start | bytes 122884
  585.9 10.7 %copy-start.16 = (pred[256,256]{1,0:T(8,128)(4,1)S(1)}, pred[256,256]{1,0:T(8,128)(4,1)}, u32[]{:S(2)}) copy-start(pred[256,256]{1,0:T(8,128)(4,1)} %copy-done.15) | copy-start | bytes 196612
  589.4 7.2 copy-start.4
  608.4 59.8 %copy-start.20 = (f32[160,4]{0,1:T(4,128)S(1)}, f32[160,4]{0,1:T(4,128)}, u32[]{:S(2)}) copy-start(f32[160,4]{0,1:T(4,128)} %fusion.68) | copy-start | bytes 7684
  668.4 41.1 %copy-start.19 = (s32[40]{0:T(128)S(1)}, s32[40]{0:T(128)}, u32[]{:S(2)}) copy-start(s32[40]{0:T(128)} %param.19) | copy-start | bytes 484
  668.4 41.1 %copy-start.22 = (f32[4]{0:T(128)S(1)}, f32[4]{0:T(128)}, u32[]{:S(2)}) copy-start(f32[4]{0:T(128)} %convert_reduce_fusion) | copy-start | bytes 52
  668.4 41.1 %copy-start.23 = (f32[40]{0:T(128)S(1)}, f32[40]{0:T(128)}, u32[]{:S(2)}) copy-start(f32[40]{0:T(128)} %psum.23) | copy-start | bytes 484
  668.4 44.8 %copy-start.1 = (bf16[1,256,2560]{2,1,0:T(8,128)(2,1)S(1)}, bf16[1,256,2560]{2,1,0:T(8,128)(2,1)}, u32[]{:S(2)}) copy-start(bf16[1,256,2560]{2,1,0:T(8,128)(2,1)} %param.16) | copy-start | bytes 3932164
  (4 other events, 5.1 us)
Sparse Core Ops, SparseCore 0:
  10.4 100.4 all-gather.6
  135.1 115.1 all-gather.8
  288.1 113.6 all-gather.10
  474.9 100.0 reduce-scatter.1
where the time goes:
time: 730 us; the launch traced here: 720 us
  waiting for transfers between devices  281 us (38%)
  blocking collectives  201 us (28%)
  matrix products  102 us (14%)
  other arithmetic  82.1 us (11%)
  local copies, waits for them, and re-layouts  26.1 us (4%)
  between operations  15.2 us (2%)
  starting transfers between devices  11.1 us (2%)
    all_gather x2, waiting for transfers between devices, prefix(): everything = jax.tree.map(lambda part: lax.all_gather(part, axis), x)  184 us
    all_gather x1, waiting for transfers between devices, per_device(): lax.all_gather(w_out, 'dp', axis=0, tiled=True)  96.2 us
    psum x1, blocking collectives, per_device(): grad_d = lax.psum(gd, ('dp', 'seq'))  77.5 us
    select_n x32, other arithmetic, hop(): return jax.tree.map(lambda a, b: jnp.where(reached, a, b), new, before)  73.5 us
    psum x1, blocking collectives, per_device(): grad_w = lax.psum(owned, 'seq')  58.5 us
    dot_general x3, matrix products, step(): intra = jnp.einsum('hij,jhp->ihp', mixed, xq, precision=high)  41.7 us
    psum x1, blocking collectives, per_device(): sumsq = lax.psum(partial_sq, 'dp')  37.8 us
    unnamed x1, blocking collectives  27.8 us
  transfers between devices with their start and end apart: 4, of which 3 were waited for; matrix products, arithmetic and copies ran while one was open for 9% of the time, Pallas kernels for 0%

commit v1 on v0

v1 whole, which is shorter than its diff:
```python
import functools

import jax
import jax.numpy as jnp
from jax import lax
from jax.experimental import pallas as pl
from jax.experimental.pallas import tpu as pltpu
from jax.sharding import Mesh
from jax.sharding import PartitionSpec as P

D = 2560
H = 40
P_SIZE = 64
N = 128
T = 256
GROUPS = 4
PAIRS = H // 2
SEQ = ("z", "core")
N_SEQ = 16
OWN = H * P_SIZE // N_SEQ
HIGH = lax.Precision.HIGHEST
BF = jnp.bfloat16
F32 = jnp.float32
VMEM = 40 * 1024 * 1024


def nn(a, b):
    return lax.dot_general(a, b, (((1,), (0,)), ((), ())), preferred_element_type=F32)


def nt(a, b):
    return lax.dot_general(a, b, (((1,), (1,)), ((), ())), preferred_element_type=F32)


def tn(a, b):
    return lax.dot_general(a, b, (((0,), (0,)), ((), ())), preferred_element_type=F32)


def iota(shape, dim):
    return lax.broadcasted_iota(jnp.int32, shape, dim)


def whole(shape):
    return pl.BlockSpec(shape, lambda *_: (0,) * len(shape))


def wide(rows):
    return pl.BlockSpec((rows, 2 * P_SIZE), lambda p: (0, p))


def state_block():
    return pl.BlockSpec((2 * P_SIZE, N), lambda p: (p, 0))


def params():
    return pltpu.CompilerParams(vmem_limit_bytes=VMEM)


def cost(flops, moved, exps):
    return pl.CostEstimate(flops=flops, bytes_accessed=moved, transcendentals=exps)


def spread(cum_t, pair):
    lane_head = 2 * pair + iota((H, 2 * P_SIZE), 1) // P_SIZE
    pick = (iota((H, 2 * P_SIZE), 0) == lane_head).astype(F32)
    return jnp.dot(cum_t, pick, precision=HIGH, preferred_element_type=F32)


def column(cum_t, head):
    return jnp.sum(jnp.where(iota(cum_t.shape, 1) == head, cum_t, 0.0), axis=1, keepdims=True)


def low_half(shape):
    return iota(shape, 1) < P_SIZE


def ends_kernel(x_ref, a_ref, b_ref, cum_ref, cum_t_ref, end_ref):
    pair = pl.program_id(0)

    @pl.when(pair == 0)
    def _():
        a = a_ref[...]
        upto = (iota((T, T), 0) <= iota((T, T), 1)).astype(F32)
        cum_ref[...] = jnp.dot(a, upto, precision=HIGH, preferred_element_type=F32)
        down = (iota((T, T), 1) <= iota((T, T), 0)).astype(F32)
        cum_t_ref[...] = lax.dot_general(
            down, a, (((1,), (1,)), ((), ())), precision=HIGH, preferred_element_type=F32
        )

    cum = spread(cum_t_ref[...], pair)
    tail = jnp.exp(cum[T - 1 : T, :] - cum)
    end_ref[...] = tn((x_ref[...] * tail).astype(BF), b_ref[...].astype(BF)).astype(BF)


def local_ends(x, a, b):
    return pl.pallas_call(
        ends_kernel,
        grid=(PAIRS,),
        in_specs=[wide(T), whole((H, T)), whole((T, N))],
        out_specs=[whole((H, T)), whole((T, H)), state_block()],
        out_shape=[
            jax.ShapeDtypeStruct((H, T), F32),
            jax.ShapeDtypeStruct((T, H), F32),
            jax.ShapeDtypeStruct((H * P_SIZE, N), BF),
        ],
        compiler_params=params(),
        cost_estimate=cost(2 * T * D * N, 4 * T * D, T * D),
        name="ends",
    )(x, a, b)


def intra_kernel(x_ref, cum_ref, cum_t_ref, b_ref, c_ref, skip_ref, y_ref, scores):
    pair = pl.program_id(0)

    @pl.when(pair == 0)
    def _():
        keep = iota((T, T), 0) >= iota((T, T), 1)
        scores[...] = jnp.where(keep, nt(c_ref[...].astype(BF), b_ref[...].astype(BF)), 0.0)

    x = x_ref[...]
    xb = x.astype(BF)
    parts = []
    for k in range(2):
        head = 2 * pair + k
        diff = column(cum_t_ref[...], head) - cum_ref[pl.ds(head, 1), :]
        mixed = (jnp.exp(jnp.minimum(diff, 0.0)) * scores[...]).astype(BF)
        parts.append(nn(mixed, xb))
    y_ref[...] = jnp.where(low_half(x.shape), parts[0], parts[1]) + skip_ref[...] * x


def intra(x, cum, cum_t, b, c, skip):
    return pl.pallas_call(
        intra_kernel,
        grid=(PAIRS,),
        in_specs=[
            wide(T), whole((H, T)), whole((T, H)), whole((T, N)), whole((T, N)), wide(1),
        ],
        out_specs=wide(T),
        out_shape=jax.ShapeDtypeStruct((T, D), F32),
        scratch_shapes=[pltpu.VMEM((T, T), F32)],
        compiler_params=params(),
        cost_estimate=cost(4 * T * T * D, 8 * T * D, H * T * T),
        name="intra",
    )(x, cum, cum_t, b, c, skip)


def inter_kernel(part_ref, cum_t_ref, c_ref, start_ref, y_ref):
    grow = jnp.exp(spread(cum_t_ref[...], pl.program_id(0)))
    y = part_ref[...] + grow * nt(c_ref[...].astype(BF), start_ref[...])
    y_ref[...] = y.astype(BF)


def inter(part, cum_t, c, start):
    return pl.pallas_call(
        inter_kernel,
        grid=(PAIRS,),
        in_specs=[wide(T), whole((T, H)), whole((T, N)), state_block()],
        out_specs=wide(T),
        out_shape=jax.ShapeDtypeStruct((T, D), BF),
        compiler_params=params(),
        cost_estimate=cost(2 * T * D * N, 6 * T * D, T * D),
        name="inter",
    )(part, cum_t, c, start)


def chain_kernel(reverse, mine_ref, parts_ref, totals_ref, out_ref):
    owner = (mine_ref[0] * OWN + iota((OWN, N), 0)) // P_SIZE == iota((OWN, N), 1)
    carry = jnp.zeros((OWN, N), F32)
    for s in range(N_SEQ - 1, -1, -1) if reverse else range(N_SEQ):
        out_ref[s] = carry.astype(BF)
        pieces = totals_ref[s].astype(F32)
        total = pieces[0:1, :] + pieces[1:2, :] + pieces[2:3, :]
        decay = jnp.sum(jnp.where(owner, total, 0.0), axis=1, keepdims=True)
        carry = jnp.exp(decay) * carry + parts_ref[s].astype(F32)


def chain(parts, totals, mine, reverse):
    return pl.pallas_call(
        functools.partial(chain_kernel, reverse),
        in_specs=[
            pl.BlockSpec(memory_space=pltpu.SMEM),
            pl.BlockSpec(memory_space=pltpu.VMEM),
            pl.BlockSpec(memory_space=pltpu.VMEM),
        ],
        out_specs=pl.BlockSpec(memory_space=pltpu.VMEM),
        out_shape=jax.ShapeDtypeStruct((N_SEQ, OWN, N), BF),
        compiler_params=params(),
        cost_estimate=cost(4 * N_SEQ * OWN * N, 4 * N_SEQ * OWN * N, N_SEQ * OWN),
        name="chain",
    )(mine, parts, totals)


def three(v):
    hi = lax.reduce_precision(v, 8, 7)
    mid = lax.reduce_precision(v - hi, 8, 7)
    rows = jnp.stack([hi, mid, v - hi - mid]).astype(BF)
    return jnp.pad(rows, ((0, 13), (0, N - v.shape[0])))


def swap_seq(states, extra):
    rows = jnp.broadcast_to(extra[None], (N_SEQ, 16, N))
    sent = jnp.concatenate([states.reshape(N_SEQ, OWN, N), rows], axis=1)
    got = lax.all_to_all(sent, SEQ, 0, 0, tiled=True)
    return got[:, :OWN], got[:, OWN:]


def back_seq(states):
    return lax.all_to_all(states, SEQ, 0, 0, tiled=True).reshape(H * P_SIZE, N)


def term_kernel(yo_ref, yx_ref, go_ref, gx_ref, first_ref, second_ref):
    half = go_ref.shape[1] // 2
    for i, out in enumerate((first_ref, second_ref)):
        cols = pl.ds(i * half, half)
        term = tn(yo_ref[...], go_ref[:, cols]) + tn(yx_ref[...], gx_ref[:, cols])
        out[...] = term.astype(BF).reshape(out.shape)


def terms(y_own, y_other, g_own, g_other):
    rows = pl.BlockSpec((T, 4 * OWN), lambda i: (0, i))
    half = g_own.shape[1] // 2
    return pl.pallas_call(
        term_kernel,
        grid=(4,),
        in_specs=[rows, rows, whole(g_own.shape), whole(g_own.shape)],
        out_specs=[
            pl.BlockSpec((4, 1, OWN, half), lambda i: (0, i, 0, 0)),
            pl.BlockSpec((1, 4, OWN, half), lambda i: (i, 0, 0, 0)),
        ],
        out_shape=[jax.ShapeDtypeStruct((4, 4, OWN, half), BF)] * 2,
        compiler_params=params(),
        cost_estimate=cost(4 * T * D * D // 2, 3 * D * D // 2, 0),
        name="terms",
    )(y_own, y_other, g_own, g_other)


def entry_kernel(own_ref, other_ref, x_ref, cum_t_ref, c_ref, gy_ref, entry_ref, gd_ref):
    gy = own_ref[...] + other_ref[...].astype(F32)
    gy_ref[...] = gy.astype(BF)
    gd_ref[...] = jnp.sum(gy * x_ref[...], axis=0, keepdims=True)
    grow = jnp.exp(spread(cum_t_ref[...], pl.program_id(0)))
    entry_ref[...] = tn((gy * grow).astype(BF), c_ref[...].astype(BF)).astype(BF)


def entries(own, other, x, cum_t, c):
    return pl.pallas_call(
        entry_kernel,
        grid=(PAIRS,),
        in_specs=[wide(T), wide(T), wide(T), whole((T, H)), whole((T, N))],
        out_specs=[wide(T), state_block(), wide(1)],
        out_shape=[
            jax.ShapeDtypeStruct((T, D), BF),
            jax.ShapeDtypeStruct((H * P_SIZE, N), BF),
            jax.ShapeDtypeStruct((1, D), F32),
        ],
        compiler_params=params(),
        cost_estimate=cost(2 * T * D * N, 12 * T * D, T * D),
        name="entries",
    )(own, other, x, cum_t, c)


def back_kernel(
    x_ref, gy_ref, cum_ref, cum_t_ref, b_ref, c_ref, skip_ref, start_ref, last_ref,
    gx_ref, ga_ref, gb_ref, gc_ref,
    scores, d_scores, rows, cols, tails, totals,
):
    pair = pl.program_id(0)
    bb = b_ref[...].astype(BF)
    cb = c_ref[...].astype(BF)

    @pl.when(pair == 0)
    def _():
        keep = iota((T, T), 1) >= iota((T, T), 0)
        scores[...] = jnp.where(keep, nt(bb, cb), 0.0)
        d_scores[...] = jnp.zeros_like(d_scores)
        cols[...] = jnp.zeros_like(cols)
        tails[...] = jnp.zeros_like(tails)
        gb_ref[...] = jnp.zeros_like(gb_ref)
        gc_ref[...] = jnp.zeros_like(gc_ref)

    x = x_ref[...]
    gyb = gy_ref[...]
    gy = gyb.astype(F32)
    xb = x.astype(BF)
    low = low_half(x.shape)
    lanes = iota((T, N), 1)
    parts = []
    for k in range(2):
        head = 2 * pair + k
        diff = cum_ref[pl.ds(head, 1), :] - column(cum_t_ref[...], head)
        weights = jnp.exp(jnp.minimum(diff, 0.0))
        mine = jnp.where(low if k == 0 else ~low, x, 0.0).astype(BF)
        d_mixed = weights * nt(mine, gyb)
        d_scores[...] += d_mixed
        parts.append(nn((weights * scores[...]).astype(BF), gyb))
        change = d_mixed * scores[...]
        rows[pl.ds(head, 1), :] = jnp.sum(change, axis=0, keepdims=True)
        down = jnp.sum(change, axis=1, keepdims=True)
        cols[...] -= jnp.where(lanes == head, down, 0.0)
    cum = spread(cum_t_ref[...], pair)
    grow = jnp.exp(cum)
    tail = jnp.exp(cum[T - 1 : T, :] - cum)
    start = start_ref[...]
    last = last_ref[...]
    pick = (lanes[:N] == 2 * pair + iota((N, N), 0) // P_SIZE).astype(BF)
    grown = gy * grow
    cols[...] += nn((grown * nt(cb, start)).astype(BF), pick)
    gc_ref[...] += nn(grown.astype(BF), start)
    faded = x * tail
    back = nt(bb, last)
    tails[...] += nn((faded * back).astype(BF), pick)
    gb_ref[...] += nn(faded.astype(BF), last)
    gx_ref[...] = jnp.where(low, parts[0], parts[1]) + tail * back + skip_ref[...] * gy
    both = start.astype(F32) * last.astype(F32)
    for k in range(2):
        part = both[k * P_SIZE : (k + 1) * P_SIZE, :]
        totals[pl.ds(2 * pair + k, 1), :] = jnp.sum(part, axis=0, keepdims=True)

    @pl.when(pair == PAIRS - 1)
    def _():
        keep = iota((T, T), 1) >= iota((T, T), 0)
        ds = jnp.where(keep, d_scores[...], 0.0).astype(BF)
        gb_ref[...] += nn(ds, cb)
        gc_ref[...] += tn(ds, bb)
        after = (iota((T, T), 0) >= iota((T, T), 1)).astype(F32)
        before = (iota((T, T), 0) < iota((T, T), 1)).astype(F32)
        dims = (((0,), (0,)), ((), ()))
        ga = jnp.dot(rows[...], after, precision=HIGH, preferred_element_type=F32)
        up = lax.dot_general(cols[...], after, dims, precision=HIGH, preferred_element_type=F32)
        up += lax.dot_general(tails[...], before, dims, precision=HIGH, preferred_element_type=F32)
        whole_decay = jnp.exp(cum_ref[:, T - 1 : T])
        ga_ref[...] = ga + up[:H] + whole_decay * jnp.sum(totals[...], axis=1, keepdims=True)


def backward(x, gy, cum, cum_t, b, c, skip, start, last):
    return pl.pallas_call(
        back_kernel,
        grid=(PAIRS,),
        in_specs=[
            wide(T), wide(T), whole((H, T)), whole((T, H)), whole((T, N)), whole((T, N)),
            wide(1), state_block(), state_block(),
        ],
        out_specs=[wide(T), whole((H, T)), whole((T, N)), whole((T, N))],
        out_shape=[
            jax.ShapeDtypeStruct((T, D), F32),
            jax.ShapeDtypeStruct((H, T), F32),
            jax.ShapeDtypeStruct((T, N), F32),
            jax.ShapeDtypeStruct((T, N), F32),
        ],
        scratch_shapes=[
            pltpu.VMEM((T, T), F32),
            pltpu.VMEM((T, T), F32),
            pltpu.VMEM((H, T), F32),
            pltpu.VMEM((T, N), F32),
            pltpu.VMEM((T, N), F32),
            pltpu.VMEM((H, N), F32),
        ],
        compiler_params=params(),
        cost_estimate=cost(8 * T * T * D, 14 * T * D, H * T * T),
        name="backward",
    )(x, gy, cum, cum_t, b, c, skip, start, last)


def add_up(parts):
    return jnp.sum(parts.astype(F32), axis=0)


def swap(v, axis):
    return lax.all_to_all(v, axis, 0, 0, tiled=True)


def other_core(v):
    return lax.ppermute(v, "core", [(0, 1), (1, 0)])


def gathered(v, axis):
    mine = lax.axis_index(axis)
    found = [v]
    for d in range(1, 4):
        found.append(lax.ppermute(v, axis, [((i + d) % 4, i) for i in range(4)]))
    return lax.dynamic_slice_in_dim(jnp.stack(found + found), (4 - mine) % 4, 4, axis=0)


def per_device(x_in, a_log, b_in, c_in, g_out, w_out, d_skip, group_ids):
    x, a, b, c, g = (x_in[0], a_log[0], b_in[0], c_in[0], g_out[0])
    core = lax.axis_index("core")
    half = D // 2
    mine = (2 * lax.axis_index("z") + core).reshape(1).astype(jnp.int32)
    tokens_all = float(T * N_SEQ * 16)

    w_mine = lax.dynamic_slice_in_dim(w_out, core * half, half, axis=1)
    w_half = lax.all_gather(w_mine, ("y", "x"), axis=0, tiled=True)
    g_mine = lax.dynamic_slice_in_dim(g, core * half, half, axis=1)
    g_other = other_core(lax.dynamic_slice_in_dim(g, (1 - core) * half, half, axis=1))
    skip = jnp.repeat(d_skip, P_SIZE)[None]

    cum, cum_t, end = local_ends(x, a, b)
    parts, totals = swap_seq(end, three(cum[:, T - 1]))
    y_part = intra(x, cum, cum_t, b, c, skip)
    start = back_seq(chain(parts, totals, mine, False))
    y_own = inter(y_part, cum_t, c, start)
    y_other = other_core(y_own)
    first, second = terms(y_own, y_other, g_mine, g_other)

    w_half, first, second = lax.optimization_barrier((w_half, first, second))
    first = swap(first, "x")
    second = swap(second, "y")

    dims = (((1,), (1,)), ((), ()))
    gy_other = lax.dot_general(g_other, w_half, dims, preferred_element_type=F32).astype(BF)
    gy_other = other_core(gy_other)
    gy_own = lax.dot_general(g_mine, w_half, dims, preferred_element_type=F32)
    gy, entry, gd = entries(gy_own, gy_other, x, cum_t, c)
    gd = jnp.sum(gd.reshape(H, P_SIZE), axis=1)
    parts, gd_parts = swap_seq(entry, three(gd))
    last = back_seq(chain(parts, totals, mine, True))

    first = swap(add_up(first).astype(BF), "y")
    second = swap(add_up(second).astype(BF), "x")
    owned = jnp.concatenate([add_up(first), add_up(second)], axis=1).astype(BF)
    owned = add_up(swap(owned.reshape(8, OWN // 8, half), "z")).astype(BF)
    owned = swap(jnp.broadcast_to(owned[None], (N_SEQ,) + owned.shape), SEQ)
    owned = owned.reshape(8, 2, OWN // 8, half).transpose(0, 2, 1, 3).reshape(OWN, D)
    grad_w = owned.astype(F32)

    gx, ga, gb, gc = backward(x, gy, cum, cum_t, b, c, skip, start, last)

    first_row = (4 * lax.axis_index("y") + lax.axis_index("x")) * OWN
    head_onehot = (group_ids[:, None] == jnp.arange(GROUPS, dtype=jnp.int32)[None, :]).astype(F32)
    row_heads = (first_row + jnp.arange(OWN, dtype=jnp.int32)) // P_SIZE
    row_onehot = (row_heads[:, None] == jnp.arange(H, dtype=jnp.int32)[None, :]).astype(F32)
    row_groups = jnp.dot(row_onehot, head_onehot, precision=HIGH)
    squares = jnp.dot(jnp.sum(grad_w * grad_w, axis=1), row_groups, precision=HIGH)
    gd_mine = jnp.sum(jnp.sum(gd_parts[:, :3, :H].astype(F32), axis=1), axis=0)
    note = jnp.concatenate([gd_mine, squares, jnp.zeros((N - H - GROUPS,), F32)])[None]
    note = jnp.sum(gathered(jnp.sum(gathered(note, "x"), axis=0), "y"), axis=0)[0]
    grad_d = note[:H]
    sumsq = note[H : H + GROUPS] + jnp.dot(grad_d * grad_d, head_onehot, precision=HIGH)
    counts = jnp.sum(head_onehot, axis=0)
    factor = jnp.minimum(
        1.0, 7.0 * jnp.sqrt(counts * (P_SIZE * D + 1.0) * tokens_all) / jnp.sqrt(sumsq + 1e-06)
    )
    clipped_w = grad_w * jnp.dot(row_groups, factor, precision=HIGH)[:, None]
    clipped_d = grad_d * jnp.dot(head_onehot, factor, precision=HIGH)
    return (gx[None], ga[None], gb[None], gc[None], clipped_w, clipped_d)


def solution(mesh):
    fine = Mesh(mesh.devices.reshape(4, 4, 8, 2), ("y", "x", "z", "core"))
    rows = ("y", "x")
    tokens = P(rows, SEQ, None)
    return jax.shard_map(
        per_device,
        mesh=fine,
        in_specs=(
            tokens, P(rows, None, SEQ), tokens, tokens, tokens, P(rows, None), P(), P(),
        ),
        out_specs=(tokens, P(rows, None, SEQ), tokens, tokens, P(rows, None), P()),
        check_vma=False,
    )
```

time: 730 us -> 386 us (0.53)
  the two profiles are of different devices: /device:TPU:2 before, /device:TPU:1 now
where the time goes in v1:
time: 386 us; the launch traced here: 381 us
  waiting for transfers between devices  110 us (28%)
  Pallas kernels  74.7 us (19%)
  starting transfers between devices  55.5 us (14%)
  local copies, waits for them, and re-layouts  45.5 us (12%)
  blocking collectives  44.1 us (11%)
  other arithmetic  25.3 us (7%)
  between operations  14.5 us (4%)
  matrix products  12.3 us (3%)
    all_to_all x5, waiting for transfers between devices, swap(): return lax.all_to_all(v, axis, 0, 0, tiled=True)  48 us
    all_to_all x1, blocking collectives, swap(): return lax.all_to_all(v, axis, 0, 0, tiled=True)  44.1 us
    all_to_all x2, waiting for transfers between devices, swap_seq(): got = lax.all_to_all(sent, SEQ, 0, 0, tiled=True)  33.5 us
    unnamed x80, local copies, waits for them, and re-layouts  28.1 us
    all_to_all x2, waiting for transfers between devices, back_seq(): return lax.all_to_all(states, SEQ, 0, 0, tiled=True).reshape(H * P_SIZE, N)  23 us
    pallas_call x1, Pallas kernels, backward(): pl.pallas_call(back_kernel, grid=(PAIRS,), in_specs=[wide(T), wide(T), wh...  22.8 us
    all_to_all x5, starting transfers between devices, swap(): return lax.all_to_all(v, axis, 0, 0, tiled=True)  21.5 us
    all_to_all x2, starting transfers between devices, swap_seq(): got = lax.all_to_all(sent, SEQ, 0, 0, tiled=True)  17.4 us
  transfers between devices with their start and end apart: 19, of which 10 were waited for; matrix products, arithmetic and copies ran while one was open for 13% of the time, Pallas kernels for 20%

profile of v1, /device:TPU:1, one launch (start us, length us, event | category | flops | bytes accessed | tf_op | source)
XLA Modules:
  0.0 381.4 jit_solution(7374959299325085843)
XLA Ops:
  12.5 11.0 %ends.1 = (f32[40,256]{1,0:T(8,128)S(1)}, f32[256,40]{1,0:T(8,128)S(1)}, bf16[2560,128]{1,0:T(8,128)(2,1)S(1)}) custom-call(f32[256,2560]{1,0:T(8,128)S(1)} %bitcast.109, f32[40,256]{1,0:T(8,128)S(1)} %bitcast.122, f32[256,128]{1,0:T(8,128)S(1)} %bitcast.117), custom_call_target="tpu_custom_call" | custom-call | flops 167772160 | bytes 2621440 | tf_op jit(solution)/shard_map/ends/pallas_call | solution.py:96
  25.3 10.0 %all-to-all-start = ((bf16[16,176,128]{2,1,0:T(8,128)(2,1)}), bf16[16,176,128]{2,1,0:T(8,128)(2,1)S(1)}, u32[]{:S(2)}, u32[]{:S(2)}) async-start(bf16[16,176,128]{2,1,0:T(8,128)(2,1)} %pad_maximum_fusion), calls=%async_computation | async-start | bytes 1441792 | tf_op jit(solution)/shard_map/all_to_all | solution.py:203
  35.3 21.3 %all-to-all-done = bf16[16,176,128]{2,1,0:T(8,128)(2,1)S(1)} async-done(((bf16[16,176,128]{2,1,0:T(8,128)(2,1)}), bf16[16,176,128]{2,1,0:T(8,128)(2,1)S(1)}, u32[]{:S(2)}, u32[]{:S(2)}) %all-to-all-start) | async-done | bytes 720928 | tf_op jit(solution)/shard_map/all_to_all | solution.py:203
  59.8 4.2 %all-to-all-start.1 = ((bf16[16,160,128]{2,1,0:T(8,128)(2,1)}), bf16[16,160,128]{2,1,0:T(8,128)(2,1)}, u32[]{:S(2)}, u32[]{:S(2)}) async-start(bf16[16,160,128]{2,1,0:T(8,128)(2,1)} %copy-done.8), calls=%async_computation.1 | async-start | bytes 1310720 | tf_op jit(solution)/shard_map/all_to_all | solution.py:208
  69.5 7.5 %intra.1.part_ref = f32[256,2560]{1,0:T(8,128)S(1)} custom-call(f32[256,2560]{1,0:T(8,128)S(1)} %bitcast.110, f32[40,256]{1,0:T(8,128)S(1)} %get-tuple-element.21.cum_ref, f32[256,40]{1,0:T(8,128)S(1)} %copy-done.14, f32[256,128]{1,0:T(8,128)S(1)} %bitcast.118, f32[256,128]{1,0:T(8,128)S(1)} %bitcast.113, f32[1,2560]{1,0:T(1,128)S(1)} %copy-done.25), custom_call_target="tpu_custom_call" | custom-call | flops 671088640 | bytes 5242880 | tf_op jit(solution)/shard_map/intra/pallas_call | solution.py:132
  78.5 4.6 %all-to-all-done.1 = bf16[16,160,128]{2,1,0:T(8,128)(2,1)} async-done(((bf16[16,160,128]{2,1,0:T(8,128)(2,1)}), bf16[16,160,128]{2,1,0:T(8,128)(2,1)}, u32[]{:S(2)}, u32[]{:S(2)}) %all-to-all-start.1) | async-done | bytes 655392 | tf_op jit(solution)/shard_map/all_to_all | solution.py:208
  86.6 12.4 %inter.1.yo_ref = bf16[256,2560]{1,0:T(8,128)(2,1)} custom-call(f32[256,2560]{1,0:T(8,128)S(1)} %copy-done.4, f32[256,40]{1,0:T(8,128)S(1)} %copy-done.15, f32[256,128]{1,0:T(8,128)S(1)} %bitcast.114, bf16[2560,128]{1,0:T(8,128)(2,1)} %bitcast.7.start_ref), custom_call_target="tpu_custom_call" | custom-call | flops 167772160 | bytes 3932160 | tf_op jit(solution)/shard_map/inter/pallas_call | solution.py:154
  103.0 6.2 %terms.1 = (bf16[4,4,160,640]{3,2,1,0:T(8,128)(2,1)S(1)}, bf16[4,4,160,640]{3,2,1,0:T(8,128)(2,1)S(1)}) custom-call(bf16[256,2560]{1,0:T(8,128)(2,1)} %inter.1.yo_ref, bf16[256,2560]{1,0:T(8,128)(2,1)} %collective-permute-done.yx_ref, bf16[256,1280]{1,0:T(8,128)(2,1)S(1)} %get-tuple-element.39.go_ref, bf16[256,1280]{1,0:T(8,128)(2,1)S(1)} %collective-permute-done.1.gx_ref), custom_call_target="tpu_custom_call" | custom-call | flops 3355443200 | bytes 9830400 | tf_op jit(solution)/shard_map/terms/pallas_call | solution.py:222
  114.4 44.1 %all_to_all.50 = bf16[4,4,160,640]{3,2,1,0:T(8,128)(2,1)} all-to-all(bf16[4,4,160,640]{3,2,1,0:T(8,128)(2,1)} %copy-done.6), channel_id=1, replica_groups=mesh['y'=4,'x'=4,'z'=8,'core'=2] {'y'}, dimensions={0} | all-to-all | bytes 6553600 | tf_op jit(solution)/shard_map/all_to_all | solution.py:369
  158.5 4.7 %all-to-all-start.4 = ((bf16[4,4,160,640]{3,2,1,0:T(8,128)(2,1)}), bf16[4,4,160,640]{3,2,1,0:T(8,128)(2,1)}, u32[]{:S(2)}, u32[]{:S(2)}) async-start(bf16[4,4,160,640]{3,2,1,0:T(8,128)(2,1)} %copy-done.5), calls=%async_computation.4 | async-start | bytes 6553600 | tf_op jit(solution)/shard_map/all_to_all | solution.py:369
  163.2 6.0 %convolution_convert_fusion = bf16[256,2560]{1,0:T(8,128)(2,1)} fusion(bf16[256,1280]{1,0:T(8,128)(2,1)} %copy-done.29, bf16[2560,1280]{1,0:T(8,128)(2,1)} %all-gather.2.cloned.1.call-done), kind=kOutput, calls=%fused_computation | convolution fusion | flops 1678376960 | bytes 8519680 | tf_op jit(solution)/shard_map/dot_general | solution.py:410
  174.0 27.0 %all-to-all-done.4 = bf16[4,4,160,640]{3,2,1,0:T(8,128)(2,1)} async-done(((bf16[4,4,160,640]{3,2,1,0:T(8,128)(2,1)}), bf16[4,4,160,640]{3,2,1,0:T(8,128)(2,1)}, u32[]{:S(2)}, u32[]{:S(2)}) %all-to-all-start.4) | async-done | bytes 3276832 | tf_op jit(solution)/shard_map/all_to_all | solution.py:369
  201.0 4.2 %all-to-all-start.7 = ((bf16[4,160,640]{2,1,0:T(8,128)(2,1)}), bf16[4,160,640]{2,1,0:T(8,128)(2,1)}, u32[]{:S(2)}, u32[]{:S(2)}) async-start(bf16[4,160,640]{2,1,0:T(8,128)(2,1)} %reduce_sum.131), calls=%async_computation.7 | async-start | bytes 1638400 | tf_op jit(solution)/shard_map/all_to_all | solution.py:369
  208.9 6.6 %all-to-all-done.7 = bf16[4,160,640]{2,1,0:T(8,128)(2,1)} async-done(((bf16[4,160,640]{2,1,0:T(8,128)(2,1)}), bf16[4,160,640]{2,1,0:T(8,128)(2,1)}, u32[]{:S(2)}, u32[]{:S(2)}) %all-to-all-start.7) | async-done | bytes 819232 | tf_op jit(solution)/shard_map/all_to_all | solution.py:369
  215.5 4.2 %all-to-all-start.5 = ((bf16[4,160,640]{2,1,0:T(8,128)(2,1)}), bf16[4,160,640]{2,1,0:T(8,128)(2,1)}, u32[]{:S(2)}, u32[]{:S(2)}) async-start(bf16[4,160,640]{2,1,0:T(8,128)(2,1)} %reduce_sum.129), calls=%async_computation.5 | async-start | bytes 1638400 | tf_op jit(solution)/shard_map/all_to_all | solution.py:369
  219.7 5.0 %fusion.34.own_ref = f32[256,2560]{1,0:T(8,128)S(1)} fusion(bf16[256,1280]{1,0:T(8,128)(2,1)} %copy-done.24, bf16[2560,1280]{1,0:T(8,128)(2,1)} %all-gather.2.cloned.1.call-done), kind=kOutput, calls=%fused_computation.85 | convolution fusion | flops 1677721600 | bytes 9830400 | tf_op jit(solution)/shard_map/dot_general | solution.py:412
  224.8 14.0 %entries.1 = (bf16[256,2560]{1,0:T(8,128)(2,1)S(1)}, bf16[2560,128]{1,0:T(8,128)(2,1)S(1)}, f32[1,2560]{1,0:T(1,128)S(1)}) custom-call(f32[256,2560]{1,0:T(8,128)S(1)} %fusion.34.own_ref, bf16[256,2560]{1,0:T(8,128)(2,1)} %collective-permute-done.2.other_ref, f32[256,2560]{1,0:T(8,128)S(1)} %bitcast.111, f32[256,40]{1,0:T(8,128)S(1)} %copy-done.16, ...), custom_call_target="tpu_custom_call" | custom-call | flops 167772160 | bytes 7864320 | tf_op jit(solution)/shard_map/entries/pallas_call | solution.py:246
  246.8 7.4 %all-to-all-start.2 = ((bf16[16,176,128]{2,1,0:T(8,128)(2,1)}), bf16[16,176,128]{2,1,0:T(8,128)(2,1)}, u32[]{:S(2)}, u32[]{:S(2)}) async-start(bf16[16,176,128]{2,1,0:T(8,128)(2,1)} %pad_maximum_fusion.1), calls=%async_computation.2 | async-start | bytes 1441792 | tf_op jit(solution)/shard_map/all_to_all | solution.py:203
  263.5 12.2 %all-to-all-done.2 = bf16[16,176,128]{2,1,0:T(8,128)(2,1)} async-done(((bf16[16,176,128]{2,1,0:T(8,128)(2,1)}), bf16[16,176,128]{2,1,0:T(8,128)(2,1)}, u32[]{:S(2)}, u32[]{:S(2)}) %all-to-all-start.2) | async-done | bytes 720928 | tf_op jit(solution)/shard_map/all_to_all | solution.py:203
  282.3 14.4 %all-to-all-done.8 = bf16[8,20,1280]{2,1,0:T(8,128)(2,1)} async-done(((bf16[8,20,1280]{2,1,0:T(8,128)(2,1)}), bf16[8,20,1280]{2,1,0:T(8,128)(2,1)}, u32[]{:S(2)}, u32[]{:S(2)}) %all-to-all-start.8) | async-done | bytes 409632 | tf_op jit(solution)/shard_map/all_to_all | solution.py:369
  296.7 4.4 %all-to-all-start.3 = ((bf16[16,160,128]{2,1,0:T(8,128)(2,1)}), bf16[16,160,128]{2,1,0:T(8,128)(2,1)}, u32[]{:S(2)}, u32[]{:S(2)}) async-start(bf16[16,160,128]{2,1,0:T(8,128)(2,1)} %copy-done.7), calls=%async_computation.3 | async-start | bytes 1310720 | tf_op jit(solution)/shard_map/all_to_all | solution.py:208
  302.8 18.4 %all-to-all-done.3 = bf16[16,160,128]{2,1,0:T(8,128)(2,1)} async-done(((bf16[16,160,128]{2,1,0:T(8,128)(2,1)}), bf16[16,160,128]{2,1,0:T(8,128)(2,1)}, u32[]{:S(2)}, u32[]{:S(2)}) %all-to-all-start.3) | async-done | bytes 655392 | tf_op jit(solution)/shard_map/all_to_all | solution.py:208
  323.1 4.2 %all-to-all-start.9 = ((bf16[16,20,1280]{2,1,0:T(8,128)(2,1)}), bf16[16,20,1280]{2,1,0:T(8,128)(2,1)}, u32[]{:S(2)}, u32[]{:S(2)}) async-start(bf16[16,20,1280]{2,1,0:T(8,128)(2,1)} %broadcast_in_dim.51), calls=%async_computation.9 | async-start | bytes 1966080 | tf_op jit(solution)/shard_map/all_to_all | solution.py:369
  332.5 22.8 %backward.1 = (f32[256,2560]{1,0:T(8,128)}, f32[40,256]{1,0:T(8,128)}, f32[256,128]{1,0:T(8,128)}, f32[256,128]{1,0:T(8,128)}) custom-call(f32[256,2560]{1,0:T(8,128)S(1)} %bitcast.112, bf16[256,2560]{1,0:T(8,128)(2,1)S(1)} %copy-done.19, f32[40,256]{1,0:T(8,128)S(1)} %get-tuple-element.21.cum_ref, f32[256,40]{1,0:T(8,128)S(1)} %copy-done.17, ...), custom_call_target="tpu_custom_call" | custom-call | flops 1342177280 | bytes 9175040 | tf_op jit(solution)/shard_map/backward/pallas_call | solution.py:336
  (156 shorter events, 90.2 us)
Async XLA Ops:
  7.2 107.2 %all-gather.2.cloned.1.call-start = ((), (), s32[]{:S(2)}) async-start(), calls=%async_computation.10 | async-start | bytes 6963200 | tf_op jit(solution)/shard_map/all_gather | solution.py:392
  25.3 31.3 %all-to-all-start = ((bf16[16,176,128]{2,1,0:T(8,128)(2,1)}), bf16[16,176,128]{2,1,0:T(8,128)(2,1)S(1)}, u32[]{:S(2)}, u32[]{:S(2)}) async-start(bf16[16,176,128]{2,1,0:T(8,128)(2,1)} %pad_maximum_fusion), calls=%async_computation | async-start | bytes 1441792 | tf_op jit(solution)/shard_map/all_to_all | solution.py:203
  57.5 6.5 %copy-start.31 = (f32[40]{0:T(128)S(1)}, f32[40]{0:T(128)}, u32[]{:S(2)}) copy-start(f32[40]{0:T(128)} %param.14) | copy-start | bytes 484
  57.5 8.6 %copy-start.2 = (f32[1,256,2560]{2,1,0:T(8,128)S(1)}, f32[1,256,2560]{2,1,0:T(8,128)}, u32[]{:S(2)}) copy-start(f32[1,256,2560]{2,1,0:T(8,128)} %param.8) | copy-start | bytes 7864324
  59.8 23.2 %all-to-all-start.1 = ((bf16[16,160,128]{2,1,0:T(8,128)(2,1)}), bf16[16,160,128]{2,1,0:T(8,128)(2,1)}, u32[]{:S(2)}, u32[]{:S(2)}) async-start(bf16[16,160,128]{2,1,0:T(8,128)(2,1)} %copy-done.8), calls=%async_computation.1 | async-start | bytes 1310720 | tf_op jit(solution)/shard_map/all_to_all | solution.py:208
  99.0 4.0 %collective-permute-start = (bf16[256,2560]{1,0:T(8,128)(2,1)}, bf16[256,2560]{1,0:T(8,128)(2,1)}, u32[]{:S(2)}, u32[]{:S(2)}) collective-permute-start(bf16[256,2560]{1,0:T(8,128)(2,1)} %inter.1.yo_ref), channel_id=1, source_target_pairs={{0,1},{1,0},{2,3},{3,2},{4,5},{5,4},{6,7},{7,6},{8,9},{9,8},{10,11... | collective-permute-start | bytes 3932168 | tf_op jit(solution)/shard_map/ppermute | solution.py:373
  100.4 2.6 collective-permute-start.1
  158.5 42.5 %all-to-all-start.4 = ((bf16[4,4,160,640]{3,2,1,0:T(8,128)(2,1)}), bf16[4,4,160,640]{3,2,1,0:T(8,128)(2,1)}, u32[]{:S(2)}, u32[]{:S(2)}) async-start(bf16[4,4,160,640]{3,2,1,0:T(8,128)(2,1)} %copy-done.5), calls=%async_computation.4 | async-start | bytes 6553600 | tf_op jit(solution)/shard_map/all_to_all | solution.py:369
  169.2 55.5 %collective-permute-start.2 = (bf16[256,2560]{1,0:T(8,128)(2,1)}, bf16[256,2560]{1,0:T(8,128)(2,1)}, u32[]{:S(2)}, u32[]{:S(2)}) collective-permute-start(bf16[256,2560]{1,0:T(8,128)(2,1)} %convolution_convert_fusion), channel_id=1, source_target_pairs={{0,1},{1,0},{2,3},{3,2},{4,5},{5,4},{6,7},{7,6},{8,9},{9,8},{10,11... | collective-permute-start | bytes 3932168 | tf_op jit(solution)/shard_map/ppermute | solution.py:373
  201.0 14.5 %all-to-all-start.7 = ((bf16[4,160,640]{2,1,0:T(8,128)(2,1)}), bf16[4,160,640]{2,1,0:T(8,128)(2,1)}, u32[]{:S(2)}, u32[]{:S(2)}) async-start(bf16[4,160,640]{2,1,0:T(8,128)(2,1)} %reduce_sum.131), calls=%async_computation.7 | async-start | bytes 1638400 | tf_op jit(solution)/shard_map/all_to_all | solution.py:369
  215.5 31.3 %all-to-all-start.5 = ((bf16[4,160,640]{2,1,0:T(8,128)(2,1)}), bf16[4,160,640]{2,1,0:T(8,128)(2,1)}, u32[]{:S(2)}, u32[]{:S(2)}) async-start(bf16[4,160,640]{2,1,0:T(8,128)(2,1)} %reduce_sum.129), calls=%async_computation.5 | async-start | bytes 1638400 | tf_op jit(solution)/shard_map/all_to_all | solution.py:369
  219.7 5.0 %copy-start.11 = (f32[1,256,128]{2,1,0:T(8,128)S(1)}, f32[1,256,128]{2,1,0:T(8,128)}, u32[]{:S(2)}) copy-start(f32[1,256,128]{2,1,0:T(8,128)} %param.11) | copy-start | bytes 393220
  246.8 28.8 %all-to-all-start.2 = ((bf16[16,176,128]{2,1,0:T(8,128)(2,1)}), bf16[16,176,128]{2,1,0:T(8,128)(2,1)}, u32[]{:S(2)}, u32[]{:S(2)}) async-start(bf16[16,176,128]{2,1,0:T(8,128)(2,1)} %pad_maximum_fusion.1), calls=%async_computation.2 | async-start | bytes 1441792 | tf_op jit(solution)/shard_map/all_to_all | solution.py:203
  275.7 21.0 %all-to-all-start.8 = ((bf16[8,20,1280]{2,1,0:T(8,128)(2,1)}), bf16[8,20,1280]{2,1,0:T(8,128)(2,1)}, u32[]{:S(2)}, u32[]{:S(2)}) async-start(bf16[8,20,1280]{2,1,0:T(8,128)(2,1)} %pad_maximum_fusion.2), calls=%async_computation.8 | async-start | bytes 983040 | tf_op jit(solution)/shard_map/all_to_all | solution.py:369
  296.7 24.5 %all-to-all-start.3 = ((bf16[16,160,128]{2,1,0:T(8,128)(2,1)}), bf16[16,160,128]{2,1,0:T(8,128)(2,1)}, u32[]{:S(2)}, u32[]{:S(2)}) async-start(bf16[16,160,128]{2,1,0:T(8,128)(2,1)} %copy-done.7), calls=%async_computation.3 | async-start | bytes 1310720 | tf_op jit(solution)/shard_map/all_to_all | solution.py:208
  302.8 24.5 %copy-start.32 = (s32[40]{0:T(128)S(1)}, s32[40]{0:T(128)}, u32[]{:S(2)}) copy-start(s32[40]{0:T(128)} %param.15) | copy-start | bytes 484
  302.8 25.7 %copy-start.26 = (f32[1,2560]{1,0:T(1,128)S(1)}, f32[1,2560]{1,0:T(1,128)}, u32[]{:S(2)}) copy-start(f32[1,2560]{1,0:T(1,128)} %broadcast_in_dim_reshape.3.skip_ref) | copy-start | bytes 30724
  323.1 32.2 %all-to-all-start.9 = ((bf16[16,20,1280]{2,1,0:T(8,128)(2,1)}), bf16[16,20,1280]{2,1,0:T(8,128)(2,1)}, u32[]{:S(2)}, u32[]{:S(2)}) async-start(bf16[16,20,1280]{2,1,0:T(8,128)(2,1)} %broadcast_in_dim.51), calls=%async_computation.9 | async-start | bytes 1966080 | tf_op jit(solution)/shard_map/all_to_all | solution.py:369
  357.2 7.7 %collective-permute-start.3 = (f32[1,128]{1,0:T(1,128)S(1)}, f32[1,128]{1,0:T(1,128)S(1)}, u32[]{:S(2)}, u32[]{:S(2)}) collective-permute-start(f32[1,128]{1,0:T(1,128)S(1)} %bitcast.128), channel_id=1, source_target_pairs={{16,0},{32,16},{48,32},{0,48},{17,1},{33,17},{49,33},{1,49},{18,2}... | collective-permute-start | bytes 1544 | tf_op jit(solution)/shard_map/ppermute | solution.py:380
  358.1 6.9 %collective-permute-start.4 = (f32[1,128]{1,0:T(1,128)S(1)}, f32[1,128]{1,0:T(1,128)S(1)}, u32[]{:S(2)}, u32[]{:S(2)}) collective-permute-start(f32[1,128]{1,0:T(1,128)S(1)} %bitcast.129), channel_id=1, source_target_pairs={{32,0},{48,16},{0,32},{16,48},{33,1},{49,17},{1,33},{17,49},{34,2}... | collective-permute-start | bytes 1544 | tf_op jit(solution)/shard_map/ppermute | solution.py:380
  359.3 5.7 %collective-permute-start.5 = (f32[1,128]{1,0:T(1,128)S(1)}, f32[1,128]{1,0:T(1,128)S(1)}, u32[]{:S(2)}, u32[]{:S(2)}) collective-permute-start(f32[1,128]{1,0:T(1,128)S(1)} %bitcast.130), channel_id=1, source_target_pairs={{48,0},{0,16},{16,32},{32,48},{49,1},{1,17},{17,33},{33,49},{50,2}... | collective-permute-start | bytes 1544 | tf_op jit(solution)/shard_map/ppermute | solution.py:380
  365.1 4.1 %collective-permute-start.6 = (f32[1,128]{1,0:T(1,128)S(1)}, f32[1,128]{1,0:T(1,128)S(1)}, u32[]{:S(2)}, u32[]{:S(2)}) collective-permute-start(f32[1,128]{1,0:T(1,128)S(1)} %bitcast.131), channel_id=1, source_target_pairs={{64,0},{128,64},{192,128},{0,192},{65,1},{129,65},{193,129},{1,193... | collective-permute-start | bytes 1544 | tf_op jit(solution)/shard_map/ppermute | solution.py:380
  368.0 3.9 %collective-permute-start.7 = (f32[1,128]{1,0:T(1,128)S(1)}, f32[1,128]{1,0:T(1,128)S(1)}, u32[]{:S(2)}, u32[]{:S(2)}) collective-permute-start(f32[1,128]{1,0:T(1,128)S(1)} %bitcast.132), channel_id=1, source_target_pairs={{128,0},{192,64},{0,128},{64,192},{129,1},{193,65},{1,129},{65,193... | collective-permute-start | bytes 1544 | tf_op jit(solution)/shard_map/ppermute | solution.py:380
  368.6 3.6 collective-permute-start.8
  (28 other events, 33.0 us)
Sparse Core Ops, SparseCore 0:
  10.4 71.3 all-gather.1

commit v2 on v1

v2 whole, which is shorter than its diff:
```python
import functools

import jax
import jax.numpy as jnp
from jax import lax
from jax.experimental import pallas as pl
from jax.experimental.pallas import tpu as pltpu
from jax.sharding import Mesh
from jax.sharding import PartitionSpec as P

D = 2560
H = 40
P_SIZE = 64
N = 128
T = 256
GROUPS = 4
PAIRS = H // 2
SEQ = ("z", "core")
N_SEQ = 16
OWN = H * P_SIZE // N_SEQ
HIGH = lax.Precision.HIGHEST
BF = jnp.bfloat16
F32 = jnp.float32
VMEM = 56 * 1024 * 1024
WIDE = 5
STEP = 2
ROWS = OWN + 16
TILES = 13


def nn(a, b):
    return lax.dot_general(a, b, (((1,), (0,)), ((), ())), preferred_element_type=F32)


def nt(a, b):
    return lax.dot_general(a, b, (((1,), (1,)), ((), ())), preferred_element_type=F32)


def tn(a, b):
    return lax.dot_general(a, b, (((0,), (0,)), ((), ())), preferred_element_type=F32)


def iota(shape, dim):
    return lax.broadcasted_iota(jnp.int32, shape, dim)


def whole(shape):
    return pl.BlockSpec(shape, lambda *_: (0,) * len(shape))


def wide(rows, pairs):
    return pl.BlockSpec((rows, pairs * 2 * P_SIZE), lambda p: (0, p))


def state_block(pairs):
    return pl.BlockSpec((pairs * 2 * P_SIZE, N), lambda p: (p, 0))


def smem():
    return pl.BlockSpec(memory_space=pltpu.SMEM)


def vmem():
    return pl.BlockSpec(memory_space=pltpu.VMEM)


def params():
    return pltpu.CompilerParams(vmem_limit_bytes=VMEM)


def cost(flops, moved, exps):
    return pl.CostEstimate(flops=flops, bytes_accessed=moved, transcendentals=exps)


def column(cum_t, head):
    return jnp.sum(jnp.where(iota(cum_t.shape, 1) == head, cum_t, 0.0), axis=1, keepdims=True)


def low_half(shape):
    return iota(shape, 1) < P_SIZE


def spread(cum_t, pair):
    return jnp.where(
        low_half((T, 2 * P_SIZE)), column(cum_t, 2 * pair), column(cum_t, 2 * pair + 1)
    )


def lanes_of(i):
    return slice(i * 2 * P_SIZE, (i + 1) * 2 * P_SIZE)


def put_states(out_ref, states, first, pairs):
    chunks = pairs * 2 * P_SIZE // OWN
    rows = states.astype(BF).reshape(chunks, OWN, N)
    out_ref[pl.ds(first * 2 * P_SIZE // OWN, chunks), :OWN, :] = rows


def put_note(out_ref, pieces):
    at = iota((16, N), 0)
    note = jnp.zeros((16, N), F32)
    for i, piece in enumerate(pieces):
        note = jnp.where(at == i, piece, note)
    for s in range(N_SEQ):
        out_ref[s, OWN:, :] = note.astype(BF)


def ends_kernel(x_ref, a_ref, b_ref, cum_ref, cum_t_ref, out_ref):
    step = pl.program_id(0)

    @pl.when(step == 0)
    def _():
        a = a_ref[...]
        upto = (iota((T, T), 0) <= iota((T, T), 1)).astype(F32)
        cum_ref[...] = jnp.dot(a, upto, precision=HIGH, preferred_element_type=F32)
        down = (iota((T, T), 1) <= iota((T, T), 0)).astype(F32)
        cum_t = lax.dot_general(
            down, a, (((1,), (1,)), ((), ())), precision=HIGH, preferred_element_type=F32
        )
        cum_t_ref[...] = cum_t
        total = jnp.concatenate([cum_t[T - 1 :, :], jnp.zeros((1, N - H), F32)], axis=1)
        hi = jnp.floor(total)
        mid = jnp.floor((total - hi) * 256.0) / 256.0
        put_note(out_ref, (hi, mid, total - hi - mid))

    cum_t = cum_t_ref[...]
    b = b_ref[...].astype(BF)
    found = []
    for i in range(WIDE):
        cum = spread(cum_t, step * WIDE + i)
        tail = jnp.exp(cum[T - 1 : T, :] - cum)
        found.append(tn((x_ref[:, lanes_of(i)] * tail).astype(BF), b))
    put_states(out_ref, jnp.concatenate(found, axis=0), step * WIDE, WIDE)


def local_ends(x, a, b):
    return pl.pallas_call(
        ends_kernel,
        grid=(PAIRS // WIDE,),
        in_specs=[wide(T, WIDE), whole((H, T)), whole((T, N))],
        out_specs=[whole((H, T)), whole((T, H)), whole((N_SEQ, ROWS, N))],
        out_shape=[
            jax.ShapeDtypeStruct((H, T), F32),
            jax.ShapeDtypeStruct((T, H), F32),
            jax.ShapeDtypeStruct((N_SEQ, ROWS, N), BF),
        ],
        compiler_params=params(),
        cost_estimate=cost(2 * T * D * N, 4 * T * D, T * D),
        name="ends",
    )(x, a, b)


def intra_kernel(x_ref, cum_ref, cum_t_ref, b_ref, c_ref, skip_ref, y_ref, scores):
    step = pl.program_id(0)

    @pl.when(step == 0)
    def _():
        keep = iota((T, T), 0) >= iota((T, T), 1)
        scores[...] = jnp.where(keep, nt(c_ref[...].astype(BF), b_ref[...].astype(BF)), 0.0)

    for i in range(STEP):
        x = x_ref[:, lanes_of(i)]
        xb = x.astype(BF)
        low = low_half(x.shape)
        head = 2 * (step * STEP + i)
        parts = []
        for k in range(2):
            diff = column(cum_t_ref[...], head + k) - cum_ref[pl.ds(head + k, 1), :]
            mixed = (jnp.exp(jnp.minimum(diff, 0.0)) * scores[...]).astype(BF)
            parts.append(nn(mixed, xb))
        skip = jnp.where(low, skip_ref[head], skip_ref[head + 1])
        y_ref[:, lanes_of(i)] = jnp.where(low, parts[0], parts[1]) + skip * x


def intra(x, cum, cum_t, b, c, skip):
    return pl.pallas_call(
        intra_kernel,
        grid=(PAIRS // STEP,),
        in_specs=[
            wide(T, STEP), whole((H, T)), whole((T, H)), whole((T, N)), whole((T, N)), smem(),
        ],
        out_specs=wide(T, STEP),
        out_shape=jax.ShapeDtypeStruct((T, D), F32),
        scratch_shapes=[pltpu.VMEM((T, T), F32)],
        compiler_params=params(),
        cost_estimate=cost(4 * T * T * D, 8 * T * D, H * T * T),
        name="intra",
    )(x, cum, cum_t, b, c, skip)


def inter_kernel(part_ref, cum_t_ref, c_ref, start_ref, y_ref):
    step = pl.program_id(0)
    cum_t = cum_t_ref[...]
    read = nt(c_ref[...].astype(BF), start_ref[...])
    for i in range(WIDE):
        grow = jnp.exp(spread(cum_t, step * WIDE + i))
        at = lanes_of(i)
        y_ref[:, at] = (part_ref[:, at] + grow * read[:, at]).astype(BF)


def inter(part, cum_t, c, start):
    return pl.pallas_call(
        inter_kernel,
        grid=(PAIRS // WIDE,),
        in_specs=[wide(T, WIDE), whole((T, H)), whole((T, N)), state_block(WIDE)],
        out_specs=wide(T, WIDE),
        out_shape=jax.ShapeDtypeStruct((T, D), BF),
        compiler_params=params(),
        cost_estimate=cost(2 * T * D * N, 6 * T * D, T * D),
        name="inter",
    )(part, cum_t, c, start)


def chain_kernel(reverse, mine_ref, parts_ref, totals_ref, out_ref):
    owner = (mine_ref[0] * OWN + iota((OWN, N), 0)) // P_SIZE == iota((OWN, N), 1)
    carry = jnp.zeros((OWN, N), F32)
    for s in range(N_SEQ - 1, -1, -1) if reverse else range(N_SEQ):
        out_ref[s] = carry.astype(BF)
        pieces = totals_ref[s, OWN:, :].astype(F32)
        total = pieces[0:1, :] + pieces[1:2, :] + pieces[2:3, :]
        decay = jnp.sum(jnp.where(owner, total, 0.0), axis=1, keepdims=True)
        carry = jnp.exp(decay) * carry + parts_ref[s, :OWN, :].astype(F32)


def chain(parts, totals, mine, reverse):
    return pl.pallas_call(
        functools.partial(chain_kernel, reverse),
        in_specs=[smem(), vmem(), vmem()],
        out_specs=vmem(),
        out_shape=jax.ShapeDtypeStruct((N_SEQ, OWN, N), BF),
        compiler_params=params(),
        cost_estimate=cost(4 * N_SEQ * OWN * N, 4 * N_SEQ * OWN * N, N_SEQ * OWN),
        name="chain",
    )(mine, parts, totals)


def swap(v, axis):
    return lax.all_to_all(v, axis, 0, 0, tiled=True)


def term_kernel(at_ref, yo_ref, yx_ref, go_ref, gx_ref, first_ref, second_ref):
    step = pl.program_id(0)
    half = go_ref.shape[1] // 2
    for i in range(2):
        cols = slice(i * half, (i + 1) * half)
        term = tn(yo_ref[...], go_ref[:, cols]) + tn(yx_ref[...], gx_ref[:, cols])
        term = term.astype(BF)
        for k in range(4):
            rel = (k + 4 - at_ref[1]) % 4
            rows = term[k * OWN : (k + 1) * OWN, :]
            if i == 0:
                first_ref[rel, step] = rows
            else:
                second_ref[0, rel] = rows


def terms(at, y_own, y_other, g_own, g_other):
    rows = pl.BlockSpec((T, 4 * OWN), lambda i, at: (0, (at[0] + i) % 4))
    half = g_own.shape[1] // 2
    return pl.pallas_call(
        term_kernel,
        grid_spec=pltpu.PrefetchScalarGridSpec(
            num_scalar_prefetch=1,
            grid=(4,),
            in_specs=[rows, rows, whole(g_own.shape), whole(g_own.shape)],
            out_specs=[
                whole((4, 4, OWN, half)),
                pl.BlockSpec((1, 4, OWN, half), lambda i, at: (i, 0, 0, 0)),
            ],
        ),
        out_shape=[jax.ShapeDtypeStruct((4, 4, OWN, half), BF)] * 2,
        compiler_params=params(),
        cost_estimate=cost(4 * T * D * D // 2, 3 * D * D // 2, 0),
        name="terms",
    )(at, y_own, y_other, g_own, g_other)


def entry_kernel(own_ref, other_ref, x_ref, cum_t_ref, c_ref, gy_ref, out_ref, sums):
    step = pl.program_id(0)
    cum_t = cum_t_ref[...]
    c = c_ref[...].astype(BF)
    found = []
    for i in range(WIDE):
        at = lanes_of(i)
        gy = own_ref[:, at] + other_ref[:, at].astype(F32)
        gy_ref[:, at] = gy.astype(BF)
        sums[pl.ds(step * WIDE + i, 1), :] = jnp.sum(gy * x_ref[:, at], axis=0, keepdims=True)
        grow = jnp.exp(spread(cum_t, step * WIDE + i))
        found.append(tn((gy * grow).astype(BF), c))
    put_states(out_ref, jnp.concatenate(found, axis=0), step * WIDE, WIDE)

    @pl.when(step == PAIRS // WIDE - 1)
    def _():
        total = sums[...]
        low = low_half(total.shape)
        head = 2 * iota(total.shape, 0)
        lane = iota(total.shape, 1)
        even = jnp.sum(jnp.where(low, total, 0.0), axis=1, keepdims=True)
        odd = jnp.sum(jnp.where(low, 0.0, total), axis=1, keepdims=True)
        each = jnp.where(lane == head, even, 0.0) + jnp.where(lane == head + 1, odd, 0.0)
        gd = jnp.sum(each, axis=0, keepdims=True)
        hi = gd.astype(BF).astype(F32)
        mid = (gd - hi).astype(BF).astype(F32)
        put_note(out_ref, (hi, mid, gd - hi - mid))


def entries(own, other, x, cum_t, c):
    return pl.pallas_call(
        entry_kernel,
        grid=(PAIRS // WIDE,),
        in_specs=[wide(T, WIDE), wide(T, WIDE), wide(T, WIDE), whole((T, H)), whole((T, N))],
        out_specs=[wide(T, WIDE), whole((N_SEQ, ROWS, N))],
        out_shape=[
            jax.ShapeDtypeStruct((T, D), BF),
            jax.ShapeDtypeStruct((N_SEQ, ROWS, N), BF),
        ],
        scratch_shapes=[pltpu.VMEM((PAIRS, 2 * P_SIZE), F32)],
        compiler_params=params(),
        cost_estimate=cost(2 * T * D * N, 12 * T * D, T * D),
        name="entries",
    )(own, other, x, cum_t, c)


def back_kernel(
    x_ref, gy_ref, cum_ref, cum_t_ref, b_ref, c_ref, skip_ref, start_ref, last_ref,
    gx_ref, ga_ref, gb_ref, gc_ref,
    scores, d_scores, rows, cols, tails, totals,
):
    step = pl.program_id(0)
    bb = b_ref[...].astype(BF)
    cb = c_ref[...].astype(BF)

    @pl.when(step == 0)
    def _():
        keep = iota((T, T), 1) >= iota((T, T), 0)
        scores[...] = jnp.where(keep, nt(bb, cb), 0.0)
        d_scores[...] = jnp.zeros_like(d_scores)
        cols[...] = jnp.zeros_like(cols)
        tails[...] = jnp.zeros_like(tails)
        gb_ref[...] = jnp.zeros_like(gb_ref)
        gc_ref[...] = jnp.zeros_like(gc_ref)

    lanes = iota((T, N), 1)
    low = low_half((T, 2 * P_SIZE))
    for i in range(STEP):
        pair = step * STEP + i
        at = lanes_of(i)
        x = x_ref[:, at]
        gyb = gy_ref[:, at]
        gy = gyb.astype(F32)
        parts = []
        sides = []
        for k in range(2):
            head = 2 * pair + k
            side = column(cum_t_ref[...], head)
            sides.append(side)
            diff = cum_ref[pl.ds(head, 1), :] - side
            weights = jnp.exp(jnp.minimum(diff, 0.0))
            mine = jnp.where(low if k == 0 else ~low, x, 0.0).astype(BF)
            d_mixed = weights * nt(mine, gyb)
            d_scores[...] += d_mixed
            parts.append(nn((weights * scores[...]).astype(BF), gyb))
            change = d_mixed * scores[...]
            rows[pl.ds(head, 1), :] = jnp.sum(change, axis=0, keepdims=True)
            down = jnp.sum(change, axis=1, keepdims=True)
            cols[...] -= jnp.where(lanes == head, down, 0.0)
        cum = jnp.where(low, sides[0], sides[1])
        grow = jnp.exp(cum)
        tail = jnp.exp(cum[T - 1 : T, :] - cum)
        states = slice(i * 2 * P_SIZE, (i + 1) * 2 * P_SIZE)
        start = start_ref[states, :]
        last = last_ref[states, :]
        pick = (lanes[:N] == 2 * pair + iota((N, N), 0) // P_SIZE).astype(BF)
        grown = gy * grow
        cols[...] += nn((grown * nt(cb, start)).astype(BF), pick)
        gc_ref[...] += nn(grown.astype(BF), start)
        faded = x * tail
        back = nt(bb, last)
        tails[...] += nn((faded * back).astype(BF), pick)
        gb_ref[...] += nn(faded.astype(BF), last)
        skip = jnp.where(low, skip_ref[2 * pair], skip_ref[2 * pair + 1])
        gx_ref[:, at] = jnp.where(low, parts[0], parts[1]) + tail * back + skip * gy
        both = start.astype(F32) * last.astype(F32)
        for k in range(2):
            part = both[k * P_SIZE : (k + 1) * P_SIZE, :]
            totals[pl.ds(2 * pair + k, 1), :] = jnp.sum(part, axis=0, keepdims=True)

    @pl.when(step == PAIRS // STEP - 1)
    def _():
        keep = iota((T, T), 1) >= iota((T, T), 0)
        ds = jnp.where(keep, d_scores[...], 0.0).astype(BF)
        gb_ref[...] += nn(ds, cb)
        gc_ref[...] += tn(ds, bb)
        after = (iota((T, T), 0) >= iota((T, T), 1)).astype(F32)
        before = (iota((T, T), 0) < iota((T, T), 1)).astype(F32)
        dims = (((0,), (0,)), ((), ()))
        ga = jnp.dot(rows[...], after, precision=HIGH, preferred_element_type=F32)
        up = lax.dot_general(cols[...], after, dims, precision=HIGH, preferred_element_type=F32)
        up += lax.dot_general(tails[...], before, dims, precision=HIGH, preferred_element_type=F32)
        whole_decay = jnp.exp(cum_ref[:, T - 1 : T])
        ga_ref[...] = ga + up[:H] + whole_decay * jnp.sum(totals[...], axis=1, keepdims=True)


def backward(x, gy, cum, cum_t, b, c, skip, start, last):
    return pl.pallas_call(
        back_kernel,
        grid=(PAIRS // STEP,),
        in_specs=[
            wide(T, STEP), wide(T, STEP), whole((H, T)), whole((T, H)), whole((T, N)),
            whole((T, N)), smem(), state_block(STEP), state_block(STEP),
        ],
        out_specs=[wide(T, STEP), whole((H, T)), whole((T, N)), whole((T, N))],
        out_shape=[
            jax.ShapeDtypeStruct((T, D), F32),
            jax.ShapeDtypeStruct((H, T), F32),
            jax.ShapeDtypeStruct((T, N), F32),
            jax.ShapeDtypeStruct((T, N), F32),
        ],
        scratch_shapes=[
            pltpu.VMEM((T, T), F32),
            pltpu.VMEM((T, T), F32),
            pltpu.VMEM((H, T), F32),
            pltpu.VMEM((T, N), F32),
            pltpu.VMEM((T, N), F32),
            pltpu.VMEM((H, N), F32),
        ],
        compiler_params=params(),
        cost_estimate=cost(8 * T * T * D, 14 * T * D, H * T * T),
        name="backward",
    )(x, gy, cum, cum_t, b, c, skip, start, last)


def fold_kernel(a0, a1, a2, b0, b1, b2, out_ref):
    sums = []
    for parts in ((a0, a1, a2), (b0, b1, b2)):
        total = parts[0][...].astype(F32) + parts[1][...].astype(F32) + parts[2][...].astype(F32)
        sums.append(total.astype(BF))
    for q in range(8 * TILES):
        r, c = divmod(q, 10)
        if r < 10:
            tile = sums[c // 5][16 * r : 16 * r + 16, 128 * (c % 5) : 128 * (c % 5) + 128]
        else:
            tile = jnp.zeros((16, 128), BF)
        out_ref[q // TILES, q % TILES] = tile


def fold(parts):
    return pl.pallas_call(
        fold_kernel,
        in_specs=[vmem()] * 6,
        out_specs=vmem(),
        out_shape=jax.ShapeDtypeStruct((8, TILES, 16, 128), BF),
        compiler_params=params(),
        cost_estimate=cost(4 * OWN * D // 2, 8 * OWN * D // 2, 0),
        name="fold",
    )(*parts)


def zsum_kernel(parts_ref, out_ref):
    total = parts_ref[0].astype(F32)
    for z in range(1, 8):
        total += parts_ref[z].astype(F32)
    for s in range(N_SEQ):
        out_ref[s] = total.astype(BF)


def zsum(parts):
    return pl.pallas_call(
        zsum_kernel,
        in_specs=[vmem()],
        out_specs=vmem(),
        out_shape=jax.ShapeDtypeStruct((N_SEQ, TILES, 16, 128), BF),
        compiler_params=params(),
        cost_estimate=cost(8 * OWN * 160, 6 * OWN * D, 0),
        name="zsum",
    )(parts)


def tile_of(ref, r, c, core):
    z, i = divmod(10 * r + c, TILES)
    return ref[2 * z + core, i].astype(F32)


def row_groups(row0, ids_ref):
    heads = (row0 + iota((OWN, N), 0)) // P_SIZE == iota((OWN, N), 1)
    return jnp.sum(jnp.where(heads, ids_ref[...], 0.0), axis=1, keepdims=True)


def squares_kernel(row0_ref, ids_ref, tiles_ref, got_ref, note_ref):
    found = []
    for r in range(10):
        total = jnp.zeros((16, 128), F32)
        for core in range(2):
            for c in range(10):
                tile = tile_of(tiles_ref, r, c, core)
                total += tile * tile
        found.append(jnp.sum(total, axis=1, keepdims=True))
    squares = jnp.concatenate(found, axis=0)
    place = iota((OWN, N), 1) - H == row_groups(row0_ref[0], ids_ref).astype(jnp.int32)
    note = jnp.sum(jnp.where(place, squares, 0.0), axis=0, keepdims=True)
    for s in range(N_SEQ):
        pieces = got_ref[s, OWN:, :].astype(F32)
        note += pieces[0:1, :] + pieces[1:2, :] + pieces[2:3, :]
    note_ref[...] = note


def squares(row0, ids, tiles, got):
    return pl.pallas_call(
        squares_kernel,
        in_specs=[smem(), vmem(), vmem(), vmem()],
        out_specs=vmem(),
        out_shape=jax.ShapeDtypeStruct((1, N), F32),
        compiler_params=params(),
        cost_estimate=cost(2 * OWN * D, 2 * OWN * D, 0),
        name="squares",
    )(row0, ids, tiles, got)


def clip_kernel(tokens_all, row0_ref, ids_ref, tiles_ref, note_ref, w_ref, d_ref):
    ids = ids_ref[...]
    lane = iota((1, N), 1)
    note = note_ref[...]
    grad_d = jnp.where(lane < H, note, 0.0)
    groups = row_groups(row0_ref[0], ids_ref)
    w_factor = jnp.zeros((OWN, 1), F32)
    d_factor = jnp.zeros((1, N), F32)
    for g in range(GROUPS):
        here = (ids == float(g)) & (lane < H)
        count = jnp.sum(jnp.where(here, 1.0, 0.0), axis=1, keepdims=True)
        sumsq = jnp.sum(jnp.where(lane == H + g, note, 0.0), axis=1, keepdims=True)
        sumsq += jnp.sum(jnp.where(here, grad_d * grad_d, 0.0), axis=1, keepdims=True)
        bound = 7.0 * jnp.sqrt(count * (P_SIZE * D + 1.0) * tokens_all)
        factor = jnp.minimum(1.0, bound / jnp.sqrt(sumsq + 1e-06))
        w_factor += jnp.where(groups == float(g), factor, 0.0)
        d_factor += jnp.where(here, factor, 0.0)
    d_ref[...] = grad_d * d_factor
    for r in range(10):
        scale = w_factor[16 * r : 16 * r + 16, :]
        for core in range(2):
            for c in range(10):
                col = core * (D // 2) + 128 * c
                w_ref[16 * r : 16 * r + 16, col : col + 128] = (
                    tile_of(tiles_ref, r, c, core) * scale
                )


def clip(tokens_all, row0, ids, tiles, note):
    return pl.pallas_call(
        functools.partial(clip_kernel, tokens_all),
        in_specs=[smem(), vmem(), vmem(), vmem()],
        out_specs=[vmem(), vmem()],
        out_shape=[jax.ShapeDtypeStruct((OWN, D), F32), jax.ShapeDtypeStruct((1, N), F32)],
        compiler_params=params(),
        cost_estimate=cost(2 * OWN * D, 6 * OWN * D, 0),
        name="clip",
    )(row0, ids, tiles, note)


def shifted(v, axis, d):
    return lax.ppermute(v, axis, [(i, (i + d) % 4) for i in range(4)])


def plus(a, b):
    return (a.astype(F32) + b.astype(F32)).astype(BF)


def relay(t, axis):
    m = t.shape[1] // 2
    ra = shifted(t[2, :m], axis, 1)
    rb = shifted(t[2, m:], axis, -1)
    up = jnp.concatenate([plus(t[1, :m], ra), t[1, m:]], axis=0)
    down = jnp.concatenate([t[3, :m], plus(t[3, m:], rb)], axis=0)
    return t[0], shifted(up, axis, 1), shifted(down, axis, -1)


def three_sum(parts):
    return (parts[0].astype(F32) + parts[1].astype(F32) + parts[2].astype(F32)).astype(BF)


def other_core(v):
    return lax.ppermute(v, "core", [(0, 1), (1, 0)])


def sum_over(v, axis):
    for bit in (1, 2):
        v = v + lax.ppermute(v, axis, [(i, i ^ bit) for i in range(4)])
    return v


def per_device(x_in, a_log, b_in, c_in, g_out, w_out, d_skip, group_ids):
    x, a, b, c, g = (x_in[0], a_log[0], b_in[0], c_in[0], g_out[0])
    core = lax.axis_index("core")
    half = D // 2
    at = jnp.stack([lax.axis_index("y"), lax.axis_index("x")]).astype(jnp.int32)
    mine = (2 * lax.axis_index("z") + core).reshape(1).astype(jnp.int32)
    row0 = ((4 * at[0] + at[1]) * OWN).reshape(1)
    ids = jnp.pad(group_ids.astype(F32), (0, N - H), constant_values=-1.0)[None]
    tokens_all = float(T * N_SEQ * 16)

    w_mine = lax.dynamic_slice_in_dim(w_out, core * half, half, axis=1)
    w_half = lax.all_gather(w_mine, ("y", "x"), axis=0, tiled=True)
    g_mine = lax.dynamic_slice_in_dim(g, core * half, half, axis=1)
    g_other = other_core(lax.dynamic_slice_in_dim(g, (1 - core) * half, half, axis=1))

    cum, cum_t, sent = local_ends(x, a, b)
    got = swap(sent, SEQ)
    y_part = intra(x, cum, cum_t, b, c, d_skip)
    start = swap(chain(got, got, mine, False), SEQ).reshape(H * P_SIZE, N)
    y_own = inter(y_part, cum_t, c, start)
    y_other = other_core(y_own)
    first, second = terms(at, y_own, y_other, g_mine, g_other)
    w_half, first, second = lax.optimization_barrier((w_half, first, second))

    first = relay(first, "x")
    second = relay(second, "y")
    dims = (((1,), (1,)), ((), ()))
    gy_other = lax.dot_general(g_other, w_half, dims, preferred_element_type=F32).astype(BF)
    gy_other = other_core(gy_other)
    gy_own = lax.dot_general(g_mine, w_half, dims, preferred_element_type=F32)
    gy, sent_back = entries(gy_own, gy_other, x, cum_t, c)
    got_back = swap(sent_back, SEQ)

    first = relay(three_sum(first), "y")
    second = relay(three_sum(second), "x")
    last = swap(chain(got_back, got, mine, True), SEQ).reshape(H * P_SIZE, N)
    tiles = swap(fold(first + second), "z")
    tiles = swap(zsum(tiles), SEQ)

    gx, ga, gb, gc = backward(x, gy, cum, cum_t, b, c, d_skip, start, last)

    note = squares(row0, ids, tiles, got_back)
    note = sum_over(sum_over(note, "x"), "y")
    clipped_w, clipped_d = clip(tokens_all, row0, ids, tiles, note)
    return (gx[None], ga[None], gb[None], gc[None], clipped_w, clipped_d[0, :H])


def solution(mesh):
    fine = Mesh(mesh.devices.reshape(4, 4, 8, 2), ("y", "x", "z", "core"))
    rows = ("y", "x")
    tokens = P(rows, SEQ, None)
    return jax.shard_map(
        per_device,
        mesh=fine,
        in_specs=(
            tokens, P(rows, None, SEQ), tokens, tokens, tokens, P(rows, None), P(), P(),
        ),
        out_specs=(tokens, P(rows, None, SEQ), tokens, tokens, P(rows, None), P()),
        check_vma=False,
    )
```

time: 386 us -> 279 us (0.72)
  blocking collectives: 44.1 us -> 0 us
  local copies, waits for them, and re-layouts: 45.5 us -> 13 us
  other arithmetic: 25.3 us -> 3.31 us
  starting transfers between devices: 55.5 us -> 65.6 us
  Pallas kernels: 74.7 us -> 65.6 us
  waiting for transfers between devices: 110 us -> 104 us
    all_to_all x4 -> x0, waiting for transfers between devices: 56.5 us -> none  [the longest x2 33.5 us: swap_seq(): got = lax.all_to_all(sent, SEQ, 0, 0, tiled=True)]
    all_to_all x1 -> x0, blocking collectives: 44.1 us -> none  [swap(): return lax.all_to_all(v, axis, 0, 0, tiled=True)]
    ppermute x6 -> x20, waiting for transfers between devices: 3.01 us -> 30 us  [the longest x16 20.3 us: shifted(): return lax.ppermute(v, axis, [(i, (i + d) % 4) for i in range(4)])]
    all_to_all x4 -> x0, starting transfers between devices: 25.9 us -> none  [the longest x2 17.4 us: swap_seq(): got = lax.all_to_all(sent, SEQ, 0, 0, tiled=True)]
    all_to_all x5 -> x6, waiting for transfers between devices: 48 us -> 72 us  [swap(): return lax.all_to_all(v, axis, 0, 0, tiled=True)]
    unnamed x80 -> x40, local copies, waits for them, and re-layouts: 28.1 us -> 6.32 us
    ppermute x6 -> x20, starting transfers between devices: 6.21 us -> 25.9 us  [the longest x16 21.6 us: shifted(): return lax.ppermute(v, axis, [(i, (i + d) % 4) for i in range(4)])]
    reduce_sum x12 -> x0, other arithmetic: 16.3 us -> none  [the longest x5 13 us: add_up(): return jnp.sum(parts.astype(F32), axis=0)]
  transfers between devices with their start and end apart: 19 -> 30, of which waited for: 10 -> 13; matrix products, arithmetic and copies ran while one was open for 13% -> 6% of each run, Pallas kernels for 20% -> 18%
where the time goes in v2:
time: 279 us; the launch traced here: 275 us
  waiting for transfers between devices  104 us (37%)
  starting transfers between devices  65.6 us (24%)
  Pallas kernels  65.6 us (24%)
  between operations  14.4 us (5%)
  local copies, waits for them, and re-layouts  13 us (5%)
  matrix products  9.19 us (3%)
  other arithmetic  3.31 us (1%)
    all_to_all x6, waiting for transfers between devices, swap(): return lax.all_to_all(v, axis, 0, 0, tiled=True)  72 us
    all_to_all x6, starting transfers between devices, swap(): return lax.all_to_all(v, axis, 0, 0, tiled=True)  37.2 us
    ppermute x16, starting transfers between devices, shifted(): return lax.ppermute(v, axis, [(i, (i + d) % 4) for i in range(4)])  21.6 us
    ppermute x16, waiting for transfers between devices, shifted(): return lax.ppermute(v, axis, [(i, (i + d) % 4) for i in range(4)])  20.3 us
    pallas_call x1, Pallas kernels, backward(): pl.pallas_call(back_kernel, grid=(PAIRS // STEP,), in_specs=[wide(T, STEP...  16 us
    ppermute x4, waiting for transfers between devices, sum_over(): v = v + lax.ppermute(v, axis, [(i, i ^ bit) for i in range(4)])  9.7 us
    pallas_call x1, Pallas kernels, terms(): pl.pallas_call(term_kernel, grid_spec=pltpu.PrefetchScalarGridSpec(num_sc...  9.34 us
    pallas_call x1, Pallas kernels, intra(): pl.pallas_call(intra_kernel, grid=(PAIRS // STEP,), in_specs=[wide(T, STE...  9.15 us
  transfers between devices with their start and end apart: 30, of which 13 were waited for; matrix products, arithmetic and copies ran while one was open for 6% of the time, Pallas kernels for 18%

profile of v2, /device:TPU:1, one launch (start us, length us, event | category | flops | bytes accessed | tf_op | source)
XLA Modules:
  0.0 275.1 jit_solution(12433011737623247332)
XLA Ops:
  9.1 5.7 %ends.1 = (f32[40,256]{1,0:T(8,128)}, f32[256,40]{1,0:T(8,128)}, bf16[16,176,128]{2,1,0:T(8,128)(2,1)}) custom-call(f32[256,2560]{1,0:T(8,128)} %bitcast.100, f32[40,256]{1,0:T(8,128)} %bitcast.114, f32[256,128]{1,0:T(8,128)} %bitcast.111), custom_call_target="tpu_custom_call" | custom-call | flops 167772160 | bytes 2621440 | tf_op jit(solution)/shard_map/ends/pallas_call | solution.py:137
  14.8 10.0 %all-to-all-start = ((bf16[16,176,128]{2,1,0:T(8,128)(2,1)}), bf16[16,176,128]{2,1,0:T(8,128)(2,1)S(1)}, u32[]{:S(2)}, u32[]{:S(2)}) async-start(bf16[16,176,128]{2,1,0:T(8,128)(2,1)} %get-tuple-element.24), calls=%async_computation | async-start | bytes 1441792 | tf_op jit(solution)/shard_map/all_to_all | solution.py:238
  24.8 21.3 %all-to-all-done.parts_ref.totals_ref = bf16[16,176,128]{2,1,0:T(8,128)(2,1)S(1)} async-done(((bf16[16,176,128]{2,1,0:T(8,128)(2,1)}), bf16[16,176,128]{2,1,0:T(8,128)(2,1)S(1)}, u32[]{:S(2)}, u32[]{:S(2)}) %all-to-all-start) | async-done | bytes 720928 | tf_op jit(solution)/shard_map/all_to_all | solution.py:238
  49.6 3.5 %all-to-all-start.1 = ((bf16[16,160,128]{2,1,0:T(8,128)(2,1)}), bf16[16,160,128]{2,1,0:T(8,128)(2,1)S(1)}, u32[]{:S(2)}, u32[]{:S(2)}) async-start(bf16[16,160,128]{2,1,0:T(8,128)(2,1)} %chain.2), calls=%async_computation.1 | async-start | bytes 1310720 | tf_op jit(solution)/shard_map/all_to_all | solution.py:238
  53.1 9.2 %intra.1.part_ref = f32[256,2560]{1,0:T(8,128)} custom-call(f32[256,2560]{1,0:T(8,128)} %bitcast.101, f32[40,256]{1,0:T(8,128)} %get-tuple-element.22.cum_ref, f32[256,40]{1,0:T(8,128)} %get-tuple-element.23.cum_t_ref, f32[256,128]{1,0:T(8,128)} %bitcast.112, f32[256,128]{1,0:T(8,128)} %bitcast.107, f32[40]{0:T(128)} %skip_ref.3), custom_call_target="tpu_custom_call" | custom-call | flops 671088640 | bytes 5242880 | tf_op jit(solution)/shard_map/intra/pallas_call | solution.py:176
  62.3 10.5 %all-to-all-done.1 = bf16[16,160,128]{2,1,0:T(8,128)(2,1)S(1)} async-done(((bf16[16,160,128]{2,1,0:T(8,128)(2,1)}), bf16[16,160,128]{2,1,0:T(8,128)(2,1)S(1)}, u32[]{:S(2)}, u32[]{:S(2)}) %all-to-all-start.1) | async-done | bytes 655392 | tf_op jit(solution)/shard_map/all_to_all | solution.py:238
  73.6 4.8 %inter.1.yo_ref = bf16[256,2560]{1,0:T(8,128)(2,1)} custom-call(f32[256,2560]{1,0:T(8,128)} %intra.1.part_ref, f32[256,40]{1,0:T(8,128)} %get-tuple-element.23.cum_t_ref, f32[256,128]{1,0:T(8,128)} %bitcast.108, bf16[2560,128]{1,0:T(8,128)(2,1)} %bitcast.104), custom_call_target="tpu_custom_call" | custom-call | flops 167772160 | bytes 3932160 | tf_op jit(solution)/shard_map/inter/pallas_call | solution.py:202
  83.2 9.3 %terms.1 = (bf16[4,4,160,640]{3,2,1,0:T(8,128)(2,1)}, bf16[4,4,160,640]{3,2,1,0:T(8,128)(2,1)}) custom-call(s32[2]{0:T(128)} %pad_add_fusion.at_ref, bf16[256,2560]{1,0:T(8,128)(2,1)} %inter.1.yo_ref, bf16[256,2560]{1,0:T(8,128)(2,1)} %collective-permute-done.yx_ref, bf16[256,1280]{1,0:T(8,128)(2,1)} %get-tuple-element.51.go_ref, bf16[256,1280]{1,0:T(8,128)(2,1)} %copy-done.17), custom_call_target="tpu_custom_call" | custom-call | flops 3355443200 | bytes 9830400 | tf_op jit(solution)/shard_map/terms/pallas_call | solution.py:260
  100.0 6.5 %collective-permute-done.11 = bf16[2,160,640]{2,1,0:T(8,128)(2,1)S(1)} collective-permute-done((bf16[2,160,640]{2,1,0:T(8,128)(2,1)S(1)}, bf16[2,160,640]{2,1,0:T(8,128)(2,1)S(1)}, u32[]{:S(2)}, u32[]{:S(2)}) %collective-permute-start.11) | collective-permute-done | bytes 409632 | tf_op jit(solution)/shard_map/ppermute | solution.py:560
  113.1 2.9 %convolution_convert_fusion = bf16[256,2560]{1,0:T(8,128)(2,1)} fusion(bf16[256,1280]{1,0:T(8,128)(2,1)S(1)} %copy-done.18, bf16[2560,1280]{1,0:T(8,128)(2,1)S(1)} %copy-done.16), kind=kOutput, calls=%fused_computation | convolution fusion | flops 1678376960 | bytes 8519680 | tf_op jit(solution)/shard_map/dot_general | solution.py:617
  118.1 8.7 %collective-permute-done.12 = bf16[4,160,640]{2,1,0:T(8,128)(2,1)S(1)} collective-permute-done((bf16[4,160,640]{2,1,0:T(8,128)(2,1)S(1)}, bf16[4,160,640]{2,1,0:T(8,128)(2,1)S(1)}, u32[]{:S(2)}, u32[]{:S(2)}) %collective-permute-start.12) | collective-permute-done | bytes 819232 | tf_op jit(solution)/shard_map/ppermute | solution.py:560
  139.4 2.7 collective-permute-done.16.b1
  147.5 3.5 %all-to-all-start.4 = ((bf16[8,13,16,128]{3,2,1,0:T(8,128)(2,1)}), bf16[8,13,16,128]{3,2,1,0:T(8,128)(2,1)S(1)}, u32[]{:S(2)}, u32[]{:S(2)}) async-start(bf16[8,13,16,128]{3,2,1,0:T(8,128)(2,1)} %fold.1), calls=%async_computation.4 | async-start | bytes 851968 | tf_op jit(solution)/shard_map/all_to_all | solution.py:238
  150.9 6.2 %fusion.12.own_ref = f32[256,2560]{1,0:T(8,128)} fusion(bf16[256,1280]{1,0:T(8,128)(2,1)S(1)} %copy-done.11, bf16[2560,1280]{1,0:T(8,128)(2,1)} %all-gather.2.cloned.1.call-done), kind=kOutput, calls=%fused_computation.59 | convolution fusion | flops 1677721600 | bytes 9830400 | tf_op jit(solution)/shard_map/dot_general | solution.py:619
  158.3 6.4 %entries.1 = (bf16[256,2560]{1,0:T(8,128)(2,1)}, bf16[16,176,128]{2,1,0:T(8,128)(2,1)}) custom-call(f32[256,2560]{1,0:T(8,128)} %fusion.12.own_ref, bf16[256,2560]{1,0:T(8,128)(2,1)} %copy-done.10, f32[256,2560]{1,0:T(8,128)} %bitcast.102, f32[256,40]{1,0:T(8,128)} %get-tuple-element.23.cum_t_ref, f32[256,128]{1,0:T(8,128)} %bitcast.109), custom_call_target="tpu_custom_call" | custom-call | flops 167772160 | bytes 7864320 | tf_op jit(solution)/shard_map/entries/pallas_call | solution.py:308
  164.7 13.2 %all-to-all-start.2 = ((bf16[16,176,128]{2,1,0:T(8,128)(2,1)}), bf16[16,176,128]{2,1,0:T(8,128)(2,1)S(1)}, u32[]{:S(2)}, u32[]{:S(2)}) async-start(bf16[16,176,128]{2,1,0:T(8,128)(2,1)} %get-tuple-element.29), calls=%async_computation.2 | async-start | bytes 1441792 | tf_op jit(solution)/shard_map/all_to_all | solution.py:238
  179.8 19.3 %all-to-all-done.2.parts_ref.got_ref = bf16[16,176,128]{2,1,0:T(8,128)(2,1)S(1)} async-done(((bf16[16,176,128]{2,1,0:T(8,128)(2,1)}), bf16[16,176,128]{2,1,0:T(8,128)(2,1)S(1)}, u32[]{:S(2)}, u32[]{:S(2)}) %all-to-all-start.2) | async-done | bytes 720928 | tf_op jit(solution)/shard_map/all_to_all | solution.py:238
  199.2 3.5 %all-to-all-start.5 = ((bf16[16,13,16,128]{3,2,1,0:T(8,128)(2,1)}), bf16[16,13,16,128]{3,2,1,0:T(8,128)(2,1)S(1)}, u32[]{:S(2)}, u32[]{:S(2)}) async-start(bf16[16,13,16,128]{3,2,1,0:T(8,128)(2,1)} %zsum.1), calls=%async_computation.5 | async-start | bytes 1703936 | tf_op jit(solution)/shard_map/all_to_all | solution.py:238
  205.4 20.9 %all-to-all-done.5.tiles_ref = bf16[16,13,16,128]{3,2,1,0:T(8,128)(2,1)S(1)} async-done(((bf16[16,13,16,128]{3,2,1,0:T(8,128)(2,1)}), bf16[16,13,16,128]{3,2,1,0:T(8,128)(2,1)S(1)}, u32[]{:S(2)}, u32[]{:S(2)}) %all-to-all-start.5) | async-done | bytes 852000 | tf_op jit(solution)/shard_map/all_to_all | solution.py:238
  226.3 3.5 %all-to-all-start.3 = ((bf16[16,160,128]{2,1,0:T(8,128)(2,1)}), bf16[16,160,128]{2,1,0:T(8,128)(2,1)S(1)}, u32[]{:S(2)}, u32[]{:S(2)}) async-start(bf16[16,160,128]{2,1,0:T(8,128)(2,1)} %chain.3), calls=%async_computation.3 | async-start | bytes 1310720 | tf_op jit(solution)/shard_map/all_to_all | solution.py:238
  236.0 2.7 collective-permute-start.20
  240.2 2.7 collective-permute-done.21
  242.9 4.2 %collective-permute-done.22 = f32[1,128]{1,0:T(1,128)S(1)} collective-permute-done((f32[1,128]{1,0:T(1,128)S(1)}, f32[1,128]{1,0:T(1,128)S(1)}, u32[]{:S(2)}, u32[]{:S(2)}) %collective-permute-start.22) | collective-permute-done | bytes 544 | tf_op jit(solution)/shard_map/ppermute | solution.py:586
  252.2 16.0 %backward.1 = (f32[256,2560]{1,0:T(8,128)}, f32[40,256]{1,0:T(8,128)}, f32[256,128]{1,0:T(8,128)}, f32[256,128]{1,0:T(8,128)}) custom-call(f32[256,2560]{1,0:T(8,128)} %bitcast.103, bf16[256,2560]{1,0:T(8,128)(2,1)} %get-tuple-element.28.gy_ref, f32[40,256]{1,0:T(8,128)} %get-tuple-element.22.cum_ref, f32[256,40]{1,0:T(8,128)} %get-tuple-element.23.cum_t_ref, ...), custom_call_target="tpu_custom_call" | custom-call | flops 1342177280 | bytes 9175040 | tf_op jit(solution)/shard_map/backward/pallas_call | solution.py:405
  (121 shorter events, 63.5 us)
Async XLA Ops:
  7.2 85.3 %all-gather.2.cloned.1.call-start = ((), (), s32[]{:S(2)}) async-start(), calls=%async_computation.6 | async-start | bytes 6963200 | tf_op jit(solution)/shard_map/all_gather | solution.py:601
  14.8 31.3 %all-to-all-start = ((bf16[16,176,128]{2,1,0:T(8,128)(2,1)}), bf16[16,176,128]{2,1,0:T(8,128)(2,1)S(1)}, u32[]{:S(2)}, u32[]{:S(2)}) async-start(bf16[16,176,128]{2,1,0:T(8,128)(2,1)} %get-tuple-element.24), calls=%async_computation | async-start | bytes 1441792 | tf_op jit(solution)/shard_map/all_to_all | solution.py:238
  49.6 23.1 %all-to-all-start.1 = ((bf16[16,160,128]{2,1,0:T(8,128)(2,1)}), bf16[16,160,128]{2,1,0:T(8,128)(2,1)S(1)}, u32[]{:S(2)}, u32[]{:S(2)}) async-start(bf16[16,160,128]{2,1,0:T(8,128)(2,1)} %chain.2), calls=%async_computation.1 | async-start | bytes 1310720 | tf_op jit(solution)/shard_map/all_to_all | solution.py:238
  94.2 12.3 %collective-permute-start.11 = (bf16[2,160,640]{2,1,0:T(8,128)(2,1)S(1)}, bf16[2,160,640]{2,1,0:T(8,128)(2,1)S(1)}, u32[]{:S(2)}, u32[]{:S(2)}) collective-permute-start(bf16[2,160,640]{2,1,0:T(8,128)(2,1)S(1)} %get-tuple-element.40), channel_id=1, source_target_pairs={{0,64},{64,128},{128,192},{192,0},{1,65},{65,129},{129,193},{193,1... | collective-permute-start | bytes 1228808 | tf_op jit(solution)/shard_map/ppermute | solution.py:560
  95.5 10.9 %collective-permute-start.13 = (bf16[2,160,640]{2,1,0:T(8,128)(2,1)S(1)}, bf16[2,160,640]{2,1,0:T(8,128)(2,1)S(1)}, u32[]{:S(2)}, u32[]{:S(2)}) collective-permute-start(bf16[2,160,640]{2,1,0:T(8,128)(2,1)S(1)} %get-tuple-element.41), channel_id=1, source_target_pairs={{0,192},{64,0},{128,64},{192,128},{1,193},{65,1},{129,65},{193,129... | collective-permute-start | bytes 1228808 | tf_op jit(solution)/shard_map/ppermute | solution.py:560
  97.2 12.5 %collective-permute-start.3 = (bf16[2,160,640]{2,1,0:T(8,128)(2,1)S(1)}, bf16[2,160,640]{2,1,0:T(8,128)(2,1)S(1)}, u32[]{:S(2)}, u32[]{:S(2)}) collective-permute-start(bf16[2,160,640]{2,1,0:T(8,128)(2,1)S(1)} %get-tuple-element.46), channel_id=1, source_target_pairs={{0,16},{16,32},{32,48},{48,0},{1,17},{17,33},{33,49},{49,1},{2,18}... | collective-permute-start | bytes 1228808 | tf_op jit(solution)/shard_map/ppermute | solution.py:560
  98.5 11.2 %collective-permute-start.5 = (bf16[2,160,640]{2,1,0:T(8,128)(2,1)S(1)}, bf16[2,160,640]{2,1,0:T(8,128)(2,1)S(1)}, u32[]{:S(2)}, u32[]{:S(2)}) collective-permute-start(bf16[2,160,640]{2,1,0:T(8,128)(2,1)S(1)} %get-tuple-element.47), channel_id=1, source_target_pairs={{0,48},{16,0},{32,16},{48,32},{1,49},{17,1},{33,17},{49,33},{2,50}... | collective-permute-start | bytes 1228808 | tf_op jit(solution)/shard_map/ppermute | solution.py:560
  106.8 20.1 %collective-permute-start.12 = (bf16[4,160,640]{2,1,0:T(8,128)(2,1)S(1)}, bf16[4,160,640]{2,1,0:T(8,128)(2,1)S(1)}, u32[]{:S(2)}, u32[]{:S(2)}) collective-permute-start(bf16[4,160,640]{2,1,0:T(8,128)(2,1)S(1)} %pad_maximum_fusion.2), channel_id=1, source_target_pairs={{0,64},{64,128},{128,192},{192,0},{1,65},{65,129},{129,193},{193,1... | collective-permute-start | bytes 2457608 | tf_op jit(solution)/shard_map/ppermute | solution.py:560
  107.9 18.9 %collective-permute-start.14 = (bf16[4,160,640]{2,1,0:T(8,128)(2,1)S(1)}, bf16[4,160,640]{2,1,0:T(8,128)(2,1)S(1)}, u32[]{:S(2)}, u32[]{:S(2)}) collective-permute-start(bf16[4,160,640]{2,1,0:T(8,128)(2,1)S(1)} %pad_maximum_fusion.3), channel_id=1, source_target_pairs={{0,192},{64,0},{128,64},{192,128},{1,193},{65,1},{129,65},{193,129... | collective-permute-start | bytes 2457608 | tf_op jit(solution)/shard_map/ppermute | solution.py:560
  110.0 19.9 %collective-permute-start.4 = (bf16[4,160,640]{2,1,0:T(8,128)(2,1)S(1)}, bf16[4,160,640]{2,1,0:T(8,128)(2,1)S(1)}, u32[]{:S(2)}, u32[]{:S(2)}) collective-permute-start(bf16[4,160,640]{2,1,0:T(8,128)(2,1)S(1)} %pad_maximum_fusion), channel_id=1, source_target_pairs={{0,16},{16,32},{32,48},{48,0},{1,17},{17,33},{33,49},{49,1},{2,18}... | collective-permute-start | bytes 2457608 | tf_op jit(solution)/shard_map/ppermute | solution.py:560
  111.5 18.4 %collective-permute-start.6 = (bf16[4,160,640]{2,1,0:T(8,128)(2,1)S(1)}, bf16[4,160,640]{2,1,0:T(8,128)(2,1)S(1)}, u32[]{:S(2)}, u32[]{:S(2)}) collective-permute-start(bf16[4,160,640]{2,1,0:T(8,128)(2,1)S(1)} %pad_maximum_fusion.1), channel_id=1, source_target_pairs={{0,48},{16,0},{32,16},{48,32},{1,49},{17,1},{33,17},{49,33},{2,50}... | collective-permute-start | bytes 2457608 | tf_op jit(solution)/shard_map/ppermute | solution.py:560
  116.1 41.1 %collective-permute-start.2 = (bf16[256,2560]{1,0:T(8,128)(2,1)}, bf16[256,2560]{1,0:T(8,128)(2,1)S(1)}, u32[]{:S(2)}, u32[]{:S(2)}) collective-permute-start(bf16[256,2560]{1,0:T(8,128)(2,1)} %convolution_convert_fusion), channel_id=1, source_target_pairs={{0,1},{1,0},{2,3},{3,2},{4,5},{5,4},{6,7},{7,6},{8,9},{9,8},{10,11... | collective-permute-start | bytes 3932168 | tf_op jit(solution)/shard_map/ppermute | solution.py:581
  127.2 6.5 %collective-permute-start.15 = (bf16[80,640]{1,0:T(8,128)(2,1)S(1)}, bf16[80,640]{1,0:T(8,128)(2,1)S(1)}, u32[]{:S(2)}, u32[]{:S(2)}) collective-permute-start(bf16[80,640]{1,0:T(8,128)(2,1)S(1)} %get-tuple-element.55), channel_id=1, source_target_pairs={{0,16},{16,32},{32,48},{48,0},{1,17},{17,33},{33,49},{49,1},{2,18}... | collective-permute-start | bytes 307208 | tf_op jit(solution)/shard_map/ppermute | solution.py:560
  128.5 5.2 %collective-permute-start.17 = (bf16[80,640]{1,0:T(8,128)(2,1)S(1)}, bf16[80,640]{1,0:T(8,128)(2,1)S(1)}, u32[]{:S(2)}, u32[]{:S(2)}) collective-permute-start(bf16[80,640]{1,0:T(8,128)(2,1)S(1)} %get-tuple-element.53), channel_id=1, source_target_pairs={{0,48},{16,0},{32,16},{48,32},{1,49},{17,1},{33,17},{49,33},{2,50}... | collective-permute-start | bytes 307208 | tf_op jit(solution)/shard_map/ppermute | solution.py:560
  131.0 5.3 %collective-permute-start.7 = (bf16[80,640]{1,0:T(8,128)(2,1)S(1)}, bf16[80,640]{1,0:T(8,128)(2,1)S(1)}, u32[]{:S(2)}, u32[]{:S(2)}) collective-permute-start(bf16[80,640]{1,0:T(8,128)(2,1)S(1)} %get-tuple-element.61), channel_id=1, source_target_pairs={{0,64},{64,128},{128,192},{192,0},{1,65},{65,129},{129,193},{193,1... | collective-permute-start | bytes 307208 | tf_op jit(solution)/shard_map/ppermute | solution.py:560
  131.3 5.0 %collective-permute-start.9 = (bf16[80,640]{1,0:T(8,128)(2,1)S(1)}, bf16[80,640]{1,0:T(8,128)(2,1)S(1)}, u32[]{:S(2)}, u32[]{:S(2)}) collective-permute-start(bf16[80,640]{1,0:T(8,128)(2,1)S(1)} %get-tuple-element.59), channel_id=1, source_target_pairs={{0,192},{64,0},{128,64},{192,128},{1,193},{65,1},{129,65},{193,129... | collective-permute-start | bytes 307208 | tf_op jit(solution)/shard_map/ppermute | solution.py:560
  133.8 5.6 %collective-permute-start.18 = (bf16[160,640]{1,0:T(8,128)(2,1)S(1)}, bf16[160,640]{1,0:T(8,128)(2,1)S(1)}, u32[]{:S(2)}, u32[]{:S(2)}) collective-permute-start(bf16[160,640]{1,0:T(8,128)(2,1)S(1)} %pad_maximum_fusion.7), channel_id=1, source_target_pairs={{0,48},{16,0},{32,16},{48,32},{1,49},{17,1},{33,17},{49,33},{2,50}... | collective-permute-start | bytes 614408 | tf_op jit(solution)/shard_map/ppermute | solution.py:560
  136.2 5.9 %collective-permute-start.16 = (bf16[160,640]{1,0:T(8,128)(2,1)S(1)}, bf16[160,640]{1,0:T(8,128)(2,1)S(1)}, u32[]{:S(2)}, u32[]{:S(2)}) collective-permute-start(bf16[160,640]{1,0:T(8,128)(2,1)S(1)} %pad_maximum_fusion.6), channel_id=1, source_target_pairs={{0,16},{16,32},{32,48},{48,0},{1,17},{17,33},{33,49},{49,1},{2,18}... | collective-permute-start | bytes 614408 | tf_op jit(solution)/shard_map/ppermute | solution.py:560
  136.4 5.7 %collective-permute-start.10 = (bf16[160,640]{1,0:T(8,128)(2,1)S(1)}, bf16[160,640]{1,0:T(8,128)(2,1)S(1)}, u32[]{:S(2)}, u32[]{:S(2)}) collective-permute-start(bf16[160,640]{1,0:T(8,128)(2,1)S(1)} %pad_maximum_fusion.5), channel_id=1, source_target_pairs={{0,192},{64,0},{128,64},{192,128},{1,193},{65,1},{129,65},{193,129... | collective-permute-start | bytes 614408 | tf_op jit(solution)/shard_map/ppermute | solution.py:560
  138.6 5.9 %collective-permute-start.8 = (bf16[160,640]{1,0:T(8,128)(2,1)S(1)}, bf16[160,640]{1,0:T(8,128)(2,1)S(1)}, u32[]{:S(2)}, u32[]{:S(2)}) collective-permute-start(bf16[160,640]{1,0:T(8,128)(2,1)S(1)} %pad_maximum_fusion.4), channel_id=1, source_target_pairs={{0,64},{64,128},{128,192},{192,0},{1,65},{65,129},{129,193},{193,1... | collective-permute-start | bytes 614408 | tf_op jit(solution)/shard_map/ppermute | solution.py:560
  147.5 17.2 %all-to-all-start.4 = ((bf16[8,13,16,128]{3,2,1,0:T(8,128)(2,1)}), bf16[8,13,16,128]{3,2,1,0:T(8,128)(2,1)S(1)}, u32[]{:S(2)}, u32[]{:S(2)}) async-start(bf16[8,13,16,128]{3,2,1,0:T(8,128)(2,1)} %fold.1), calls=%async_computation.4 | async-start | bytes 851968 | tf_op jit(solution)/shard_map/all_to_all | solution.py:238
  164.7 34.5 %all-to-all-start.2 = ((bf16[16,176,128]{2,1,0:T(8,128)(2,1)}), bf16[16,176,128]{2,1,0:T(8,128)(2,1)S(1)}, u32[]{:S(2)}, u32[]{:S(2)}) async-start(bf16[16,176,128]{2,1,0:T(8,128)(2,1)} %get-tuple-element.29), calls=%async_computation.2 | async-start | bytes 1441792 | tf_op jit(solution)/shard_map/all_to_all | solution.py:238
  199.2 27.1 %all-to-all-start.5 = ((bf16[16,13,16,128]{3,2,1,0:T(8,128)(2,1)}), bf16[16,13,16,128]{3,2,1,0:T(8,128)(2,1)S(1)}, u32[]{:S(2)}, u32[]{:S(2)}) async-start(bf16[16,13,16,128]{3,2,1,0:T(8,128)(2,1)} %zsum.1), calls=%async_computation.5 | async-start | bytes 1703936 | tf_op jit(solution)/shard_map/all_to_all | solution.py:238
  226.3 25.1 %all-to-all-start.3 = ((bf16[16,160,128]{2,1,0:T(8,128)(2,1)}), bf16[16,160,128]{2,1,0:T(8,128)(2,1)S(1)}, u32[]{:S(2)}, u32[]{:S(2)}) async-start(bf16[16,160,128]{2,1,0:T(8,128)(2,1)} %chain.3), calls=%async_computation.3 | async-start | bytes 1310720 | tf_op jit(solution)/shard_map/all_to_all | solution.py:238
  (26 other events, 170.2 us)
Sparse Core Ops, SparseCore 0:
  10.4 71.2 all-gather.1

commit v3 on v2

--- a/solution.py
+++ b/solution.py
@@ -249,7 +249,7 @@
             rel = (k + 4 - at_ref[1]) % 4
             rows = term[k * OWN : (k + 1) * OWN, :]
             if i == 0:
-                first_ref[rel, step] = rows
+                first_ref[rel, 0] = rows
             else:
                 second_ref[0, rel] = rows
 
@@ -264,7 +264,7 @@
             grid=(4,),
             in_specs=[rows, rows, whole(g_own.shape), whole(g_own.shape)],
             out_specs=[
-                whole((4, 4, OWN, half)),
+                pl.BlockSpec((4, 1, OWN, half), lambda i, at: (0, i, 0, 0)),
                 pl.BlockSpec((1, 4, OWN, half), lambda i, at: (i, 0, 0, 0)),
             ],
         ),
@@ -430,10 +430,12 @@
     )(x, gy, cum, cum_t, b, c, skip, start, last)
 
 
-def fold_kernel(a0, a1, a2, b0, b1, b2, out_ref):
+def fold_kernel(a0, a1, a2, a3, b0, b1, b2, b3, out_ref):
     sums = []
-    for parts in ((a0, a1, a2), (b0, b1, b2)):
-        total = parts[0][...].astype(F32) + parts[1][...].astype(F32) + parts[2][...].astype(F32)
+    for parts in ((a0, a1, a2, a3), (b0, b1, b2, b3)):
+        total = parts[0][...].astype(F32)
+        for part in parts[1:]:
+            total += part[...].astype(F32)
         sums.append(total.astype(BF))
     for q in range(8 * TILES):
         r, c = divmod(q, 10)
@@ -447,7 +449,7 @@
 def fold(parts):
     return pl.pallas_call(
         fold_kernel,
-        in_specs=[vmem()] * 6,
+        in_specs=[vmem()] * 8,
         out_specs=vmem(),
         out_shape=jax.ShapeDtypeStruct((8, TILES, 16, 128), BF),
         compiler_params=params(),
@@ -456,64 +458,48 @@
     )(*parts)
 
 
-def zsum_kernel(parts_ref, out_ref):
+def groups_of(row0, count, ids_ref):
+    heads = (row0 + iota((count, N), 0)) // P_SIZE == iota((count, N), 1)
+    return jnp.sum(jnp.where(heads, ids_ref[...], 0.0), axis=1, keepdims=True)
+
+
+def zsum_kernel(row0_ref, z_ref, ids_ref, parts_ref, got_ref, out_ref, note_ref):
     total = parts_ref[0].astype(F32)
     for z in range(1, 8):
         total += parts_ref[z].astype(F32)
     for s in range(N_SEQ):
         out_ref[s] = total.astype(BF)
-
-
-def zsum(parts):
+    found = jnp.zeros((16, N), F32)
+    for i in range(TILES):
+        row = row0_ref[0] + 16 * ((z_ref[0] * TILES + i) // 10)
+        place = iota((16, N), 1) - H == groups_of(row, 16, ids_ref).astype(jnp.int32)
+        tile = total[i]
+        found += jnp.where(place, jnp.sum(tile * tile, axis=1, keepdims=True), 0.0)
+    d_sum = jnp.zeros((1, N), F32)
+    for s in range(N_SEQ):
+        pieces = got_ref[s, OWN:, :].astype(F32)
+        d_sum += pieces[0:1, :] + pieces[1:2, :] + pieces[2:3, :]
+    note_ref[...] = jnp.sum(found, axis=0, keepdims=True) + d_sum / N_SEQ
+
+
+def zsum(row0, z, ids, parts, got):
     return pl.pallas_call(
         zsum_kernel,
-        in_specs=[vmem()],
-        out_specs=vmem(),
-        out_shape=jax.ShapeDtypeStruct((N_SEQ, TILES, 16, 128), BF),
+        in_specs=[smem(), smem(), vmem(), vmem(), vmem()],
+        out_specs=[vmem(), vmem()],
+        out_shape=[
+            jax.ShapeDtypeStruct((N_SEQ, TILES, 16, 128), BF),
+            jax.ShapeDtypeStruct((1, N), F32),
+        ],
         compiler_params=params(),
         cost_estimate=cost(8 * OWN * 160, 6 * OWN * D, 0),
         name="zsum",
-    )(parts)
+    )(row0, z, ids, parts, got)
 
 
 def tile_of(ref, r, c, core):
     z, i = divmod(10 * r + c, TILES)
     return ref[2 * z + core, i].astype(F32)
-
-
-def row_groups(row0, ids_ref):
-    heads = (row0 + iota((OWN, N), 0)) // P_SIZE == iota((OWN, N), 1)
-    return jnp.sum(jnp.where(heads, ids_ref[...], 0.0), axis=1, keepdims=True)
-
-
-def squares_kernel(row0_ref, ids_ref, tiles_ref, got_ref, note_ref):
-    found = []
-    for r in range(10):
-        total = jnp.zeros((16, 128), F32)
-        for core in range(2):
-            for c in range(10):
-                tile = tile_of(tiles_ref, r, c, core)
-                total += tile * tile
-        found.append(jnp.sum(total, axis=1, keepdims=True))
-    squares = jnp.concatenate(found, axis=0)
-    place = iota((OWN, N), 1) - H == row_groups(row0_ref[0], ids_ref).astype(jnp.int32)
-    note = jnp.sum(jnp.where(place, squares, 0.0), axis=0, keepdims=True)
-    for s in range(N_SEQ):
-        pieces = got_ref[s, OWN:, :].astype(F32)
-        note += pieces[0:1, :] + pieces[1:2, :] + pieces[2:3, :]
-    note_ref[...] = note
-
-
-def squares(row0, ids, tiles, got):
-    return pl.pallas_call(
-        squares_kernel,
-        in_specs=[smem(), vmem(), vmem(), vmem()],
-        out_specs=vmem(),
-        out_shape=jax.ShapeDtypeStruct((1, N), F32),
-        compiler_params=params(),
-        cost_estimate=cost(2 * OWN * D, 2 * OWN * D, 0),
-        name="squares",
-    )(row0, ids, tiles, got)
 
 
 def clip_kernel(tokens_all, row0_ref, ids_ref, tiles_ref, note_ref, w_ref, d_ref):
@@ -521,7 +507,7 @@
     lane = iota((1, N), 1)
     note = note_ref[...]
     grad_d = jnp.where(lane < H, note, 0.0)
-    groups = row_groups(row0_ref[0], ids_ref)
+    groups = groups_of(row0_ref[0], OWN, ids_ref)
     w_factor = jnp.zeros((OWN, 1), F32)
     d_factor = jnp.zeros((1, N), F32)
     for g in range(GROUPS):
@@ -564,17 +550,21 @@
     return (a.astype(F32) + b.astype(F32)).astype(BF)
 
 
-def relay(t, axis):
+def far(t, axis):
     m = t.shape[1] // 2
-    ra = shifted(t[2, :m], axis, 1)
-    rb = shifted(t[2, m:], axis, -1)
+    return shifted(t[2, :m], axis, 1), shifted(t[2, m:], axis, -1)
+
+
+def near(t, ra, rb, axis):
+    m = t.shape[1] // 2
     up = jnp.concatenate([plus(t[1, :m], ra), t[1, m:]], axis=0)
     down = jnp.concatenate([t[3, :m], plus(t[3, m:], rb)], axis=0)
-    return t[0], shifted(up, axis, 1), shifted(down, axis, -1)
-
-
-def three_sum(parts):
-    return (parts[0].astype(F32) + parts[1].astype(F32) + parts[2].astype(F32)).astype(BF)
+    got = (t[0], shifted(up, axis, 1), shifted(down, axis, -1))
+    return (got[0].astype(F32) + got[1].astype(F32) + got[2].astype(F32)).astype(BF)
+
+
+def direct(t, axis):
+    return (t[0],) + tuple(shifted(t[d], axis, d) for d in (1, 3, 2))
 
 
 def other_core(v):
@@ -582,9 +572,16 @@
 
 
 def sum_over(v, axis):
-    for bit in (1, 2):
-        v = v + lax.ppermute(v, axis, [(i, i ^ bit) for i in range(4)])
+    n = lax.axis_size(axis)
+    bit = 1
+    while bit < n:
+        v = v + lax.ppermute(v, axis, [(i, i ^ bit) for i in range(n)])
+        bit *= 2
     return v
+
+
+def tie(*values):
+    return lax.optimization_barrier(values)
 
 
 def per_device(x_in, a_log, b_in, c_in, g_out, w_out, d_skip, group_ids):
@@ -593,6 +590,7 @@
     half = D // 2
     at = jnp.stack([lax.axis_index("y"), lax.axis_index("x")]).astype(jnp.int32)
     mine = (2 * lax.axis_index("z") + core).reshape(1).astype(jnp.int32)
+    at_z = lax.axis_index("z").reshape(1).astype(jnp.int32)
     row0 = ((4 * at[0] + at[1]) * OWN).reshape(1)
     ids = jnp.pad(group_ids.astype(F32), (0, N - H), constant_values=-1.0)[None]
     tokens_all = float(T * N_SEQ * 16)
@@ -608,28 +606,35 @@
     start = swap(chain(got, got, mine, False), SEQ).reshape(H * P_SIZE, N)
     y_own = inter(y_part, cum_t, c, start)
     y_other = other_core(y_own)
-    first, second = terms(at, y_own, y_other, g_mine, g_other)
-    w_half, first, second = lax.optimization_barrier((w_half, first, second))
-
-    first = relay(first, "x")
-    second = relay(second, "y")
+
+    w_half, _ = tie(w_half, y_own)
     dims = (((1,), (1,)), ((), ()))
     gy_other = lax.dot_general(g_other, w_half, dims, preferred_element_type=F32).astype(BF)
+    gy_own = lax.dot_general(g_mine, w_half, dims, preferred_element_type=F32)
+    y_other, gy_other, gy_own = tie(y_other, gy_other, gy_own)
     gy_other = other_core(gy_other)
-    gy_own = lax.dot_general(g_mine, w_half, dims, preferred_element_type=F32)
+    first, second = terms(at, y_own, y_other, g_mine, g_other)
+    far_x = far(first, "x")
+    far_y = far(second, "y")
+    gy_own, gy_other, *_ = tie(gy_own, gy_other, first)
     gy, sent_back = entries(gy_own, gy_other, x, cum_t, c)
+    far_x, far_y, sent_back = tie(far_x, far_y, sent_back)
     got_back = swap(sent_back, SEQ)
-
-    first = relay(three_sum(first), "y")
-    second = relay(three_sum(second), "x")
+    first = near(first, *far_x, "x")
+    second = near(second, *far_y, "y")
+    first, second, got_back = tie(first, second, got_back)
+    first = direct(first, "y")
+    second = direct(second, "x")
     last = swap(chain(got_back, got, mine, True), SEQ).reshape(H * P_SIZE, N)
     tiles = swap(fold(first + second), "z")
-    tiles = swap(zsum(tiles), SEQ)
 
     gx, ga, gb, gc = backward(x, gy, cum, cum_t, b, c, d_skip, start, last)
 
-    note = squares(row0, ids, tiles, got_back)
-    note = sum_over(sum_over(note, "x"), "y")
+    tiles, gx = tie(tiles, gx)
+    tiles, note = zsum(row0, at_z, ids, tiles, got_back)
+    tiles = swap(tiles, SEQ)
+    for axis in ("x", "y", "z", "core"):
+        note = sum_over(note, axis)
     clipped_w, clipped_d = clip(tokens_all, row0, ids, tiles, note)
     return (gx[None], ga[None], gb[None], gc[None], clipped_w, clipped_d[0, :H])
 

time: 279 us -> 275 us (0.986)
  waiting for transfers between devices: 104 us -> 92.2 us
  other arithmetic: 3.31 us -> 9.39 us
  starting transfers between devices: 65.6 us -> 69.6 us
    all_to_all x6, waiting for transfers between devices: 72 us -> 33.3 us  [swap(): return lax.all_to_all(v, axis, 0, 0, tiled=True)]
    ppermute x16 -> x14, waiting for transfers between devices: 20.3 us -> 34.4 us  [shifted(): return lax.ppermute(v, axis, [(i, (i + d) % 4) for i in range(4)])]
    ppermute x4 -> x8, waiting for transfers between devices: 9.7 us -> 21.9 us  [sum_over(): v = v + lax.ppermute(v, axis, [(i, i ^ bit) for i in range(n)])]
    ppermute x16 -> x14, starting transfers between devices: 21.6 us -> 10.9 us  [shifted(): return lax.ppermute(v, axis, [(i, (i + d) % 4) for i in range(4)])]
    all_to_all x6, starting transfers between devices: 37.2 us -> 45.6 us  [swap(): return lax.all_to_all(v, axis, 0, 0, tiled=True)]
    ppermute x4 -> x8, starting transfers between devices: 4.26 us -> 11.8 us  [sum_over(): v = v + lax.ppermute(v, axis, [(i, i ^ bit) for i in range(n)])]
    convert_element_type x2, other arithmetic: 0.6 us -> 3.4 us  [near(): (got[0].astype(F32) + got[1].astype(F32) + got[2].astype(F32)).astype(BF)]
    pallas_call x3 -> x2, Pallas kernels: 6.38 us -> 4.75 us  [the longest x1 2.46 us: fold(): pl.pallas_call(fold_kernel, in_specs=[vmem()] * 8, out_specs=vmem(), out_...]
  transfers between devices with their start and end apart: 30 -> 32, of which waited for: 13 -> 21; matrix products, arithmetic and copies ran while one was open for 6% -> 8% of each run, Pallas kernels for 18% -> 21%
where the time goes in v3:
time: 275 us; the launch traced here: 273 us
  waiting for transfers between devices  92.2 us (34%)
  starting transfers between devices  69.6 us (25%)
  Pallas kernels  63.5 us (23%)
  local copies, waits for them, and re-layouts  15 us (5%)
  between operations  14.3 us (5%)
  other arithmetic  9.39 us (3%)
  matrix products  9.33 us (3%)
    all_to_all x6, starting transfers between devices, swap(): return lax.all_to_all(v, axis, 0, 0, tiled=True)  45.6 us
    ppermute x14, waiting for transfers between devices, shifted(): return lax.ppermute(v, axis, [(i, (i + d) % 4) for i in range(4)])  34.4 us
    all_to_all x6, waiting for transfers between devices, swap(): return lax.all_to_all(v, axis, 0, 0, tiled=True)  33.3 us
    ppermute x8, waiting for transfers between devices, sum_over(): v = v + lax.ppermute(v, axis, [(i, i ^ bit) for i in range(n)])  21.9 us
    pallas_call x1, Pallas kernels, backward(): pl.pallas_call(back_kernel, grid=(PAIRS // STEP,), in_specs=[wide(T, STEP...  16 us
    ppermute x8, starting transfers between devices, sum_over(): v = v + lax.ppermute(v, axis, [(i, i ^ bit) for i in range(n)])  11.8 us
    ppermute x14, starting transfers between devices, shifted(): return lax.ppermute(v, axis, [(i, (i + d) % 4) for i in range(4)])  10.9 us
    pallas_call x1, Pallas kernels, intra(): pl.pallas_call(intra_kernel, grid=(PAIRS // STEP,), in_specs=[wide(T, STE...  9.15 us
  transfers between devices with their start and end apart: 32, of which 21 were waited for; matrix products, arithmetic and copies ran while one was open for 8% of the time, Pallas kernels for 21%

profile of v3, /device:TPU:1, one launch (start us, length us, event | category | flops | bytes accessed | tf_op | source)
XLA Modules:
  0.0 273.2 jit_solution(1808335856781854022)
XLA Ops:
  9.1 5.7 %ends.1 = (f32[40,256]{1,0:T(8,128)}, f32[256,40]{1,0:T(8,128)}, bf16[16,176,128]{2,1,0:T(8,128)(2,1)}) custom-call(f32[256,2560]{1,0:T(8,128)} %bitcast.77, f32[40,256]{1,0:T(8,128)} %bitcast.91, f32[256,128]{1,0:T(8,128)} %bitcast.88), custom_call_target="tpu_custom_call" | custom-call | flops 167772160 | bytes 2621440 | tf_op jit(solution)/shard_map/ends/pallas_call | solution.py:137
  14.8 10.0 %all-to-all-start = ((bf16[16,176,128]{2,1,0:T(8,128)(2,1)}), bf16[16,176,128]{2,1,0:T(8,128)(2,1)S(1)}, u32[]{:S(2)}, u32[]{:S(2)}) async-start(bf16[16,176,128]{2,1,0:T(8,128)(2,1)} %get-tuple-element.39), calls=%async_computation | async-start | bytes 1441792 | tf_op jit(solution)/shard_map/all_to_all | solution.py:238
  24.8 21.3 %all-to-all-done.parts_ref.totals_ref = bf16[16,176,128]{2,1,0:T(8,128)(2,1)S(1)} async-done(((bf16[16,176,128]{2,1,0:T(8,128)(2,1)}), bf16[16,176,128]{2,1,0:T(8,128)(2,1)S(1)}, u32[]{:S(2)}, u32[]{:S(2)}) %all-to-all-start) | async-done | bytes 720928 | tf_op jit(solution)/shard_map/all_to_all | solution.py:238
  49.6 3.5 %all-to-all-start.1 = ((bf16[16,160,128]{2,1,0:T(8,128)(2,1)}), bf16[16,160,128]{2,1,0:T(8,128)(2,1)S(1)}, u32[]{:S(2)}, u32[]{:S(2)}) async-start(bf16[16,160,128]{2,1,0:T(8,128)(2,1)} %chain.2), calls=%async_computation.1 | async-start | bytes 1310720 | tf_op jit(solution)/shard_map/all_to_all | solution.py:238
  53.1 9.2 %intra.1.part_ref = f32[256,2560]{1,0:T(8,128)} custom-call(f32[256,2560]{1,0:T(8,128)} %bitcast.78, f32[40,256]{1,0:T(8,128)} %get-tuple-element.37.cum_ref, f32[256,40]{1,0:T(8,128)} %get-tuple-element.38.cum_t_ref, f32[256,128]{1,0:T(8,128)} %bitcast.89, f32[256,128]{1,0:T(8,128)} %bitcast.84, f32[40]{0:T(128)} %skip_ref.3), custom_call_target="tpu_custom_call" | custom-call | flops 671088640 | bytes 5242880 | tf_op jit(solution)/shard_map/intra/pallas_call | solution.py:176
  62.3 10.5 %all-to-all-done.1 = bf16[16,160,128]{2,1,0:T(8,128)(2,1)S(1)} async-done(((bf16[16,160,128]{2,1,0:T(8,128)(2,1)}), bf16[16,160,128]{2,1,0:T(8,128)(2,1)S(1)}, u32[]{:S(2)}, u32[]{:S(2)}) %all-to-all-start.1) | async-done | bytes 655392 | tf_op jit(solution)/shard_map/all_to_all | solution.py:238
  73.6 4.9 %inter.1.yo_ref = bf16[256,2560]{1,0:T(8,128)(2,1)} custom-call(f32[256,2560]{1,0:T(8,128)} %intra.1.part_ref, f32[256,40]{1,0:T(8,128)} %get-tuple-element.38.cum_t_ref, f32[256,128]{1,0:T(8,128)} %bitcast.85, bf16[2560,128]{1,0:T(8,128)(2,1)} %bitcast.81), custom_call_target="tpu_custom_call" | custom-call | flops 167772160 | bytes 3932160 | tf_op jit(solution)/shard_map/inter/pallas_call | solution.py:202
  81.8 6.4 %fusion.8.own_ref = f32[256,2560]{1,0:T(8,128)} fusion(bf16[256,1280]{1,0:T(8,128)(2,1)S(1)} %get-tuple-element.80.go_ref, bf16[2560,1280]{1,0:T(8,128)(2,1)} %all-gather.2.cloned.1.call-done), kind=kOutput, calls=%fused_computation.41 | convolution fusion | flops 1677721600 | bytes 9830400 | tf_op jit(solution)/shard_map/dot_general | solution.py:613
  88.2 2.9 %convolution_convert_fusion = bf16[256,2560]{1,0:T(8,128)(2,1)} fusion(bf16[256,1280]{1,0:T(8,128)(2,1)S(1)} %collective-permute-done.1.gx_ref, bf16[2560,1280]{1,0:T(8,128)(2,1)S(1)} %copy-done.19), kind=kOutput, calls=%fused_computation | convolution fusion | flops 1678376960 | bytes 8519680 | tf_op jit(solution)/shard_map/dot_general | solution.py:612
  92.5 8.9 %terms.1 = (bf16[4,4,160,640]{3,2,1,0:T(8,128)(2,1)}, bf16[4,4,160,640]{3,2,1,0:T(8,128)(2,1)}) custom-call(s32[2]{0:T(128)} %pad_add_fusion.at_ref, bf16[256,2560]{1,0:T(8,128)(2,1)} %inter.1.yo_ref, bf16[256,2560]{1,0:T(8,128)(2,1)} %collective-permute-done.yx_ref, bf16[256,1280]{1,0:T(8,128)(2,1)} %copy-done.10, bf16[256,1280]{1,0:T(8,128)(2,1)} %copy-done.20), custom_call_target="tpu_custom_call" | custom-call | flops 3355443200 | bytes 9830400 | tf_op jit(solution)/shard_map/terms/pallas_call | solution.py:260
  109.9 6.3 %entries.1 = (bf16[256,2560]{1,0:T(8,128)(2,1)}, bf16[16,176,128]{2,1,0:T(8,128)(2,1)}) custom-call(f32[256,2560]{1,0:T(8,128)} %fusion.8.own_ref, bf16[256,2560]{1,0:T(8,128)(2,1)} %copy-done.9, f32[256,2560]{1,0:T(8,128)} %bitcast.79, f32[256,40]{1,0:T(8,128)} %get-tuple-element.38.cum_t_ref, f32[256,128]{1,0:T(8,128)} %bitcast.86), custom_call_target="tpu_custom_call" | custom-call | flops 167772160 | bytes 7864320 | tf_op jit(solution)/shard_map/entries/pallas_call | solution.py:308
  127.2 9.3 %all-to-all-start.2 = ((bf16[16,176,128]{2,1,0:T(8,128)(2,1)}), bf16[16,176,128]{2,1,0:T(8,128)(2,1)S(1)}, u32[]{:S(2)}, u32[]{:S(2)}) async-start(bf16[16,176,128]{2,1,0:T(8,128)(2,1)} %get-tuple-element.53), calls=%async_computation.2 | async-start | bytes 1441792 | tf_op jit(solution)/shard_map/all_to_all | solution.py:238
  138.7 4.3 %collective-permute-done.7 = bf16[4,160,640]{2,1,0:T(8,128)(2,1)} collective-permute-done((bf16[4,160,640]{2,1,0:T(8,128)(2,1)}, bf16[4,160,640]{2,1,0:T(8,128)(2,1)}, u32[]{:S(2)}, u32[]{:S(2)}) %collective-permute-start.7) | collective-permute-done | bytes 819232 | tf_op jit(solution)/shard_map/ppermute | solution.py:546
  145.0 11.5 %collective-permute-done.10 = bf16[4,160,640]{2,1,0:T(8,128)(2,1)S(1)} collective-permute-done((bf16[4,160,640]{2,1,0:T(8,128)(2,1)S(1)}, bf16[4,160,640]{2,1,0:T(8,128)(2,1)S(1)}, u32[]{:S(2)}, u32[]{:S(2)}) %collective-permute-start.10) | collective-permute-done | bytes 819232 | tf_op jit(solution)/shard_map/ppermute | solution.py:546
  164.3 8.0 %all-to-all-start.4 = ((bf16[16,160,128]{2,1,0:T(8,128)(2,1)}), bf16[16,160,128]{2,1,0:T(8,128)(2,1)S(1)}, u32[]{:S(2)}, u32[]{:S(2)}) async-start(bf16[16,160,128]{2,1,0:T(8,128)(2,1)} %chain.3), calls=%async_computation.4 | async-start | bytes 1310720 | tf_op jit(solution)/shard_map/all_to_all | solution.py:238
  176.3 5.0 %collective-permute-done.13.a3 = bf16[160,640]{1,0:T(8,128)(2,1)S(1)} collective-permute-done((bf16[160,640]{1,0:T(8,128)(2,1)S(1)}, bf16[160,640]{1,0:T(8,128)(2,1)S(1)}, u32[]{:S(2)}, u32[]{:S(2)}) %collective-permute-start.13) | collective-permute-done | bytes 204832 | tf_op jit(solution)/shard_map/ppermute | solution.py:546
  183.1 2.9 %collective-permute-done.11.a1 = bf16[160,640]{1,0:T(8,128)(2,1)S(1)} collective-permute-done((bf16[160,640]{1,0:T(8,128)(2,1)S(1)}, bf16[160,640]{1,0:T(8,128)(2,1)S(1)}, u32[]{:S(2)}, u32[]{:S(2)}) %collective-permute-start.11) | collective-permute-done | bytes 204832 | tf_op jit(solution)/shard_map/ppermute | solution.py:546
  192.4 4.4 %all-to-all-start.3 = ((bf16[8,13,16,128]{3,2,1,0:T(8,128)(2,1)}), bf16[8,13,16,128]{3,2,1,0:T(8,128)(2,1)S(1)}, u32[]{:S(2)}, u32[]{:S(2)}) async-start(bf16[8,13,16,128]{3,2,1,0:T(8,128)(2,1)} %fold.1), calls=%async_computation.3 | async-start | bytes 851968 | tf_op jit(solution)/shard_map/all_to_all | solution.py:238
  197.4 16.0 %backward.1 = (f32[256,2560]{1,0:T(8,128)}, f32[40,256]{1,0:T(8,128)}, f32[256,128]{1,0:T(8,128)}, f32[256,128]{1,0:T(8,128)}) custom-call(f32[256,2560]{1,0:T(8,128)} %bitcast.80, bf16[256,2560]{1,0:T(8,128)(2,1)} %get-tuple-element.56.gy_ref, f32[40,256]{1,0:T(8,128)} %get-tuple-element.37.cum_ref, f32[256,40]{1,0:T(8,128)} %get-tuple-element.38.cum_t_ref, ...), custom_call_target="tpu_custom_call" | custom-call | flops 1342177280 | bytes 9175040 | tf_op jit(solution)/shard_map/backward/pallas_call | solution.py:405
  216.5 10.3 %all-to-all-start.5 = ((bf16[16,13,16,128]{3,2,1,0:T(8,128)(2,1)}), bf16[16,13,16,128]{3,2,1,0:T(8,128)(2,1)S(1)}, u32[]{:S(2)}, u32[]{:S(2)}) async-start(bf16[16,13,16,128]{3,2,1,0:T(8,128)(2,1)} %get-tuple-element.64), calls=%async_computation.5 | async-start | bytes 1703936 | tf_op jit(solution)/shard_map/all_to_all | solution.py:238
  230.1 4.2 %collective-permute-done.18 = f32[1,128]{1,0:T(1,128)S(1)} collective-permute-done((f32[1,128]{1,0:T(1,128)S(1)}, f32[1,128]{1,0:T(1,128)S(1)}, u32[]{:S(2)}, u32[]{:S(2)}) %collective-permute-start.18) | collective-permute-done | bytes 544 | tf_op jit(solution)/shard_map/ppermute | solution.py:578
  242.2 4.9 %collective-permute-done.21 = f32[1,128]{1,0:T(1,128)S(1)} collective-permute-done((f32[1,128]{1,0:T(1,128)S(1)}, f32[1,128]{1,0:T(1,128)S(1)}, u32[]{:S(2)}, u32[]{:S(2)}) %collective-permute-start.21) | collective-permute-done | bytes 544 | tf_op jit(solution)/shard_map/ppermute | solution.py:578
  250.4 4.6 %collective-permute-start.23 = (f32[1,128]{1,0:T(1,128)S(1)}, f32[1,128]{1,0:T(1,128)S(1)}, u32[]{:S(2)}, u32[]{:S(2)}) collective-permute-start(f32[1,128]{1,0:T(1,128)S(1)} %add.80), channel_id=1, source_target_pairs={{0,8},{2,10},{4,12},{6,14},{8,0},{10,2},{12,4},{14,6},{1,9},{3,11}... | collective-permute-start | bytes 1544 | tf_op jit(solution)/shard_map/ppermute | solution.py:578
  256.7 3.6 %collective-permute-start.24 = (f32[1,128]{1,0:T(1,128)S(1)}, f32[1,128]{1,0:T(1,128)S(1)}, u32[]{:S(2)}, u32[]{:S(2)}) collective-permute-start(f32[1,128]{1,0:T(1,128)S(1)} %add.81), channel_id=1, source_target_pairs={{0,1},{1,0},{2,3},{3,2},{4,5},{5,4},{6,7},{7,6},{8,9},{9,8},{10,11... | collective-permute-start | bytes 1544 | tf_op jit(solution)/shard_map/ppermute | solution.py:578
  (123 shorter events, 80.2 us)
Async XLA Ops:
  7.2 74.6 %all-gather.2.cloned.1.call-start = ((), (), s32[]{:S(2)}) async-start(), calls=%async_computation.6 | async-start | bytes 6963200 | tf_op jit(solution)/shard_map/all_gather | solution.py:599
  14.8 31.3 %all-to-all-start = ((bf16[16,176,128]{2,1,0:T(8,128)(2,1)}), bf16[16,176,128]{2,1,0:T(8,128)(2,1)S(1)}, u32[]{:S(2)}, u32[]{:S(2)}) async-start(bf16[16,176,128]{2,1,0:T(8,128)(2,1)} %get-tuple-element.39), calls=%async_computation | async-start | bytes 1441792 | tf_op jit(solution)/shard_map/all_to_all | solution.py:238
  49.6 23.1 %all-to-all-start.1 = ((bf16[16,160,128]{2,1,0:T(8,128)(2,1)}), bf16[16,160,128]{2,1,0:T(8,128)(2,1)S(1)}, u32[]{:S(2)}, u32[]{:S(2)}) async-start(bf16[16,160,128]{2,1,0:T(8,128)(2,1)} %chain.2), calls=%async_computation.1 | async-start | bytes 1310720 | tf_op jit(solution)/shard_map/all_to_all | solution.py:238
  78.5 12.7 %collective-permute-start = (bf16[256,2560]{1,0:T(8,128)(2,1)}, bf16[256,2560]{1,0:T(8,128)(2,1)}, u32[]{:S(2)}, u32[]{:S(2)}) collective-permute-start(bf16[256,2560]{1,0:T(8,128)(2,1)} %inter.1.yo_ref), channel_id=1, source_target_pairs={{0,1},{1,0},{2,3},{3,2},{4,5},{5,4},{6,7},{7,6},{8,9},{9,8},{10,11... | collective-permute-start | bytes 3932168 | tf_op jit(solution)/shard_map/ppermute | solution.py:571
  78.6 9.6 %collective-permute-start.1 = (bf16[256,1280]{1,0:T(8,128)(2,1)S(1)}, bf16[256,1280]{1,0:T(8,128)(2,1)S(1)}, u32[]{:S(2)}, u32[]{:S(2)}) collective-permute-start(bf16[256,1280]{1,0:T(8,128)(2,1)S(1)} %get-tuple-element.81), channel_id=1, source_target_pairs={{0,1},{1,0},{2,3},{3,2},{4,5},{5,4},{6,7},{7,6},{8,9},{9,8},{10,11... | collective-permute-start | bytes 1966088 | tf_op jit(solution)/shard_map/ppermute | solution.py:571
  91.1 17.7 %collective-permute-start.6 = (bf16[256,2560]{1,0:T(8,128)(2,1)}, bf16[256,2560]{1,0:T(8,128)(2,1)S(1)}, u32[]{:S(2)}, u32[]{:S(2)}) collective-permute-start(bf16[256,2560]{1,0:T(8,128)(2,1)} %convolution_convert_fusion), channel_id=1, source_target_pairs={{0,1},{1,0},{2,3},{3,2},{4,5},{5,4},{6,7},{7,6},{8,9},{9,8},{10,11... | collective-permute-start | bytes 3932168 | tf_op jit(solution)/shard_map/ppermute | solution.py:571
  103.9 12.3 %collective-permute-start.5 = (bf16[2,160,640]{2,1,0:T(8,128)(2,1)}, bf16[2,160,640]{2,1,0:T(8,128)(2,1)S(1)}, u32[]{:S(2)}, u32[]{:S(2)}) collective-permute-start(bf16[2,160,640]{2,1,0:T(8,128)(2,1)} %get-tuple-element.72), channel_id=1, source_target_pairs={{0,192},{64,0},{128,64},{192,128},{1,193},{65,1},{129,65},{193,129... | collective-permute-start | bytes 1228808 | tf_op jit(solution)/shard_map/ppermute | solution.py:546
  106.3 12.3 %collective-permute-start.4 = (bf16[2,160,640]{2,1,0:T(8,128)(2,1)}, bf16[2,160,640]{2,1,0:T(8,128)(2,1)S(1)}, u32[]{:S(2)}, u32[]{:S(2)}) collective-permute-start(bf16[2,160,640]{2,1,0:T(8,128)(2,1)} %get-tuple-element.73), channel_id=1, source_target_pairs={{0,64},{64,128},{128,192},{192,0},{1,65},{65,129},{129,193},{193,1... | collective-permute-start | bytes 1228808 | tf_op jit(solution)/shard_map/ppermute | solution.py:546
  107.4 11.3 %collective-permute-start.3 = (bf16[2,160,640]{2,1,0:T(8,128)(2,1)}, bf16[2,160,640]{2,1,0:T(8,128)(2,1)}, u32[]{:S(2)}, u32[]{:S(2)}) collective-permute-start(bf16[2,160,640]{2,1,0:T(8,128)(2,1)} %get-tuple-element.78), channel_id=1, source_target_pairs={{0,48},{16,0},{32,16},{48,32},{1,49},{17,1},{33,17},{49,33},{2,50}... | collective-permute-start | bytes 1228808 | tf_op jit(solution)/shard_map/ppermute | solution.py:546
  108.9 11.7 %collective-permute-start.2 = (bf16[2,160,640]{2,1,0:T(8,128)(2,1)}, bf16[2,160,640]{2,1,0:T(8,128)(2,1)}, u32[]{:S(2)}, u32[]{:S(2)}) collective-permute-start(bf16[2,160,640]{2,1,0:T(8,128)(2,1)} %get-tuple-element.79), channel_id=1, source_target_pairs={{0,16},{16,32},{32,48},{48,0},{1,17},{17,33},{33,49},{49,1},{2,18}... | collective-permute-start | bytes 1228808 | tf_op jit(solution)/shard_map/ppermute | solution.py:546
  123.5 19.5 %collective-permute-start.7 = (bf16[4,160,640]{2,1,0:T(8,128)(2,1)}, bf16[4,160,640]{2,1,0:T(8,128)(2,1)}, u32[]{:S(2)}, u32[]{:S(2)}) collective-permute-start(bf16[4,160,640]{2,1,0:T(8,128)(2,1)} %pad_maximum_fusion), channel_id=1, source_target_pairs={{0,16},{16,32},{32,48},{48,0},{1,17},{17,33},{33,49},{49,1},{2,18}... | collective-permute-start | bytes 2457608 | tf_op jit(solution)/shard_map/ppermute | solution.py:546
  124.5 18.5 %collective-permute-start.8 = (bf16[4,160,640]{2,1,0:T(8,128)(2,1)}, bf16[4,160,640]{2,1,0:T(8,128)(2,1)}, u32[]{:S(2)}, u32[]{:S(2)}) collective-permute-start(bf16[4,160,640]{2,1,0:T(8,128)(2,1)} %pad_maximum_fusion.1), channel_id=1, source_target_pairs={{0,48},{16,0},{32,16},{48,32},{1,49},{17,1},{33,17},{49,33},{2,50}... | collective-permute-start | bytes 2457608 | tf_op jit(solution)/shard_map/ppermute | solution.py:546
  127.2 33.6 %all-to-all-start.2 = ((bf16[16,176,128]{2,1,0:T(8,128)(2,1)}), bf16[16,176,128]{2,1,0:T(8,128)(2,1)S(1)}, u32[]{:S(2)}, u32[]{:S(2)}) async-start(bf16[16,176,128]{2,1,0:T(8,128)(2,1)} %get-tuple-element.53), calls=%async_computation.2 | async-start | bytes 1441792 | tf_op jit(solution)/shard_map/all_to_all | solution.py:238
  136.6 19.9 %collective-permute-start.10 = (bf16[4,160,640]{2,1,0:T(8,128)(2,1)S(1)}, bf16[4,160,640]{2,1,0:T(8,128)(2,1)S(1)}, u32[]{:S(2)}, u32[]{:S(2)}) collective-permute-start(bf16[4,160,640]{2,1,0:T(8,128)(2,1)S(1)} %pad_maximum_fusion.3), channel_id=1, source_target_pairs={{0,192},{64,0},{128,64},{192,128},{1,193},{65,1},{129,65},{193,129... | collective-permute-start | bytes 2457608 | tf_op jit(solution)/shard_map/ppermute | solution.py:546
  138.6 20.8 %collective-permute-start.9 = (bf16[4,160,640]{2,1,0:T(8,128)(2,1)S(1)}, bf16[4,160,640]{2,1,0:T(8,128)(2,1)S(1)}, u32[]{:S(2)}, u32[]{:S(2)}) collective-permute-start(bf16[4,160,640]{2,1,0:T(8,128)(2,1)S(1)} %pad_maximum_fusion.2), channel_id=1, source_target_pairs={{0,64},{64,128},{128,192},{192,0},{1,65},{65,129},{129,193},{193,1... | collective-permute-start | bytes 2457608 | tf_op jit(solution)/shard_map/ppermute | solution.py:546
  164.3 28.1 %all-to-all-start.4 = ((bf16[16,160,128]{2,1,0:T(8,128)(2,1)}), bf16[16,160,128]{2,1,0:T(8,128)(2,1)S(1)}, u32[]{:S(2)}, u32[]{:S(2)}) async-start(bf16[16,160,128]{2,1,0:T(8,128)(2,1)} %chain.3), calls=%async_computation.4 | async-start | bytes 1310720 | tf_op jit(solution)/shard_map/all_to_all | solution.py:238
  173.1 8.2 %collective-permute-start.13 = (bf16[160,640]{1,0:T(8,128)(2,1)S(1)}, bf16[160,640]{1,0:T(8,128)(2,1)S(1)}, u32[]{:S(2)}, u32[]{:S(2)}) collective-permute-start(bf16[160,640]{1,0:T(8,128)(2,1)S(1)} %get-tuple-element.86), channel_id=1, source_target_pairs={{0,128},{64,192},{128,0},{192,64},{1,129},{65,193},{129,1},{193,65... | collective-permute-start | bytes 614408 | tf_op jit(solution)/shard_map/ppermute | solution.py:546
  173.1 10.0 %collective-permute-start.12 = (bf16[160,640]{1,0:T(8,128)(2,1)S(1)}, bf16[160,640]{1,0:T(8,128)(2,1)S(1)}, u32[]{:S(2)}, u32[]{:S(2)}) collective-permute-start(bf16[160,640]{1,0:T(8,128)(2,1)S(1)} %get-tuple-element.87), channel_id=1, source_target_pairs={{0,192},{64,0},{128,64},{192,128},{1,193},{65,1},{129,65},{193,129... | collective-permute-start | bytes 614408 | tf_op jit(solution)/shard_map/ppermute | solution.py:546
  174.3 11.7 %collective-permute-start.11 = (bf16[160,640]{1,0:T(8,128)(2,1)S(1)}, bf16[160,640]{1,0:T(8,128)(2,1)S(1)}, u32[]{:S(2)}, u32[]{:S(2)}) collective-permute-start(bf16[160,640]{1,0:T(8,128)(2,1)S(1)} %get-tuple-element.88), channel_id=1, source_target_pairs={{0,64},{64,128},{128,192},{192,0},{1,65},{65,129},{129,193},{193,1... | collective-permute-start | bytes 614408 | tf_op jit(solution)/shard_map/ppermute | solution.py:546
  175.4 10.7 %collective-permute-start.16 = (bf16[160,640]{1,0:T(8,128)(2,1)S(1)}, bf16[160,640]{1,0:T(8,128)(2,1)S(1)}, u32[]{:S(2)}, u32[]{:S(2)}) collective-permute-start(bf16[160,640]{1,0:T(8,128)(2,1)S(1)} %get-tuple-element.82), channel_id=1, source_target_pairs={{0,32},{16,48},{32,0},{48,16},{1,33},{17,49},{33,1},{49,17},{2,34}... | collective-permute-start | bytes 614408 | tf_op jit(solution)/shard_map/ppermute | solution.py:546
  175.4 10.7 %collective-permute-start.15 = (bf16[160,640]{1,0:T(8,128)(2,1)S(1)}, bf16[160,640]{1,0:T(8,128)(2,1)S(1)}, u32[]{:S(2)}, u32[]{:S(2)}) collective-permute-start(bf16[160,640]{1,0:T(8,128)(2,1)S(1)} %get-tuple-element.83), channel_id=1, source_target_pairs={{0,48},{16,0},{32,16},{48,32},{1,49},{17,1},{33,17},{49,33},{2,50}... | collective-permute-start | bytes 614408 | tf_op jit(solution)/shard_map/ppermute | solution.py:546
  181.3 6.4 %collective-permute-start.14 = (bf16[160,640]{1,0:T(8,128)(2,1)S(1)}, bf16[160,640]{1,0:T(8,128)(2,1)S(1)}, u32[]{:S(2)}, u32[]{:S(2)}) collective-permute-start(bf16[160,640]{1,0:T(8,128)(2,1)S(1)} %get-tuple-element.84), channel_id=1, source_target_pairs={{0,16},{16,32},{32,48},{48,0},{1,17},{17,33},{33,49},{49,1},{2,18}... | collective-permute-start | bytes 614408 | tf_op jit(solution)/shard_map/ppermute | solution.py:546
  192.4 21.0 %all-to-all-start.3 = ((bf16[8,13,16,128]{3,2,1,0:T(8,128)(2,1)}), bf16[8,13,16,128]{3,2,1,0:T(8,128)(2,1)S(1)}, u32[]{:S(2)}, u32[]{:S(2)}) async-start(bf16[8,13,16,128]{3,2,1,0:T(8,128)(2,1)} %fold.1), calls=%async_computation.3 | async-start | bytes 851968 | tf_op jit(solution)/shard_map/all_to_all | solution.py:238
  216.5 45.2 %all-to-all-start.5 = ((bf16[16,13,16,128]{3,2,1,0:T(8,128)(2,1)}), bf16[16,13,16,128]{3,2,1,0:T(8,128)(2,1)S(1)}, u32[]{:S(2)}, u32[]{:S(2)}) async-start(bf16[16,13,16,128]{3,2,1,0:T(8,128)(2,1)} %get-tuple-element.64), calls=%async_computation.5 | async-start | bytes 1703936 | tf_op jit(solution)/shard_map/all_to_all | solution.py:238
  (30 other events, 132.2 us)
Sparse Core Ops, SparseCore 0:
  10.4 71.2 all-gather.1

commit v4 on v3

--- a/solution.py
+++ b/solution.py
@@ -150,7 +150,7 @@
     )(x, a, b)
 
 
-def intra_kernel(x_ref, cum_ref, cum_t_ref, b_ref, c_ref, skip_ref, y_ref, scores):
+def intra_kernel(x_ref, cum_ref, cum_t_ref, b_ref, c_ref, skip_ref, y_ref, grow_ref, scores):
     step = pl.program_id(0)
 
     @pl.when(step == 0)
@@ -164,12 +164,15 @@
         low = low_half(x.shape)
         head = 2 * (step * STEP + i)
         parts = []
+        sides = []
         for k in range(2):
-            diff = column(cum_t_ref[...], head + k) - cum_ref[pl.ds(head + k, 1), :]
+            sides.append(column(cum_t_ref[...], head + k))
+            diff = sides[k] - cum_ref[pl.ds(head + k, 1), :]
             mixed = (jnp.exp(jnp.minimum(diff, 0.0)) * scores[...]).astype(BF)
             parts.append(nn(mixed, xb))
         skip = jnp.where(low, skip_ref[head], skip_ref[head + 1])
         y_ref[:, lanes_of(i)] = jnp.where(low, parts[0], parts[1]) + skip * x
+        grow_ref[:, lanes_of(i)] = jnp.exp(jnp.where(low, sides[0], sides[1]))
 
 
 def intra(x, cum, cum_t, b, c, skip):
@@ -179,8 +182,8 @@
         in_specs=[
             wide(T, STEP), whole((H, T)), whole((T, H)), whole((T, N)), whole((T, N)), smem(),
         ],
-        out_specs=wide(T, STEP),
-        out_shape=jax.ShapeDtypeStruct((T, D), F32),
+        out_specs=[wide(T, STEP)] * 2,
+        out_shape=[jax.ShapeDtypeStruct((T, D), F32)] * 2,
         scratch_shapes=[pltpu.VMEM((T, T), F32)],
         compiler_params=params(),
         cost_estimate=cost(4 * T * T * D, 8 * T * D, H * T * T),
@@ -188,27 +191,22 @@
     )(x, cum, cum_t, b, c, skip)
 
 
-def inter_kernel(part_ref, cum_t_ref, c_ref, start_ref, y_ref):
-    step = pl.program_id(0)
-    cum_t = cum_t_ref[...]
+def inter_kernel(part_ref, grow_ref, c_ref, start_ref, y_ref):
     read = nt(c_ref[...].astype(BF), start_ref[...])
-    for i in range(WIDE):
-        grow = jnp.exp(spread(cum_t, step * WIDE + i))
-        at = lanes_of(i)
-        y_ref[:, at] = (part_ref[:, at] + grow * read[:, at]).astype(BF)
-
-
-def inter(part, cum_t, c, start):
+    y_ref[...] = (part_ref[...] + grow_ref[...] * read).astype(BF)
+
+
+def inter(part, grow, c, start):
     return pl.pallas_call(
         inter_kernel,
         grid=(PAIRS // WIDE,),
-        in_specs=[wide(T, WIDE), whole((T, H)), whole((T, N)), state_block(WIDE)],
+        in_specs=[wide(T, WIDE), wide(T, WIDE), whole((T, N)), state_block(WIDE)],
         out_specs=wide(T, WIDE),
         out_shape=jax.ShapeDtypeStruct((T, D), BF),
         compiler_params=params(),
-        cost_estimate=cost(2 * T * D * N, 6 * T * D, T * D),
+        cost_estimate=cost(2 * T * D * N, 10 * T * D, 0),
         name="inter",
-    )(part, cum_t, c, start)
+    )(part, grow, c, start)
 
 
 def chain_kernel(reverse, mine_ref, parts_ref, totals_ref, out_ref):
@@ -239,19 +237,13 @@
 
 
 def term_kernel(at_ref, yo_ref, yx_ref, go_ref, gx_ref, first_ref, second_ref):
-    step = pl.program_id(0)
     half = go_ref.shape[1] // 2
-    for i in range(2):
-        cols = slice(i * half, (i + 1) * half)
-        term = tn(yo_ref[...], go_ref[:, cols]) + tn(yx_ref[...], gx_ref[:, cols])
-        term = term.astype(BF)
-        for k in range(4):
-            rel = (k + 4 - at_ref[1]) % 4
-            rows = term[k * OWN : (k + 1) * OWN, :]
-            if i == 0:
-                first_ref[rel, 0] = rows
-            else:
-                second_ref[0, rel] = rows
+    term = tn(yo_ref[...], go_ref[...]) + tn(yx_ref[...], gx_ref[...])
+    term = term.astype(BF)
+    for k in range(4):
+        rows = slice(k * OWN, (k + 1) * OWN)
+        first_ref[k, 0] = term[rows, :half]
+        second_ref[0, (k + 4 - at_ref[1]) % 4] = term[rows, half:]
 
 
 def terms(at, y_own, y_other, g_own, g_other):
@@ -275,9 +267,8 @@
     )(at, y_own, y_other, g_own, g_other)
 
 
-def entry_kernel(own_ref, other_ref, x_ref, cum_t_ref, c_ref, gy_ref, out_ref, sums):
+def entry_kernel(own_ref, other_ref, x_ref, grow_ref, c_ref, gy_ref, out_ref, sums):
     step = pl.program_id(0)
-    cum_t = cum_t_ref[...]
     c = c_ref[...].astype(BF)
     found = []
     for i in range(WIDE):
@@ -285,8 +276,7 @@
         gy = own_ref[:, at] + other_ref[:, at].astype(F32)
         gy_ref[:, at] = gy.astype(BF)
         sums[pl.ds(step * WIDE + i, 1), :] = jnp.sum(gy * x_ref[:, at], axis=0, keepdims=True)
-        grow = jnp.exp(spread(cum_t, step * WIDE + i))
-        found.append(tn((gy * grow).astype(BF), c))
+        found.append(tn((gy * grow_ref[:, at]).astype(BF), c))
     put_states(out_ref, jnp.concatenate(found, axis=0), step * WIDE, WIDE)
 
     @pl.when(step == PAIRS // WIDE - 1)
@@ -304,11 +294,11 @@
         put_note(out_ref, (hi, mid, gd - hi - mid))
 
 
-def entries(own, other, x, cum_t, c):
+def entries(own, other, x, grow, c):
     return pl.pallas_call(
         entry_kernel,
         grid=(PAIRS // WIDE,),
-        in_specs=[wide(T, WIDE), wide(T, WIDE), wide(T, WIDE), whole((T, H)), whole((T, N))],
+        in_specs=[wide(T, WIDE)] * 4 + [whole((T, N))],
         out_specs=[wide(T, WIDE), whole((N_SEQ, ROWS, N))],
         out_shape=[
             jax.ShapeDtypeStruct((T, D), BF),
@@ -318,27 +308,22 @@
         compiler_params=params(),
         cost_estimate=cost(2 * T * D * N, 12 * T * D, T * D),
         name="entries",
-    )(own, other, x, cum_t, c)
-
-
-def back_kernel(
-    x_ref, gy_ref, cum_ref, cum_t_ref, b_ref, c_ref, skip_ref, start_ref, last_ref,
+    )(own, other, x, grow, c)
+
+
+def within_kernel(
+    x_ref, gy_ref, cum_ref, cum_t_ref, b_ref, c_ref, skip_ref,
     gx_ref, ga_ref, gb_ref, gc_ref,
-    scores, d_scores, rows, cols, tails, totals,
+    scores, d_scores, rows, cols,
 ):
     step = pl.program_id(0)
-    bb = b_ref[...].astype(BF)
-    cb = c_ref[...].astype(BF)
 
     @pl.when(step == 0)
     def _():
         keep = iota((T, T), 1) >= iota((T, T), 0)
-        scores[...] = jnp.where(keep, nt(bb, cb), 0.0)
+        scores[...] = jnp.where(keep, nt(b_ref[...].astype(BF), c_ref[...].astype(BF)), 0.0)
         d_scores[...] = jnp.zeros_like(d_scores)
         cols[...] = jnp.zeros_like(cols)
-        tails[...] = jnp.zeros_like(tails)
-        gb_ref[...] = jnp.zeros_like(gb_ref)
-        gc_ref[...] = jnp.zeros_like(gc_ref)
 
     lanes = iota((T, N), 1)
     low = low_half((T, 2 * P_SIZE))
@@ -347,14 +332,10 @@
         at = lanes_of(i)
         x = x_ref[:, at]
         gyb = gy_ref[:, at]
-        gy = gyb.astype(F32)
         parts = []
-        sides = []
         for k in range(2):
             head = 2 * pair + k
-            side = column(cum_t_ref[...], head)
-            sides.append(side)
-            diff = cum_ref[pl.ds(head, 1), :] - side
+            diff = cum_ref[pl.ds(head, 1), :] - column(cum_t_ref[...], head)
             weights = jnp.exp(jnp.minimum(diff, 0.0))
             mine = jnp.where(low if k == 0 else ~low, x, 0.0).astype(BF)
             d_mixed = weights * nt(mine, gyb)
@@ -364,50 +345,29 @@
             rows[pl.ds(head, 1), :] = jnp.sum(change, axis=0, keepdims=True)
             down = jnp.sum(change, axis=1, keepdims=True)
             cols[...] -= jnp.where(lanes == head, down, 0.0)
-        cum = jnp.where(low, sides[0], sides[1])
-        grow = jnp.exp(cum)
-        tail = jnp.exp(cum[T - 1 : T, :] - cum)
-        states = slice(i * 2 * P_SIZE, (i + 1) * 2 * P_SIZE)
-        start = start_ref[states, :]
-        last = last_ref[states, :]
-        pick = (lanes[:N] == 2 * pair + iota((N, N), 0) // P_SIZE).astype(BF)
-        grown = gy * grow
-        cols[...] += nn((grown * nt(cb, start)).astype(BF), pick)
-        gc_ref[...] += nn(grown.astype(BF), start)
-        faded = x * tail
-        back = nt(bb, last)
-        tails[...] += nn((faded * back).astype(BF), pick)
-        gb_ref[...] += nn(faded.astype(BF), last)
         skip = jnp.where(low, skip_ref[2 * pair], skip_ref[2 * pair + 1])
-        gx_ref[:, at] = jnp.where(low, parts[0], parts[1]) + tail * back + skip * gy
-        both = start.astype(F32) * last.astype(F32)
-        for k in range(2):
-            part = both[k * P_SIZE : (k + 1) * P_SIZE, :]
-            totals[pl.ds(2 * pair + k, 1), :] = jnp.sum(part, axis=0, keepdims=True)
+        gx_ref[:, at] = jnp.where(low, parts[0], parts[1]) + skip * gyb.astype(F32)
 
     @pl.when(step == PAIRS // STEP - 1)
     def _():
         keep = iota((T, T), 1) >= iota((T, T), 0)
         ds = jnp.where(keep, d_scores[...], 0.0).astype(BF)
-        gb_ref[...] += nn(ds, cb)
-        gc_ref[...] += tn(ds, bb)
+        gb_ref[...] = nn(ds, c_ref[...].astype(BF))
+        gc_ref[...] = tn(ds, b_ref[...].astype(BF))
         after = (iota((T, T), 0) >= iota((T, T), 1)).astype(F32)
-        before = (iota((T, T), 0) < iota((T, T), 1)).astype(F32)
         dims = (((0,), (0,)), ((), ()))
         ga = jnp.dot(rows[...], after, precision=HIGH, preferred_element_type=F32)
         up = lax.dot_general(cols[...], after, dims, precision=HIGH, preferred_element_type=F32)
-        up += lax.dot_general(tails[...], before, dims, precision=HIGH, preferred_element_type=F32)
-        whole_decay = jnp.exp(cum_ref[:, T - 1 : T])
-        ga_ref[...] = ga + up[:H] + whole_decay * jnp.sum(totals[...], axis=1, keepdims=True)
-
-
-def backward(x, gy, cum, cum_t, b, c, skip, start, last):
-    return pl.pallas_call(
-        back_kernel,
+        ga_ref[...] = ga + up[:H]
+
+
+def within(x, gy, cum, cum_t, b, c, skip):
+    return pl.pallas_call(
+        within_kernel,
         grid=(PAIRS // STEP,),
         in_specs=[
             wide(T, STEP), wide(T, STEP), whole((H, T)), whole((T, H)), whole((T, N)),
-            whole((T, N)), smem(), state_block(STEP), state_block(STEP),
+            whole((T, N)), smem(),
         ],
         out_specs=[wide(T, STEP), whole((H, T)), whole((T, N)), whole((T, N))],
         out_shape=[
@@ -421,41 +381,115 @@
             pltpu.VMEM((T, T), F32),
             pltpu.VMEM((H, T), F32),
             pltpu.VMEM((T, N), F32),
+        ],
+        compiler_params=params(),
+        cost_estimate=cost(6 * T * T * D, 10 * T * D, H * T * T),
+        name="within",
+    )(x, gy, cum, cum_t, b, c, skip)
+
+
+def across_kernel(
+    x_ref, gy_ref, grow_ref, part_ref, cum_ref, cum_t_ref, b_ref, c_ref, start_ref, last_ref,
+    ga_in, gb_in, gc_in,
+    gx_ref, ga_ref, gb_ref, gc_ref,
+    cols, tails, totals,
+):
+    step = pl.program_id(0)
+    bb = b_ref[...].astype(BF)
+    cb = c_ref[...].astype(BF)
+
+    @pl.when(step == 0)
+    def _():
+        cols[...] = jnp.zeros_like(cols)
+        tails[...] = jnp.zeros_like(tails)
+        gb_ref[...] = gb_in[...]
+        gc_ref[...] = gc_in[...]
+
+    width = WIDE * 2 * P_SIZE
+    start = start_ref[...]
+    last = last_ref[...]
+    cum_t = cum_t_ref[...]
+    sides = [spread(cum_t, step * WIDE + i) for i in range(WIDE)]
+    cum = jnp.concatenate(sides, axis=1)
+    tail = jnp.exp(cum[T - 1 : T, :] - cum)
+    pick = iota((width, N), 1) == step * 2 * WIDE + iota((width, N), 0) // P_SIZE
+    grown = gy_ref[...].astype(F32) * grow_ref[...]
+    cols[...] += nn((grown * nt(cb, start)).astype(BF), pick.astype(BF))
+    gc_ref[...] += nn(grown.astype(BF), start)
+    faded = x_ref[...] * tail
+    back = nt(bb, last)
+    tails[...] += nn((faded * back).astype(BF), pick.astype(BF))
+    gb_ref[...] += nn(faded.astype(BF), last)
+    gx_ref[...] = part_ref[...] + tail * back
+    both = jnp.sum(start.astype(F32) * last.astype(F32), axis=1, keepdims=True)
+    totals[pl.ds(step, 1), :] = jnp.sum(jnp.where(pick, both, 0.0), axis=0, keepdims=True)
+
+    @pl.when(step == PAIRS // WIDE - 1)
+    def _():
+        after = (iota((T, T), 0) >= iota((T, T), 1)).astype(F32)
+        before = (iota((T, T), 0) < iota((T, T), 1)).astype(F32)
+        dims = (((0,), (0,)), ((), ()))
+        up = lax.dot_general(cols[...], after, dims, precision=HIGH, preferred_element_type=F32)
+        up += lax.dot_general(tails[...], before, dims, precision=HIGH, preferred_element_type=F32)
+        total = jnp.sum(totals[...], axis=0, keepdims=True)
+        total = jnp.sum(jnp.where(iota((H, N), 0) == iota((H, N), 1), total, 0.0), axis=1, keepdims=True)
+        ga_ref[...] = ga_in[...] + up[:H] + jnp.exp(cum_ref[:, T - 1 : T]) * total
+
+
+def across(x, gy, grow, part, cum, cum_t, b, c, start, last, ga, gb, gc):
+    return pl.pallas_call(
+        across_kernel,
+        grid=(PAIRS // WIDE,),
+        in_specs=[wide(T, WIDE)] * 4
+        + [whole((H, T)), whole((T, H)), whole((T, N)), whole((T, N))]
+        + [state_block(WIDE), state_block(WIDE), whole((H, T)), whole((T, N)), whole((T, N))],
+        out_specs=[wide(T, WIDE), whole((H, T)), whole((T, N)), whole((T, N))],
+        out_shape=[
+            jax.ShapeDtypeStruct((T, D), F32),
+            jax.ShapeDtypeStruct((H, T), F32),
+            jax.ShapeDtypeStruct((T, N), F32),
+            jax.ShapeDtypeStruct((T, N), F32),
+        ],
+        scratch_shapes=[
             pltpu.VMEM((T, N), F32),
-            pltpu.VMEM((H, N), F32),
-        ],
-        compiler_params=params(),
-        cost_estimate=cost(8 * T * T * D, 14 * T * D, H * T * T),
-        name="backward",
-    )(x, gy, cum, cum_t, b, c, skip, start, last)
-
-
-def fold_kernel(a0, a1, a2, a3, b0, b1, b2, b3, out_ref):
-    sums = []
-    for parts in ((a0, a1, a2, a3), (b0, b1, b2, b3)):
+            pltpu.VMEM((T, N), F32),
+            pltpu.VMEM((PAIRS // WIDE, N), F32),
+        ],
+        compiler_params=params(),
+        cost_estimate=cost(8 * T * D * N, 20 * T * D, T * D),
+        name="across",
+    )(x, gy, grow, part, cum, cum_t, b, c, start, last, ga, gb, gc)
+
+
+def fold_kernel(z_ref, a0, a1, a2, a3, b0, b1, b2, b3, *rest):
+    outs, sums = rest[:8], rest[8]
+    half = a0.shape[1]
+    for i, parts in enumerate(((a0, a1, a2, a3), (b0, b1, b2, b3))):
         total = parts[0][...].astype(F32)
         for part in parts[1:]:
             total += part[...].astype(F32)
-        sums.append(total.astype(BF))
-    for q in range(8 * TILES):
-        r, c = divmod(q, 10)
-        if r < 10:
-            tile = sums[c // 5][16 * r : 16 * r + 16, 128 * (c % 5) : 128 * (c % 5) + 128]
-        else:
-            tile = jnp.zeros((16, 128), BF)
-        out_ref[q // TILES, q % TILES] = tile
-
-
-def fold(parts):
+        sums[:, i * half : (i + 1) * half] = total
+    for d in range(8):
+        for i in range(TILES):
+            q = TILES * ((z_ref[0] + d) % 8) + i
+            r = jnp.minimum(q // 10, 9)
+            row = pl.multiple_of(16 * r, 16)
+            col = pl.multiple_of(128 * (q % 10), 128)
+            tile = sums[pl.ds(row, 16), pl.ds(col, 128)]
+            outs[d][i] = jnp.where(q < 100, tile, 0.0).astype(BF)
+
+
+def fold(z, parts):
     return pl.pallas_call(
         fold_kernel,
-        in_specs=[vmem()] * 8,
-        out_specs=vmem(),
-        out_shape=jax.ShapeDtypeStruct((8, TILES, 16, 128), BF),
+        in_specs=[smem()] + [vmem()] * 8,
+        out_specs=[vmem()] * 8,
+        out_shape=[jax.ShapeDtypeStruct((TILES, 16, 128), BF)] * 8,
+        scratch_shapes=[pltpu.VMEM((OWN, D // 2), F32)],
         compiler_params=params(),
         cost_estimate=cost(4 * OWN * D // 2, 8 * OWN * D // 2, 0),
         name="fold",
-    )(*parts)
+    )(z, *parts)
 
 
 def groups_of(row0, count, ids_ref):
@@ -463,11 +497,12 @@
     return jnp.sum(jnp.where(heads, ids_ref[...], 0.0), axis=1, keepdims=True)
 
 
-def zsum_kernel(row0_ref, z_ref, ids_ref, parts_ref, got_ref, out_ref, note_ref):
-    total = parts_ref[0].astype(F32)
-    for z in range(1, 8):
-        total += parts_ref[z].astype(F32)
-    for s in range(N_SEQ):
+def zsum_kernel(row0_ref, z_ref, ids_ref, got_ref, *rest):
+    parts, out_ref, note_ref = rest[:8], rest[8], rest[9]
+    total = parts[0][...].astype(F32)
+    for part in parts[1:]:
+        total += part[...].astype(F32)
+    for s in range(8):
         out_ref[s] = total.astype(BF)
     found = jnp.zeros((16, N), F32)
     for i in range(TILES):
@@ -485,27 +520,29 @@
 def zsum(row0, z, ids, parts, got):
     return pl.pallas_call(
         zsum_kernel,
-        in_specs=[smem(), smem(), vmem(), vmem(), vmem()],
+        in_specs=[smem(), smem()] + [vmem()] * 10,
         out_specs=[vmem(), vmem()],
         out_shape=[
-            jax.ShapeDtypeStruct((N_SEQ, TILES, 16, 128), BF),
+            jax.ShapeDtypeStruct((8, TILES, 16, 128), BF),
             jax.ShapeDtypeStruct((1, N), F32),
         ],
         compiler_params=params(),
         cost_estimate=cost(8 * OWN * 160, 6 * OWN * D, 0),
         name="zsum",
-    )(row0, z, ids, parts, got)
-
-
-def tile_of(ref, r, c, core):
+    )(row0, z, ids, got, *parts)
+
+
+def tile_of(ref, r, c):
     z, i = divmod(10 * r + c, TILES)
-    return ref[2 * z + core, i].astype(F32)
-
-
-def clip_kernel(tokens_all, row0_ref, ids_ref, tiles_ref, note_ref, w_ref, d_ref):
+    return ref[z, i].astype(F32)
+
+
+def clip_kernel(tokens_all, row0_ref, core_ref, ids_ref, own_ref, other_ref, note_ref, w_ref, d_ref):
     ids = ids_ref[...]
     lane = iota((1, N), 1)
-    note = note_ref[...]
+    note = note_ref[0]
+    for s in range(1, N_SEQ):
+        note = note + note_ref[s]
     grad_d = jnp.where(lane < H, note, 0.0)
     groups = groups_of(row0_ref[0], OWN, ids_ref)
     w_factor = jnp.zeros((OWN, 1), F32)
@@ -522,24 +559,22 @@
     d_ref[...] = grad_d * d_factor
     for r in range(10):
         scale = w_factor[16 * r : 16 * r + 16, :]
-        for core in range(2):
+        for ref, core in ((own_ref, core_ref[0]), (other_ref, 1 - core_ref[0])):
             for c in range(10):
-                col = core * (D // 2) + 128 * c
-                w_ref[16 * r : 16 * r + 16, col : col + 128] = (
-                    tile_of(tiles_ref, r, c, core) * scale
-                )
-
-
-def clip(tokens_all, row0, ids, tiles, note):
+                col = pl.multiple_of(core * (D // 2) + 128 * c, 128)
+                w_ref[16 * r : 16 * r + 16, pl.ds(col, 128)] = tile_of(ref, r, c) * scale
+
+
+def clip(tokens_all, row0, core, ids, own, other, note):
     return pl.pallas_call(
         functools.partial(clip_kernel, tokens_all),
-        in_specs=[smem(), vmem(), vmem(), vmem()],
+        in_specs=[smem(), smem()] + [vmem()] * 4,
         out_specs=[vmem(), vmem()],
         out_shape=[jax.ShapeDtypeStruct((OWN, D), F32), jax.ShapeDtypeStruct((1, N), F32)],
         compiler_params=params(),
         cost_estimate=cost(2 * OWN * D, 6 * OWN * D, 0),
         name="clip",
-    )(row0, ids, tiles, note)
+    )(row0, core, ids, own, other, note)
 
 
 def shifted(v, axis, d):
@@ -555,12 +590,16 @@
     return shifted(t[2, :m], axis, 1), shifted(t[2, m:], axis, -1)
 
 
-def near(t, ra, rb, axis):
+def passed(t, ra, rb):
     m = t.shape[1] // 2
     up = jnp.concatenate([plus(t[1, :m], ra), t[1, m:]], axis=0)
     down = jnp.concatenate([t[3, :m], plus(t[3, m:], rb)], axis=0)
-    got = (t[0], shifted(up, axis, 1), shifted(down, axis, -1))
-    return (got[0].astype(F32) + got[1].astype(F32) + got[2].astype(F32)).astype(BF)
+    return up, down
+
+
+def near(t, up, down, axis):
+    total = t[0].astype(F32) + shifted(up, axis, 1).astype(F32)
+    return (total + shifted(down, axis, -1).astype(F32)).astype(BF)
 
 
 def direct(t, axis):
@@ -572,12 +611,13 @@
 
 
 def sum_over(v, axis):
-    n = lax.axis_size(axis)
-    bit = 1
-    while bit < n:
-        v = v + lax.ppermute(v, axis, [(i, i ^ bit) for i in range(n)])
-        bit *= 2
-    return v
+    got = [lax.ppermute(v, axis, [(i, i ^ k) for i in range(4)]) for k in (1, 2, 3)]
+    return (v + got[0]) + (got[1] + got[2])
+
+
+def along_z(parts):
+    got = [lax.ppermute(parts[d], "z", [(i, (i + d) % 8) for i in range(8)]) for d in range(1, 8)]
+    return [parts[0]] + got
 
 
 def tie(*values):
@@ -602,40 +642,41 @@
 
     cum, cum_t, sent = local_ends(x, a, b)
     got = swap(sent, SEQ)
-    y_part = intra(x, cum, cum_t, b, c, d_skip)
+    y_part, grow = intra(x, cum, cum_t, b, c, d_skip)
     start = swap(chain(got, got, mine, False), SEQ).reshape(H * P_SIZE, N)
-    y_own = inter(y_part, cum_t, c, start)
+    y_own = inter(y_part, grow, c, start)
     y_other = other_core(y_own)
-
-    w_half, _ = tie(w_half, y_own)
+    first, second = terms(at, y_own, y_other, g_mine, g_other)
+
+    first = lax.psum_scatter(first.reshape(-1, half // 2), "x", scatter_dimension=0, tiled=True)
+    far_y = far(second, "y")
+    w_half, _ = tie(w_half, second)
     dims = (((1,), (1,)), ((), ()))
     gy_other = lax.dot_general(g_other, w_half, dims, preferred_element_type=F32).astype(BF)
     gy_own = lax.dot_general(g_mine, w_half, dims, preferred_element_type=F32)
-    y_other, gy_other, gy_own = tie(y_other, gy_other, gy_own)
     gy_other = other_core(gy_other)
-    first, second = terms(at, y_own, y_other, g_mine, g_other)
-    far_x = far(first, "x")
-    far_y = far(second, "y")
-    gy_own, gy_other, *_ = tie(gy_own, gy_other, first)
-    gy, sent_back = entries(gy_own, gy_other, x, cum_t, c)
-    far_x, far_y, sent_back = tie(far_x, far_y, sent_back)
+    far_y = tie(*far_y, gy_own)[:2]
+    up, down = passed(second, *far_y)
+    up, down, gy_own, gy_other = tie(up, down, gy_own, gy_other)
+    second = near(second, up, down, "y")
+    gy, sent_back = entries(gy_own, gy_other, x, grow, c)
     got_back = swap(sent_back, SEQ)
-    first = near(first, *far_x, "x")
-    second = near(second, *far_y, "y")
-    first, second, got_back = tie(first, second, got_back)
-    first = direct(first, "y")
+    gx, ga, gb, gc = within(x, gy, cum, cum_t, b, c, d_skip)
+    first, second, gx = tie(first, second, gx)
+    first = direct(first.reshape(4, OWN, half // 2), "y")
     second = direct(second, "x")
+    mine, _ = tie(mine, second[0])
     last = swap(chain(got_back, got, mine, True), SEQ).reshape(H * P_SIZE, N)
-    tiles = swap(fold(first + second), "z")
-
-    gx, ga, gb, gc = backward(x, gy, cum, cum_t, b, c, d_skip, start, last)
-
-    tiles, gx = tie(tiles, gx)
+
+    tiles = along_z(fold(at_z, first + second))
     tiles, note = zsum(row0, at_z, ids, tiles, got_back)
-    tiles = swap(tiles, SEQ)
-    for axis in ("x", "y", "z", "core"):
-        note = sum_over(note, axis)
-    clipped_w, clipped_d = clip(tokens_all, row0, ids, tiles, note)
+    tiles = swap(tiles, "z")
+    note = sum_over(sum_over(note, "x"), "y")
+    tiles_other = other_core(tiles)
+    gx, ga, gb, gc = across(x, gy, grow, gx, cum, cum_t, b, c, start, last, ga, gb, gc)
+    note = swap(jnp.broadcast_to(note[None], (N_SEQ, 1, N)), SEQ)
+    core = core.reshape(1).astype(jnp.int32)
+    clipped_w, clipped_d = clip(tokens_all, row0, core, ids, tiles, tiles_other, note)
     return (gx[None], ga[None], gb[None], gc[None], clipped_w, clipped_d[0, :H])
 
 

time: 275 us -> 276 us (level)
  blocking collectives: 0 us -> 14.8 us
  starting transfers between devices: 69.6 us -> 59.4 us
  other arithmetic: 9.39 us -> 3.51 us
  Pallas kernels: 63.5 us -> 67.7 us
    all_to_all x6 -> x5, waiting for transfers between devices: 33.3 us -> 58.6 us  [swap(): return lax.all_to_all(v, axis, 0, 0, tiled=True)]
    all_to_all x6 -> x5, starting transfers between devices: 45.6 us -> 26.2 us  [swap(): return lax.all_to_all(v, axis, 0, 0, tiled=True)]
    ppermute x14 -> x10, waiting for transfers between devices: 34.4 us -> 19.5 us  [shifted(): return lax.ppermute(v, axis, [(i, (i + d) % 4) for i in range(4)])]
    all_to_all x0 -> x1, blocking collectives: none -> 14.8 us  [swap(): return lax.all_to_all(v, axis, 0, 0, tiled=True)]
    ppermute x8 -> x13, waiting for transfers between devices: 21.9 us -> 8.92 us  [the longest x7 5.27 us: along_z(): lax.ppermute(parts[d], 'z', [(i, (i + d) % 8) for i in range(8)])]
    ppermute x8 -> x13, starting transfers between devices: 11.8 us -> 21.2 us  [the longest x7 14.7 us: along_z(): lax.ppermute(parts[d], 'z', [(i, (i + d) % 8) for i in range(8)])]
    pallas_call x3 -> x4, Pallas kernels: 20.8 us -> 25.3 us  [the longest x1 11.4 us: within(): pl.pallas_call(within_kernel, grid=(PAIRS // STEP,), in_specs=[wide(T, ST...]
    squeeze x2 -> x1, local copies, waits for them, and re-layouts: 3.64 us -> 0.14 us  [passed(): down = jnp.concatenate([t[3, :m], plus(t[3, m:], rb)], axis=0)]
  transfers between devices with their start and end apart: 32 -> 34, of which waited for: 21 -> 19; matrix products, arithmetic and copies ran while one was open for 8% -> 6% of each run, Pallas kernels for 21% -> 21%
where the time goes in v4:
time: 276 us; the launch traced here: 274 us
  waiting for transfers between devices  90.5 us (33%)
  Pallas kernels  67.7 us (25%)
  starting transfers between devices  59.4 us (22%)
  between operations  15.8 us (6%)
  blocking collectives  14.8 us (5%)
  local copies, waits for them, and re-layouts  14.1 us (5%)
  matrix products  8.27 us (3%)
  other arithmetic  3.51 us (1%)
    all_to_all x5, waiting for transfers between devices, swap(): return lax.all_to_all(v, axis, 0, 0, tiled=True)  58.6 us
    all_to_all x5, starting transfers between devices, swap(): return lax.all_to_all(v, axis, 0, 0, tiled=True)  26.2 us
    ppermute x10, waiting for transfers between devices, shifted(): return lax.ppermute(v, axis, [(i, (i + d) % 4) for i in range(4)])  19.5 us
    all_to_all x1, blocking collectives, swap(): return lax.all_to_all(v, axis, 0, 0, tiled=True)  14.8 us
    ppermute x7, starting transfers between devices, along_z(): lax.ppermute(parts[d], 'z', [(i, (i + d) % 8) for i in range(8)])  14.7 us
    pallas_call x1, Pallas kernels, within(): pl.pallas_call(within_kernel, grid=(PAIRS // STEP,), in_specs=[wide(T, ST...  11.4 us
    ppermute x10, starting transfers between devices, shifted(): return lax.ppermute(v, axis, [(i, (i + d) % 4) for i in range(4)])  10.8 us
    pallas_call x1, Pallas kernels, intra(): pl.pallas_call(intra_kernel, grid=(PAIRS // STEP,), in_specs=[wide(T, STE...  9.25 us
  transfers between devices with their start and end apart: 34, of which 19 were waited for; matrix products, arithmetic and copies ran while one was open for 6% of the time, Pallas kernels for 21%

profile of v4, /device:TPU:1, one launch (start us, length us, event | category | flops | bytes accessed | tf_op | source)
XLA Modules:
  0.0 274.0 jit_solution(9536368300886609005)
XLA Ops:
  9.9 5.7 %ends.1 = (f32[40,256]{1,0:T(8,128)}, f32[256,40]{1,0:T(8,128)}, bf16[16,176,128]{2,1,0:T(8,128)(2,1)}) custom-call(f32[256,2560]{1,0:T(8,128)} %bitcast.56, f32[40,256]{1,0:T(8,128)} %bitcast.74, f32[256,128]{1,0:T(8,128)} %bitcast.70), custom_call_target="tpu_custom_call" | custom-call | flops 167772160 | bytes 2621440 | tf_op jit(solution)/shard_map/ends/pallas_call | solution.py:137
  15.6 10.0 %all-to-all-start = ((bf16[16,176,128]{2,1,0:T(8,128)(2,1)}), bf16[16,176,128]{2,1,0:T(8,128)(2,1)S(1)}, u32[]{:S(2)}, u32[]{:S(2)}) async-start(bf16[16,176,128]{2,1,0:T(8,128)(2,1)} %get-tuple-element.50), calls=%async_computation | async-start | bytes 1441792 | tf_op jit(solution)/shard_map/all_to_all | solution.py:236
  25.6 21.3 %all-to-all-done.parts_ref.totals_ref = bf16[16,176,128]{2,1,0:T(8,128)(2,1)S(1)} async-done(((bf16[16,176,128]{2,1,0:T(8,128)(2,1)}), bf16[16,176,128]{2,1,0:T(8,128)(2,1)S(1)}, u32[]{:S(2)}, u32[]{:S(2)}) %all-to-all-start) | async-done | bytes 720928 | tf_op jit(solution)/shard_map/all_to_all | solution.py:236
  50.4 3.5 %all-to-all-start.1 = ((bf16[16,160,128]{2,1,0:T(8,128)(2,1)}), bf16[16,160,128]{2,1,0:T(8,128)(2,1)S(1)}, u32[]{:S(2)}, u32[]{:S(2)}) async-start(bf16[16,160,128]{2,1,0:T(8,128)(2,1)} %chain.2), calls=%async_computation.1 | async-start | bytes 1310720 | tf_op jit(solution)/shard_map/all_to_all | solution.py:236
  54.0 9.3 %intra.1 = (f32[256,2560]{1,0:T(8,128)}, f32[256,2560]{1,0:T(8,128)}) custom-call(f32[256,2560]{1,0:T(8,128)} %bitcast.57, f32[40,256]{1,0:T(8,128)} %get-tuple-element.46.cum_ref, f32[256,40]{1,0:T(8,128)} %get-tuple-element.47.cum_t_ref, f32[256,128]{1,0:T(8,128)} %bitcast.71, f32[256,128]{1,0:T(8,128)} %bitcast.65, f32[40]{0:T(128)} %skip_ref.3), custom_call_target="tpu_custom_call" | custom-call | flops 671088640 | bytes 5242880 | tf_op jit(solution)/shard_map/intra/pallas_call | solution.py:179
  63.2 10.3 %all-to-all-done.1 = bf16[16,160,128]{2,1,0:T(8,128)(2,1)S(1)} async-done(((bf16[16,160,128]{2,1,0:T(8,128)(2,1)}), bf16[16,160,128]{2,1,0:T(8,128)(2,1)S(1)}, u32[]{:S(2)}, u32[]{:S(2)}) %all-to-all-start.1) | async-done | bytes 655392 | tf_op jit(solution)/shard_map/all_to_all | solution.py:236
  74.3 5.1 %inter.1.yo_ref = bf16[256,2560]{1,0:T(8,128)(2,1)} custom-call(f32[256,2560]{1,0:T(8,128)} %get-tuple-element.48.part_ref, f32[256,2560]{1,0:T(8,128)} %get-tuple-element.49.grow_ref, f32[256,128]{1,0:T(8,128)} %bitcast.66, bf16[2560,128]{1,0:T(8,128)(2,1)} %bitcast.61), custom_call_target="tpu_custom_call" | custom-call | flops 167772160 | bytes 6553600 | tf_op jit(solution)/shard_map/inter/pallas_call | solution.py:200
  84.2 8.2 %terms.1 = (bf16[4,4,160,640]{3,2,1,0:T(8,128)(2,1)}, bf16[4,4,160,640]{3,2,1,0:T(8,128)(2,1)}) custom-call(s32[2]{0:T(128)} %pad_add_fusion.at_ref, bf16[256,2560]{1,0:T(8,128)(2,1)} %inter.1.yo_ref, bf16[256,2560]{1,0:T(8,128)(2,1)} %collective-permute-done.yx_ref, bf16[256,1280]{1,0:T(8,128)(2,1)} %get-tuple-element.93.go_ref, bf16[256,1280]{1,0:T(8,128)(2,1)} %copy-done.25), custom_call_target="tpu_custom_call" | custom-call | flops 3355443200 | bytes 9830400 | tf_op jit(solution)/shard_map/terms/pallas_call | solution.py:252
  93.6 4.9 %convolution_convert_fusion = bf16[256,2560]{1,0:T(8,128)(2,1)S(1)} fusion(bf16[256,1280]{1,0:T(8,128)(2,1)S(1)} %copy-done.26, bf16[2560,1280]{1,0:T(8,128)(2,1)} %all-gather.2.cloned.1.call-done), kind=kOutput, calls=%fused_computation | convolution fusion | flops 1678376960 | bytes 8519680 | tf_op jit(solution)/shard_map/dot_general | solution.py:655
  101.6 3.4 %fusion.5.own_ref = f32[256,2560]{1,0:T(8,128)} fusion(bf16[256,1280]{1,0:T(8,128)(2,1)S(1)} %copy-done.9, bf16[2560,1280]{1,0:T(8,128)(2,1)S(1)} %copy-done.24), kind=kOutput, calls=%fused_computation.27 | convolution fusion | flops 1677721600 | bytes 9830400 | tf_op jit(solution)/shard_map/dot_general | solution.py:656
  105.0 5.1 %collective-permute-done.3 = bf16[2,160,640]{2,1,0:T(8,128)(2,1)S(1)} collective-permute-done((bf16[2,160,640]{2,1,0:T(8,128)(2,1)S(1)}, bf16[2,160,640]{2,1,0:T(8,128)(2,1)S(1)}, u32[]{:S(2)}, u32[]{:S(2)}) %collective-permute-start.3) | collective-permute-done | bytes 409632 | tf_op jit(solution)/shard_map/ppermute | solution.py:581
  116.5 6.3 %entries.1 = (bf16[256,2560]{1,0:T(8,128)(2,1)}, bf16[16,176,128]{2,1,0:T(8,128)(2,1)}) custom-call(f32[256,2560]{1,0:T(8,128)} %fusion.5.own_ref, bf16[256,2560]{1,0:T(8,128)(2,1)} %copy-done.7, f32[256,2560]{1,0:T(8,128)} %bitcast.58, f32[256,2560]{1,0:T(8,128)} %get-tuple-element.49.grow_ref, f32[256,128]{1,0:T(8,128)} %bitcast.67), custom_call_target="tpu_custom_call" | custom-call | flops 167772160 | bytes 7864320 | tf_op jit(solution)/shard_map/entries/pallas_call | solution.py:298
  122.7 5.4 %all-to-all-start.2 = ((bf16[16,176,128]{2,1,0:T(8,128)(2,1)}), bf16[16,176,128]{2,1,0:T(8,128)(2,1)S(1)}, u32[]{:S(2)}, u32[]{:S(2)}) async-start(bf16[16,176,128]{2,1,0:T(8,128)(2,1)} %get-tuple-element.65), calls=%async_computation.3 | async-start | bytes 1441792 | tf_op jit(solution)/shard_map/all_to_all | solution.py:236
  128.1 11.4 %within.1 = (f32[256,2560]{1,0:T(8,128)}, f32[40,256]{1,0:T(8,128)}, f32[256,128]{1,0:T(8,128)}, f32[256,128]{1,0:T(8,128)}) custom-call(f32[256,2560]{1,0:T(8,128)} %bitcast.59, bf16[256,2560]{1,0:T(8,128)(2,1)} %get-tuple-element.57.gy_ref, f32[40,256]{1,0:T(8,128)} %get-tuple-element.46.cum_ref, f32[256,40]{1,0:T(8,128)} %get-tuple-element.47.cum_t_ref, ...), custom_call_target="tpu_custom_call" | custom-call | flops 1006632960 | bytes 6553600 | tf_op jit(solution)/shard_map/within/pallas_call | solution.py:365
  150.2 4.4 %collective-permute-done.11.b2 = bf16[160,640]{1,0:T(8,128)(2,1)S(1)} collective-permute-done((bf16[160,640]{1,0:T(8,128)(2,1)S(1)}, bf16[160,640]{1,0:T(8,128)(2,1)S(1)}, u32[]{:S(2)}, u32[]{:S(2)}) %collective-permute-start.11) | collective-permute-done | bytes 204832 | tf_op jit(solution)/shard_map/ppermute | solution.py:581
  157.5 3.3 %collective-permute-done.7.a1 = bf16[160,640]{1,0:T(8,128)(2,1)S(1)} collective-permute-done((bf16[160,640]{1,0:T(8,128)(2,1)S(1)}, bf16[160,640]{1,0:T(8,128)(2,1)S(1)}, u32[]{:S(2)}, u32[]{:S(2)}) %collective-permute-start.7) | collective-permute-done | bytes 204832 | tf_op jit(solution)/shard_map/ppermute | solution.py:581
  161.5 3.4 %fold.1 = (bf16[13,16,128]{2,1,0:T(8,128)(2,1)}, bf16[13,16,128]{2,1,0:T(8,128)(2,1)}, bf16[13,16,128]{2,1,0:T(8,128)(2,1)}, bf16[13,16,128]{2,1,0:T(8,128)(2,1)...) custom-call(s32[1]{0:T(128)} %bitcast.27.z_ref, ...), custom_call_target="tpu_custom_call" | custom-call | flops 819200 | bytes 1638400 | tf_op jit(solution)/shard_map/fold/pallas_call | solution.py:483
  180.1 5.3 %collective-permute-done.18.rest_6_ = bf16[13,16,128]{2,1,0:T(8,128)(2,1)S(1)} collective-permute-done((bf16[13,16,128]{2,1,0:T(8,128)(2,1)}, bf16[13,16,128]{2,1,0:T(8,128)(2,1)S(1)}, u32[]{:S(2)}, u32[]{:S(2)}) %collective-permute-start.18) | collective-permute-done | bytes 53280 | tf_op jit(solution)/shard_map/ppermute | solution.py:619
  199.1 14.8 %all_to_all.30.note_ref = f32[16,1,128]{2,1,0:T(1,128)} all-to-all(f32[16,1,128]{2,1,0:T(1,128)S(1)} %broadcast_in_dim.29), channel_id=1, replica_groups=mesh['y'=4,'x'=4,'z'=8,'core'=2] {'z','core'}, dimensions={0} | all-to-all | bytes 16384 | tf_op jit(solution)/shard_map/all_to_all | solution.py:236
  213.9 3.5 %all-to-all-start.4 = ((bf16[8,13,16,128]{3,2,1,0:T(8,128)(2,1)}), bf16[8,13,16,128]{3,2,1,0:T(8,128)(2,1)S(1)}, u32[]{:S(2)}, u32[]{:S(2)}) async-start(bf16[8,13,16,128]{3,2,1,0:T(8,128)(2,1)} %get-tuple-element.82), calls=%async_computation.5 | async-start | bytes 851968 | tf_op jit(solution)/shard_map/all_to_all | solution.py:236
  220.0 13.1 %all-to-all-done.4.own_ref = bf16[8,13,16,128]{3,2,1,0:T(8,128)(2,1)S(1)} async-done(((bf16[8,13,16,128]{3,2,1,0:T(8,128)(2,1)}), bf16[8,13,16,128]{3,2,1,0:T(8,128)(2,1)S(1)}, u32[]{:S(2)}, u32[]{:S(2)}) %all-to-all-start.4) | async-done | bytes 426016 | tf_op jit(solution)/shard_map/all_to_all | solution.py:236
  233.2 3.9 %all-to-all-start.3 = ((bf16[16,160,128]{2,1,0:T(8,128)(2,1)}), bf16[16,160,128]{2,1,0:T(8,128)(2,1)S(1)}, u32[]{:S(2)}, u32[]{:S(2)}) async-start(bf16[16,160,128]{2,1,0:T(8,128)(2,1)} %chain.3), calls=%async_computation.4 | async-start | bytes 1310720 | tf_op jit(solution)/shard_map/all_to_all | solution.py:236
  243.3 13.8 %all-to-all-done.3 = bf16[16,160,128]{2,1,0:T(8,128)(2,1)S(1)} async-done(((bf16[16,160,128]{2,1,0:T(8,128)(2,1)}), bf16[16,160,128]{2,1,0:T(8,128)(2,1)S(1)}, u32[]{:S(2)}, u32[]{:S(2)}) %all-to-all-start.3) | async-done | bytes 655392 | tf_op jit(solution)/shard_map/all_to_all | solution.py:236
  257.9 8.6 %across.1 = (f32[256,2560]{1,0:T(8,128)}, f32[40,256]{1,0:T(8,128)}, f32[256,128]{1,0:T(8,128)}, f32[256,128]{1,0:T(8,128)}) custom-call(f32[256,2560]{1,0:T(8,128)} %bitcast.60, bf16[256,2560]{1,0:T(8,128)(2,1)} %get-tuple-element.57.gy_ref, f32[256,2560]{1,0:T(8,128)} %get-tuple-element.49.grow_ref, f32[256,2560]{1,0:T(8,128)} %get-tuple-element.62.part_ref, ...), custom_call_target="tpu_custom_call" | custom-call | flops 671088640 | bytes 13107200 | tf_op jit(solution)/shard_map/across/pallas_call | solution.py:440
  (132 shorter events, 74.5 us)
Async XLA Ops:
  8.0 84.5 %all-gather.2.cloned.1.call-start = ((), (), s32[]{:S(2)}) async-start(), calls=%async_computation.7 | async-start | bytes 6963200 | tf_op jit(solution)/shard_map/all_gather | solution.py:639
  15.6 31.3 %all-to-all-start = ((bf16[16,176,128]{2,1,0:T(8,128)(2,1)}), bf16[16,176,128]{2,1,0:T(8,128)(2,1)S(1)}, u32[]{:S(2)}, u32[]{:S(2)}) async-start(bf16[16,176,128]{2,1,0:T(8,128)(2,1)} %get-tuple-element.50), calls=%async_computation | async-start | bytes 1441792 | tf_op jit(solution)/shard_map/all_to_all | solution.py:236
  50.4 23.1 %all-to-all-start.1 = ((bf16[16,160,128]{2,1,0:T(8,128)(2,1)}), bf16[16,160,128]{2,1,0:T(8,128)(2,1)S(1)}, u32[]{:S(2)}, u32[]{:S(2)}) async-start(bf16[16,160,128]{2,1,0:T(8,128)(2,1)} %chain.2), calls=%async_computation.1 | async-start | bytes 1310720 | tf_op jit(solution)/shard_map/all_to_all | solution.py:236
  53.9 87.6 %reduce-scatter.2.cloned.1.call-start = ((), (), s32[]{:S(2)}) async-start(), calls=%async_computation.8 | async-start | bytes 4096000 | tf_op jit(solution)/shard_map/reduce_scatter | solution.py:651
  98.5 15.2 %collective-permute-start.4 = (bf16[256,2560]{1,0:T(8,128)(2,1)S(1)}, bf16[256,2560]{1,0:T(8,128)(2,1)S(1)}, u32[]{:S(2)}, u32[]{:S(2)}) collective-permute-start(bf16[256,2560]{1,0:T(8,128)(2,1)S(1)} %convolution_convert_fusion), channel_id=1, source_target_pairs={{0,1},{1,0},{2,3},{3,2},{4,5},{5,4},{6,7},{7,6},{8,9},{9,8},{10,11... | collective-permute-start | bytes 3932168 | tf_op jit(solution)/shard_map/ppermute | solution.py:610
  98.9 11.2 %collective-permute-start.3 = (bf16[2,160,640]{2,1,0:T(8,128)(2,1)S(1)}, bf16[2,160,640]{2,1,0:T(8,128)(2,1)S(1)}, u32[]{:S(2)}, u32[]{:S(2)}) collective-permute-start(bf16[2,160,640]{2,1,0:T(8,128)(2,1)S(1)} %get-tuple-element.88), channel_id=1, source_target_pairs={{0,192},{64,0},{128,64},{192,128},{1,193},{65,1},{129,65},{193,129... | collective-permute-start | bytes 1228808 | tf_op jit(solution)/shard_map/ppermute | solution.py:581
  101.6 11.7 %collective-permute-start.2 = (bf16[2,160,640]{2,1,0:T(8,128)(2,1)S(1)}, bf16[2,160,640]{2,1,0:T(8,128)(2,1)S(1)}, u32[]{:S(2)}, u32[]{:S(2)}) collective-permute-start(bf16[2,160,640]{2,1,0:T(8,128)(2,1)S(1)} %get-tuple-element.89), channel_id=1, source_target_pairs={{0,64},{64,128},{128,192},{192,0},{1,65},{65,129},{129,193},{193,1... | collective-permute-start | bytes 1228808 | tf_op jit(solution)/shard_map/ppermute | solution.py:581
  113.7 25.8 %collective-permute-start.5 = (bf16[4,160,640]{2,1,0:T(8,128)(2,1)S(1)}, bf16[4,160,640]{2,1,0:T(8,128)(2,1)}, u32[]{:S(2)}, u32[]{:S(2)}) collective-permute-start(bf16[4,160,640]{2,1,0:T(8,128)(2,1)S(1)} %get-tuple-element.59), channel_id=1, source_target_pairs={{0,64},{64,128},{128,192},{192,0},{1,65},{65,129},{129,193},{193,1... | collective-permute-start | bytes 2457608 | tf_op jit(solution)/shard_map/ppermute | solution.py:581
  113.8 25.7 %collective-permute-start.6 = (bf16[4,160,640]{2,1,0:T(8,128)(2,1)S(1)}, bf16[4,160,640]{2,1,0:T(8,128)(2,1)}, u32[]{:S(2)}, u32[]{:S(2)}) collective-permute-start(bf16[4,160,640]{2,1,0:T(8,128)(2,1)S(1)} %get-tuple-element.60), channel_id=1, source_target_pairs={{0,192},{64,0},{128,64},{192,128},{1,193},{65,1},{129,65},{193,129... | collective-permute-start | bytes 2457608 | tf_op jit(solution)/shard_map/ppermute | solution.py:581
  122.7 62.7 %all-to-all-start.2 = ((bf16[16,176,128]{2,1,0:T(8,128)(2,1)}), bf16[16,176,128]{2,1,0:T(8,128)(2,1)S(1)}, u32[]{:S(2)}, u32[]{:S(2)}) async-start(bf16[16,176,128]{2,1,0:T(8,128)(2,1)} %get-tuple-element.65), calls=%async_computation.3 | async-start | bytes 1441792 | tf_op jit(solution)/shard_map/all_to_all | solution.py:236
  142.2 8.0 %collective-permute-start.12 = (bf16[160,640]{1,0:T(8,128)(2,1)S(1)}, bf16[160,640]{1,0:T(8,128)(2,1)S(1)}, u32[]{:S(2)}, u32[]{:S(2)}) collective-permute-start(bf16[160,640]{1,0:T(8,128)(2,1)S(1)} %get-tuple-element.94), channel_id=1, source_target_pairs={{0,32},{16,48},{32,0},{48,16},{1,33},{17,49},{33,1},{49,17},{2,34}... | collective-permute-start | bytes 614408 | tf_op jit(solution)/shard_map/ppermute | solution.py:581
  144.9 9.7 %collective-permute-start.11 = (bf16[160,640]{1,0:T(8,128)(2,1)S(1)}, bf16[160,640]{1,0:T(8,128)(2,1)S(1)}, u32[]{:S(2)}, u32[]{:S(2)}) collective-permute-start(bf16[160,640]{1,0:T(8,128)(2,1)S(1)} %get-tuple-element.95), channel_id=1, source_target_pairs={{0,48},{16,0},{32,16},{48,32},{1,49},{17,1},{33,17},{49,33},{2,50}... | collective-permute-start | bytes 614408 | tf_op jit(solution)/shard_map/ppermute | solution.py:581
  145.7 9.1 %collective-permute-start.10 = (bf16[160,640]{1,0:T(8,128)(2,1)S(1)}, bf16[160,640]{1,0:T(8,128)(2,1)S(1)}, u32[]{:S(2)}, u32[]{:S(2)}) collective-permute-start(bf16[160,640]{1,0:T(8,128)(2,1)S(1)} %get-tuple-element.96), channel_id=1, source_target_pairs={{0,16},{16,32},{32,48},{48,0},{1,17},{17,33},{33,49},{49,1},{2,18}... | collective-permute-start | bytes 614408 | tf_op jit(solution)/shard_map/ppermute | solution.py:581
  148.3 7.0 %collective-permute-start.9 = (bf16[160,640]{1,0:T(8,128)(2,1)S(1)}, bf16[160,640]{1,0:T(8,128)(2,1)S(1)}, u32[]{:S(2)}, u32[]{:S(2)}) collective-permute-start(bf16[160,640]{1,0:T(8,128)(2,1)S(1)} %get-tuple-element.98), channel_id=1, source_target_pairs={{0,128},{64,192},{128,0},{192,64},{1,129},{65,193},{129,1},{193,65... | collective-permute-start | bytes 614408 | tf_op jit(solution)/shard_map/ppermute | solution.py:581
  148.3 9.2 %collective-permute-start.8 = (bf16[160,640]{1,0:T(8,128)(2,1)S(1)}, bf16[160,640]{1,0:T(8,128)(2,1)S(1)}, u32[]{:S(2)}, u32[]{:S(2)}) collective-permute-start(bf16[160,640]{1,0:T(8,128)(2,1)S(1)} %get-tuple-element.99), channel_id=1, source_target_pairs={{0,192},{64,0},{128,64},{192,128},{1,193},{65,1},{129,65},{193,129... | collective-permute-start | bytes 614408 | tf_op jit(solution)/shard_map/ppermute | solution.py:581
  150.2 10.6 %collective-permute-start.7 = (bf16[160,640]{1,0:T(8,128)(2,1)S(1)}, bf16[160,640]{1,0:T(8,128)(2,1)S(1)}, u32[]{:S(2)}, u32[]{:S(2)}) collective-permute-start(bf16[160,640]{1,0:T(8,128)(2,1)S(1)} %get-tuple-element.100), channel_id=1, source_target_pairs={{0,64},{64,128},{128,192},{192,0},{1,65},{65,129},{129,193},{193,1... | collective-permute-start | bytes 614408 | tf_op jit(solution)/shard_map/ppermute | solution.py:581
  164.8 10.3 %collective-permute-start.13 = (bf16[13,16,128]{2,1,0:T(8,128)(2,1)}, bf16[13,16,128]{2,1,0:T(8,128)(2,1)S(1)}, u32[]{:S(2)}, u32[]{:S(2)}) collective-permute-start(bf16[13,16,128]{2,1,0:T(8,128)(2,1)} %get-tuple-element.75), channel_id=1, source_target_pairs={{0,2},{2,4},{4,6},{6,8},{8,10},{10,12},{12,14},{14,0},{1,3},{3,5},... | collective-permute-start | bytes 159752 | tf_op jit(solution)/shard_map/ppermute | solution.py:619
  166.1 12.3 %collective-permute-start.14 = (bf16[13,16,128]{2,1,0:T(8,128)(2,1)}, bf16[13,16,128]{2,1,0:T(8,128)(2,1)S(1)}, u32[]{:S(2)}, u32[]{:S(2)}) collective-permute-start(bf16[13,16,128]{2,1,0:T(8,128)(2,1)} %get-tuple-element.76), channel_id=1, source_target_pairs={{0,4},{2,6},{4,8},{6,10},{8,12},{10,14},{12,0},{14,2},{1,5},{3,7},... | collective-permute-start | bytes 159752 | tf_op jit(solution)/shard_map/ppermute | solution.py:619
  168.2 11.9 %collective-permute-start.15 = (bf16[13,16,128]{2,1,0:T(8,128)(2,1)}, bf16[13,16,128]{2,1,0:T(8,128)(2,1)S(1)}, u32[]{:S(2)}, u32[]{:S(2)}) collective-permute-start(bf16[13,16,128]{2,1,0:T(8,128)(2,1)} %get-tuple-element.77), channel_id=1, source_target_pairs={{0,6},{2,8},{4,10},{6,12},{8,14},{10,0},{12,2},{14,4},{1,7},{3,9},... | collective-permute-start | bytes 159752 | tf_op jit(solution)/shard_map/ppermute | solution.py:619
  170.6 9.5 %collective-permute-start.16 = (bf16[13,16,128]{2,1,0:T(8,128)(2,1)}, bf16[13,16,128]{2,1,0:T(8,128)(2,1)S(1)}, u32[]{:S(2)}, u32[]{:S(2)}) collective-permute-start(bf16[13,16,128]{2,1,0:T(8,128)(2,1)} %get-tuple-element.78), channel_id=1, source_target_pairs={{0,8},{2,10},{4,12},{6,14},{8,0},{10,2},{12,4},{14,6},{1,9},{3,11}... | collective-permute-start | bytes 159752 | tf_op jit(solution)/shard_map/ppermute | solution.py:619
  172.7 7.4 %collective-permute-start.17 = (bf16[13,16,128]{2,1,0:T(8,128)(2,1)}, bf16[13,16,128]{2,1,0:T(8,128)(2,1)S(1)}, u32[]{:S(2)}, u32[]{:S(2)}) collective-permute-start(bf16[13,16,128]{2,1,0:T(8,128)(2,1)} %get-tuple-element.79), channel_id=1, source_target_pairs={{0,10},{2,12},{4,14},{6,0},{8,2},{10,4},{12,6},{14,8},{1,11},{3,13... | collective-permute-start | bytes 159752 | tf_op jit(solution)/shard_map/ppermute | solution.py:619
  175.1 10.3 %collective-permute-start.18 = (bf16[13,16,128]{2,1,0:T(8,128)(2,1)}, bf16[13,16,128]{2,1,0:T(8,128)(2,1)S(1)}, u32[]{:S(2)}, u32[]{:S(2)}) collective-permute-start(bf16[13,16,128]{2,1,0:T(8,128)(2,1)} %get-tuple-element.80), channel_id=1, source_target_pairs={{0,12},{2,14},{4,0},{6,2},{8,4},{10,6},{12,8},{14,10},{1,13},{3,15... | collective-permute-start | bytes 159752 | tf_op jit(solution)/shard_map/ppermute | solution.py:619
  213.9 19.2 %all-to-all-start.4 = ((bf16[8,13,16,128]{3,2,1,0:T(8,128)(2,1)}), bf16[8,13,16,128]{3,2,1,0:T(8,128)(2,1)S(1)}, u32[]{:S(2)}, u32[]{:S(2)}) async-start(bf16[8,13,16,128]{3,2,1,0:T(8,128)(2,1)} %get-tuple-element.82), calls=%async_computation.5 | async-start | bytes 851968 | tf_op jit(solution)/shard_map/all_to_all | solution.py:236
  233.2 23.9 %all-to-all-start.3 = ((bf16[16,160,128]{2,1,0:T(8,128)(2,1)}), bf16[16,160,128]{2,1,0:T(8,128)(2,1)S(1)}, u32[]{:S(2)}, u32[]{:S(2)}) async-start(bf16[16,160,128]{2,1,0:T(8,128)(2,1)} %chain.3), calls=%async_computation.4 | async-start | bytes 1310720 | tf_op jit(solution)/shard_map/all_to_all | solution.py:236
  (38 other events, 168.5 us)
Sparse Core Ops, SparseCore 0:
  11.3 71.2 all-gather.1
Sparse Core Ops, SparseCore 1:
  92.6 38.6 reduce-scatter.1

commit v5 on v4

--- a/solution.py
+++ b/solution.py
@@ -68,8 +68,8 @@
     return pltpu.CompilerParams(vmem_limit_bytes=VMEM)
 
 
-def cost(flops, moved, exps):
-    return pl.CostEstimate(flops=flops, bytes_accessed=moved, transcendentals=exps)
+def cost():
+    return pl.CostEstimate(flops=1, bytes_accessed=1, transcendentals=0)
 
 
 def column(cum_t, head):
@@ -78,12 +78,6 @@
 
 def low_half(shape):
     return iota(shape, 1) < P_SIZE
-
-
-def spread(cum_t, pair):
-    return jnp.where(
-        low_half((T, 2 * P_SIZE)), column(cum_t, 2 * pair), column(cum_t, 2 * pair + 1)
-    )
 
 
 def lanes_of(i):
@@ -105,7 +99,7 @@
         out_ref[s, OWN:, :] = note.astype(BF)
 
 
-def ends_kernel(x_ref, a_ref, b_ref, cum_ref, cum_t_ref, out_ref):
+def ends_kernel(x_ref, a_ref, b_ref, cum_ref, cum_t_ref, tail_ref, out_ref, pieces):
     step = pl.program_id(0)
 
     @pl.when(step == 0)
@@ -122,15 +116,18 @@
         hi = jnp.floor(total)
         mid = jnp.floor((total - hi) * 256.0) / 256.0
         put_note(out_ref, (hi, mid, total - hi - mid))
-
-    cum_t = cum_t_ref[...]
-    b = b_ref[...].astype(BF)
-    found = []
-    for i in range(WIDE):
-        cum = spread(cum_t, step * WIDE + i)
-        tail = jnp.exp(cum[T - 1 : T, :] - cum)
-        found.append(tn((x_ref[:, lanes_of(i)] * tail).astype(BF), b))
-    put_states(out_ref, jnp.concatenate(found, axis=0), step * WIDE, WIDE)
+        tail = jnp.exp(cum_t[T - 1 :, :] - cum_t)
+        high = tail.astype(BF)
+        pieces[0] = high
+        pieces[1] = (tail - high.astype(F32)).astype(BF)
+
+    width = WIDE * 2 * P_SIZE
+    pick = iota((H, width), 0) == step * 2 * WIDE + iota((H, width), 1) // P_SIZE
+    pick = pick.astype(BF)
+    tail = nn(pieces[0], pick) + nn(pieces[1], pick)
+    tail_ref[...] = tail
+    states = tn((x_ref[...] * tail).astype(BF), b_ref[...].astype(BF))
+    put_states(out_ref, states, step * WIDE, WIDE)
 
 
 def local_ends(x, a, b):
@@ -138,14 +135,16 @@
         ends_kernel,
         grid=(PAIRS // WIDE,),
         in_specs=[wide(T, WIDE), whole((H, T)), whole((T, N))],
-        out_specs=[whole((H, T)), whole((T, H)), whole((N_SEQ, ROWS, N))],
+        out_specs=[whole((H, T)), whole((T, H)), wide(T, WIDE), whole((N_SEQ, ROWS, N))],
         out_shape=[
             jax.ShapeDtypeStruct((H, T), F32),
             jax.ShapeDtypeStruct((T, H), F32),
+            jax.ShapeDtypeStruct((T, D), F32),
             jax.ShapeDtypeStruct((N_SEQ, ROWS, N), BF),
         ],
-        compiler_params=params(),
-        cost_estimate=cost(2 * T * D * N, 4 * T * D, T * D),
+        scratch_shapes=[pltpu.VMEM((2, T, H), BF)],
+        compiler_params=params(),
+        cost_estimate=cost(),
         name="ends",
     )(x, a, b)
 
@@ -186,7 +185,7 @@
         out_shape=[jax.ShapeDtypeStruct((T, D), F32)] * 2,
         scratch_shapes=[pltpu.VMEM((T, T), F32)],
         compiler_params=params(),
-        cost_estimate=cost(4 * T * T * D, 8 * T * D, H * T * T),
+        cost_estimate=cost(),
         name="intra",
     )(x, cum, cum_t, b, c, skip)
 
@@ -204,7 +203,7 @@
         out_specs=wide(T, WIDE),
         out_shape=jax.ShapeDtypeStruct((T, D), BF),
         compiler_params=params(),
-        cost_estimate=cost(2 * T * D * N, 10 * T * D, 0),
+        cost_estimate=cost(),
         name="inter",
     )(part, grow, c, start)
 
@@ -227,7 +226,7 @@
         out_specs=vmem(),
         out_shape=jax.ShapeDtypeStruct((N_SEQ, OWN, N), BF),
         compiler_params=params(),
-        cost_estimate=cost(4 * N_SEQ * OWN * N, 4 * N_SEQ * OWN * N, N_SEQ * OWN),
+        cost_estimate=cost(),
         name="chain",
     )(mine, parts, totals)
 
@@ -236,25 +235,24 @@
     return lax.all_to_all(v, axis, 0, 0, tiled=True)
 
 
-def term_kernel(at_ref, yo_ref, yx_ref, go_ref, gx_ref, first_ref, second_ref):
-    half = go_ref.shape[1] // 2
-    term = tn(yo_ref[...], go_ref[...]) + tn(yx_ref[...], gx_ref[...])
-    term = term.astype(BF)
+def term_kernel(at_ref, yo_ref, yx_ref, g_ref, first_ref, second_ref):
+    half = g_ref.shape[1] // 2
+    term = tn(jnp.concatenate([yo_ref[...], yx_ref[...]], axis=0), g_ref[...]).astype(BF)
     for k in range(4):
         rows = slice(k * OWN, (k + 1) * OWN)
         first_ref[k, 0] = term[rows, :half]
         second_ref[0, (k + 4 - at_ref[1]) % 4] = term[rows, half:]
 
 
-def terms(at, y_own, y_other, g_own, g_other):
+def terms(at, y_own, y_other, g):
     rows = pl.BlockSpec((T, 4 * OWN), lambda i, at: (0, (at[0] + i) % 4))
-    half = g_own.shape[1] // 2
+    half = g.shape[1] // 2
     return pl.pallas_call(
         term_kernel,
         grid_spec=pltpu.PrefetchScalarGridSpec(
             num_scalar_prefetch=1,
             grid=(4,),
-            in_specs=[rows, rows, whole(g_own.shape), whole(g_own.shape)],
+            in_specs=[rows, rows, whole(g.shape)],
             out_specs=[
                 pl.BlockSpec((4, 1, OWN, half), lambda i, at: (0, i, 0, 0)),
                 pl.BlockSpec((1, 4, OWN, half), lambda i, at: (i, 0, 0, 0)),
@@ -262,9 +260,29 @@
         ),
         out_shape=[jax.ShapeDtypeStruct((4, 4, OWN, half), BF)] * 2,
         compiler_params=params(),
-        cost_estimate=cost(4 * T * D * D // 2, 3 * D * D // 2, 0),
+        cost_estimate=cost(),
         name="terms",
-    )(at, y_own, y_other, g_own, g_other)
+    )(at, y_own, y_other, g)
+
+
+def gy_kernel(g_ref, w_ref, own_ref, other_ref):
+    got = nt(g_ref[...], w_ref[...])
+    own_ref[...] = got[:T]
+    other_ref[...] = got[T:].astype(BF)
+
+
+def gy_parts(g, w):
+    rows = 4 * OWN
+    return pl.pallas_call(
+        gy_kernel,
+        grid=(4,),
+        in_specs=[whole(g.shape), pl.BlockSpec((rows, w.shape[1]), lambda i: (i, 0))],
+        out_specs=[pl.BlockSpec((T, rows), lambda i: (0, i))] * 2,
+        out_shape=[jax.ShapeDtypeStruct((T, D), F32), jax.ShapeDtypeStruct((T, D), BF)],
+        compiler_params=params(),
+        cost_estimate=cost(),
+        name="gy_parts",
+    )(g, w)
 
 
 def entry_kernel(own_ref, other_ref, x_ref, grow_ref, c_ref, gy_ref, out_ref, sums):
@@ -306,16 +324,16 @@
         ],
         scratch_shapes=[pltpu.VMEM((PAIRS, 2 * P_SIZE), F32)],
         compiler_params=params(),
-        cost_estimate=cost(2 * T * D * N, 12 * T * D, T * D),
+        cost_estimate=cost(),
         name="entries",
     )(own, other, x, grow, c)
 
 
 def within_kernel(
-    x_ref, gy_ref, cum_ref, cum_t_ref, b_ref, c_ref, skip_ref,
-    gx_ref, ga_ref, gb_ref, gc_ref,
-    scores, d_scores, rows, cols,
+    first, steps, x_ref, gy_ref, cum_ref, cum_t_ref, b_ref, c_ref, skip_ref, *rest
 ):
+    before = rest[:-8]
+    gx_ref, ga_ref, gb_ref, gc_ref, scores, d_scores, rows, cols = rest[-8:]
     step = pl.program_id(0)
 
     @pl.when(step == 0)
@@ -323,12 +341,13 @@
         keep = iota((T, T), 1) >= iota((T, T), 0)
         scores[...] = jnp.where(keep, nt(b_ref[...].astype(BF), c_ref[...].astype(BF)), 0.0)
         d_scores[...] = jnp.zeros_like(d_scores)
+        rows[...] = jnp.zeros_like(rows)
         cols[...] = jnp.zeros_like(cols)
 
     lanes = iota((T, N), 1)
     low = low_half((T, 2 * P_SIZE))
     for i in range(STEP):
-        pair = step * STEP + i
+        pair = (first + step) * STEP + i
         at = lanes_of(i)
         x = x_ref[:, at]
         gyb = gy_ref[:, at]
@@ -348,30 +367,32 @@
         skip = jnp.where(low, skip_ref[2 * pair], skip_ref[2 * pair + 1])
         gx_ref[:, at] = jnp.where(low, parts[0], parts[1]) + skip * gyb.astype(F32)
 
-    @pl.when(step == PAIRS // STEP - 1)
+    @pl.when(step == steps - 1)
     def _():
         keep = iota((T, T), 1) >= iota((T, T), 0)
         ds = jnp.where(keep, d_scores[...], 0.0).astype(BF)
-        gb_ref[...] = nn(ds, c_ref[...].astype(BF))
-        gc_ref[...] = tn(ds, b_ref[...].astype(BF))
+        gb = nn(ds, c_ref[...].astype(BF))
+        gc = tn(ds, b_ref[...].astype(BF))
         after = (iota((T, T), 0) >= iota((T, T), 1)).astype(F32)
         dims = (((0,), (0,)), ((), ()))
         ga = jnp.dot(rows[...], after, precision=HIGH, preferred_element_type=F32)
         up = lax.dot_general(cols[...], after, dims, precision=HIGH, preferred_element_type=F32)
-        ga_ref[...] = ga + up[:H]
-
-
-def within(x, gy, cum, cum_t, b, c, skip):
-    return pl.pallas_call(
-        within_kernel,
-        grid=(PAIRS // STEP,),
+        for out, add, ref in zip((ga_ref, gb_ref, gc_ref), (ga + up[:H], gb, gc), before or (None,) * 3):
+            out[...] = add if ref is None else add + ref[...]
+
+
+def within(first, steps, x, gy, cum, cum_t, b, c, skip, before=()):
+    here = pl.BlockSpec((T, STEP * 2 * P_SIZE), lambda p: (0, first + p))
+    return pl.pallas_call(
+        functools.partial(within_kernel, first, steps),
+        grid=(steps,),
         in_specs=[
-            wide(T, STEP), wide(T, STEP), whole((H, T)), whole((T, H)), whole((T, N)),
-            whole((T, N)), smem(),
-        ],
+            here, here, whole((H, T)), whole((T, H)), whole((T, N)), whole((T, N)), smem(),
+        ]
+        + [whole(v.shape) for v in before],
         out_specs=[wide(T, STEP), whole((H, T)), whole((T, N)), whole((T, N))],
         out_shape=[
-            jax.ShapeDtypeStruct((T, D), F32),
+            jax.ShapeDtypeStruct((T, steps * STEP * 2 * P_SIZE), F32),
             jax.ShapeDtypeStruct((H, T), F32),
             jax.ShapeDtypeStruct((T, N), F32),
             jax.ShapeDtypeStruct((T, N), F32),
@@ -383,13 +404,13 @@
             pltpu.VMEM((T, N), F32),
         ],
         compiler_params=params(),
-        cost_estimate=cost(6 * T * T * D, 10 * T * D, H * T * T),
+        cost_estimate=cost(),
         name="within",
-    )(x, gy, cum, cum_t, b, c, skip)
+    )(x, gy, cum, cum_t, b, c, skip, *before)
 
 
 def across_kernel(
-    x_ref, gy_ref, grow_ref, part_ref, cum_ref, cum_t_ref, b_ref, c_ref, start_ref, last_ref,
+    x_ref, gy_ref, grow_ref, tail_ref, part_ref, part2_ref, cum_ref, b_ref, c_ref, start_ref, last_ref,
     ga_in, gb_in, gc_in,
     gx_ref, ga_ref, gb_ref, gc_ref,
     cols, tails, totals,
@@ -408,10 +429,7 @@
     width = WIDE * 2 * P_SIZE
     start = start_ref[...]
     last = last_ref[...]
-    cum_t = cum_t_ref[...]
-    sides = [spread(cum_t, step * WIDE + i) for i in range(WIDE)]
-    cum = jnp.concatenate(sides, axis=1)
-    tail = jnp.exp(cum[T - 1 : T, :] - cum)
+    tail = tail_ref[...]
     pick = iota((width, N), 1) == step * 2 * WIDE + iota((width, N), 0) // P_SIZE
     grown = gy_ref[...].astype(F32) * grow_ref[...]
     cols[...] += nn((grown * nt(cb, start)).astype(BF), pick.astype(BF))
@@ -420,7 +438,8 @@
     back = nt(bb, last)
     tails[...] += nn((faded * back).astype(BF), pick.astype(BF))
     gb_ref[...] += nn(faded.astype(BF), last)
-    gx_ref[...] = part_ref[...] + tail * back
+    part = jnp.where(step < PAIRS // WIDE // 2, part_ref[...], part2_ref[...])
+    gx_ref[...] = part + tail * back
     both = jnp.sum(start.astype(F32) * last.astype(F32), axis=1, keepdims=True)
     totals[pl.ds(step, 1), :] = jnp.sum(jnp.where(pick, both, 0.0), axis=0, keepdims=True)
 
@@ -436,12 +455,18 @@
         ga_ref[...] = ga_in[...] + up[:H] + jnp.exp(cum_ref[:, T - 1 : T]) * total
 
 
-def across(x, gy, grow, part, cum, cum_t, b, c, start, last, ga, gb, gc):
+def across(x, gy, grow, tail, part, part2, cum, b, c, start, last, ga, gb, gc):
+    width = WIDE * 2 * P_SIZE
+    last_part = PAIRS // WIDE // 2 - 1
     return pl.pallas_call(
         across_kernel,
         grid=(PAIRS // WIDE,),
         in_specs=[wide(T, WIDE)] * 4
-        + [whole((H, T)), whole((T, H)), whole((T, N)), whole((T, N))]
+        + [
+            pl.BlockSpec((T, width), lambda p: (0, jnp.minimum(p, last_part))),
+            pl.BlockSpec((T, width), lambda p: (0, jnp.maximum(p - last_part - 1, 0))),
+        ]
+        + [whole((H, T)), whole((T, N)), whole((T, N))]
         + [state_block(WIDE), state_block(WIDE), whole((H, T)), whole((T, N)), whole((T, N))],
         out_specs=[wide(T, WIDE), whole((H, T)), whole((T, N)), whole((T, N))],
         out_shape=[
@@ -456,9 +481,9 @@
             pltpu.VMEM((PAIRS // WIDE, N), F32),
         ],
         compiler_params=params(),
-        cost_estimate=cost(8 * T * D * N, 20 * T * D, T * D),
+        cost_estimate=cost(),
         name="across",
-    )(x, gy, grow, part, cum, cum_t, b, c, start, last, ga, gb, gc)
+    )(x, gy, grow, tail, part, part2, cum, b, c, start, last, ga, gb, gc)
 
 
 def fold_kernel(z_ref, a0, a1, a2, a3, b0, b1, b2, b3, *rest):
@@ -487,7 +512,7 @@
         out_shape=[jax.ShapeDtypeStruct((TILES, 16, 128), BF)] * 8,
         scratch_shapes=[pltpu.VMEM((OWN, D // 2), F32)],
         compiler_params=params(),
-        cost_estimate=cost(4 * OWN * D // 2, 8 * OWN * D // 2, 0),
+        cost_estimate=cost(),
         name="fold",
     )(z, *parts)
 
@@ -527,7 +552,7 @@
             jax.ShapeDtypeStruct((1, N), F32),
         ],
         compiler_params=params(),
-        cost_estimate=cost(8 * OWN * 160, 6 * OWN * D, 0),
+        cost_estimate=cost(),
         name="zsum",
     )(row0, z, ids, got, *parts)
 
@@ -572,7 +597,7 @@
         out_specs=[vmem(), vmem()],
         out_shape=[jax.ShapeDtypeStruct((OWN, D), F32), jax.ShapeDtypeStruct((1, N), F32)],
         compiler_params=params(),
-        cost_estimate=cost(2 * OWN * D, 6 * OWN * D, 0),
+        cost_estimate=cost(),
         name="clip",
     )(row0, core, ids, own, other, note)
 
@@ -640,41 +665,49 @@
     g_mine = lax.dynamic_slice_in_dim(g, core * half, half, axis=1)
     g_other = other_core(lax.dynamic_slice_in_dim(g, (1 - core) * half, half, axis=1))
 
-    cum, cum_t, sent = local_ends(x, a, b)
+    g_both = jnp.concatenate([g_mine, g_other], axis=0)
+
+    cum, cum_t, tail, sent = local_ends(x, a, b)
     got = swap(sent, SEQ)
     y_part, grow = intra(x, cum, cum_t, b, c, d_skip)
     start = swap(chain(got, got, mine, False), SEQ).reshape(H * P_SIZE, N)
     y_own = inter(y_part, grow, c, start)
     y_other = other_core(y_own)
-    first, second = terms(at, y_own, y_other, g_mine, g_other)
+    first, second = terms(at, y_own, y_other, g_both)
 
     first = lax.psum_scatter(first.reshape(-1, half // 2), "x", scatter_dimension=0, tiled=True)
     far_y = far(second, "y")
     w_half, _ = tie(w_half, second)
-    dims = (((1,), (1,)), ((), ()))
-    gy_other = lax.dot_general(g_other, w_half, dims, preferred_element_type=F32).astype(BF)
-    gy_own = lax.dot_general(g_mine, w_half, dims, preferred_element_type=F32)
+    gy_own, gy_other = gy_parts(g_both, w_half)
+    far_y = tie(*far_y, gy_own)[:2]
     gy_other = other_core(gy_other)
-    far_y = tie(*far_y, gy_own)[:2]
     up, down = passed(second, *far_y)
     up, down, gy_own, gy_other = tie(up, down, gy_own, gy_other)
     second = near(second, up, down, "y")
     gy, sent_back = entries(gy_own, gy_other, x, grow, c)
     got_back = swap(sent_back, SEQ)
-    gx, ga, gb, gc = within(x, gy, cum, cum_t, b, c, d_skip)
-    first, second, gx = tie(first, second, gx)
+    steps = PAIRS // STEP // 2
+    gx1, *sums = within(0, steps, x, gy, cum, cum_t, b, c, d_skip)
+    first, second, gx1 = tie(first, second, gx1)
     first = direct(first.reshape(4, OWN, half // 2), "y")
     second = direct(second, "x")
     mine, _ = tie(mine, second[0])
-    last = swap(chain(got_back, got, mine, True), SEQ).reshape(H * P_SIZE, N)
-
-    tiles = along_z(fold(at_z, first + second))
+    states = chain(got_back, got, mine, True)
+    states, parts = tie(states, first + second)
+    last = swap(states, SEQ).reshape(H * P_SIZE, N)
+
+    tiles = along_z(fold(at_z, parts))
     tiles, note = zsum(row0, at_z, ids, tiles, got_back)
+    tiles, last = tie(tiles, last)
     tiles = swap(tiles, "z")
+    gy, note = tie(gy, note)
+    gx2, *sums = within(steps, steps, x, gy, cum, cum_t, b, c, d_skip, sums)
     note = sum_over(sum_over(note, "x"), "y")
+    tiles, note, gx2, last = tie(tiles, note, gx2, last)
+    note = swap(jnp.broadcast_to(note[None], (N_SEQ, 1, N)), SEQ)
     tiles_other = other_core(tiles)
-    gx, ga, gb, gc = across(x, gy, grow, gx, cum, cum_t, b, c, start, last, ga, gb, gc)
-    note = swap(jnp.broadcast_to(note[None], (N_SEQ, 1, N)), SEQ)
+    gx, ga, gb, gc = across(x, gy, grow, tail, gx1, gx2, cum, b, c, start, last, *sums)
+    note, ga = tie(note, ga)
     core = core.reshape(1).astype(jnp.int32)
     clipped_w, clipped_d = clip(tokens_all, row0, core, ids, tiles, tiles_other, note)
     return (gx[None], ga[None], gb[None], gc[None], clipped_w, clipped_d[0, :H])

time: 276 us -> 253 us (0.917)
  waiting for transfers between devices: 90.5 us -> 66.3 us
  starting transfers between devices: 59.4 us -> 74.9 us
  blocking collectives: 14.8 us -> 0 us
  Pallas kernels: 67.7 us -> 79.4 us
  matrix products: 8.27 us -> 0 us
  local copies, waits for them, and re-layouts: 14.1 us -> 10 us
    all_to_all x5 -> x6, waiting for transfers between devices: 58.6 us -> 35.9 us  [swap(): return lax.all_to_all(v, axis, 0, 0, tiled=True)]
    all_to_all x1 -> x0, blocking collectives: 14.8 us -> none  [swap(): return lax.all_to_all(v, axis, 0, 0, tiled=True)]
    all_to_all x5 -> x6, starting transfers between devices: 26.2 us -> 38.4 us  [swap(): return lax.all_to_all(v, axis, 0, 0, tiled=True)]
    pallas_call x1 -> x3, Pallas kernels: 11.4 us -> 22.4 us  [the longest x2 13.9 us: within(): pl.pallas_call(functools.partial(within_kernel, first, steps), grid=(step...]
    dot_general x2 -> x0, matrix products: 8.27 us -> none  [the longest x1 4.89 us: per_device(): lax.dot_general(g_other, w_half, dims, preferred_element_type=F32)]
    ppermute x10, waiting for transfers between devices: 19.5 us -> 14.7 us  [shifted(): return lax.ppermute(v, axis, [(i, (i + d) % 4) for i in range(4)])]
    ppermute x7, waiting for transfers between devices: 5.27 us -> 9.99 us  [along_z(): lax.ppermute(parts[d], 'z', [(i, (i + d) % 8) for i in range(8)])]
    ppermute x4, starting transfers between devices: 1.03 us -> 5.39 us  [other_core(): return lax.ppermute(v, 'core', [(0, 1), (1, 0)])]
  transfers between devices with their start and end apart: 34 -> 35, of which waited for: 19 -> 14; matrix products, arithmetic and copies ran while one was open for 6% -> 3% of each run, Pallas kernels for 21% -> 31%
where the time goes in v5:
time: 253 us; the launch traced here: 251 us
  Pallas kernels  79.4 us (31%)
  starting transfers between devices  74.9 us (30%)
  waiting for transfers between devices  66.3 us (26%)
  between operations  15.9 us (6%)
  local copies, waits for them, and re-layouts  10 us (4%)
  other arithmetic  4.72 us (2%)
    all_to_all x6, starting transfers between devices, swap(): return lax.all_to_all(v, axis, 0, 0, tiled=True)  38.4 us
    all_to_all x6, waiting for transfers between devices, swap(): return lax.all_to_all(v, axis, 0, 0, tiled=True)  35.9 us
    ppermute x10, waiting for transfers between devices, shifted(): return lax.ppermute(v, axis, [(i, (i + d) % 4) for i in range(4)])  14.7 us
    pallas_call x2, Pallas kernels, within(): pl.pallas_call(functools.partial(within_kernel, first, steps), grid=(step...  13.9 us
    ppermute x7, starting transfers between devices, along_z(): lax.ppermute(parts[d], 'z', [(i, (i + d) % 8) for i in range(8)])  13.8 us
    ppermute x10, starting transfers between devices, shifted(): return lax.ppermute(v, axis, [(i, (i + d) % 4) for i in range(4)])  10.7 us
    ppermute x7, waiting for transfers between devices, along_z(): lax.ppermute(parts[d], 'z', [(i, (i + d) % 8) for i in range(8)])  9.99 us
    pallas_call x1, Pallas kernels, intra(): pl.pallas_call(intra_kernel, grid=(PAIRS // STEP,), in_specs=[wide(T, STE...  9.25 us
  transfers between devices with their start and end apart: 35, of which 14 were waited for; matrix products, arithmetic and copies ran while one was open for 3% of the time, Pallas kernels for 31%

profile of v5, /device:TPU:1, one launch (start us, length us, event | category | flops | bytes accessed | tf_op | source)
XLA Modules:
  0.0 251.3 jit_solution(3572787774676399445)
XLA Ops:
  10.0 5.7 %ends.1 = (f32[40,256]{1,0:T(8,128)}, f32[256,40]{1,0:T(8,128)}, f32[256,2560]{1,0:T(8,128)}, bf16[16,176,128]{2,1,0:T(8,128)(2,1)}) custom-call(f32[256,2560]{1,0:T(8,128)} %bitcast.51, f32[40,256]{1,0:T(8,128)} %bitcast.72, f32[256,128]{1,0:T(8,128)} %bitcast.66), custom_call_target="tpu_custom_call" | custom-call | flops 1 | bytes 1 | tf_op jit(solution)/shard_map/ends/pallas_call | solution.py:134
  15.7 10.0 %all-to-all-start = ((bf16[16,176,128]{2,1,0:T(8,128)(2,1)}), bf16[16,176,128]{2,1,0:T(8,128)(2,1)S(1)}, u32[]{:S(2)}, u32[]{:S(2)}) async-start(bf16[16,176,128]{2,1,0:T(8,128)(2,1)} %get-tuple-element.76), calls=%async_computation | async-start | bytes 1441792 | tf_op jit(solution)/shard_map/all_to_all | solution.py:235
  25.7 21.3 %all-to-all-done.parts_ref.totals_ref = bf16[16,176,128]{2,1,0:T(8,128)(2,1)S(1)} async-done(((bf16[16,176,128]{2,1,0:T(8,128)(2,1)}), bf16[16,176,128]{2,1,0:T(8,128)(2,1)S(1)}, u32[]{:S(2)}, u32[]{:S(2)}) %all-to-all-start) | async-done | bytes 720928 | tf_op jit(solution)/shard_map/all_to_all | solution.py:235
  50.6 3.5 %all-to-all-start.1 = ((bf16[16,160,128]{2,1,0:T(8,128)(2,1)}), bf16[16,160,128]{2,1,0:T(8,128)(2,1)S(1)}, u32[]{:S(2)}, u32[]{:S(2)}) async-start(bf16[16,160,128]{2,1,0:T(8,128)(2,1)} %chain.2), calls=%async_computation.1 | async-start | bytes 1310720 | tf_op jit(solution)/shard_map/all_to_all | solution.py:235
  54.1 9.2 %intra.1 = (f32[256,2560]{1,0:T(8,128)}, f32[256,2560]{1,0:T(8,128)}) custom-call(f32[256,2560]{1,0:T(8,128)} %bitcast.52, f32[40,256]{1,0:T(8,128)} %get-tuple-element.72.cum_ref, f32[256,40]{1,0:T(8,128)} %get-tuple-element.73.cum_t_ref, f32[256,128]{1,0:T(8,128)} %bitcast.67, f32[256,128]{1,0:T(8,128)} %bitcast.59, f32[40]{0:T(128)} %skip_ref.5), custom_call_target="tpu_custom_call" | custom-call | flops 1 | bytes 1 | tf_op jit(solution)/shard_map/intra/pallas_call | solution.py:178
  63.4 10.3 %all-to-all-done.1 = bf16[16,160,128]{2,1,0:T(8,128)(2,1)S(1)} async-done(((bf16[16,160,128]{2,1,0:T(8,128)(2,1)}), bf16[16,160,128]{2,1,0:T(8,128)(2,1)S(1)}, u32[]{:S(2)}, u32[]{:S(2)}) %all-to-all-start.1) | async-done | bytes 655392 | tf_op jit(solution)/shard_map/all_to_all | solution.py:235
  74.5 5.2 %inter.1.yo_ref = bf16[256,2560]{1,0:T(8,128)(2,1)} custom-call(f32[256,2560]{1,0:T(8,128)} %get-tuple-element.74.part_ref, f32[256,2560]{1,0:T(8,128)} %get-tuple-element.75.grow_ref, f32[256,128]{1,0:T(8,128)} %bitcast.60, bf16[2560,128]{1,0:T(8,128)(2,1)} %bitcast.57), custom_call_target="tpu_custom_call" | custom-call | flops 1 | bytes 1 | tf_op jit(solution)/shard_map/inter/pallas_call | solution.py:199
  84.9 8.3 %terms.1 = (bf16[4,4,160,640]{3,2,1,0:T(8,128)(2,1)}, bf16[4,4,160,640]{3,2,1,0:T(8,128)(2,1)}) custom-call(s32[2]{0:T(128)} %pad_add_fusion.at_ref, bf16[256,2560]{1,0:T(8,128)(2,1)} %inter.1.yo_ref, bf16[256,2560]{1,0:T(8,128)(2,1)} %collective-permute-done.yx_ref, bf16[512,1280]{1,0:T(8,128)(2,1)} %pad_maximum_fusion.g_ref), custom_call_target="tpu_custom_call" | custom-call | flops 1 | bytes 1 | tf_op jit(solution)/shard_map/terms/pallas_call | solution.py:250
  93.2 8.4 %gy_parts.1 = (f32[256,2560]{1,0:T(8,128)}, bf16[256,2560]{1,0:T(8,128)(2,1)}) custom-call(bf16[512,1280]{1,0:T(8,128)(2,1)} %pad_maximum_fusion.g_ref, bf16[2560,1280]{1,0:T(8,128)(2,1)} %all-gather.2.cloned.1.call-done.w_ref), custom_call_target="tpu_custom_call" | custom-call | flops 1 | bytes 1 | tf_op jit(solution)/shard_map/gy_parts/pallas_call | solution.py:276
  104.7 8.5 %collective-permute-done.3 = bf16[2,160,640]{2,1,0:T(8,128)(2,1)S(1)} collective-permute-done((bf16[2,160,640]{2,1,0:T(8,128)(2,1)S(1)}, bf16[2,160,640]{2,1,0:T(8,128)(2,1)S(1)}, u32[]{:S(2)}, u32[]{:S(2)}) %collective-permute-start.3) | collective-permute-done | bytes 409632 | tf_op jit(solution)/shard_map/ppermute | solution.py:606
  113.2 3.2 %collective-permute-done.2 = bf16[2,160,640]{2,1,0:T(8,128)(2,1)S(1)} collective-permute-done((bf16[2,160,640]{2,1,0:T(8,128)(2,1)S(1)}, bf16[2,160,640]{2,1,0:T(8,128)(2,1)S(1)}, u32[]{:S(2)}, u32[]{:S(2)}) %collective-permute-start.2) | collective-permute-done | bytes 409632 | tf_op jit(solution)/shard_map/ppermute | solution.py:606
  119.6 6.2 %entries.1 = (bf16[256,2560]{1,0:T(8,128)(2,1)}, bf16[16,176,128]{2,1,0:T(8,128)(2,1)}) custom-call(f32[256,2560]{1,0:T(8,128)} %get-tuple-element.83.own_ref, bf16[256,2560]{1,0:T(8,128)(2,1)} %copy-done.7, f32[256,2560]{1,0:T(8,128)} %bitcast.53, f32[256,2560]{1,0:T(8,128)} %get-tuple-element.75.grow_ref, f32[256,128]{1,0:T(8,128)} %bitcast.61), custom_call_target="tpu_custom_call" | custom-call | flops 1 | bytes 1 | tf_op jit(solution)/shard_map/entries/pallas_call | solution.py:316
  125.8 5.4 %all-to-all-start.2 = ((bf16[16,176,128]{2,1,0:T(8,128)(2,1)}), bf16[16,176,128]{2,1,0:T(8,128)(2,1)S(1)}, u32[]{:S(2)}, u32[]{:S(2)}) async-start(bf16[16,176,128]{2,1,0:T(8,128)(2,1)} %get-tuple-element.86), calls=%async_computation.2 | async-start | bytes 1441792 | tf_op jit(solution)/shard_map/all_to_all | solution.py:235
  131.2 6.9 %within.2 = (f32[256,1280]{1,0:T(8,128)}, f32[40,256]{1,0:T(8,128)}, f32[256,128]{1,0:T(8,128)}, f32[256,128]{1,0:T(8,128)}) custom-call(f32[256,2560]{1,0:T(8,128)} %bitcast.54, bf16[256,2560]{1,0:T(8,128)(2,1)} %get-tuple-element.111.gy_ref, f32[40,256]{1,0:T(8,128)} %get-tuple-element.72.cum_ref, f32[256,40]{1,0:T(8,128)} %get-tuple-element.73.cum_t_ref, ...), custom_call_target="tpu_custom_call" | custom-call | flops 1 | bytes 1 | tf_op jit(solution)/shard_map/within/pallas_call | solution.py:386
  148.3 4.3 %all-to-all-done.2.parts_ref.got_ref = bf16[16,176,128]{2,1,0:T(8,128)(2,1)S(1)} async-done(((bf16[16,176,128]{2,1,0:T(8,128)(2,1)}), bf16[16,176,128]{2,1,0:T(8,128)(2,1)S(1)}, u32[]{:S(2)}, u32[]{:S(2)}) %all-to-all-start.2) | async-done | bytes 720928 | tf_op jit(solution)/shard_map/all_to_all | solution.py:235
  157.7 8.7 %all-to-all-start.3 = ((bf16[16,160,128]{2,1,0:T(8,128)(2,1)}), bf16[16,160,128]{2,1,0:T(8,128)(2,1)S(1)}, u32[]{:S(2)}, u32[]{:S(2)}) async-start(bf16[16,160,128]{2,1,0:T(8,128)(2,1)} %chain.3), calls=%async_computation.4 | async-start | bytes 1310720 | tf_op jit(solution)/shard_map/all_to_all | solution.py:235
  166.5 3.4 %fold.1 = (bf16[13,16,128]{2,1,0:T(8,128)(2,1)}, bf16[13,16,128]{2,1,0:T(8,128)(2,1)}, bf16[13,16,128]{2,1,0:T(8,128)(2,1)}, bf16[13,16,128]{2,1,0:T(8,128)(2,1)...) custom-call(s32[1]{0:T(128)} %bitcast.17.z_ref, ...), custom_call_target="tpu_custom_call" | custom-call | flops 1 | bytes 1 | tf_op jit(solution)/shard_map/fold/pallas_call | solution.py:508
  180.3 4.7 %collective-permute-done.13.rest_1_ = bf16[13,16,128]{2,1,0:T(8,128)(2,1)S(1)} collective-permute-done((bf16[13,16,128]{2,1,0:T(8,128)(2,1)}, bf16[13,16,128]{2,1,0:T(8,128)(2,1)S(1)}, u32[]{:S(2)}, u32[]{:S(2)}) %collective-permute-start.13) | collective-permute-done | bytes 53280 | tf_op jit(solution)/shard_map/ppermute | solution.py:644
  190.2 4.0 %collective-permute-done.16.rest_4_ = bf16[13,16,128]{2,1,0:T(8,128)(2,1)S(1)} collective-permute-done((bf16[13,16,128]{2,1,0:T(8,128)(2,1)}, bf16[13,16,128]{2,1,0:T(8,128)(2,1)S(1)}, u32[]{:S(2)}, u32[]{:S(2)}) %collective-permute-start.16) | collective-permute-done | bytes 53280 | tf_op jit(solution)/shard_map/ppermute | solution.py:644
  196.9 3.5 %all-to-all-start.4 = ((bf16[8,13,16,128]{3,2,1,0:T(8,128)(2,1)}), bf16[8,13,16,128]{3,2,1,0:T(8,128)(2,1)S(1)}, u32[]{:S(2)}, u32[]{:S(2)}) async-start(bf16[8,13,16,128]{3,2,1,0:T(8,128)(2,1)} %get-tuple-element.116), calls=%async_computation.5 | async-start | bytes 851968 | tf_op jit(solution)/shard_map/all_to_all | solution.py:235
  210.6 7.0 %within.3 = (f32[256,1280]{1,0:T(8,128)}, f32[40,256]{1,0:T(8,128)}, f32[256,128]{1,0:T(8,128)}, f32[256,128]{1,0:T(8,128)}) custom-call(f32[256,2560]{1,0:T(8,128)} %bitcast.55, bf16[256,2560]{1,0:T(8,128)(2,1)} %get-tuple-element.111.gy_ref, f32[40,256]{1,0:T(8,128)} %get-tuple-element.72.cum_ref, f32[256,40]{1,0:T(8,128)} %get-tuple-element.73.cum_t_ref, ...), custom_call_target="tpu_custom_call" | custom-call | flops 1 | bytes 1 | tf_op jit(solution)/shard_map/within/pallas_call | solution.py:386
  217.7 4.7 %collective-permute-start.26 = (bf16[8,13,16,128]{3,2,1,0:T(8,128)(2,1)S(1)}, bf16[8,13,16,128]{3,2,1,0:T(8,128)(2,1)S(1)}, u32[]{:S(2)}, u32[]{:S(2)}) collective-permute-start(bf16[8,13,16,128]{3,2,1,0:T(8,128)(2,1)S(1)} %all-to-all-done.4.own_ref), channel_id=1, source_target_pairs={{0,1},{1,0},{2,3},{3,2},{4,5},{5,4},{6,7},{7,6},{8,9},{9,8},{10,11... | collective-permute-start | bytes 1277960 | tf_op jit(solution)/shard_map/ppermute | solution.py:635
  222.9 7.3 %all-to-all-start.5 = ((f32[16,1,128]{2,1,0:T(1,128)}), f32[16,1,128]{2,1,0:T(1,128)S(1)}, u32[]{:S(2)}, u32[]{:S(2)}) async-start(f32[16,1,128]{2,1,0:T(1,128)} %broadcast_in_dim.26), calls=%async_computation.6 | async-start | bytes 16384 | tf_op jit(solution)/shard_map/all_to_all | solution.py:235
  230.3 9.1 %across.1 = (f32[256,2560]{1,0:T(8,128)}, f32[40,256]{1,0:T(8,128)}, f32[256,128]{1,0:T(8,128)}, f32[256,128]{1,0:T(8,128)}) custom-call(f32[256,2560]{1,0:T(8,128)} %bitcast.56, bf16[256,2560]{1,0:T(8,128)(2,1)} %get-tuple-element.111.gy_ref, f32[256,2560]{1,0:T(8,128)} %get-tuple-element.75.grow_ref, f32[256,2560]{1,0:T(8,128)} %get-tuple-element.112.tail_ref, ...), custom_call_target="tpu_custom_call" | custom-call | flops 1 | bytes 1 | tf_op jit(solution)/shard_map/across/pallas_call | solution.py:461
  (130 shorter events, 66.5 us)
Async XLA Ops:
  8.0 85.2 %all-gather.2.cloned.1.call-start = ((), (), s32[]{:S(2)}) async-start(), calls=%async_computation.7 | async-start | bytes 6963200 | tf_op jit(solution)/shard_map/all_gather | solution.py:664
  15.7 31.3 %all-to-all-start = ((bf16[16,176,128]{2,1,0:T(8,128)(2,1)}), bf16[16,176,128]{2,1,0:T(8,128)(2,1)S(1)}, u32[]{:S(2)}, u32[]{:S(2)}) async-start(bf16[16,176,128]{2,1,0:T(8,128)(2,1)} %get-tuple-element.76), calls=%async_computation | async-start | bytes 1441792 | tf_op jit(solution)/shard_map/all_to_all | solution.py:235
  50.6 23.1 %all-to-all-start.1 = ((bf16[16,160,128]{2,1,0:T(8,128)(2,1)}), bf16[16,160,128]{2,1,0:T(8,128)(2,1)S(1)}, u32[]{:S(2)}, u32[]{:S(2)}) async-start(bf16[16,160,128]{2,1,0:T(8,128)(2,1)} %chain.2), calls=%async_computation.1 | async-start | bytes 1310720 | tf_op jit(solution)/shard_map/all_to_all | solution.py:235
  54.1 86.0 %reduce-scatter.2.cloned.1.call-start = ((), (), s32[]{:S(2)}) async-start(), calls=%async_computation.8 | async-start | bytes 4096000 | tf_op jit(solution)/shard_map/reduce_scatter | solution.py:678
  101.7 15.1 %collective-permute-start.4 = (bf16[256,2560]{1,0:T(8,128)(2,1)}, bf16[256,2560]{1,0:T(8,128)(2,1)S(1)}, u32[]{:S(2)}, u32[]{:S(2)}) collective-permute-start(bf16[256,2560]{1,0:T(8,128)(2,1)} %get-tuple-element.82), channel_id=1, source_target_pairs={{0,1},{1,0},{2,3},{3,2},{4,5},{5,4},{6,7},{7,6},{8,9},{9,8},{10,11... | collective-permute-start | bytes 3932168 | tf_op jit(solution)/shard_map/ppermute | solution.py:635
  101.9 11.2 %collective-permute-start.3 = (bf16[2,160,640]{2,1,0:T(8,128)(2,1)S(1)}, bf16[2,160,640]{2,1,0:T(8,128)(2,1)S(1)}, u32[]{:S(2)}, u32[]{:S(2)}) collective-permute-start(bf16[2,160,640]{2,1,0:T(8,128)(2,1)S(1)} %get-tuple-element.140), channel_id=1, source_target_pairs={{0,192},{64,0},{128,64},{192,128},{1,193},{65,1},{129,65},{193,129... | collective-permute-start | bytes 1228808 | tf_op jit(solution)/shard_map/ppermute | solution.py:606
  104.7 11.7 %collective-permute-start.2 = (bf16[2,160,640]{2,1,0:T(8,128)(2,1)S(1)}, bf16[2,160,640]{2,1,0:T(8,128)(2,1)S(1)}, u32[]{:S(2)}, u32[]{:S(2)}) collective-permute-start(bf16[2,160,640]{2,1,0:T(8,128)(2,1)S(1)} %get-tuple-element.141), channel_id=1, source_target_pairs={{0,64},{64,128},{128,192},{192,0},{1,65},{65,129},{129,193},{193,1... | collective-permute-start | bytes 1228808 | tf_op jit(solution)/shard_map/ppermute | solution.py:606
  116.8 21.3 %collective-permute-start.5 = (bf16[4,160,640]{2,1,0:T(8,128)(2,1)S(1)}, bf16[4,160,640]{2,1,0:T(8,128)(2,1)}, u32[]{:S(2)}, u32[]{:S(2)}) collective-permute-start(bf16[4,160,640]{2,1,0:T(8,128)(2,1)S(1)} %get-tuple-element.88), channel_id=1, source_target_pairs={{0,64},{64,128},{128,192},{192,0},{1,65},{65,129},{129,193},{193,1... | collective-permute-start | bytes 2457608 | tf_op jit(solution)/shard_map/ppermute | solution.py:606
  116.9 21.2 %collective-permute-start.6 = (bf16[4,160,640]{2,1,0:T(8,128)(2,1)S(1)}, bf16[4,160,640]{2,1,0:T(8,128)(2,1)}, u32[]{:S(2)}, u32[]{:S(2)}) collective-permute-start(bf16[4,160,640]{2,1,0:T(8,128)(2,1)S(1)} %get-tuple-element.89), channel_id=1, source_target_pairs={{0,192},{64,0},{128,64},{192,128},{1,193},{65,1},{129,65},{193,129... | collective-permute-start | bytes 2457608 | tf_op jit(solution)/shard_map/ppermute | solution.py:606
  125.8 26.8 %all-to-all-start.2 = ((bf16[16,176,128]{2,1,0:T(8,128)(2,1)}), bf16[16,176,128]{2,1,0:T(8,128)(2,1)S(1)}, u32[]{:S(2)}, u32[]{:S(2)}) async-start(bf16[16,176,128]{2,1,0:T(8,128)(2,1)} %get-tuple-element.86), calls=%async_computation.2 | async-start | bytes 1441792 | tf_op jit(solution)/shard_map/all_to_all | solution.py:235
  143.6 12.4 %collective-permute-start.11 = (bf16[160,640]{1,0:T(8,128)(2,1)S(1)}, bf16[160,640]{1,0:T(8,128)(2,1)S(1)}, u32[]{:S(2)}, u32[]{:S(2)}) collective-permute-start(bf16[160,640]{1,0:T(8,128)(2,1)S(1)} %get-tuple-element.147), channel_id=1, source_target_pairs={{0,48},{16,0},{32,16},{48,32},{1,49},{17,1},{33,17},{49,33},{2,50}... | collective-permute-start | bytes 614408 | tf_op jit(solution)/shard_map/ppermute | solution.py:606
  144.5 11.6 %collective-permute-start.10 = (bf16[160,640]{1,0:T(8,128)(2,1)S(1)}, bf16[160,640]{1,0:T(8,128)(2,1)S(1)}, u32[]{:S(2)}, u32[]{:S(2)}) collective-permute-start(bf16[160,640]{1,0:T(8,128)(2,1)S(1)} %get-tuple-element.148), channel_id=1, source_target_pairs={{0,16},{16,32},{32,48},{48,0},{1,17},{17,33},{33,49},{49,1},{2,18}... | collective-permute-start | bytes 614408 | tf_op jit(solution)/shard_map/ppermute | solution.py:606
  146.0 10.1 %collective-permute-start.9 = (bf16[160,640]{1,0:T(8,128)(2,1)}, bf16[160,640]{1,0:T(8,128)(2,1)S(1)}, u32[]{:S(2)}, u32[]{:S(2)}) collective-permute-start(bf16[160,640]{1,0:T(8,128)(2,1)} %get-tuple-element.150), channel_id=1, source_target_pairs={{0,128},{64,192},{128,0},{192,64},{1,129},{65,193},{129,1},{193,65... | collective-permute-start | bytes 614408 | tf_op jit(solution)/shard_map/ppermute | solution.py:606
  146.0 10.1 %collective-permute-start.8 = (bf16[160,640]{1,0:T(8,128)(2,1)}, bf16[160,640]{1,0:T(8,128)(2,1)S(1)}, u32[]{:S(2)}, u32[]{:S(2)}) collective-permute-start(bf16[160,640]{1,0:T(8,128)(2,1)} %get-tuple-element.151), channel_id=1, source_target_pairs={{0,192},{64,0},{128,64},{192,128},{1,193},{65,1},{129,65},{193,129... | collective-permute-start | bytes 614408 | tf_op jit(solution)/shard_map/ppermute | solution.py:606
  157.7 39.2 %all-to-all-start.3 = ((bf16[16,160,128]{2,1,0:T(8,128)(2,1)}), bf16[16,160,128]{2,1,0:T(8,128)(2,1)S(1)}, u32[]{:S(2)}, u32[]{:S(2)}) async-start(bf16[16,160,128]{2,1,0:T(8,128)(2,1)} %chain.3), calls=%async_computation.4 | async-start | bytes 1310720 | tf_op jit(solution)/shard_map/all_to_all | solution.py:235
  169.9 15.1 %collective-permute-start.13 = (bf16[13,16,128]{2,1,0:T(8,128)(2,1)}, bf16[13,16,128]{2,1,0:T(8,128)(2,1)S(1)}, u32[]{:S(2)}, u32[]{:S(2)}) collective-permute-start(bf16[13,16,128]{2,1,0:T(8,128)(2,1)} %get-tuple-element.103), channel_id=1, source_target_pairs={{0,2},{2,4},{4,6},{6,8},{8,10},{10,12},{12,14},{14,0},{1,3},{3,5},... | collective-permute-start | bytes 159752 | tf_op jit(solution)/shard_map/ppermute | solution.py:644
  171.3 16.2 %collective-permute-start.14 = (bf16[13,16,128]{2,1,0:T(8,128)(2,1)}, bf16[13,16,128]{2,1,0:T(8,128)(2,1)S(1)}, u32[]{:S(2)}, u32[]{:S(2)}) collective-permute-start(bf16[13,16,128]{2,1,0:T(8,128)(2,1)} %get-tuple-element.104), channel_id=1, source_target_pairs={{0,4},{2,6},{4,8},{6,10},{8,12},{10,14},{12,0},{14,2},{1,5},{3,7},... | collective-permute-start | bytes 159752 | tf_op jit(solution)/shard_map/ppermute | solution.py:644
  173.4 16.8 %collective-permute-start.15 = (bf16[13,16,128]{2,1,0:T(8,128)(2,1)}, bf16[13,16,128]{2,1,0:T(8,128)(2,1)S(1)}, u32[]{:S(2)}, u32[]{:S(2)}) collective-permute-start(bf16[13,16,128]{2,1,0:T(8,128)(2,1)} %get-tuple-element.105), channel_id=1, source_target_pairs={{0,6},{2,8},{4,10},{6,12},{8,14},{10,0},{12,2},{14,4},{1,7},{3,9},... | collective-permute-start | bytes 159752 | tf_op jit(solution)/shard_map/ppermute | solution.py:644
  175.8 18.4 %collective-permute-start.16 = (bf16[13,16,128]{2,1,0:T(8,128)(2,1)}, bf16[13,16,128]{2,1,0:T(8,128)(2,1)S(1)}, u32[]{:S(2)}, u32[]{:S(2)}) collective-permute-start(bf16[13,16,128]{2,1,0:T(8,128)(2,1)} %get-tuple-element.106), channel_id=1, source_target_pairs={{0,8},{2,10},{4,12},{6,14},{8,0},{10,2},{12,4},{14,6},{1,9},{3,11}... | collective-permute-start | bytes 159752 | tf_op jit(solution)/shard_map/ppermute | solution.py:644
  177.9 16.3 %collective-permute-start.17 = (bf16[13,16,128]{2,1,0:T(8,128)(2,1)}, bf16[13,16,128]{2,1,0:T(8,128)(2,1)S(1)}, u32[]{:S(2)}, u32[]{:S(2)}) collective-permute-start(bf16[13,16,128]{2,1,0:T(8,128)(2,1)} %get-tuple-element.107), channel_id=1, source_target_pairs={{0,10},{2,12},{4,14},{6,0},{8,2},{10,4},{12,6},{14,8},{1,11},{3,13... | collective-permute-start | bytes 159752 | tf_op jit(solution)/shard_map/ppermute | solution.py:644
  196.9 20.7 %all-to-all-start.4 = ((bf16[8,13,16,128]{3,2,1,0:T(8,128)(2,1)}), bf16[8,13,16,128]{3,2,1,0:T(8,128)(2,1)S(1)}, u32[]{:S(2)}, u32[]{:S(2)}) async-start(bf16[8,13,16,128]{3,2,1,0:T(8,128)(2,1)} %get-tuple-element.116), calls=%async_computation.5 | async-start | bytes 851968 | tf_op jit(solution)/shard_map/all_to_all | solution.py:235
  207.3 10.3 %collective-permute-start.25 = (f32[1,128]{1,0:T(1,128)S(1)}, f32[1,128]{1,0:T(1,128)S(1)}, u32[]{:S(2)}, u32[]{:S(2)}) collective-permute-start(f32[1,128]{1,0:T(1,128)S(1)} %add_add_fusion.1), channel_id=1, source_target_pairs={{0,192},{64,128},{128,64},{192,0},{1,193},{65,129},{129,65},{193,1... | collective-permute-start | bytes 1544 | tf_op jit(solution)/shard_map/ppermute | solution.py:639
  217.7 21.7 %collective-permute-start.26 = (bf16[8,13,16,128]{3,2,1,0:T(8,128)(2,1)S(1)}, bf16[8,13,16,128]{3,2,1,0:T(8,128)(2,1)S(1)}, u32[]{:S(2)}, u32[]{:S(2)}) collective-permute-start(bf16[8,13,16,128]{3,2,1,0:T(8,128)(2,1)S(1)} %all-to-all-done.4.own_ref), channel_id=1, source_target_pairs={{0,1},{1,0},{2,3},{3,2},{4,5},{5,4},{6,7},{7,6},{8,9},{9,8},{10,11... | collective-permute-start | bytes 1277960 | tf_op jit(solution)/shard_map/ppermute | solution.py:635
  222.9 16.4 %all-to-all-start.5 = ((f32[16,1,128]{2,1,0:T(1,128)}), f32[16,1,128]{2,1,0:T(1,128)S(1)}, u32[]{:S(2)}, u32[]{:S(2)}) async-start(f32[16,1,128]{2,1,0:T(1,128)} %broadcast_in_dim.26), calls=%async_computation.6 | async-start | bytes 16384 | tf_op jit(solution)/shard_map/all_to_all | solution.py:235
  (37 other events, 251.1 us)
Sparse Core Ops, SparseCore 0:
  11.3 71.2 all-gather.1
Sparse Core Ops, SparseCore 1:
  93.3 38.6 reduce-scatter.1

commit v6 on v5

--- a/solution.py
+++ b/solution.py
@@ -68,8 +68,8 @@
     return pltpu.CompilerParams(vmem_limit_bytes=VMEM)
 
 
-def cost():
-    return pl.CostEstimate(flops=1, bytes_accessed=1, transcendentals=0)
+def cost(micros):
+    return pl.CostEstimate(flops=0, bytes_accessed=int(micros * 3e6), transcendentals=0)
 
 
 def column(cum_t, head):
@@ -144,7 +144,7 @@
         ],
         scratch_shapes=[pltpu.VMEM((2, T, H), BF)],
         compiler_params=params(),
-        cost_estimate=cost(),
+        cost_estimate=cost(6),
         name="ends",
     )(x, a, b)
 
@@ -185,7 +185,7 @@
         out_shape=[jax.ShapeDtypeStruct((T, D), F32)] * 2,
         scratch_shapes=[pltpu.VMEM((T, T), F32)],
         compiler_params=params(),
-        cost_estimate=cost(),
+        cost_estimate=cost(9),
         name="intra",
     )(x, cum, cum_t, b, c, skip)
 
@@ -203,7 +203,7 @@
         out_specs=wide(T, WIDE),
         out_shape=jax.ShapeDtypeStruct((T, D), BF),
         compiler_params=params(),
-        cost_estimate=cost(),
+        cost_estimate=cost(5),
         name="inter",
     )(part, grow, c, start)
 
@@ -226,7 +226,7 @@
         out_specs=vmem(),
         out_shape=jax.ShapeDtypeStruct((N_SEQ, OWN, N), BF),
         compiler_params=params(),
-        cost_estimate=cost(),
+        cost_estimate=cost(3),
         name="chain",
     )(mine, parts, totals)
 
@@ -260,7 +260,7 @@
         ),
         out_shape=[jax.ShapeDtypeStruct((4, 4, OWN, half), BF)] * 2,
         compiler_params=params(),
-        cost_estimate=cost(),
+        cost_estimate=cost(8),
         name="terms",
     )(at, y_own, y_other, g)
 
@@ -280,7 +280,7 @@
         out_specs=[pl.BlockSpec((T, rows), lambda i: (0, i))] * 2,
         out_shape=[jax.ShapeDtypeStruct((T, D), F32), jax.ShapeDtypeStruct((T, D), BF)],
         compiler_params=params(),
-        cost_estimate=cost(),
+        cost_estimate=cost(8),
         name="gy_parts",
     )(g, w)
 
@@ -324,7 +324,7 @@
         ],
         scratch_shapes=[pltpu.VMEM((PAIRS, 2 * P_SIZE), F32)],
         compiler_params=params(),
-        cost_estimate=cost(),
+        cost_estimate=cost(6),
         name="entries",
     )(own, other, x, grow, c)
 
@@ -404,7 +404,7 @@
             pltpu.VMEM((T, N), F32),
         ],
         compiler_params=params(),
-        cost_estimate=cost(),
+        cost_estimate=cost(7),
         name="within",
     )(x, gy, cum, cum_t, b, c, skip, *before)
 
@@ -481,40 +481,37 @@
             pltpu.VMEM((PAIRS // WIDE, N), F32),
         ],
         compiler_params=params(),
-        cost_estimate=cost(),
+        cost_estimate=cost(8),
         name="across",
     )(x, gy, grow, tail, part, part2, cum, b, c, start, last, ga, gb, gc)
 
 
-def fold_kernel(z_ref, a0, a1, a2, a3, b0, b1, b2, b3, *rest):
-    outs, sums = rest[:8], rest[8]
-    half = a0.shape[1]
-    for i, parts in enumerate(((a0, a1, a2, a3), (b0, b1, b2, b3))):
+def fold_kernel(a0, a1, a2, a3, b0, b1, b2, b3, out_ref):
+    sums = []
+    for parts in ((a0, a1, a2, a3), (b0, b1, b2, b3)):
         total = parts[0][...].astype(F32)
         for part in parts[1:]:
             total += part[...].astype(F32)
-        sums[:, i * half : (i + 1) * half] = total
-    for d in range(8):
-        for i in range(TILES):
-            q = TILES * ((z_ref[0] + d) % 8) + i
-            r = jnp.minimum(q // 10, 9)
-            row = pl.multiple_of(16 * r, 16)
-            col = pl.multiple_of(128 * (q % 10), 128)
-            tile = sums[pl.ds(row, 16), pl.ds(col, 128)]
-            outs[d][i] = jnp.where(q < 100, tile, 0.0).astype(BF)
-
-
-def fold(z, parts):
+        sums.append(total.astype(BF))
+    for q in range(8 * TILES):
+        r, c = divmod(q, 10)
+        if r < 10:
+            tile = sums[c // 5][16 * r : 16 * r + 16, 128 * (c % 5) : 128 * (c % 5) + 128]
+        else:
+            tile = jnp.zeros((16, 128), BF)
+        out_ref[q // TILES, q % TILES] = tile
+
+
+def fold(parts):
     return pl.pallas_call(
         fold_kernel,
-        in_specs=[smem()] + [vmem()] * 8,
-        out_specs=[vmem()] * 8,
-        out_shape=[jax.ShapeDtypeStruct((TILES, 16, 128), BF)] * 8,
-        scratch_shapes=[pltpu.VMEM((OWN, D // 2), F32)],
-        compiler_params=params(),
-        cost_estimate=cost(),
+        in_specs=[vmem()] * 8,
+        out_specs=vmem(),
+        out_shape=jax.ShapeDtypeStruct((8, TILES, 16, 128), BF),
+        compiler_params=params(),
+        cost_estimate=cost(3),
         name="fold",
-    )(z, *parts)
+    )(*parts)
 
 
 def groups_of(row0, count, ids_ref):
@@ -522,11 +519,10 @@
     return jnp.sum(jnp.where(heads, ids_ref[...], 0.0), axis=1, keepdims=True)
 
 
-def zsum_kernel(row0_ref, z_ref, ids_ref, got_ref, *rest):
-    parts, out_ref, note_ref = rest[:8], rest[8], rest[9]
-    total = parts[0][...].astype(F32)
-    for part in parts[1:]:
-        total += part[...].astype(F32)
+def zsum_kernel(row0_ref, z_ref, ids_ref, got_ref, parts_ref, out_ref, note_ref):
+    total = parts_ref[0].astype(F32)
+    for z in range(1, 8):
+        total += parts_ref[z].astype(F32)
     for s in range(8):
         out_ref[s] = total.astype(BF)
     found = jnp.zeros((16, N), F32)
@@ -545,16 +541,16 @@
 def zsum(row0, z, ids, parts, got):
     return pl.pallas_call(
         zsum_kernel,
-        in_specs=[smem(), smem()] + [vmem()] * 10,
+        in_specs=[smem(), smem()] + [vmem()] * 3,
         out_specs=[vmem(), vmem()],
         out_shape=[
             jax.ShapeDtypeStruct((8, TILES, 16, 128), BF),
             jax.ShapeDtypeStruct((1, N), F32),
         ],
         compiler_params=params(),
-        cost_estimate=cost(),
+        cost_estimate=cost(2),
         name="zsum",
-    )(row0, z, ids, got, *parts)
+    )(row0, z, ids, got, parts)
 
 
 def tile_of(ref, r, c):
@@ -565,9 +561,7 @@
 def clip_kernel(tokens_all, row0_ref, core_ref, ids_ref, own_ref, other_ref, note_ref, w_ref, d_ref):
     ids = ids_ref[...]
     lane = iota((1, N), 1)
-    note = note_ref[0]
-    for s in range(1, N_SEQ):
-        note = note + note_ref[s]
+    note = note_ref[...]
     grad_d = jnp.where(lane < H, note, 0.0)
     groups = groups_of(row0_ref[0], OWN, ids_ref)
     w_factor = jnp.zeros((OWN, 1), F32)
@@ -597,7 +591,7 @@
         out_specs=[vmem(), vmem()],
         out_shape=[jax.ShapeDtypeStruct((OWN, D), F32), jax.ShapeDtypeStruct((1, N), F32)],
         compiler_params=params(),
-        cost_estimate=cost(),
+        cost_estimate=cost(3),
         name="clip",
     )(row0, core, ids, own, other, note)
 
@@ -635,14 +629,13 @@
     return lax.ppermute(v, "core", [(0, 1), (1, 0)])
 
 
-def sum_over(v, axis):
-    got = [lax.ppermute(v, axis, [(i, i ^ k) for i in range(4)]) for k in (1, 2, 3)]
-    return (v + got[0]) + (got[1] + got[2])
-
-
-def along_z(parts):
-    got = [lax.ppermute(parts[d], "z", [(i, (i + d) % 8) for i in range(8)]) for d in range(1, 8)]
-    return [parts[0]] + got
+def sum_over(v, axes):
+    for unit in (1, 4):
+        got = [
+            lax.ppermute(v, axes, [(i, i ^ (unit * k)) for i in range(16)]) for k in (1, 2, 3)
+        ]
+        v = (v + got[0]) + (got[1] + got[2])
+    return v
 
 
 def tie(*values):
@@ -673,41 +666,39 @@
     start = swap(chain(got, got, mine, False), SEQ).reshape(H * P_SIZE, N)
     y_own = inter(y_part, grow, c, start)
     y_other = other_core(y_own)
+    w_half, _ = tie(w_half, y_own)
+    gy_own, gy_other = gy_parts(g_both, w_half)
+    y_other, gy_own, gy_other = tie(y_other, gy_own, gy_other)
+    gy_other = other_core(gy_other)
     first, second = terms(at, y_own, y_other, g_both)
 
     first = lax.psum_scatter(first.reshape(-1, half // 2), "x", scatter_dimension=0, tiled=True)
     far_y = far(second, "y")
-    w_half, _ = tie(w_half, second)
-    gy_own, gy_other = gy_parts(g_both, w_half)
-    far_y = tie(*far_y, gy_own)[:2]
-    gy_other = other_core(gy_other)
+    gy_own, gy_other, _ = tie(gy_own, gy_other, second)
+    gy, sent_back = entries(gy_own, gy_other, x, grow, c)
+    *far_y, sent_back = tie(*far_y, sent_back)
+    got_back = swap(sent_back, SEQ)
     up, down = passed(second, *far_y)
-    up, down, gy_own, gy_other = tie(up, down, gy_own, gy_other)
+    up, down, gy = tie(up, down, gy)
     second = near(second, up, down, "y")
-    gy, sent_back = entries(gy_own, gy_other, x, grow, c)
-    got_back = swap(sent_back, SEQ)
     steps = PAIRS // STEP // 2
     gx1, *sums = within(0, steps, x, gy, cum, cum_t, b, c, d_skip)
-    first, second, gx1 = tie(first, second, gx1)
+    states = chain(got_back, got, mine, True)
+    first, second, gx1, states = tie(first, second, gx1, states)
+    last = swap(states, SEQ).reshape(H * P_SIZE, N)
     first = direct(first.reshape(4, OWN, half // 2), "y")
     second = direct(second, "x")
-    mine, _ = tie(mine, second[0])
-    states = chain(got_back, got, mine, True)
-    states, parts = tie(states, first + second)
-    last = swap(states, SEQ).reshape(H * P_SIZE, N)
-
-    tiles = along_z(fold(at_z, parts))
+    parts, last = tie(first + second, last)
+    tiles = fold(parts)
+    gy, tiles = tie(gy, tiles)
+    tiles = swap(tiles, "z")
+    gx2, *sums = within(steps, steps, x, gy, cum, cum_t, b, c, d_skip, sums)
+    gx, ga, gb, gc = across(x, gy, grow, tail, gx1, gx2, cum, b, c, start, last, *sums)
+    tiles, ga = tie(tiles, ga)
     tiles, note = zsum(row0, at_z, ids, tiles, got_back)
-    tiles, last = tie(tiles, last)
     tiles = swap(tiles, "z")
-    gy, note = tie(gy, note)
-    gx2, *sums = within(steps, steps, x, gy, cum, cum_t, b, c, d_skip, sums)
-    note = sum_over(sum_over(note, "x"), "y")
-    tiles, note, gx2, last = tie(tiles, note, gx2, last)
-    note = swap(jnp.broadcast_to(note[None], (N_SEQ, 1, N)), SEQ)
+    note = sum_over(sum_over(note, ("y", "x")), SEQ)
     tiles_other = other_core(tiles)
-    gx, ga, gb, gc = across(x, gy, grow, tail, gx1, gx2, cum, b, c, start, last, *sums)
-    note, ga = tie(note, ga)
     core = core.reshape(1).astype(jnp.int32)
     clipped_w, clipped_d = clip(tokens_all, row0, core, ids, tiles, tiles_other, note)
     return (gx[None], ga[None], gb[None], gc[None], clipped_w, clipped_d[0, :H])

time: 253 us -> 256 us (1.012)
  waiting for transfers between devices: 66.3 us -> 72.9 us
  starting transfers between devices: 74.9 us -> 68.9 us
    ppermute x10, waiting for transfers between devices: 14.7 us -> 25.1 us  [shifted(): return lax.ppermute(v, axis, [(i, (i + d) % 4) for i in range(4)])]
    ppermute x4, starting transfers between devices: 5.39 us -> 0.89 us  [other_core(): return lax.ppermute(v, 'core', [(0, 1), (1, 0)])]
    ppermute x13 -> x12, waiting for transfers between devices: 12.9 us -> 10.3 us  [sum_over(): lax.ppermute(v, axes, [(i, i ^ unit * k) for i in range(16)])]
    ppermute x13 -> x12, starting transfers between devices: 20.3 us -> 18.5 us  [sum_over(): lax.ppermute(v, axes, [(i, i ^ unit * k) for i in range(16)])]
    unnamed x52 -> x36, local copies, waits for them, and re-layouts: 5.14 us -> 6.31 us
  transfers between devices with their start and end apart: 35 -> 34, of which waited for: 14 -> 19; matrix products, arithmetic and copies ran while one was open for 3% -> 4% of each run, Pallas kernels for 31% -> 25%
where the time goes in v6:
time: 256 us; the launch traced here: 253 us
  Pallas kernels  79 us (31%)
  waiting for transfers between devices  72.9 us (28%)
  starting transfers between devices  68.9 us (27%)
  between operations  14.2 us (6%)
  local copies, waits for them, and re-layouts  11.9 us (5%)
  other arithmetic  5.88 us (2%)
    all_to_all x6, starting transfers between devices, swap(): return lax.all_to_all(v, axis, 0, 0, tiled=True)  38.2 us
    all_to_all x6, waiting for transfers between devices, swap(): return lax.all_to_all(v, axis, 0, 0, tiled=True)  34.7 us
    ppermute x10, waiting for transfers between devices, shifted(): return lax.ppermute(v, axis, [(i, (i + d) % 4) for i in range(4)])  25.1 us
    ppermute x12, starting transfers between devices, sum_over(): lax.ppermute(v, axes, [(i, i ^ unit * k) for i in range(16)])  18.5 us
    pallas_call x2, Pallas kernels, within(): pl.pallas_call(functools.partial(within_kernel, first, steps), grid=(step...  13.9 us
    ppermute x10, starting transfers between devices, shifted(): return lax.ppermute(v, axis, [(i, (i + d) % 4) for i in range(4)])  11.2 us
    ppermute x12, waiting for transfers between devices, sum_over(): lax.ppermute(v, axes, [(i, i ^ unit * k) for i in range(16)])  10.3 us
    pallas_call x1, Pallas kernels, intra(): pl.pallas_call(intra_kernel, grid=(PAIRS // STEP,), in_specs=[wide(T, STE...  9.25 us
  transfers between devices with their start and end apart: 34, of which 19 were waited for; matrix products, arithmetic and copies ran while one was open for 4% of the time, Pallas kernels for 25%

profile of v6, /device:TPU:1, one launch (start us, length us, event | category | flops | bytes accessed | tf_op | source)
XLA Modules:
  0.0 252.7 jit_solution(6920104855364074308)
XLA Ops:
  9.1 5.7 %ends.1 = (f32[40,256]{1,0:T(8,128)}, f32[256,40]{1,0:T(8,128)}, f32[256,2560]{1,0:T(8,128)}, bf16[16,176,128]{2,1,0:T(8,128)(2,1)}) custom-call(f32[256,2560]{1,0:T(8,128)} %bitcast.50, f32[40,256]{1,0:T(8,128)} %bitcast.71, f32[256,128]{1,0:T(8,128)} %bitcast.65), custom_call_target="tpu_custom_call" | custom-call | bytes 18000000 | tf_op jit(solution)/shard_map/ends/pallas_call | solution.py:134
  14.8 10.0 %all-to-all-start = ((bf16[16,176,128]{2,1,0:T(8,128)(2,1)}), bf16[16,176,128]{2,1,0:T(8,128)(2,1)S(1)}, u32[]{:S(2)}, u32[]{:S(2)}) async-start(bf16[16,176,128]{2,1,0:T(8,128)(2,1)} %get-tuple-element.67), calls=%async_computation | async-start | bytes 1441792 | tf_op jit(solution)/shard_map/all_to_all | solution.py:235
  24.8 21.3 %all-to-all-done.parts_ref.totals_ref = bf16[16,176,128]{2,1,0:T(8,128)(2,1)S(1)} async-done(((bf16[16,176,128]{2,1,0:T(8,128)(2,1)}), bf16[16,176,128]{2,1,0:T(8,128)(2,1)S(1)}, u32[]{:S(2)}, u32[]{:S(2)}) %all-to-all-start) | async-done | bytes 720928 | tf_op jit(solution)/shard_map/all_to_all | solution.py:235
  49.7 3.5 %all-to-all-start.1 = ((bf16[16,160,128]{2,1,0:T(8,128)(2,1)}), bf16[16,160,128]{2,1,0:T(8,128)(2,1)S(1)}, u32[]{:S(2)}, u32[]{:S(2)}) async-start(bf16[16,160,128]{2,1,0:T(8,128)(2,1)} %chain.2), calls=%async_computation.1 | async-start | bytes 1310720 | tf_op jit(solution)/shard_map/all_to_all | solution.py:235
  53.3 9.2 %intra.1 = (f32[256,2560]{1,0:T(8,128)}, f32[256,2560]{1,0:T(8,128)}) custom-call(f32[256,2560]{1,0:T(8,128)} %bitcast.51, f32[40,256]{1,0:T(8,128)} %get-tuple-element.63.cum_ref, f32[256,40]{1,0:T(8,128)} %get-tuple-element.64.cum_t_ref, f32[256,128]{1,0:T(8,128)} %bitcast.66, f32[256,128]{1,0:T(8,128)} %bitcast.58, f32[40]{0:T(128)} %skip_ref.5), custom_call_target="tpu_custom_call" | custom-call | bytes 27000000 | tf_op jit(solution)/shard_map/intra/pallas_call | solution.py:178
  62.5 10.3 %all-to-all-done.1 = bf16[16,160,128]{2,1,0:T(8,128)(2,1)S(1)} async-done(((bf16[16,160,128]{2,1,0:T(8,128)(2,1)}), bf16[16,160,128]{2,1,0:T(8,128)(2,1)S(1)}, u32[]{:S(2)}, u32[]{:S(2)}) %all-to-all-start.1) | async-done | bytes 655392 | tf_op jit(solution)/shard_map/all_to_all | solution.py:235
  73.7 5.1 %inter.1.yo_ref = bf16[256,2560]{1,0:T(8,128)(2,1)} custom-call(f32[256,2560]{1,0:T(8,128)} %get-tuple-element.65.part_ref, f32[256,2560]{1,0:T(8,128)} %get-tuple-element.66.grow_ref, f32[256,128]{1,0:T(8,128)} %bitcast.59, bf16[2560,128]{1,0:T(8,128)(2,1)} %bitcast.56), custom_call_target="tpu_custom_call" | custom-call | bytes 15000000 | tf_op jit(solution)/shard_map/inter/pallas_call | solution.py:199
  83.9 8.2 %gy_parts.1 = (f32[256,2560]{1,0:T(8,128)}, bf16[256,2560]{1,0:T(8,128)(2,1)}) custom-call(bf16[512,1280]{1,0:T(8,128)(2,1)} %pad_maximum_fusion.g_ref, bf16[2560,1280]{1,0:T(8,128)(2,1)} %all-gather.2.cloned.1.call-done.w_ref), custom_call_target="tpu_custom_call" | custom-call | bytes 24000000 | tf_op jit(solution)/shard_map/gy_parts/pallas_call | solution.py:276
  92.2 8.3 %terms.1 = (bf16[4,4,160,640]{3,2,1,0:T(8,128)(2,1)}, bf16[4,4,160,640]{3,2,1,0:T(8,128)(2,1)}) custom-call(s32[2]{0:T(128)} %pad_add_fusion.at_ref, bf16[256,2560]{1,0:T(8,128)(2,1)} %inter.1.yo_ref, bf16[256,2560]{1,0:T(8,128)(2,1)} %collective-permute-done.yx_ref, bf16[512,1280]{1,0:T(8,128)(2,1)} %pad_maximum_fusion.g_ref), custom_call_target="tpu_custom_call" | custom-call | bytes 24000000 | tf_op jit(solution)/shard_map/terms/pallas_call | solution.py:250
  106.1 6.7 %entries.1 = (bf16[256,2560]{1,0:T(8,128)(2,1)}, bf16[16,176,128]{2,1,0:T(8,128)(2,1)}) custom-call(f32[256,2560]{1,0:T(8,128)} %get-tuple-element.75.own_ref, bf16[256,2560]{1,0:T(8,128)(2,1)} %copy-done.7, f32[256,2560]{1,0:T(8,128)} %bitcast.52, f32[256,2560]{1,0:T(8,128)} %get-tuple-element.66.grow_ref, f32[256,128]{1,0:T(8,128)} %bitcast.60), custom_call_target="tpu_custom_call" | custom-call | bytes 18000000 | tf_op jit(solution)/shard_map/entries/pallas_call | solution.py:316
  113.5 3.2 %collective-permute-done.2 = bf16[2,160,640]{2,1,0:T(8,128)(2,1)S(1)} collective-permute-done((bf16[2,160,640]{2,1,0:T(8,128)(2,1)S(1)}, bf16[2,160,640]{2,1,0:T(8,128)(2,1)S(1)}, u32[]{:S(2)}, u32[]{:S(2)}) %collective-permute-start.2) | collective-permute-done | bytes 409632 | tf_op jit(solution)/shard_map/ppermute | solution.py:600
  116.7 6.5 %all-to-all-start.2 = ((bf16[16,176,128]{2,1,0:T(8,128)(2,1)}), bf16[16,176,128]{2,1,0:T(8,128)(2,1)S(1)}, u32[]{:S(2)}, u32[]{:S(2)}) async-start(bf16[16,176,128]{2,1,0:T(8,128)(2,1)} %get-tuple-element.86), calls=%async_computation.3 | async-start | bytes 1441792 | tf_op jit(solution)/shard_map/all_to_all | solution.py:235
  127.5 6.8 %within.2 = (f32[256,1280]{1,0:T(8,128)}, f32[40,256]{1,0:T(8,128)}, f32[256,128]{1,0:T(8,128)}, f32[256,128]{1,0:T(8,128)}) custom-call(f32[256,2560]{1,0:T(8,128)} %bitcast.53, bf16[256,2560]{1,0:T(8,128)(2,1)} %get-tuple-element.98.gy_ref, f32[40,256]{1,0:T(8,128)} %get-tuple-element.63.cum_ref, f32[256,40]{1,0:T(8,128)} %get-tuple-element.64.cum_t_ref, ...), custom_call_target="tpu_custom_call" | custom-call | bytes 21000000 | tf_op jit(solution)/shard_map/within/pallas_call | solution.py:386
  134.4 11.4 %collective-permute-done.5 = bf16[4,160,640]{2,1,0:T(8,128)(2,1)S(1)} collective-permute-done((bf16[4,160,640]{2,1,0:T(8,128)(2,1)S(1)}, bf16[4,160,640]{2,1,0:T(8,128)(2,1)S(1)}, u32[]{:S(2)}, u32[]{:S(2)}) %collective-permute-start.5) | collective-permute-done | bytes 819232 | tf_op jit(solution)/shard_map/ppermute | solution.py:600
  150.7 7.9 %all-to-all-start.3 = ((bf16[16,160,128]{2,1,0:T(8,128)(2,1)}), bf16[16,160,128]{2,1,0:T(8,128)(2,1)S(1)}, u32[]{:S(2)}, u32[]{:S(2)}) async-start(bf16[16,160,128]{2,1,0:T(8,128)(2,1)} %chain.3), calls=%async_computation.4 | async-start | bytes 1310720 | tf_op jit(solution)/shard_map/all_to_all | solution.py:235
  167.6 4.7 %collective-permute-done.8.a2 = bf16[160,640]{1,0:T(8,128)(2,1)S(1)} collective-permute-done((bf16[160,640]{1,0:T(8,128)(2,1)S(1)}, bf16[160,640]{1,0:T(8,128)(2,1)S(1)}, u32[]{:S(2)}, u32[]{:S(2)}) %collective-permute-start.8) | collective-permute-done | bytes 204832 | tf_op jit(solution)/shard_map/ppermute | solution.py:600
  175.7 3.0 %all-to-all-done.3 = bf16[16,160,128]{2,1,0:T(8,128)(2,1)S(1)} async-done(((bf16[16,160,128]{2,1,0:T(8,128)(2,1)}), bf16[16,160,128]{2,1,0:T(8,128)(2,1)S(1)}, u32[]{:S(2)}, u32[]{:S(2)}) %all-to-all-start.3) | async-done | bytes 655392 | tf_op jit(solution)/shard_map/all_to_all | solution.py:235
  181.4 3.7 %all-to-all-start.4 = ((bf16[8,13,16,128]{3,2,1,0:T(8,128)(2,1)}), bf16[8,13,16,128]{3,2,1,0:T(8,128)(2,1)S(1)}, u32[]{:S(2)}, u32[]{:S(2)}) async-start(bf16[8,13,16,128]{3,2,1,0:T(8,128)(2,1)} %fold.1), calls=%async_computation.5 | async-start | bytes 851968 | tf_op jit(solution)/shard_map/all_to_all | solution.py:235
  185.6 7.0 %within.3 = (f32[256,1280]{1,0:T(8,128)}, f32[40,256]{1,0:T(8,128)}, f32[256,128]{1,0:T(8,128)}, f32[256,128]{1,0:T(8,128)}) custom-call(f32[256,2560]{1,0:T(8,128)} %bitcast.54, bf16[256,2560]{1,0:T(8,128)(2,1)} %get-tuple-element.98.gy_ref, f32[40,256]{1,0:T(8,128)} %get-tuple-element.63.cum_ref, f32[256,40]{1,0:T(8,128)} %get-tuple-element.64.cum_t_ref, ...), custom_call_target="tpu_custom_call" | custom-call | bytes 21000000 | tf_op jit(solution)/shard_map/within/pallas_call | solution.py:386
  192.6 9.1 %across.1 = (f32[256,2560]{1,0:T(8,128)}, f32[40,256]{1,0:T(8,128)}, f32[256,128]{1,0:T(8,128)}, f32[256,128]{1,0:T(8,128)}) custom-call(f32[256,2560]{1,0:T(8,128)} %bitcast.55, bf16[256,2560]{1,0:T(8,128)(2,1)} %get-tuple-element.98.gy_ref, f32[256,2560]{1,0:T(8,128)} %get-tuple-element.66.grow_ref, f32[256,2560]{1,0:T(8,128)} %get-tuple-element.99.tail_ref, ...), custom_call_target="tpu_custom_call" | custom-call | bytes 24000000 | tf_op jit(solution)/shard_map/across/pallas_call | solution.py:461
  204.6 6.6 %all-to-all-start.5 = ((bf16[8,13,16,128]{3,2,1,0:T(8,128)(2,1)}), bf16[8,13,16,128]{3,2,1,0:T(8,128)(2,1)S(1)}, u32[]{:S(2)}, u32[]{:S(2)}) async-start(bf16[8,13,16,128]{3,2,1,0:T(8,128)(2,1)} %get-tuple-element.116), calls=%async_computation.6 | async-start | bytes 851968 | tf_op jit(solution)/shard_map/all_to_all | solution.py:235
  223.9 5.8 %collective-permute-start.22 = (f32[1,128]{1,0:T(1,128)S(1)}, f32[1,128]{1,0:T(1,128)S(1)}, u32[]{:S(2)}, u32[]{:S(2)}) collective-permute-start(f32[1,128]{1,0:T(1,128)S(1)} %add_add_fusion.2), channel_id=1, source_target_pairs={{0,3},{1,2},{2,1},{3,0},{4,7},{5,6},{6,5},{7,4},{8,11},{9,10},{10,... | collective-permute-start | bytes 1544 | tf_op jit(solution)/shard_map/ppermute | solution.py:635
  234.6 3.0 %collective-permute-start.24 = (f32[1,128]{1,0:T(1,128)S(1)}, f32[1,128]{1,0:T(1,128)S(1)}, u32[]{:S(2)}, u32[]{:S(2)}) collective-permute-start(f32[1,128]{1,0:T(1,128)S(1)} %add_add_fusion.1), channel_id=1, source_target_pairs={{0,8},{1,9},{2,10},{3,11},{4,12},{5,13},{6,14},{7,15},{8,0},{9,1},... | collective-permute-start | bytes 1544 | tf_op jit(solution)/shard_map/ppermute | solution.py:635
  237.8 3.0 %collective-permute-done.24 = f32[1,128]{1,0:T(1,128)S(1)} collective-permute-done((f32[1,128]{1,0:T(1,128)S(1)}, f32[1,128]{1,0:T(1,128)S(1)}, u32[]{:S(2)}, u32[]{:S(2)}) %collective-permute-start.24) | collective-permute-done | bytes 544 | tf_op jit(solution)/shard_map/ppermute | solution.py:635
  (113 shorter events, 68.1 us)
Async XLA Ops:
  7.2 76.8 %all-gather.2.cloned.1.call-start = ((), (), s32[]{:S(2)}) async-start(), calls=%async_computation.7 | async-start | bytes 6963200 | tf_op jit(solution)/shard_map/all_gather | solution.py:657
  14.8 31.3 %all-to-all-start = ((bf16[16,176,128]{2,1,0:T(8,128)(2,1)}), bf16[16,176,128]{2,1,0:T(8,128)(2,1)S(1)}, u32[]{:S(2)}, u32[]{:S(2)}) async-start(bf16[16,176,128]{2,1,0:T(8,128)(2,1)} %get-tuple-element.67), calls=%async_computation | async-start | bytes 1441792 | tf_op jit(solution)/shard_map/all_to_all | solution.py:235
  49.7 23.1 %all-to-all-start.1 = ((bf16[16,160,128]{2,1,0:T(8,128)(2,1)}), bf16[16,160,128]{2,1,0:T(8,128)(2,1)S(1)}, u32[]{:S(2)}, u32[]{:S(2)}) async-start(bf16[16,160,128]{2,1,0:T(8,128)(2,1)} %chain.2), calls=%async_computation.1 | async-start | bytes 1310720 | tf_op jit(solution)/shard_map/all_to_all | solution.py:235
  53.2 97.5 %reduce-scatter.2.cloned.1.call-start = ((), (), s32[]{:S(2)}) async-start(), calls=%async_computation.8 | async-start | bytes 4096000 | tf_op jit(solution)/shard_map/reduce_scatter | solution.py:675
  78.8 13.3 %collective-permute-start = (bf16[256,2560]{1,0:T(8,128)(2,1)}, bf16[256,2560]{1,0:T(8,128)(2,1)}, u32[]{:S(2)}, u32[]{:S(2)}) collective-permute-start(bf16[256,2560]{1,0:T(8,128)(2,1)} %inter.1.yo_ref), channel_id=1, source_target_pairs={{0,1},{1,0},{2,3},{3,2},{4,5},{5,4},{6,7},{7,6},{8,9},{9,8},{10,11... | collective-permute-start | bytes 3932168 | tf_op jit(solution)/shard_map/ppermute | solution.py:629
  100.5 4.5 %collective-permute-start.4 = (bf16[256,2560]{1,0:T(8,128)(2,1)}, bf16[256,2560]{1,0:T(8,128)(2,1)S(1)}, u32[]{:S(2)}, u32[]{:S(2)}) collective-permute-start(bf16[256,2560]{1,0:T(8,128)(2,1)} %get-tuple-element.74), channel_id=1, source_target_pairs={{0,1},{1,0},{2,3},{3,2},{4,5},{5,4},{6,7},{7,6},{8,9},{9,8},{10,11... | collective-permute-start | bytes 3932168 | tf_op jit(solution)/shard_map/ppermute | solution.py:629
  102.3 11.3 %collective-permute-start.3 = (bf16[2,160,640]{2,1,0:T(8,128)(2,1)S(1)}, bf16[2,160,640]{2,1,0:T(8,128)(2,1)S(1)}, u32[]{:S(2)}, u32[]{:S(2)}) collective-permute-start(bf16[2,160,640]{2,1,0:T(8,128)(2,1)S(1)} %get-tuple-element.122), channel_id=1, source_target_pairs={{0,192},{64,0},{128,64},{192,128},{1,193},{65,1},{129,65},{193,129... | collective-permute-start | bytes 1228808 | tf_op jit(solution)/shard_map/ppermute | solution.py:600
  105.1 11.7 %collective-permute-start.2 = (bf16[2,160,640]{2,1,0:T(8,128)(2,1)S(1)}, bf16[2,160,640]{2,1,0:T(8,128)(2,1)S(1)}, u32[]{:S(2)}, u32[]{:S(2)}) collective-permute-start(bf16[2,160,640]{2,1,0:T(8,128)(2,1)S(1)} %get-tuple-element.123), channel_id=1, source_target_pairs={{0,64},{64,128},{128,192},{192,0},{1,65},{65,129},{129,193},{193,1... | collective-permute-start | bytes 1228808 | tf_op jit(solution)/shard_map/ppermute | solution.py:600
  116.7 30.5 %all-to-all-start.2 = ((bf16[16,176,128]{2,1,0:T(8,128)(2,1)}), bf16[16,176,128]{2,1,0:T(8,128)(2,1)S(1)}, u32[]{:S(2)}, u32[]{:S(2)}) async-start(bf16[16,176,128]{2,1,0:T(8,128)(2,1)} %get-tuple-element.86), calls=%async_computation.3 | async-start | bytes 1441792 | tf_op jit(solution)/shard_map/all_to_all | solution.py:235
  124.8 21.0 %collective-permute-start.5 = (bf16[4,160,640]{2,1,0:T(8,128)(2,1)S(1)}, bf16[4,160,640]{2,1,0:T(8,128)(2,1)S(1)}, u32[]{:S(2)}, u32[]{:S(2)}) collective-permute-start(bf16[4,160,640]{2,1,0:T(8,128)(2,1)S(1)} %get-tuple-element.83), channel_id=1, source_target_pairs={{0,64},{64,128},{128,192},{192,0},{1,65},{65,129},{129,193},{193,1... | collective-permute-start | bytes 2457608 | tf_op jit(solution)/shard_map/ppermute | solution.py:600
  124.9 20.9 %collective-permute-start.6 = (bf16[4,160,640]{2,1,0:T(8,128)(2,1)S(1)}, bf16[4,160,640]{2,1,0:T(8,128)(2,1)S(1)}, u32[]{:S(2)}, u32[]{:S(2)}) collective-permute-start(bf16[4,160,640]{2,1,0:T(8,128)(2,1)S(1)} %get-tuple-element.84), channel_id=1, source_target_pairs={{0,192},{64,0},{128,64},{192,128},{1,193},{65,1},{129,65},{193,129... | collective-permute-start | bytes 2457608 | tf_op jit(solution)/shard_map/ppermute | solution.py:600
  150.7 28.0 %all-to-all-start.3 = ((bf16[16,160,128]{2,1,0:T(8,128)(2,1)}), bf16[16,160,128]{2,1,0:T(8,128)(2,1)S(1)}, u32[]{:S(2)}, u32[]{:S(2)}) async-start(bf16[16,160,128]{2,1,0:T(8,128)(2,1)} %chain.3), calls=%async_computation.4 | async-start | bytes 1310720 | tf_op jit(solution)/shard_map/all_to_all | solution.py:235
  159.4 8.2 %collective-permute-start.9 = (bf16[160,640]{1,0:T(8,128)(2,1)S(1)}, bf16[160,640]{1,0:T(8,128)(2,1)S(1)}, u32[]{:S(2)}, u32[]{:S(2)}) collective-permute-start(bf16[160,640]{1,0:T(8,128)(2,1)S(1)} %get-tuple-element.132), channel_id=1, source_target_pairs={{0,128},{64,192},{128,0},{192,64},{1,129},{65,193},{129,1},{193,65... | collective-permute-start | bytes 614408 | tf_op jit(solution)/shard_map/ppermute | solution.py:600
  160.6 11.7 %collective-permute-start.8 = (bf16[160,640]{1,0:T(8,128)(2,1)S(1)}, bf16[160,640]{1,0:T(8,128)(2,1)S(1)}, u32[]{:S(2)}, u32[]{:S(2)}) collective-permute-start(bf16[160,640]{1,0:T(8,128)(2,1)S(1)} %get-tuple-element.133), channel_id=1, source_target_pairs={{0,192},{64,0},{128,64},{192,128},{1,193},{65,1},{129,65},{193,129... | collective-permute-start | bytes 614408 | tf_op jit(solution)/shard_map/ppermute | solution.py:600
  162.1 10.2 %collective-permute-start.7 = (bf16[160,640]{1,0:T(8,128)(2,1)S(1)}, bf16[160,640]{1,0:T(8,128)(2,1)S(1)}, u32[]{:S(2)}, u32[]{:S(2)}) collective-permute-start(bf16[160,640]{1,0:T(8,128)(2,1)S(1)} %get-tuple-element.134), channel_id=1, source_target_pairs={{0,64},{64,128},{128,192},{192,0},{1,65},{65,129},{129,193},{193,1... | collective-permute-start | bytes 614408 | tf_op jit(solution)/shard_map/ppermute | solution.py:600
  163.5 8.9 %collective-permute-start.12 = (bf16[160,640]{1,0:T(8,128)(2,1)S(1)}, bf16[160,640]{1,0:T(8,128)(2,1)S(1)}, u32[]{:S(2)}, u32[]{:S(2)}) collective-permute-start(bf16[160,640]{1,0:T(8,128)(2,1)S(1)} %get-tuple-element.128), channel_id=1, source_target_pairs={{0,32},{16,48},{32,0},{48,16},{1,33},{17,49},{33,1},{49,17},{2,34}... | collective-permute-start | bytes 614408 | tf_op jit(solution)/shard_map/ppermute | solution.py:600
  164.6 9.2 %collective-permute-start.11 = (bf16[160,640]{1,0:T(8,128)(2,1)S(1)}, bf16[160,640]{1,0:T(8,128)(2,1)S(1)}, u32[]{:S(2)}, u32[]{:S(2)}) collective-permute-start(bf16[160,640]{1,0:T(8,128)(2,1)S(1)} %get-tuple-element.129), channel_id=1, source_target_pairs={{0,48},{16,0},{32,16},{48,32},{1,49},{17,1},{33,17},{49,33},{2,50}... | collective-permute-start | bytes 614408 | tf_op jit(solution)/shard_map/ppermute | solution.py:600
  167.6 8.1 %collective-permute-start.10 = (bf16[160,640]{1,0:T(8,128)(2,1)S(1)}, bf16[160,640]{1,0:T(8,128)(2,1)S(1)}, u32[]{:S(2)}, u32[]{:S(2)}) collective-permute-start(bf16[160,640]{1,0:T(8,128)(2,1)S(1)} %get-tuple-element.130), channel_id=1, source_target_pairs={{0,16},{16,32},{32,48},{48,0},{1,17},{17,33},{33,49},{49,1},{2,18}... | collective-permute-start | bytes 614408 | tf_op jit(solution)/shard_map/ppermute | solution.py:600
  181.4 20.3 %all-to-all-start.4 = ((bf16[8,13,16,128]{3,2,1,0:T(8,128)(2,1)}), bf16[8,13,16,128]{3,2,1,0:T(8,128)(2,1)S(1)}, u32[]{:S(2)}, u32[]{:S(2)}) async-start(bf16[8,13,16,128]{3,2,1,0:T(8,128)(2,1)} %fold.1), calls=%async_computation.5 | async-start | bytes 851968 | tf_op jit(solution)/shard_map/all_to_all | solution.py:235
  204.6 25.5 %all-to-all-start.5 = ((bf16[8,13,16,128]{3,2,1,0:T(8,128)(2,1)}), bf16[8,13,16,128]{3,2,1,0:T(8,128)(2,1)S(1)}, u32[]{:S(2)}, u32[]{:S(2)}) async-start(bf16[8,13,16,128]{3,2,1,0:T(8,128)(2,1)} %get-tuple-element.116), calls=%async_computation.6 | async-start | bytes 851968 | tf_op jit(solution)/shard_map/all_to_all | solution.py:235
  223.9 7.0 %collective-permute-start.22 = (f32[1,128]{1,0:T(1,128)S(1)}, f32[1,128]{1,0:T(1,128)S(1)}, u32[]{:S(2)}, u32[]{:S(2)}) collective-permute-start(f32[1,128]{1,0:T(1,128)S(1)} %add_add_fusion.2), channel_id=1, source_target_pairs={{0,3},{1,2},{2,1},{3,0},{4,7},{5,6},{6,5},{7,4},{8,11},{9,10},{10,... | collective-permute-start | bytes 1544 | tf_op jit(solution)/shard_map/ppermute | solution.py:635
  230.2 11.2 %collective-permute-start.13 = (bf16[8,13,16,128]{3,2,1,0:T(8,128)(2,1)S(1)}, bf16[8,13,16,128]{3,2,1,0:T(8,128)(2,1)S(1)}, u32[]{:S(2)}, u32[]{:S(2)}) collective-permute-start(bf16[8,13,16,128]{3,2,1,0:T(8,128)(2,1)S(1)} %all-to-all-done.5.own_ref), channel_id=1, source_target_pairs={{0,1},{1,0},{2,3},{3,2},{4,5},{5,4},{6,7},{7,6},{8,9},{9,8},{10,11... | collective-permute-start | bytes 1277960 | tf_op jit(solution)/shard_map/ppermute | solution.py:629
  232.1 5.7 %collective-permute-start.25 = (f32[1,128]{1,0:T(1,128)S(1)}, f32[1,128]{1,0:T(1,128)S(1)}, u32[]{:S(2)}, u32[]{:S(2)}) collective-permute-start(f32[1,128]{1,0:T(1,128)S(1)} %add_add_fusion.1), channel_id=1, source_target_pairs={{0,12},{1,13},{2,14},{3,15},{4,8},{5,9},{6,10},{7,11},{8,4},{9,5},... | collective-permute-start | bytes 1544 | tf_op jit(solution)/shard_map/ppermute | solution.py:635
  234.6 6.3 %collective-permute-start.24 = (f32[1,128]{1,0:T(1,128)S(1)}, f32[1,128]{1,0:T(1,128)S(1)}, u32[]{:S(2)}, u32[]{:S(2)}) collective-permute-start(f32[1,128]{1,0:T(1,128)S(1)} %add_add_fusion.1), channel_id=1, source_target_pairs={{0,8},{1,9},{2,10},{3,11},{4,12},{5,13},{6,14},{7,15},{8,0},{9,1},... | collective-permute-start | bytes 1544 | tf_op jit(solution)/shard_map/ppermute | solution.py:635
  (28 other events, 138.2 us)
Sparse Core Ops, SparseCore 0:
  10.4 71.2 all-gather.1
  100.7 39.4 reduce-scatter.1

commit v7 on v6

--- a/solution.py
+++ b/solution.py
@@ -125,7 +125,7 @@
     pick = iota((H, width), 0) == step * 2 * WIDE + iota((H, width), 1) // P_SIZE
     pick = pick.astype(BF)
     tail = nn(pieces[0], pick) + nn(pieces[1], pick)
-    tail_ref[...] = tail
+    tail_ref[...] = tail.astype(BF)
     states = tn((x_ref[...] * tail).astype(BF), b_ref[...].astype(BF))
     put_states(out_ref, states, step * WIDE, WIDE)
 
@@ -139,7 +139,7 @@
         out_shape=[
             jax.ShapeDtypeStruct((H, T), F32),
             jax.ShapeDtypeStruct((T, H), F32),
-            jax.ShapeDtypeStruct((T, D), F32),
+            jax.ShapeDtypeStruct((T, D), BF),
             jax.ShapeDtypeStruct((N_SEQ, ROWS, N), BF),
         ],
         scratch_shapes=[pltpu.VMEM((2, T, H), BF)],
@@ -171,7 +171,8 @@
             parts.append(nn(mixed, xb))
         skip = jnp.where(low, skip_ref[head], skip_ref[head + 1])
         y_ref[:, lanes_of(i)] = jnp.where(low, parts[0], parts[1]) + skip * x
-        grow_ref[:, lanes_of(i)] = jnp.exp(jnp.where(low, sides[0], sides[1]))
+        grow = jnp.exp(jnp.where(low, sides[0], sides[1]))
+        grow_ref[:, lanes_of(i)] = grow.astype(BF)
 
 
 def intra(x, cum, cum_t, b, c, skip):
@@ -182,7 +183,7 @@
             wide(T, STEP), whole((H, T)), whole((T, H)), whole((T, N)), whole((T, N)), smem(),
         ],
         out_specs=[wide(T, STEP)] * 2,
-        out_shape=[jax.ShapeDtypeStruct((T, D), F32)] * 2,
+        out_shape=[jax.ShapeDtypeStruct((T, D), F32), jax.ShapeDtypeStruct((T, D), BF)],
         scratch_shapes=[pltpu.VMEM((T, T), F32)],
         compiler_params=params(),
         cost_estimate=cost(9),
@@ -192,7 +193,7 @@
 
 def inter_kernel(part_ref, grow_ref, c_ref, start_ref, y_ref):
     read = nt(c_ref[...].astype(BF), start_ref[...])
-    y_ref[...] = (part_ref[...] + grow_ref[...] * read).astype(BF)
+    y_ref[...] = (part_ref[...] + grow_ref[...].astype(F32) * read).astype(BF)
 
 
 def inter(part, grow, c, start):
@@ -294,7 +295,7 @@
         gy = own_ref[:, at] + other_ref[:, at].astype(F32)
         gy_ref[:, at] = gy.astype(BF)
         sums[pl.ds(step * WIDE + i, 1), :] = jnp.sum(gy * x_ref[:, at], axis=0, keepdims=True)
-        found.append(tn((gy * grow_ref[:, at]).astype(BF), c))
+        found.append(tn((gy * grow_ref[:, at].astype(F32)).astype(BF), c))
     put_states(out_ref, jnp.concatenate(found, axis=0), step * WIDE, WIDE)
 
     @pl.when(step == PAIRS // WIDE - 1)
@@ -429,9 +430,9 @@
     width = WIDE * 2 * P_SIZE
     start = start_ref[...]
     last = last_ref[...]
-    tail = tail_ref[...]
+    tail = tail_ref[...].astype(F32)
     pick = iota((width, N), 1) == step * 2 * WIDE + iota((width, N), 0) // P_SIZE
-    grown = gy_ref[...].astype(F32) * grow_ref[...]
+    grown = gy_ref[...].astype(F32) * grow_ref[...].astype(F32)
     cols[...] += nn((grown * nt(cb, start)).astype(BF), pick.astype(BF))
     gc_ref[...] += nn(grown.astype(BF), start)
     faded = x_ref[...] * tail
@@ -653,51 +654,53 @@
     ids = jnp.pad(group_ids.astype(F32), (0, N - H), constant_values=-1.0)[None]
     tokens_all = float(T * N_SEQ * 16)
 
+    g_mine = lax.dynamic_slice_in_dim(g, core * half, half, axis=1)
+    g_other = other_core(lax.dynamic_slice_in_dim(g, (1 - core) * half, half, axis=1))
+
+    g_both = jnp.concatenate([g_mine, g_other], axis=0)
+
+    cum, cum_t, tail, sent = local_ends(x, a, b)
+    w_out, sent = tie(w_out, sent)
     w_mine = lax.dynamic_slice_in_dim(w_out, core * half, half, axis=1)
     w_half = lax.all_gather(w_mine, ("y", "x"), axis=0, tiled=True)
-    g_mine = lax.dynamic_slice_in_dim(g, core * half, half, axis=1)
-    g_other = other_core(lax.dynamic_slice_in_dim(g, (1 - core) * half, half, axis=1))
-
-    g_both = jnp.concatenate([g_mine, g_other], axis=0)
-
-    cum, cum_t, tail, sent = local_ends(x, a, b)
     got = swap(sent, SEQ)
     y_part, grow = intra(x, cum, cum_t, b, c, d_skip)
     start = swap(chain(got, got, mine, False), SEQ).reshape(H * P_SIZE, N)
     y_own = inter(y_part, grow, c, start)
     y_other = other_core(y_own)
-    w_half, _ = tie(w_half, y_own)
-    gy_own, gy_other = gy_parts(g_both, w_half)
-    y_other, gy_own, gy_other = tie(y_other, gy_own, gy_other)
-    gy_other = other_core(gy_other)
     first, second = terms(at, y_own, y_other, g_both)
 
     first = lax.psum_scatter(first.reshape(-1, half // 2), "x", scatter_dimension=0, tiled=True)
     far_y = far(second, "y")
-    gy_own, gy_other, _ = tie(gy_own, gy_other, second)
+    w_half, _ = tie(w_half, second)
+    gy_own, gy_other = gy_parts(g_both, w_half)
+    *far_y, gy_own, gy_other = tie(*far_y, gy_own, gy_other)
+    gy_other = other_core(gy_other)
+    up, down = passed(second, *far_y)
+    up, down, gy_own, gy_other = tie(up, down, gy_own, gy_other)
+    second = near(second, up, down, "y")
     gy, sent_back = entries(gy_own, gy_other, x, grow, c)
-    *far_y, sent_back = tie(*far_y, sent_back)
     got_back = swap(sent_back, SEQ)
-    up, down = passed(second, *far_y)
-    up, down, gy = tie(up, down, gy)
-    second = near(second, up, down, "y")
     steps = PAIRS // STEP // 2
     gx1, *sums = within(0, steps, x, gy, cum, cum_t, b, c, d_skip)
-    states = chain(got_back, got, mine, True)
-    first, second, gx1, states = tie(first, second, gx1, states)
-    last = swap(states, SEQ).reshape(H * P_SIZE, N)
+    first, second, gx1 = tie(first, second, gx1)
     first = direct(first.reshape(4, OWN, half // 2), "y")
     second = direct(second, "x")
-    parts, last = tie(first + second, last)
-    tiles = fold(parts)
-    gy, tiles = tie(gy, tiles)
+    tiles = fold(first + second)
+    gy, mine, tiles = tie(gy, mine, tiles)
     tiles = swap(tiles, "z")
+    states = chain(got_back, got, mine, True)
     gx2, *sums = within(steps, steps, x, gy, cum, cum_t, b, c, d_skip, sums)
+    tiles, gx2, states = tie(tiles, gx2, states)
+    tiles, note = zsum(row0, at_z, ids, tiles, got_back)
+    note, states = tie(note, states)
+    last = swap(states, SEQ).reshape(H * P_SIZE, N)
+    tiles, last = tie(tiles, last)
+    tiles = swap(tiles, "z")
+    note = sum_over(sum_over(note, ("y", "x")), SEQ)
+    last, note = tie(last, note)
     gx, ga, gb, gc = across(x, gy, grow, tail, gx1, gx2, cum, b, c, start, last, *sums)
     tiles, ga = tie(tiles, ga)
-    tiles, note = zsum(row0, at_z, ids, tiles, got_back)
-    tiles = swap(tiles, "z")
-    note = sum_over(sum_over(note, ("y", "x")), SEQ)
     tiles_other = other_core(tiles)
     core = core.reshape(1).astype(jnp.int32)
     clipped_w, clipped_d = clip(tokens_all, row0, core, ids, tiles, tiles_other, note)

time: 256 us -> 253 us (0.988)
    all_to_all x6, waiting for transfers between devices: 34.7 us -> 49.9 us  [swap(): return lax.all_to_all(v, axis, 0, 0, tiled=True)]
    ppermute x10, waiting for transfers between devices: 25.1 us -> 10.8 us  [shifted(): return lax.ppermute(v, axis, [(i, (i + d) % 4) for i in range(4)])]
    all_to_all x6, starting transfers between devices: 38.2 us -> 34.9 us  [swap(): return lax.all_to_all(v, axis, 0, 0, tiled=True)]
    ppermute x4, starting transfers between devices: 0.89 us -> 4.11 us  [other_core(): return lax.ppermute(v, 'core', [(0, 1), (1, 0)])]
    ppermute x12, waiting for transfers between devices: 10.3 us -> 7.42 us  [sum_over(): lax.ppermute(v, axes, [(i, i ^ unit * k) for i in range(16)])]
    ppermute x4, waiting for transfers between devices: 2.71 us -> 5.44 us  [other_core(): return lax.ppermute(v, 'core', [(0, 1), (1, 0)])]
  transfers between devices with their start and end apart: 34 -> 34, of which waited for: 19 -> 17; matrix products, arithmetic and copies ran while one was open for 4% -> 4% of each run, Pallas kernels for 25% -> 27%
where the time goes in v7:
time: 253 us; the launch traced here: 252 us
  Pallas kernels  77.7 us (31%)
  waiting for transfers between devices  73.7 us (29%)
  starting transfers between devices  68 us (27%)
  between operations  15.7 us (6%)
  local copies, waits for them, and re-layouts  10.9 us (4%)
  other arithmetic  5.76 us (2%)
    all_to_all x6, waiting for transfers between devices, swap(): return lax.all_to_all(v, axis, 0, 0, tiled=True)  49.9 us
    all_to_all x6, starting transfers between devices, swap(): return lax.all_to_all(v, axis, 0, 0, tiled=True)  34.9 us
    ppermute x12, starting transfers between devices, sum_over(): lax.ppermute(v, axes, [(i, i ^ unit * k) for i in range(16)])  16.1 us
    pallas_call x2, Pallas kernels, within(): pl.pallas_call(functools.partial(within_kernel, first, steps), grid=(step...  13.9 us
    ppermute x10, starting transfers between devices, shifted(): return lax.ppermute(v, axis, [(i, (i + d) % 4) for i in range(4)])  12.8 us
    ppermute x10, waiting for transfers between devices, shifted(): return lax.ppermute(v, axis, [(i, (i + d) % 4) for i in range(4)])  10.8 us
    pallas_call x1, Pallas kernels, intra(): pl.pallas_call(intra_kernel, grid=(PAIRS // STEP,), in_specs=[wide(T, STE...  9.3 us
    pallas_call x1, Pallas kernels, across(): pl.pallas_call(across_kernel, grid=(PAIRS // WIDE,), in_specs=[wide(T, WI...  8.68 us
  transfers between devices with their start and end apart: 34, of which 17 were waited for; matrix products, arithmetic and copies ran while one was open for 4% of the time, Pallas kernels for 27%

profile of v7, /device:TPU:1, one launch (start us, length us, event | category | flops | bytes accessed | tf_op | source)
XLA Modules:
  0.0 251.6 jit_solution(1443431193535081695)
XLA Ops:
  8.1 5.8 %ends.1 = (f32[40,256]{1,0:T(8,128)}, f32[256,40]{1,0:T(8,128)}, bf16[256,2560]{1,0:T(8,128)(2,1)}, bf16[16,176,128]{2,1,0:T(8,128)(2,1)}) custom-call(f32[256,2560]{1,0:T(8,128)} %bitcast.50, f32[40,256]{1,0:T(8,128)} %bitcast.71, f32[256,128]{1,0:T(8,128)} %bitcast.64), custom_call_target="tpu_custom_call" | custom-call | bytes 18000000 | tf_op jit(solution)/shard_map/ends/pallas_call | solution.py:134
  14.7 10.0 %all-to-all-start = ((bf16[16,176,128]{2,1,0:T(8,128)(2,1)}), bf16[16,176,128]{2,1,0:T(8,128)(2,1)S(1)}, u32[]{:S(2)}, u32[]{:S(2)}) async-start(bf16[16,176,128]{2,1,0:T(8,128)(2,1)} %get-tuple-element.67), calls=%async_computation | async-start | bytes 1441792 | tf_op jit(solution)/shard_map/all_to_all | solution.py:236
  24.7 21.3 %all-to-all-done.parts_ref.totals_ref = bf16[16,176,128]{2,1,0:T(8,128)(2,1)S(1)} async-done(((bf16[16,176,128]{2,1,0:T(8,128)(2,1)}), bf16[16,176,128]{2,1,0:T(8,128)(2,1)S(1)}, u32[]{:S(2)}, u32[]{:S(2)}) %all-to-all-start) | async-done | bytes 720928 | tf_op jit(solution)/shard_map/all_to_all | solution.py:236
  49.5 3.5 %all-to-all-start.1 = ((bf16[16,160,128]{2,1,0:T(8,128)(2,1)}), bf16[16,160,128]{2,1,0:T(8,128)(2,1)S(1)}, u32[]{:S(2)}, u32[]{:S(2)}) async-start(bf16[16,160,128]{2,1,0:T(8,128)(2,1)} %chain.2), calls=%async_computation.1 | async-start | bytes 1310720 | tf_op jit(solution)/shard_map/all_to_all | solution.py:236
  53.0 9.3 %intra.1 = (f32[256,2560]{1,0:T(8,128)}, bf16[256,2560]{1,0:T(8,128)(2,1)}) custom-call(f32[256,2560]{1,0:T(8,128)} %bitcast.51, f32[40,256]{1,0:T(8,128)} %get-tuple-element.62.cum_ref, f32[256,40]{1,0:T(8,128)} %get-tuple-element.63.cum_t_ref, f32[256,128]{1,0:T(8,128)} %bitcast.65, f32[256,128]{1,0:T(8,128)} %bitcast.58, f32[40]{0:T(128)} %skip_ref.5), custom_call_target="tpu_custom_call" | custom-call | bytes 27000000 | tf_op jit(solution)/shard_map/intra/pallas_call | solution.py:179
  62.3 10.3 %all-to-all-done.1 = bf16[16,160,128]{2,1,0:T(8,128)(2,1)S(1)} async-done(((bf16[16,160,128]{2,1,0:T(8,128)(2,1)}), bf16[16,160,128]{2,1,0:T(8,128)(2,1)S(1)}, u32[]{:S(2)}, u32[]{:S(2)}) %all-to-all-start.1) | async-done | bytes 655392 | tf_op jit(solution)/shard_map/all_to_all | solution.py:236
  73.5 4.9 %inter.1.yo_ref = bf16[256,2560]{1,0:T(8,128)(2,1)} custom-call(f32[256,2560]{1,0:T(8,128)} %get-tuple-element.64.part_ref, bf16[256,2560]{1,0:T(8,128)(2,1)} %get-tuple-element.65.grow_ref, f32[256,128]{1,0:T(8,128)} %bitcast.59, bf16[2560,128]{1,0:T(8,128)(2,1)} %bitcast.56), custom_call_target="tpu_custom_call" | custom-call | bytes 15000000 | tf_op jit(solution)/shard_map/inter/pallas_call | solution.py:200
  83.5 8.3 %terms.1 = (bf16[4,4,160,640]{3,2,1,0:T(8,128)(2,1)}, bf16[4,4,160,640]{3,2,1,0:T(8,128)(2,1)}) custom-call(s32[2]{0:T(128)} %pad_add_fusion.at_ref, bf16[256,2560]{1,0:T(8,128)(2,1)} %inter.1.yo_ref, bf16[256,2560]{1,0:T(8,128)(2,1)} %collective-permute-done.yx_ref, bf16[512,1280]{1,0:T(8,128)(2,1)} %pad_maximum_fusion.g_ref), custom_call_target="tpu_custom_call" | custom-call | bytes 24000000 | tf_op jit(solution)/shard_map/terms/pallas_call | solution.py:251
  96.1 8.5 %gy_parts.1 = (f32[256,2560]{1,0:T(8,128)}, bf16[256,2560]{1,0:T(8,128)(2,1)}) custom-call(bf16[512,1280]{1,0:T(8,128)(2,1)} %pad_maximum_fusion.g_ref, bf16[2560,1280]{1,0:T(8,128)(2,1)} %all-gather.2.cloned.1.call-done.w_ref), custom_call_target="tpu_custom_call" | custom-call | bytes 24000000 | tf_op jit(solution)/shard_map/gy_parts/pallas_call | solution.py:277
  104.8 3.2 %collective-permute-done.2 = bf16[2,160,640]{2,1,0:T(8,128)(2,1)S(1)} collective-permute-done((bf16[2,160,640]{2,1,0:T(8,128)(2,1)S(1)}, bf16[2,160,640]{2,1,0:T(8,128)(2,1)S(1)}, u32[]{:S(2)}, u32[]{:S(2)}) %collective-permute-start.2) | collective-permute-done | bytes 409632 | tf_op jit(solution)/shard_map/ppermute | solution.py:601
  114.7 5.9 %entries.1 = (bf16[256,2560]{1,0:T(8,128)(2,1)}, bf16[16,176,128]{2,1,0:T(8,128)(2,1)}) custom-call(f32[256,2560]{1,0:T(8,128)} %get-tuple-element.77.own_ref, bf16[256,2560]{1,0:T(8,128)(2,1)} %copy-done.8, f32[256,2560]{1,0:T(8,128)} %bitcast.52, bf16[256,2560]{1,0:T(8,128)(2,1)} %get-tuple-element.65.grow_ref, f32[256,128]{1,0:T(8,128)} %bitcast.60), custom_call_target="tpu_custom_call" | custom-call | bytes 18000000 | tf_op jit(solution)/shard_map/entries/pallas_call | solution.py:317
  120.7 4.3 %all-to-all-start.3 = ((bf16[16,176,128]{2,1,0:T(8,128)(2,1)}), bf16[16,176,128]{2,1,0:T(8,128)(2,1)S(1)}, u32[]{:S(2)}, u32[]{:S(2)}) async-start(bf16[16,176,128]{2,1,0:T(8,128)(2,1)} %get-tuple-element.95), calls=%async_computation.4 | async-start | bytes 1441792 | tf_op jit(solution)/shard_map/all_to_all | solution.py:236
  125.0 6.9 %within.2 = (f32[256,1280]{1,0:T(8,128)}, f32[40,256]{1,0:T(8,128)}, f32[256,128]{1,0:T(8,128)}, f32[256,128]{1,0:T(8,128)}) custom-call(f32[256,2560]{1,0:T(8,128)} %bitcast.53, bf16[256,2560]{1,0:T(8,128)(2,1)} %get-tuple-element.86.gy_ref, f32[40,256]{1,0:T(8,128)} %get-tuple-element.62.cum_ref, f32[256,40]{1,0:T(8,128)} %get-tuple-element.63.cum_t_ref, ...), custom_call_target="tpu_custom_call" | custom-call | bytes 21000000 | tf_op jit(solution)/shard_map/within/pallas_call | solution.py:387
  140.5 2.8 %collective-permute-start.12 = (bf16[160,640]{1,0:T(8,128)(2,1)S(1)}, bf16[160,640]{1,0:T(8,128)(2,1)S(1)}, u32[]{:S(2)}, u32[]{:S(2)}) collective-permute-start(bf16[160,640]{1,0:T(8,128)(2,1)S(1)} %get-tuple-element.126), channel_id=1, source_target_pairs={{0,32},{16,48},{32,0},{48,16},{1,33},{17,49},{33,1},{49,17},{2,34}... | collective-permute-start | bytes 614408 | tf_op jit(solution)/shard_map/ppermute | solution.py:601
  144.9 3.1 %collective-permute-done.8.a2 = bf16[160,640]{1,0:T(8,128)(2,1)S(1)} collective-permute-done((bf16[160,640]{1,0:T(8,128)(2,1)S(1)}, bf16[160,640]{1,0:T(8,128)(2,1)S(1)}, u32[]{:S(2)}, u32[]{:S(2)}) %collective-permute-start.8) | collective-permute-done | bytes 204832 | tf_op jit(solution)/shard_map/ppermute | solution.py:601
  154.6 5.3 %all-to-all-start.2 = ((bf16[8,13,16,128]{3,2,1,0:T(8,128)(2,1)}), bf16[8,13,16,128]{3,2,1,0:T(8,128)(2,1)S(1)}, u32[]{:S(2)}, u32[]{:S(2)}) async-start(bf16[8,13,16,128]{3,2,1,0:T(8,128)(2,1)} %fold.1), calls=%async_computation.3 | async-start | bytes 851968 | tf_op jit(solution)/shard_map/all_to_all | solution.py:236
  160.4 7.0 %within.3 = (f32[256,1280]{1,0:T(8,128)}, f32[40,256]{1,0:T(8,128)}, f32[256,128]{1,0:T(8,128)}, f32[256,128]{1,0:T(8,128)}) custom-call(f32[256,2560]{1,0:T(8,128)} %bitcast.54, bf16[256,2560]{1,0:T(8,128)(2,1)} %get-tuple-element.86.gy_ref, f32[40,256]{1,0:T(8,128)} %get-tuple-element.62.cum_ref, f32[256,40]{1,0:T(8,128)} %get-tuple-element.63.cum_t_ref, ...), custom_call_target="tpu_custom_call" | custom-call | bytes 21000000 | tf_op jit(solution)/shard_map/within/pallas_call | solution.py:387
  174.9 8.3 %all-to-all-start.4 = ((bf16[16,160,128]{2,1,0:T(8,128)(2,1)}), bf16[16,160,128]{2,1,0:T(8,128)(2,1)S(1)}, u32[]{:S(2)}, u32[]{:S(2)}) async-start(bf16[16,160,128]{2,1,0:T(8,128)(2,1)} %chain.3), calls=%async_computation.5 | async-start | bytes 1310720 | tf_op jit(solution)/shard_map/all_to_all | solution.py:236
  183.1 2.9 %collective-permute-start.15 = (f32[1,128]{1,0:T(1,128)}, f32[1,128]{1,0:T(1,128)S(1)}, u32[]{:S(2)}, u32[]{:S(2)}) collective-permute-start(f32[1,128]{1,0:T(1,128)} %get-tuple-element.103), channel_id=1, source_target_pairs={{0,48},{16,32},{32,16},{48,0},{64,112},{80,96},{96,80},{112,64},{1... | collective-permute-start | bytes 1544 | tf_op jit(solution)/shard_map/ppermute | solution.py:636
  186.7 16.4 %all-to-all-done.4 = bf16[16,160,128]{2,1,0:T(8,128)(2,1)S(1)} async-done(((bf16[16,160,128]{2,1,0:T(8,128)(2,1)}), bf16[16,160,128]{2,1,0:T(8,128)(2,1)S(1)}, u32[]{:S(2)}, u32[]{:S(2)}) %all-to-all-start.4) | async-done | bytes 655392 | tf_op jit(solution)/shard_map/all_to_all | solution.py:236
  203.2 3.5 %all-to-all-start.5 = ((bf16[8,13,16,128]{3,2,1,0:T(8,128)(2,1)}), bf16[8,13,16,128]{3,2,1,0:T(8,128)(2,1)S(1)}, u32[]{:S(2)}, u32[]{:S(2)}) async-start(bf16[8,13,16,128]{3,2,1,0:T(8,128)(2,1)} %get-tuple-element.109), calls=%async_computation.6 | async-start | bytes 851968 | tf_op jit(solution)/shard_map/all_to_all | solution.py:236
  212.3 2.9 %collective-permute-start.21 = (f32[1,128]{1,0:T(1,128)S(1)}, f32[1,128]{1,0:T(1,128)S(1)}, u32[]{:S(2)}, u32[]{:S(2)}) collective-permute-start(f32[1,128]{1,0:T(1,128)S(1)} %add_add_fusion.2), channel_id=1, source_target_pairs={{0,3},{1,2},{2,1},{3,0},{4,7},{5,6},{6,5},{7,4},{8,11},{9,10},{10,... | collective-permute-start | bytes 1544 | tf_op jit(solution)/shard_map/ppermute | solution.py:636
  220.3 3.0 %collective-permute-start.23 = (f32[1,128]{1,0:T(1,128)S(1)}, f32[1,128]{1,0:T(1,128)S(1)}, u32[]{:S(2)}, u32[]{:S(2)}) collective-permute-start(f32[1,128]{1,0:T(1,128)S(1)} %add_add_fusion.1), channel_id=1, source_target_pairs={{0,8},{1,9},{2,10},{3,11},{4,12},{5,13},{6,14},{7,15},{8,0},{9,1},... | collective-permute-start | bytes 1544 | tf_op jit(solution)/shard_map/ppermute | solution.py:636
  227.2 8.7 %across.1 = (f32[256,2560]{1,0:T(8,128)}, f32[40,256]{1,0:T(8,128)}, f32[256,128]{1,0:T(8,128)}, f32[256,128]{1,0:T(8,128)}) custom-call(f32[256,2560]{1,0:T(8,128)} %bitcast.55, bf16[256,2560]{1,0:T(8,128)(2,1)} %get-tuple-element.86.gy_ref, bf16[256,2560]{1,0:T(8,128)(2,1)} %get-tuple-element.65.grow_ref, bf16[256,2560]{1,0:T(8,128)(2,1)} %get-tuple-element.87.tail_ref, ...), custom_call_target="tpu_custom_call" | custom-call | bytes 24000000 | tf_op jit(solution)/shard_map/across/pallas_call | solution.py:462
  (113 shorter events, 69.8 us)
Async XLA Ops:
  8.0 88.1 %all-gather.2.cloned.1.call-start = ((), (), s32[]{:S(2)}) async-start(), calls=%async_computation.7 | async-start | bytes 6963200 | tf_op jit(solution)/shard_map/all_gather | solution.py:665
  14.7 31.3 %all-to-all-start = ((bf16[16,176,128]{2,1,0:T(8,128)(2,1)}), bf16[16,176,128]{2,1,0:T(8,128)(2,1)S(1)}, u32[]{:S(2)}, u32[]{:S(2)}) async-start(bf16[16,176,128]{2,1,0:T(8,128)(2,1)} %get-tuple-element.67), calls=%async_computation | async-start | bytes 1441792 | tf_op jit(solution)/shard_map/all_to_all | solution.py:236
  49.5 23.2 %all-to-all-start.1 = ((bf16[16,160,128]{2,1,0:T(8,128)(2,1)}), bf16[16,160,128]{2,1,0:T(8,128)(2,1)S(1)}, u32[]{:S(2)}, u32[]{:S(2)}) async-start(bf16[16,160,128]{2,1,0:T(8,128)(2,1)} %chain.2), calls=%async_computation.1 | async-start | bytes 1310720 | tf_op jit(solution)/shard_map/all_to_all | solution.py:236
  53.0 81.8 %reduce-scatter.2.cloned.1.call-start = ((), (), s32[]{:S(2)}) async-start(), calls=%async_computation.8 | async-start | bytes 4096000 | tf_op jit(solution)/shard_map/reduce_scatter | solution.py:673
  93.3 11.5 %collective-permute-start.3 = (bf16[2,160,640]{2,1,0:T(8,128)(2,1)S(1)}, bf16[2,160,640]{2,1,0:T(8,128)(2,1)S(1)}, u32[]{:S(2)}, u32[]{:S(2)}) collective-permute-start(bf16[2,160,640]{2,1,0:T(8,128)(2,1)S(1)} %get-tuple-element.120), channel_id=1, source_target_pairs={{0,192},{64,0},{128,64},{192,128},{1,193},{65,1},{129,65},{193,129... | collective-permute-start | bytes 1228808 | tf_op jit(solution)/shard_map/ppermute | solution.py:601
  96.1 11.9 %collective-permute-start.2 = (bf16[2,160,640]{2,1,0:T(8,128)(2,1)S(1)}, bf16[2,160,640]{2,1,0:T(8,128)(2,1)S(1)}, u32[]{:S(2)}, u32[]{:S(2)}) collective-permute-start(bf16[2,160,640]{2,1,0:T(8,128)(2,1)S(1)} %get-tuple-element.121), channel_id=1, source_target_pairs={{0,64},{64,128},{128,192},{192,0},{1,65},{65,129},{129,193},{193,1... | collective-permute-start | bytes 1228808 | tf_op jit(solution)/shard_map/ppermute | solution.py:601
  112.0 20.8 %collective-permute-start.5 = (bf16[4,160,640]{2,1,0:T(8,128)(2,1)S(1)}, bf16[4,160,640]{2,1,0:T(8,128)(2,1)}, u32[]{:S(2)}, u32[]{:S(2)}) collective-permute-start(bf16[4,160,640]{2,1,0:T(8,128)(2,1)S(1)} %get-tuple-element.81), channel_id=1, source_target_pairs={{0,64},{64,128},{128,192},{192,0},{1,65},{65,129},{129,193},{193,1... | collective-permute-start | bytes 2457608 | tf_op jit(solution)/shard_map/ppermute | solution.py:601
  112.1 20.8 %collective-permute-start.6 = (bf16[4,160,640]{2,1,0:T(8,128)(2,1)S(1)}, bf16[4,160,640]{2,1,0:T(8,128)(2,1)}, u32[]{:S(2)}, u32[]{:S(2)}) collective-permute-start(bf16[4,160,640]{2,1,0:T(8,128)(2,1)S(1)} %get-tuple-element.82), channel_id=1, source_target_pairs={{0,192},{64,0},{128,64},{192,128},{1,193},{65,1},{129,65},{193,129... | collective-permute-start | bytes 2457608 | tf_op jit(solution)/shard_map/ppermute | solution.py:601
  120.7 33.9 %all-to-all-start.3 = ((bf16[16,176,128]{2,1,0:T(8,128)(2,1)}), bf16[16,176,128]{2,1,0:T(8,128)(2,1)S(1)}, u32[]{:S(2)}, u32[]{:S(2)}) async-start(bf16[16,176,128]{2,1,0:T(8,128)(2,1)} %get-tuple-element.95), calls=%async_computation.4 | async-start | bytes 1441792 | tf_op jit(solution)/shard_map/all_to_all | solution.py:236
  136.8 7.3 %collective-permute-start.9 = (bf16[160,640]{1,0:T(8,128)(2,1)S(1)}, bf16[160,640]{1,0:T(8,128)(2,1)S(1)}, u32[]{:S(2)}, u32[]{:S(2)}) collective-permute-start(bf16[160,640]{1,0:T(8,128)(2,1)S(1)} %get-tuple-element.130), channel_id=1, source_target_pairs={{0,128},{64,192},{128,0},{192,64},{1,129},{65,193},{129,1},{193,65... | collective-permute-start | bytes 614408 | tf_op jit(solution)/shard_map/ppermute | solution.py:601
  138.0 10.0 %collective-permute-start.8 = (bf16[160,640]{1,0:T(8,128)(2,1)S(1)}, bf16[160,640]{1,0:T(8,128)(2,1)S(1)}, u32[]{:S(2)}, u32[]{:S(2)}) collective-permute-start(bf16[160,640]{1,0:T(8,128)(2,1)S(1)} %get-tuple-element.131), channel_id=1, source_target_pairs={{0,192},{64,0},{128,64},{192,128},{1,193},{65,1},{129,65},{193,129... | collective-permute-start | bytes 614408 | tf_op jit(solution)/shard_map/ppermute | solution.py:601
  139.1 9.7 %collective-permute-start.7 = (bf16[160,640]{1,0:T(8,128)(2,1)S(1)}, bf16[160,640]{1,0:T(8,128)(2,1)S(1)}, u32[]{:S(2)}, u32[]{:S(2)}) collective-permute-start(bf16[160,640]{1,0:T(8,128)(2,1)S(1)} %get-tuple-element.132), channel_id=1, source_target_pairs={{0,64},{64,128},{128,192},{192,0},{1,65},{65,129},{129,193},{193,1... | collective-permute-start | bytes 614408 | tf_op jit(solution)/shard_map/ppermute | solution.py:601
  140.5 8.4 %collective-permute-start.12 = (bf16[160,640]{1,0:T(8,128)(2,1)S(1)}, bf16[160,640]{1,0:T(8,128)(2,1)S(1)}, u32[]{:S(2)}, u32[]{:S(2)}) collective-permute-start(bf16[160,640]{1,0:T(8,128)(2,1)S(1)} %get-tuple-element.126), channel_id=1, source_target_pairs={{0,32},{16,48},{32,0},{48,16},{1,33},{17,49},{33,1},{49,17},{2,34}... | collective-permute-start | bytes 614408 | tf_op jit(solution)/shard_map/ppermute | solution.py:601
  143.2 8.2 %collective-permute-start.11 = (bf16[160,640]{1,0:T(8,128)(2,1)S(1)}, bf16[160,640]{1,0:T(8,128)(2,1)S(1)}, u32[]{:S(2)}, u32[]{:S(2)}) collective-permute-start(bf16[160,640]{1,0:T(8,128)(2,1)S(1)} %get-tuple-element.127), channel_id=1, source_target_pairs={{0,48},{16,0},{32,16},{48,32},{1,49},{17,1},{33,17},{49,33},{2,50}... | collective-permute-start | bytes 614408 | tf_op jit(solution)/shard_map/ppermute | solution.py:601
  144.1 7.3 %collective-permute-start.10 = (bf16[160,640]{1,0:T(8,128)(2,1)S(1)}, bf16[160,640]{1,0:T(8,128)(2,1)S(1)}, u32[]{:S(2)}, u32[]{:S(2)}) collective-permute-start(bf16[160,640]{1,0:T(8,128)(2,1)S(1)} %get-tuple-element.128), channel_id=1, source_target_pairs={{0,16},{16,32},{32,48},{48,0},{1,17},{17,33},{33,49},{49,1},{2,18}... | collective-permute-start | bytes 614408 | tf_op jit(solution)/shard_map/ppermute | solution.py:601
  154.6 17.4 %all-to-all-start.2 = ((bf16[8,13,16,128]{3,2,1,0:T(8,128)(2,1)}), bf16[8,13,16,128]{3,2,1,0:T(8,128)(2,1)S(1)}, u32[]{:S(2)}, u32[]{:S(2)}) async-start(bf16[8,13,16,128]{3,2,1,0:T(8,128)(2,1)} %fold.1), calls=%async_computation.3 | async-start | bytes 851968 | tf_op jit(solution)/shard_map/all_to_all | solution.py:236
  174.9 28.3 %all-to-all-start.4 = ((bf16[16,160,128]{2,1,0:T(8,128)(2,1)}), bf16[16,160,128]{2,1,0:T(8,128)(2,1)S(1)}, u32[]{:S(2)}, u32[]{:S(2)}) async-start(bf16[16,160,128]{2,1,0:T(8,128)(2,1)} %chain.3), calls=%async_computation.5 | async-start | bytes 1310720 | tf_op jit(solution)/shard_map/all_to_all | solution.py:236
  183.1 23.5 %collective-permute-start.15 = (f32[1,128]{1,0:T(1,128)}, f32[1,128]{1,0:T(1,128)S(1)}, u32[]{:S(2)}, u32[]{:S(2)}) collective-permute-start(f32[1,128]{1,0:T(1,128)} %get-tuple-element.103), channel_id=1, source_target_pairs={{0,48},{16,32},{32,16},{48,0},{64,112},{80,96},{96,80},{112,64},{1... | collective-permute-start | bytes 1544 | tf_op jit(solution)/shard_map/ppermute | solution.py:636
  186.1 20.6 %collective-permute-start.14 = (f32[1,128]{1,0:T(1,128)}, f32[1,128]{1,0:T(1,128)S(1)}, u32[]{:S(2)}, u32[]{:S(2)}) collective-permute-start(f32[1,128]{1,0:T(1,128)} %get-tuple-element.103), channel_id=1, source_target_pairs={{0,32},{16,48},{32,0},{48,16},{64,96},{80,112},{96,64},{112,80},{1... | collective-permute-start | bytes 1544 | tf_op jit(solution)/shard_map/ppermute | solution.py:636
  186.6 20.1 %collective-permute-start.13 = (f32[1,128]{1,0:T(1,128)}, f32[1,128]{1,0:T(1,128)S(1)}, u32[]{:S(2)}, u32[]{:S(2)}) collective-permute-start(f32[1,128]{1,0:T(1,128)} %get-tuple-element.103), channel_id=1, source_target_pairs={{0,16},{16,0},{32,48},{48,32},{64,80},{80,64},{96,112},{112,96},{1... | collective-permute-start | bytes 1544 | tf_op jit(solution)/shard_map/ppermute | solution.py:636
  203.2 32.7 %all-to-all-start.5 = ((bf16[8,13,16,128]{3,2,1,0:T(8,128)(2,1)}), bf16[8,13,16,128]{3,2,1,0:T(8,128)(2,1)S(1)}, u32[]{:S(2)}, u32[]{:S(2)}) async-start(bf16[8,13,16,128]{3,2,1,0:T(8,128)(2,1)} %get-tuple-element.109), calls=%async_computation.6 | async-start | bytes 851968 | tf_op jit(solution)/shard_map/all_to_all | solution.py:236
  212.3 6.0 %collective-permute-start.21 = (f32[1,128]{1,0:T(1,128)S(1)}, f32[1,128]{1,0:T(1,128)S(1)}, u32[]{:S(2)}, u32[]{:S(2)}) collective-permute-start(f32[1,128]{1,0:T(1,128)S(1)} %add_add_fusion.2), channel_id=1, source_target_pairs={{0,3},{1,2},{2,1},{3,0},{4,7},{5,6},{6,5},{7,4},{8,11},{9,10},{10,... | collective-permute-start | bytes 1544 | tf_op jit(solution)/shard_map/ppermute | solution.py:636
  218.3 5.7 %collective-permute-start.24 = (f32[1,128]{1,0:T(1,128)S(1)}, f32[1,128]{1,0:T(1,128)S(1)}, u32[]{:S(2)}, u32[]{:S(2)}) collective-permute-start(f32[1,128]{1,0:T(1,128)S(1)} %add_add_fusion.1), channel_id=1, source_target_pairs={{0,12},{1,13},{2,14},{3,15},{4,8},{5,9},{6,10},{7,11},{8,4},{9,5},... | collective-permute-start | bytes 1544 | tf_op jit(solution)/shard_map/ppermute | solution.py:636
  220.3 6.3 %collective-permute-start.23 = (f32[1,128]{1,0:T(1,128)S(1)}, f32[1,128]{1,0:T(1,128)S(1)}, u32[]{:S(2)}, u32[]{:S(2)}) collective-permute-start(f32[1,128]{1,0:T(1,128)S(1)} %add_add_fusion.1), channel_id=1, source_target_pairs={{0,8},{1,9},{2,10},{3,11},{4,12},{5,13},{6,14},{7,15},{8,0},{9,1},... | collective-permute-start | bytes 1544 | tf_op jit(solution)/shard_map/ppermute | solution.py:636
  (28 other events, 162.6 us)
Sparse Core Ops, SparseCore 0:
  14.8 71.2 all-gather.1
Sparse Core Ops, SparseCore 1:
  91.9 38.5 reduce-scatter.1

commit v8 on v7

--- a/solution.py
+++ b/solution.py
@@ -693,17 +693,16 @@
     gx2, *sums = within(steps, steps, x, gy, cum, cum_t, b, c, d_skip, sums)
     tiles, gx2, states = tie(tiles, gx2, states)
     tiles, note = zsum(row0, at_z, ids, tiles, got_back)
-    note, states = tie(note, states)
+    tiles = swap(tiles, "z")
+    note = sum_over(note, ("y", "x"))
+    tiles, note, states = tie(tiles, note, states)
     last = swap(states, SEQ).reshape(H * P_SIZE, N)
-    tiles, last = tie(tiles, last)
-    tiles = swap(tiles, "z")
-    note = sum_over(sum_over(note, ("y", "x")), SEQ)
-    last, note = tie(last, note)
-    gx, ga, gb, gc = across(x, gy, grow, tail, gx1, gx2, cum, b, c, start, last, *sums)
-    tiles, ga = tie(tiles, ga)
     tiles_other = other_core(tiles)
+    note = sum_over(note, SEQ)
     core = core.reshape(1).astype(jnp.int32)
     clipped_w, clipped_d = clip(tokens_all, row0, core, ids, tiles, tiles_other, note)
+    clipped_w, last = tie(clipped_w, last)
+    gx, ga, gb, gc = across(x, gy, grow, tail, gx1, gx2, cum, b, c, start, last, *sums)
     return (gx[None], ga[None], gb[None], gc[None], clipped_w, clipped_d[0, :H])
 
 

time: 253 us -> 256 us (1.012)
  starting transfers between devices: 68 us -> 70.9 us
    all_to_all x6, waiting for transfers between devices: 49.9 us -> 33.4 us  [swap(): return lax.all_to_all(v, axis, 0, 0, tiled=True)]
    ppermute x12, waiting for transfers between devices: 7.42 us -> 23.6 us  [sum_over(): lax.ppermute(v, axes, [(i, i ^ unit * k) for i in range(16)])]
    all_to_all x6, starting transfers between devices: 34.9 us -> 38.3 us  [swap(): return lax.all_to_all(v, axis, 0, 0, tiled=True)]
  transfers between devices with their start and end apart: 34 -> 34, of which waited for: 17 -> 17; matrix products, arithmetic and copies ran while one was open for 4% -> 5% of each run, Pallas kernels for 27% -> 24%
where the time goes in v8:
time: 256 us; the launch traced here: 254 us
  Pallas kernels  77.5 us (30%)
  waiting for transfers between devices  71.9 us (28%)
  starting transfers between devices  70.9 us (28%)
  between operations  15.7 us (6%)
  local copies, waits for them, and re-layouts  11.7 us (5%)
  other arithmetic  6.38 us (2%)
    all_to_all x6, starting transfers between devices, swap(): return lax.all_to_all(v, axis, 0, 0, tiled=True)  38.3 us
    all_to_all x6, waiting for transfers between devices, swap(): return lax.all_to_all(v, axis, 0, 0, tiled=True)  33.4 us
    ppermute x12, waiting for transfers between devices, sum_over(): lax.ppermute(v, axes, [(i, i ^ unit * k) for i in range(16)])  23.6 us
    ppermute x12, starting transfers between devices, sum_over(): lax.ppermute(v, axes, [(i, i ^ unit * k) for i in range(16)])  17.8 us
    pallas_call x2, Pallas kernels, within(): pl.pallas_call(functools.partial(within_kernel, first, steps), grid=(step...  13.9 us
    ppermute x10, starting transfers between devices, shifted(): return lax.ppermute(v, axis, [(i, (i + d) % 4) for i in range(4)])  12.8 us
    ppermute x10, waiting for transfers between devices, shifted(): return lax.ppermute(v, axis, [(i, (i + d) % 4) for i in range(4)])  10.8 us
    pallas_call x1, Pallas kernels, intra(): pl.pallas_call(intra_kernel, grid=(PAIRS // STEP,), in_specs=[wide(T, STE...  9.3 us
  transfers between devices with their start and end apart: 34, of which 17 were waited for; matrix products, arithmetic and copies ran while one was open for 5% of the time, Pallas kernels for 24%

profile of v8, /device:TPU:1, one launch (start us, length us, event | category | flops | bytes accessed | tf_op | source)
XLA Modules:
  0.0 254.1 jit_solution(14284016061889063666)
XLA Ops:
  8.1 5.8 %ends.1 = (f32[40,256]{1,0:T(8,128)}, f32[256,40]{1,0:T(8,128)}, bf16[256,2560]{1,0:T(8,128)(2,1)}, bf16[16,176,128]{2,1,0:T(8,128)(2,1)}) custom-call(f32[256,2560]{1,0:T(8,128)} %bitcast.50, f32[40,256]{1,0:T(8,128)} %bitcast.71, f32[256,128]{1,0:T(8,128)} %bitcast.64), custom_call_target="tpu_custom_call" | custom-call | bytes 18000000 | tf_op jit(solution)/shard_map/ends/pallas_call | solution.py:134
  14.7 10.0 %all-to-all-start = ((bf16[16,176,128]{2,1,0:T(8,128)(2,1)}), bf16[16,176,128]{2,1,0:T(8,128)(2,1)S(1)}, u32[]{:S(2)}, u32[]{:S(2)}) async-start(bf16[16,176,128]{2,1,0:T(8,128)(2,1)} %get-tuple-element.64), calls=%async_computation | async-start | bytes 1441792 | tf_op jit(solution)/shard_map/all_to_all | solution.py:236
  24.7 21.3 %all-to-all-done.parts_ref.totals_ref = bf16[16,176,128]{2,1,0:T(8,128)(2,1)S(1)} async-done(((bf16[16,176,128]{2,1,0:T(8,128)(2,1)}), bf16[16,176,128]{2,1,0:T(8,128)(2,1)S(1)}, u32[]{:S(2)}, u32[]{:S(2)}) %all-to-all-start) | async-done | bytes 720928 | tf_op jit(solution)/shard_map/all_to_all | solution.py:236
  49.5 3.5 %all-to-all-start.1 = ((bf16[16,160,128]{2,1,0:T(8,128)(2,1)}), bf16[16,160,128]{2,1,0:T(8,128)(2,1)S(1)}, u32[]{:S(2)}, u32[]{:S(2)}) async-start(bf16[16,160,128]{2,1,0:T(8,128)(2,1)} %chain.2), calls=%async_computation.1 | async-start | bytes 1310720 | tf_op jit(solution)/shard_map/all_to_all | solution.py:236
  53.0 9.3 %intra.1 = (f32[256,2560]{1,0:T(8,128)}, bf16[256,2560]{1,0:T(8,128)(2,1)}) custom-call(f32[256,2560]{1,0:T(8,128)} %bitcast.51, f32[40,256]{1,0:T(8,128)} %get-tuple-element.59.cum_ref, f32[256,40]{1,0:T(8,128)} %get-tuple-element.60.cum_t_ref, f32[256,128]{1,0:T(8,128)} %bitcast.65, f32[256,128]{1,0:T(8,128)} %bitcast.58, f32[40]{0:T(128)} %skip_ref.5), custom_call_target="tpu_custom_call" | custom-call | bytes 27000000 | tf_op jit(solution)/shard_map/intra/pallas_call | solution.py:179
  62.3 10.3 %all-to-all-done.1 = bf16[16,160,128]{2,1,0:T(8,128)(2,1)S(1)} async-done(((bf16[16,160,128]{2,1,0:T(8,128)(2,1)}), bf16[16,160,128]{2,1,0:T(8,128)(2,1)S(1)}, u32[]{:S(2)}, u32[]{:S(2)}) %all-to-all-start.1) | async-done | bytes 655392 | tf_op jit(solution)/shard_map/all_to_all | solution.py:236
  73.5 4.8 %inter.1.yo_ref = bf16[256,2560]{1,0:T(8,128)(2,1)} custom-call(f32[256,2560]{1,0:T(8,128)} %get-tuple-element.61.part_ref, bf16[256,2560]{1,0:T(8,128)(2,1)} %get-tuple-element.62.grow_ref, f32[256,128]{1,0:T(8,128)} %bitcast.59, bf16[2560,128]{1,0:T(8,128)(2,1)} %bitcast.56), custom_call_target="tpu_custom_call" | custom-call | bytes 15000000 | tf_op jit(solution)/shard_map/inter/pallas_call | solution.py:200
  83.5 8.3 %terms.1 = (bf16[4,4,160,640]{3,2,1,0:T(8,128)(2,1)}, bf16[4,4,160,640]{3,2,1,0:T(8,128)(2,1)}) custom-call(s32[2]{0:T(128)} %pad_add_fusion.at_ref, bf16[256,2560]{1,0:T(8,128)(2,1)} %inter.1.yo_ref, bf16[256,2560]{1,0:T(8,128)(2,1)} %collective-permute-done.yx_ref, bf16[512,1280]{1,0:T(8,128)(2,1)} %pad_maximum_fusion.g_ref), custom_call_target="tpu_custom_call" | custom-call | bytes 24000000 | tf_op jit(solution)/shard_map/terms/pallas_call | solution.py:251
  96.1 8.5 %gy_parts.1 = (f32[256,2560]{1,0:T(8,128)}, bf16[256,2560]{1,0:T(8,128)(2,1)}) custom-call(bf16[512,1280]{1,0:T(8,128)(2,1)} %pad_maximum_fusion.g_ref, bf16[2560,1280]{1,0:T(8,128)(2,1)} %all-gather.2.cloned.1.call-done.w_ref), custom_call_target="tpu_custom_call" | custom-call | bytes 24000000 | tf_op jit(solution)/shard_map/gy_parts/pallas_call | solution.py:277
  104.8 3.2 %collective-permute-done.2 = bf16[2,160,640]{2,1,0:T(8,128)(2,1)S(1)} collective-permute-done((bf16[2,160,640]{2,1,0:T(8,128)(2,1)S(1)}, bf16[2,160,640]{2,1,0:T(8,128)(2,1)S(1)}, u32[]{:S(2)}, u32[]{:S(2)}) %collective-permute-start.2) | collective-permute-done | bytes 409632 | tf_op jit(solution)/shard_map/ppermute | solution.py:601
  114.7 6.0 %entries.1 = (bf16[256,2560]{1,0:T(8,128)(2,1)}, bf16[16,176,128]{2,1,0:T(8,128)(2,1)}) custom-call(f32[256,2560]{1,0:T(8,128)} %get-tuple-element.74.own_ref, bf16[256,2560]{1,0:T(8,128)(2,1)} %copy-done.8, f32[256,2560]{1,0:T(8,128)} %bitcast.52, bf16[256,2560]{1,0:T(8,128)(2,1)} %get-tuple-element.62.grow_ref, f32[256,128]{1,0:T(8,128)} %bitcast.60), custom_call_target="tpu_custom_call" | custom-call | bytes 18000000 | tf_op jit(solution)/shard_map/entries/pallas_call | solution.py:317
  120.7 4.3 %all-to-all-start.3 = ((bf16[16,176,128]{2,1,0:T(8,128)(2,1)}), bf16[16,176,128]{2,1,0:T(8,128)(2,1)S(1)}, u32[]{:S(2)}, u32[]{:S(2)}) async-start(bf16[16,176,128]{2,1,0:T(8,128)(2,1)} %get-tuple-element.92), calls=%async_computation.4 | async-start | bytes 1441792 | tf_op jit(solution)/shard_map/all_to_all | solution.py:236
  125.0 6.9 %within.2 = (f32[256,1280]{1,0:T(8,128)}, f32[40,256]{1,0:T(8,128)}, f32[256,128]{1,0:T(8,128)}, f32[256,128]{1,0:T(8,128)}) custom-call(f32[256,2560]{1,0:T(8,128)} %bitcast.53, bf16[256,2560]{1,0:T(8,128)(2,1)} %get-tuple-element.83.gy_ref, f32[40,256]{1,0:T(8,128)} %get-tuple-element.59.cum_ref, f32[256,40]{1,0:T(8,128)} %get-tuple-element.60.cum_t_ref, ...), custom_call_target="tpu_custom_call" | custom-call | bytes 21000000 | tf_op jit(solution)/shard_map/within/pallas_call | solution.py:387
  140.5 2.8 %collective-permute-start.12 = (bf16[160,640]{1,0:T(8,128)(2,1)S(1)}, bf16[160,640]{1,0:T(8,128)(2,1)S(1)}, u32[]{:S(2)}, u32[]{:S(2)}) collective-permute-start(bf16[160,640]{1,0:T(8,128)(2,1)S(1)} %get-tuple-element.120), channel_id=1, source_target_pairs={{0,32},{16,48},{32,0},{48,16},{1,33},{17,49},{33,1},{49,17},{2,34}... | collective-permute-start | bytes 614408 | tf_op jit(solution)/shard_map/ppermute | solution.py:601
  144.9 3.1 %collective-permute-done.8.a2 = bf16[160,640]{1,0:T(8,128)(2,1)S(1)} collective-permute-done((bf16[160,640]{1,0:T(8,128)(2,1)S(1)}, bf16[160,640]{1,0:T(8,128)(2,1)S(1)}, u32[]{:S(2)}, u32[]{:S(2)}) %collective-permute-start.8) | collective-permute-done | bytes 204832 | tf_op jit(solution)/shard_map/ppermute | solution.py:601
  154.6 5.3 %all-to-all-start.2 = ((bf16[8,13,16,128]{3,2,1,0:T(8,128)(2,1)}), bf16[8,13,16,128]{3,2,1,0:T(8,128)(2,1)S(1)}, u32[]{:S(2)}, u32[]{:S(2)}) async-start(bf16[8,13,16,128]{3,2,1,0:T(8,128)(2,1)} %fold.1), calls=%async_computation.3 | async-start | bytes 851968 | tf_op jit(solution)/shard_map/all_to_all | solution.py:236
  160.5 7.0 %within.3 = (f32[256,1280]{1,0:T(8,128)}, f32[40,256]{1,0:T(8,128)}, f32[256,128]{1,0:T(8,128)}, f32[256,128]{1,0:T(8,128)}) custom-call(f32[256,2560]{1,0:T(8,128)} %bitcast.54, bf16[256,2560]{1,0:T(8,128)(2,1)} %get-tuple-element.83.gy_ref, f32[40,256]{1,0:T(8,128)} %get-tuple-element.59.cum_ref, f32[256,40]{1,0:T(8,128)} %get-tuple-element.60.cum_t_ref, ...), custom_call_target="tpu_custom_call" | custom-call | bytes 21000000 | tf_op jit(solution)/shard_map/within/pallas_call | solution.py:387
  174.9 4.8 %all-to-all-start.4 = ((bf16[8,13,16,128]{3,2,1,0:T(8,128)(2,1)}), bf16[8,13,16,128]{3,2,1,0:T(8,128)(2,1)S(1)}, u32[]{:S(2)}, u32[]{:S(2)}) async-start(bf16[8,13,16,128]{3,2,1,0:T(8,128)(2,1)} %get-tuple-element.95), calls=%async_computation.5 | async-start | bytes 851968 | tf_op jit(solution)/shard_map/all_to_all | solution.py:236
  179.7 5.9 %collective-permute-start.15 = (f32[1,128]{1,0:T(1,128)}, f32[1,128]{1,0:T(1,128)S(1)}, u32[]{:S(2)}, u32[]{:S(2)}) collective-permute-start(f32[1,128]{1,0:T(1,128)} %get-tuple-element.96), channel_id=1, source_target_pairs={{0,48},{16,32},{32,16},{48,0},{64,112},{80,96},{96,80},{112,64},{1... | collective-permute-start | bytes 1544 | tf_op jit(solution)/shard_map/ppermute | solution.py:636
  186.7 3.3 %collective-permute-done.14 = f32[1,128]{1,0:T(1,128)S(1)} collective-permute-done((f32[1,128]{1,0:T(1,128)}, f32[1,128]{1,0:T(1,128)S(1)}, u32[]{:S(2)}, u32[]{:S(2)}) %collective-permute-start.14) | collective-permute-done | bytes 544 | tf_op jit(solution)/shard_map/ppermute | solution.py:636
  196.4 10.3 %all-to-all-start.5 = ((bf16[16,160,128]{2,1,0:T(8,128)(2,1)}), bf16[16,160,128]{2,1,0:T(8,128)(2,1)S(1)}, u32[]{:S(2)}, u32[]{:S(2)}) async-start(bf16[16,160,128]{2,1,0:T(8,128)(2,1)} %chain.3), calls=%async_computation.6 | async-start | bytes 1310720 | tf_op jit(solution)/shard_map/all_to_all | solution.py:236
  209.0 14.6 %collective-permute-done.22 = f32[1,128]{1,0:T(1,128)S(1)} collective-permute-done((f32[1,128]{1,0:T(1,128)S(1)}, f32[1,128]{1,0:T(1,128)S(1)}, u32[]{:S(2)}, u32[]{:S(2)}) %collective-permute-start.22) | collective-permute-done | bytes 544 | tf_op jit(solution)/shard_map/ppermute | solution.py:636
  229.4 2.8 %collective-permute-done.24 = f32[1,128]{1,0:T(1,128)S(1)} collective-permute-done((f32[1,128]{1,0:T(1,128)S(1)}, f32[1,128]{1,0:T(1,128)S(1)}, u32[]{:S(2)}, u32[]{:S(2)}) %collective-permute-start.24) | collective-permute-done | bytes 544 | tf_op jit(solution)/shard_map/ppermute | solution.py:636
  238.1 8.5 %across.1 = (f32[256,2560]{1,0:T(8,128)}, f32[40,256]{1,0:T(8,128)}, f32[256,128]{1,0:T(8,128)}, f32[256,128]{1,0:T(8,128)}) custom-call(f32[256,2560]{1,0:T(8,128)} %bitcast.55, bf16[256,2560]{1,0:T(8,128)(2,1)} %get-tuple-element.83.gy_ref, bf16[256,2560]{1,0:T(8,128)(2,1)} %get-tuple-element.62.grow_ref, bf16[256,2560]{1,0:T(8,128)(2,1)} %get-tuple-element.84.tail_ref, ...), custom_call_target="tpu_custom_call" | custom-call | bytes 24000000 | tf_op jit(solution)/shard_map/across/pallas_call | solution.py:462
  (111 shorter events, 67.7 us)
Async XLA Ops:
  8.0 88.1 %all-gather.2.cloned.1.call-start = ((), (), s32[]{:S(2)}) async-start(), calls=%async_computation.7 | async-start | bytes 6963200 | tf_op jit(solution)/shard_map/all_gather | solution.py:665
  14.7 31.3 %all-to-all-start = ((bf16[16,176,128]{2,1,0:T(8,128)(2,1)}), bf16[16,176,128]{2,1,0:T(8,128)(2,1)S(1)}, u32[]{:S(2)}, u32[]{:S(2)}) async-start(bf16[16,176,128]{2,1,0:T(8,128)(2,1)} %get-tuple-element.64), calls=%async_computation | async-start | bytes 1441792 | tf_op jit(solution)/shard_map/all_to_all | solution.py:236
  49.5 23.2 %all-to-all-start.1 = ((bf16[16,160,128]{2,1,0:T(8,128)(2,1)}), bf16[16,160,128]{2,1,0:T(8,128)(2,1)S(1)}, u32[]{:S(2)}, u32[]{:S(2)}) async-start(bf16[16,160,128]{2,1,0:T(8,128)(2,1)} %chain.2), calls=%async_computation.1 | async-start | bytes 1310720 | tf_op jit(solution)/shard_map/all_to_all | solution.py:236
  53.0 81.8 %reduce-scatter.2.cloned.1.call-start = ((), (), s32[]{:S(2)}) async-start(), calls=%async_computation.8 | async-start | bytes 4096000 | tf_op jit(solution)/shard_map/reduce_scatter | solution.py:673
  93.3 11.5 %collective-permute-start.3 = (bf16[2,160,640]{2,1,0:T(8,128)(2,1)S(1)}, bf16[2,160,640]{2,1,0:T(8,128)(2,1)S(1)}, u32[]{:S(2)}, u32[]{:S(2)}) collective-permute-start(bf16[2,160,640]{2,1,0:T(8,128)(2,1)S(1)} %get-tuple-element.114), channel_id=1, source_target_pairs={{0,192},{64,0},{128,64},{192,128},{1,193},{65,1},{129,65},{193,129... | collective-permute-start | bytes 1228808 | tf_op jit(solution)/shard_map/ppermute | solution.py:601
  96.1 11.9 %collective-permute-start.2 = (bf16[2,160,640]{2,1,0:T(8,128)(2,1)S(1)}, bf16[2,160,640]{2,1,0:T(8,128)(2,1)S(1)}, u32[]{:S(2)}, u32[]{:S(2)}) collective-permute-start(bf16[2,160,640]{2,1,0:T(8,128)(2,1)S(1)} %get-tuple-element.115), channel_id=1, source_target_pairs={{0,64},{64,128},{128,192},{192,0},{1,65},{65,129},{129,193},{193,1... | collective-permute-start | bytes 1228808 | tf_op jit(solution)/shard_map/ppermute | solution.py:601
  112.0 20.8 %collective-permute-start.5 = (bf16[4,160,640]{2,1,0:T(8,128)(2,1)S(1)}, bf16[4,160,640]{2,1,0:T(8,128)(2,1)}, u32[]{:S(2)}, u32[]{:S(2)}) collective-permute-start(bf16[4,160,640]{2,1,0:T(8,128)(2,1)S(1)} %get-tuple-element.78), channel_id=1, source_target_pairs={{0,64},{64,128},{128,192},{192,0},{1,65},{65,129},{129,193},{193,1... | collective-permute-start | bytes 2457608 | tf_op jit(solution)/shard_map/ppermute | solution.py:601
  112.1 20.8 %collective-permute-start.6 = (bf16[4,160,640]{2,1,0:T(8,128)(2,1)S(1)}, bf16[4,160,640]{2,1,0:T(8,128)(2,1)}, u32[]{:S(2)}, u32[]{:S(2)}) collective-permute-start(bf16[4,160,640]{2,1,0:T(8,128)(2,1)S(1)} %get-tuple-element.79), channel_id=1, source_target_pairs={{0,192},{64,0},{128,64},{192,128},{1,193},{65,1},{129,65},{193,129... | collective-permute-start | bytes 2457608 | tf_op jit(solution)/shard_map/ppermute | solution.py:601
  120.7 33.9 %all-to-all-start.3 = ((bf16[16,176,128]{2,1,0:T(8,128)(2,1)}), bf16[16,176,128]{2,1,0:T(8,128)(2,1)S(1)}, u32[]{:S(2)}, u32[]{:S(2)}) async-start(bf16[16,176,128]{2,1,0:T(8,128)(2,1)} %get-tuple-element.92), calls=%async_computation.4 | async-start | bytes 1441792 | tf_op jit(solution)/shard_map/all_to_all | solution.py:236
  136.8 7.3 %collective-permute-start.9 = (bf16[160,640]{1,0:T(8,128)(2,1)S(1)}, bf16[160,640]{1,0:T(8,128)(2,1)S(1)}, u32[]{:S(2)}, u32[]{:S(2)}) collective-permute-start(bf16[160,640]{1,0:T(8,128)(2,1)S(1)} %get-tuple-element.124), channel_id=1, source_target_pairs={{0,128},{64,192},{128,0},{192,64},{1,129},{65,193},{129,1},{193,65... | collective-permute-start | bytes 614408 | tf_op jit(solution)/shard_map/ppermute | solution.py:601
  138.0 10.0 %collective-permute-start.8 = (bf16[160,640]{1,0:T(8,128)(2,1)S(1)}, bf16[160,640]{1,0:T(8,128)(2,1)S(1)}, u32[]{:S(2)}, u32[]{:S(2)}) collective-permute-start(bf16[160,640]{1,0:T(8,128)(2,1)S(1)} %get-tuple-element.125), channel_id=1, source_target_pairs={{0,192},{64,0},{128,64},{192,128},{1,193},{65,1},{129,65},{193,129... | collective-permute-start | bytes 614408 | tf_op jit(solution)/shard_map/ppermute | solution.py:601
  139.1 9.7 %collective-permute-start.7 = (bf16[160,640]{1,0:T(8,128)(2,1)S(1)}, bf16[160,640]{1,0:T(8,128)(2,1)S(1)}, u32[]{:S(2)}, u32[]{:S(2)}) collective-permute-start(bf16[160,640]{1,0:T(8,128)(2,1)S(1)} %get-tuple-element.126), channel_id=1, source_target_pairs={{0,64},{64,128},{128,192},{192,0},{1,65},{65,129},{129,193},{193,1... | collective-permute-start | bytes 614408 | tf_op jit(solution)/shard_map/ppermute | solution.py:601
  140.5 8.4 %collective-permute-start.12 = (bf16[160,640]{1,0:T(8,128)(2,1)S(1)}, bf16[160,640]{1,0:T(8,128)(2,1)S(1)}, u32[]{:S(2)}, u32[]{:S(2)}) collective-permute-start(bf16[160,640]{1,0:T(8,128)(2,1)S(1)} %get-tuple-element.120), channel_id=1, source_target_pairs={{0,32},{16,48},{32,0},{48,16},{1,33},{17,49},{33,1},{49,17},{2,34}... | collective-permute-start | bytes 614408 | tf_op jit(solution)/shard_map/ppermute | solution.py:601
  143.2 8.2 %collective-permute-start.11 = (bf16[160,640]{1,0:T(8,128)(2,1)S(1)}, bf16[160,640]{1,0:T(8,128)(2,1)S(1)}, u32[]{:S(2)}, u32[]{:S(2)}) collective-permute-start(bf16[160,640]{1,0:T(8,128)(2,1)S(1)} %get-tuple-element.121), channel_id=1, source_target_pairs={{0,48},{16,0},{32,16},{48,32},{1,49},{17,1},{33,17},{49,33},{2,50}... | collective-permute-start | bytes 614408 | tf_op jit(solution)/shard_map/ppermute | solution.py:601
  144.1 7.3 %collective-permute-start.10 = (bf16[160,640]{1,0:T(8,128)(2,1)S(1)}, bf16[160,640]{1,0:T(8,128)(2,1)S(1)}, u32[]{:S(2)}, u32[]{:S(2)}) collective-permute-start(bf16[160,640]{1,0:T(8,128)(2,1)S(1)} %get-tuple-element.122), channel_id=1, source_target_pairs={{0,16},{16,32},{32,48},{48,0},{1,17},{17,33},{33,49},{49,1},{2,18}... | collective-permute-start | bytes 614408 | tf_op jit(solution)/shard_map/ppermute | solution.py:601
  154.6 17.4 %all-to-all-start.2 = ((bf16[8,13,16,128]{3,2,1,0:T(8,128)(2,1)}), bf16[8,13,16,128]{3,2,1,0:T(8,128)(2,1)S(1)}, u32[]{:S(2)}, u32[]{:S(2)}) async-start(bf16[8,13,16,128]{3,2,1,0:T(8,128)(2,1)} %fold.1), calls=%async_computation.3 | async-start | bytes 851968 | tf_op jit(solution)/shard_map/all_to_all | solution.py:236
  174.9 21.5 %all-to-all-start.4 = ((bf16[8,13,16,128]{3,2,1,0:T(8,128)(2,1)}), bf16[8,13,16,128]{3,2,1,0:T(8,128)(2,1)S(1)}, u32[]{:S(2)}, u32[]{:S(2)}) async-start(bf16[8,13,16,128]{3,2,1,0:T(8,128)(2,1)} %get-tuple-element.95), calls=%async_computation.5 | async-start | bytes 851968 | tf_op jit(solution)/shard_map/all_to_all | solution.py:236
  179.7 7.0 %collective-permute-start.15 = (f32[1,128]{1,0:T(1,128)}, f32[1,128]{1,0:T(1,128)S(1)}, u32[]{:S(2)}, u32[]{:S(2)}) collective-permute-start(f32[1,128]{1,0:T(1,128)} %get-tuple-element.96), channel_id=1, source_target_pairs={{0,48},{16,32},{32,16},{48,0},{64,112},{80,96},{96,80},{112,64},{1... | collective-permute-start | bytes 1544 | tf_op jit(solution)/shard_map/ppermute | solution.py:636
  196.4 40.8 %all-to-all-start.5 = ((bf16[16,160,128]{2,1,0:T(8,128)(2,1)}), bf16[16,160,128]{2,1,0:T(8,128)(2,1)S(1)}, u32[]{:S(2)}, u32[]{:S(2)}) async-start(bf16[16,160,128]{2,1,0:T(8,128)(2,1)} %chain.3), calls=%async_computation.6 | async-start | bytes 1310720 | tf_op jit(solution)/shard_map/all_to_all | solution.py:236
  206.7 16.9 %collective-permute-start.22 = (f32[1,128]{1,0:T(1,128)S(1)}, f32[1,128]{1,0:T(1,128)S(1)}, u32[]{:S(2)}, u32[]{:S(2)}) collective-permute-start(f32[1,128]{1,0:T(1,128)S(1)} %add_add_fusion.2), channel_id=1, source_target_pairs={{0,3},{1,2},{2,1},{3,0},{4,7},{5,6},{6,5},{7,4},{8,11},{9,10},{10,... | collective-permute-start | bytes 1544 | tf_op jit(solution)/shard_map/ppermute | solution.py:636
  208.3 15.3 %collective-permute-start.21 = (f32[1,128]{1,0:T(1,128)S(1)}, f32[1,128]{1,0:T(1,128)S(1)}, u32[]{:S(2)}, u32[]{:S(2)}) collective-permute-start(f32[1,128]{1,0:T(1,128)S(1)} %add_add_fusion.2), channel_id=1, source_target_pairs={{0,2},{1,3},{2,0},{3,1},{4,6},{5,7},{6,4},{7,5},{8,10},{9,11},{10,... | collective-permute-start | bytes 1544 | tf_op jit(solution)/shard_map/ppermute | solution.py:636
  208.5 15.2 %collective-permute-start.20 = (f32[1,128]{1,0:T(1,128)S(1)}, f32[1,128]{1,0:T(1,128)S(1)}, u32[]{:S(2)}, u32[]{:S(2)}) collective-permute-start(f32[1,128]{1,0:T(1,128)S(1)} %add_add_fusion.2), channel_id=1, source_target_pairs={{0,1},{1,0},{2,3},{3,2},{4,5},{5,4},{6,7},{7,6},{8,9},{9,8},{10,11... | collective-permute-start | bytes 1544 | tf_op jit(solution)/shard_map/ppermute | solution.py:636
  208.9 23.9 %collective-permute-start.19 = (bf16[8,13,16,128]{3,2,1,0:T(8,128)(2,1)S(1)}, bf16[8,13,16,128]{3,2,1,0:T(8,128)(2,1)S(1)}, u32[]{:S(2)}, u32[]{:S(2)}) collective-permute-start(bf16[8,13,16,128]{3,2,1,0:T(8,128)(2,1)S(1)} %all-to-all-done.4.own_ref), channel_id=1, source_target_pairs={{0,1},{1,0},{2,3},{3,2},{4,5},{5,4},{6,7},{7,6},{8,9},{9,8},{10,11... | collective-permute-start | bytes 1277960 | tf_op jit(solution)/shard_map/ppermute | solution.py:630
  225.9 6.3 %collective-permute-start.24 = (f32[1,128]{1,0:T(1,128)S(1)}, f32[1,128]{1,0:T(1,128)S(1)}, u32[]{:S(2)}, u32[]{:S(2)}) collective-permute-start(f32[1,128]{1,0:T(1,128)S(1)} %add_add_fusion.1), channel_id=1, source_target_pairs={{0,8},{1,9},{2,10},{3,11},{4,12},{5,13},{6,14},{7,15},{8,0},{9,1},... | collective-permute-start | bytes 1544 | tf_op jit(solution)/shard_map/ppermute | solution.py:636
  (27 other events, 145.3 us)
Sparse Core Ops, SparseCore 0:
  14.8 71.2 all-gather.1
Sparse Core Ops, SparseCore 1:
  91.9 38.5 reduce-scatter.1

commit v9 on v8

--- a/solution.py
+++ b/solution.py
@@ -576,7 +576,7 @@
         factor = jnp.minimum(1.0, bound / jnp.sqrt(sumsq + 1e-06))
         w_factor += jnp.where(groups == float(g), factor, 0.0)
         d_factor += jnp.where(here, factor, 0.0)
-    d_ref[...] = grad_d * d_factor
+    d_ref[...] = (grad_d * d_factor)[:, :H]
     for r in range(10):
         scale = w_factor[16 * r : 16 * r + 16, :]
         for ref, core in ((own_ref, core_ref[0]), (other_ref, 1 - core_ref[0])):
@@ -590,7 +590,7 @@
         functools.partial(clip_kernel, tokens_all),
         in_specs=[smem(), smem()] + [vmem()] * 4,
         out_specs=[vmem(), vmem()],
-        out_shape=[jax.ShapeDtypeStruct((OWN, D), F32), jax.ShapeDtypeStruct((1, N), F32)],
+        out_shape=[jax.ShapeDtypeStruct((OWN, D), F32), jax.ShapeDtypeStruct((1, H), F32)],
         compiler_params=params(),
         cost_estimate=cost(3),
         name="clip",
@@ -665,6 +665,7 @@
     w_half = lax.all_gather(w_mine, ("y", "x"), axis=0, tiled=True)
     got = swap(sent, SEQ)
     y_part, grow = intra(x, cum, cum_t, b, c, d_skip)
+    y_part, g_both, at = tie(y_part, g_both, at)
     start = swap(chain(got, got, mine, False), SEQ).reshape(H * P_SIZE, N)
     y_own = inter(y_part, grow, c, start)
     y_other = other_core(y_own)
@@ -686,24 +687,24 @@
     first, second, gx1 = tie(first, second, gx1)
     first = direct(first.reshape(4, OWN, half // 2), "y")
     second = direct(second, "x")
-    tiles = fold(first + second)
-    gy, mine, tiles = tie(gy, mine, tiles)
+    states = chain(got_back, got, mine, True)
+    last = swap(states, SEQ).reshape(H * P_SIZE, N)
+    parts, states = tie(first + second, states)
+    tiles = fold(parts)
+    gy, last, tiles = tie(gy, last, tiles)
     tiles = swap(tiles, "z")
-    states = chain(got_back, got, mine, True)
     gx2, *sums = within(steps, steps, x, gy, cum, cum_t, b, c, d_skip, sums)
-    tiles, gx2, states = tie(tiles, gx2, states)
+    gx, ga, gb, gc = across(x, gy, grow, tail, gx1, gx2, cum, b, c, start, last, *sums)
+    tiles, ga = tie(tiles, ga)
     tiles, note = zsum(row0, at_z, ids, tiles, got_back)
     tiles = swap(tiles, "z")
     note = sum_over(note, ("y", "x"))
-    tiles, note, states = tie(tiles, note, states)
-    last = swap(states, SEQ).reshape(H * P_SIZE, N)
+    tiles, note = tie(tiles, note)
+    note = sum_over(note, SEQ)
     tiles_other = other_core(tiles)
-    note = sum_over(note, SEQ)
     core = core.reshape(1).astype(jnp.int32)
     clipped_w, clipped_d = clip(tokens_all, row0, core, ids, tiles, tiles_other, note)
-    clipped_w, last = tie(clipped_w, last)
-    gx, ga, gb, gc = across(x, gy, grow, tail, gx1, gx2, cum, b, c, start, last, *sums)
-    return (gx[None], ga[None], gb[None], gc[None], clipped_w, clipped_d[0, :H])
+    return (gx[None], ga[None], gb[None], gc[None], clipped_w, clipped_d[0])
 
 
 def solution(mesh):

time: 256 us -> 255 us (level)
  starting transfers between devices: 70.9 us -> 64.3 us
  waiting for transfers between devices: 71.9 us -> 75.1 us
    all_to_all x6, waiting for transfers between devices: 33.4 us -> 47.6 us  [swap(): return lax.all_to_all(v, axis, 0, 0, tiled=True)]
    ppermute x12, waiting for transfers between devices: 23.6 us -> 11.4 us  [sum_over(): lax.ppermute(v, axes, [(i, i ^ unit * k) for i in range(16)])]
    all_to_all x6, starting transfers between devices: 38.3 us -> 31.9 us  [swap(): return lax.all_to_all(v, axis, 0, 0, tiled=True)]
    unnamed x34 -> x36, local copies, waits for them, and re-layouts: 4.87 us -> 6.87 us
  transfers between devices with their start and end apart: 34 -> 34, of which waited for: 17 -> 19; matrix products, arithmetic and copies ran while one was open for 5% -> 5% of each run, Pallas kernels for 24% -> 27%
where the time goes in v9:
time: 255 us; the launch traced here: 253 us
  Pallas kernels  77.6 us (30%)
  waiting for transfers between devices  75.1 us (29%)
  starting transfers between devices  64.3 us (25%)
  between operations  15.7 us (6%)
  local copies, waits for them, and re-layouts  13.4 us (5%)
  other arithmetic  7.36 us (3%)
    all_to_all x6, waiting for transfers between devices, swap(): return lax.all_to_all(v, axis, 0, 0, tiled=True)  47.6 us
    all_to_all x6, starting transfers between devices, swap(): return lax.all_to_all(v, axis, 0, 0, tiled=True)  31.9 us
    ppermute x12, starting transfers between devices, sum_over(): lax.ppermute(v, axes, [(i, i ^ unit * k) for i in range(16)])  19.3 us
    pallas_call x2, Pallas kernels, within(): pl.pallas_call(functools.partial(within_kernel, first, steps), grid=(step...  13.9 us
    ppermute x10, waiting for transfers between devices, shifted(): return lax.ppermute(v, axis, [(i, (i + d) % 4) for i in range(4)])  12.3 us
    ppermute x10, starting transfers between devices, shifted(): return lax.ppermute(v, axis, [(i, (i + d) % 4) for i in range(4)])  11.8 us
    ppermute x12, waiting for transfers between devices, sum_over(): lax.ppermute(v, axes, [(i, i ^ unit * k) for i in range(16)])  11.4 us
    pallas_call x1, Pallas kernels, intra(): pl.pallas_call(intra_kernel, grid=(PAIRS // STEP,), in_specs=[wide(T, STE...  9.31 us
  transfers between devices with their start and end apart: 34, of which 19 were waited for; matrix products, arithmetic and copies ran while one was open for 5% of the time, Pallas kernels for 27%

profile of v9, /device:TPU:1, one launch (start us, length us, event | category | flops | bytes accessed | tf_op | source)
XLA Modules:
  0.0 253.4 jit_solution(8621551196514772558)
XLA Ops:
  8.1 5.8 %ends.1 = (f32[40,256]{1,0:T(8,128)}, f32[256,40]{1,0:T(8,128)}, bf16[256,2560]{1,0:T(8,128)(2,1)}, bf16[16,176,128]{2,1,0:T(8,128)(2,1)}) custom-call(f32[256,2560]{1,0:T(8,128)} %bitcast.49, f32[40,256]{1,0:T(8,128)} %bitcast.70, f32[256,128]{1,0:T(8,128)} %bitcast.63), custom_call_target="tpu_custom_call" | custom-call | bytes 18000000 | tf_op jit(solution)/shard_map/ends/pallas_call | solution.py:134
  14.7 10.0 %all-to-all-start = ((bf16[16,176,128]{2,1,0:T(8,128)(2,1)}), bf16[16,176,128]{2,1,0:T(8,128)(2,1)S(1)}, u32[]{:S(2)}, u32[]{:S(2)}) async-start(bf16[16,176,128]{2,1,0:T(8,128)(2,1)} %get-tuple-element.73), calls=%async_computation | async-start | bytes 1441792 | tf_op jit(solution)/shard_map/all_to_all | solution.py:236
  24.7 21.3 %all-to-all-done.parts_ref.totals_ref = bf16[16,176,128]{2,1,0:T(8,128)(2,1)S(1)} async-done(((bf16[16,176,128]{2,1,0:T(8,128)(2,1)}), bf16[16,176,128]{2,1,0:T(8,128)(2,1)S(1)}, u32[]{:S(2)}, u32[]{:S(2)}) %all-to-all-start) | async-done | bytes 720928 | tf_op jit(solution)/shard_map/all_to_all | solution.py:236
  49.6 3.5 %all-to-all-start.1 = ((bf16[16,160,128]{2,1,0:T(8,128)(2,1)}), bf16[16,160,128]{2,1,0:T(8,128)(2,1)S(1)}, u32[]{:S(2)}, u32[]{:S(2)}) async-start(bf16[16,160,128]{2,1,0:T(8,128)(2,1)} %chain.2), calls=%async_computation.1 | async-start | bytes 1310720 | tf_op jit(solution)/shard_map/all_to_all | solution.py:236
  54.1 9.3 %intra.1 = (f32[256,2560]{1,0:T(8,128)}, bf16[256,2560]{1,0:T(8,128)(2,1)}) custom-call(f32[256,2560]{1,0:T(8,128)} %bitcast.50, f32[40,256]{1,0:T(8,128)} %get-tuple-element.66.cum_ref, f32[256,40]{1,0:T(8,128)} %get-tuple-element.67.cum_t_ref, f32[256,128]{1,0:T(8,128)} %bitcast.64, f32[256,128]{1,0:T(8,128)} %bitcast.57, f32[40]{0:T(128)} %skip_ref.5), custom_call_target="tpu_custom_call" | custom-call | bytes 27000000 | tf_op jit(solution)/shard_map/intra/pallas_call | solution.py:179
  65.1 7.6 %all-to-all-done.1 = bf16[16,160,128]{2,1,0:T(8,128)(2,1)S(1)} async-done(((bf16[16,160,128]{2,1,0:T(8,128)(2,1)}), bf16[16,160,128]{2,1,0:T(8,128)(2,1)S(1)}, u32[]{:S(2)}, u32[]{:S(2)}) %all-to-all-start.1) | async-done | bytes 655392 | tf_op jit(solution)/shard_map/all_to_all | solution.py:236
  73.6 4.8 %inter.1.yo_ref = bf16[256,2560]{1,0:T(8,128)(2,1)} custom-call(f32[256,2560]{1,0:T(8,128)} %get-tuple-element.70.part_ref, bf16[256,2560]{1,0:T(8,128)(2,1)} %get-tuple-element.71.grow_ref, f32[256,128]{1,0:T(8,128)} %bitcast.58, bf16[2560,128]{1,0:T(8,128)(2,1)} %bitcast.55), custom_call_target="tpu_custom_call" | custom-call | bytes 15000000 | tf_op jit(solution)/shard_map/inter/pallas_call | solution.py:200
  78.4 3.2 %collective-permute-done.1.yx_ref = bf16[256,2560]{1,0:T(8,128)(2,1)S(1)} collective-permute-done((bf16[256,2560]{1,0:T(8,128)(2,1)}, bf16[256,2560]{1,0:T(8,128)(2,1)S(1)}, u32[]{:S(2)}, u32[]{:S(2)}) %collective-permute-start.1) | collective-permute-done | bytes 1310752 | tf_op jit(solution)/shard_map/ppermute | solution.py:630
  82.7 8.3 %terms.1 = (bf16[4,4,160,640]{3,2,1,0:T(8,128)(2,1)}, bf16[4,4,160,640]{3,2,1,0:T(8,128)(2,1)}) custom-call(s32[2]{0:T(128)} %pad_add_fusion.at_ref, bf16[256,2560]{1,0:T(8,128)(2,1)} %inter.1.yo_ref, bf16[256,2560]{1,0:T(8,128)(2,1)} %copy-done.8, bf16[512,1280]{1,0:T(8,128)(2,1)} %pad_maximum_fusion.g_ref), custom_call_target="tpu_custom_call" | custom-call | bytes 24000000 | tf_op jit(solution)/shard_map/terms/pallas_call | solution.py:251
  95.3 8.5 %gy_parts.1 = (f32[256,2560]{1,0:T(8,128)}, bf16[256,2560]{1,0:T(8,128)(2,1)}) custom-call(bf16[512,1280]{1,0:T(8,128)(2,1)} %pad_maximum_fusion.g_ref, bf16[2560,1280]{1,0:T(8,128)(2,1)} %all-gather.2.cloned.1.call-done.w_ref), custom_call_target="tpu_custom_call" | custom-call | bytes 24000000 | tf_op jit(solution)/shard_map/gy_parts/pallas_call | solution.py:277
  104.0 3.2 %collective-permute-done.2 = bf16[2,160,640]{2,1,0:T(8,128)(2,1)S(1)} collective-permute-done((bf16[2,160,640]{2,1,0:T(8,128)(2,1)S(1)}, bf16[2,160,640]{2,1,0:T(8,128)(2,1)S(1)}, u32[]{:S(2)}, u32[]{:S(2)}) %collective-permute-start.2) | collective-permute-done | bytes 409632 | tf_op jit(solution)/shard_map/ppermute | solution.py:601
  112.3 5.9 %entries.1 = (bf16[256,2560]{1,0:T(8,128)(2,1)}, bf16[16,176,128]{2,1,0:T(8,128)(2,1)}) custom-call(f32[256,2560]{1,0:T(8,128)} %get-tuple-element.84.own_ref, bf16[256,2560]{1,0:T(8,128)(2,1)} %copy-done.9, f32[256,2560]{1,0:T(8,128)} %bitcast.51, bf16[256,2560]{1,0:T(8,128)(2,1)} %get-tuple-element.71.grow_ref, f32[256,128]{1,0:T(8,128)} %bitcast.59), custom_call_target="tpu_custom_call" | custom-call | bytes 18000000 | tf_op jit(solution)/shard_map/entries/pallas_call | solution.py:317
  118.2 3.8 %all-to-all-start.2 = ((bf16[16,176,128]{2,1,0:T(8,128)(2,1)}), bf16[16,176,128]{2,1,0:T(8,128)(2,1)S(1)}, u32[]{:S(2)}, u32[]{:S(2)}) async-start(bf16[16,176,128]{2,1,0:T(8,128)(2,1)} %get-tuple-element.87), calls=%async_computation.2 | async-start | bytes 1441792 | tf_op jit(solution)/shard_map/all_to_all | solution.py:236
  124.7 18.7 %all-to-all-done.2.parts_ref.got_ref = bf16[16,176,128]{2,1,0:T(8,128)(2,1)S(1)} async-done(((bf16[16,176,128]{2,1,0:T(8,128)(2,1)}), bf16[16,176,128]{2,1,0:T(8,128)(2,1)S(1)}, u32[]{:S(2)}, u32[]{:S(2)}) %all-to-all-start.2) | async-done | bytes 720928 | tf_op jit(solution)/shard_map/all_to_all | solution.py:236
  146.9 3.7 %all-to-all-start.3 = ((bf16[16,160,128]{2,1,0:T(8,128)(2,1)}), bf16[16,160,128]{2,1,0:T(8,128)(2,1)S(1)}, u32[]{:S(2)}, u32[]{:S(2)}) async-start(bf16[16,160,128]{2,1,0:T(8,128)(2,1)} %chain.3), calls=%async_computation.3 | async-start | bytes 1310720 | tf_op jit(solution)/shard_map/all_to_all | solution.py:236
  150.6 6.9 %within.2 = (f32[256,1280]{1,0:T(8,128)}, f32[40,256]{1,0:T(8,128)}, f32[256,128]{1,0:T(8,128)}, f32[256,128]{1,0:T(8,128)}) custom-call(f32[256,2560]{1,0:T(8,128)} %bitcast.52, bf16[256,2560]{1,0:T(8,128)(2,1)} %get-tuple-element.102.gy_ref, f32[40,256]{1,0:T(8,128)} %get-tuple-element.66.cum_ref, f32[256,40]{1,0:T(8,128)} %get-tuple-element.67.cum_t_ref, ...), custom_call_target="tpu_custom_call" | custom-call | bytes 21000000 | tf_op jit(solution)/shard_map/within/pallas_call | solution.py:387
  180.6 4.3 %all-to-all-start.4 = ((bf16[8,13,16,128]{3,2,1,0:T(8,128)(2,1)}), bf16[8,13,16,128]{3,2,1,0:T(8,128)(2,1)S(1)}, u32[]{:S(2)}, u32[]{:S(2)}) async-start(bf16[8,13,16,128]{3,2,1,0:T(8,128)(2,1)} %fold.1), calls=%async_computation.5 | async-start | bytes 851968 | tf_op jit(solution)/shard_map/all_to_all | solution.py:236
  185.4 7.0 %within.3 = (f32[256,1280]{1,0:T(8,128)}, f32[40,256]{1,0:T(8,128)}, f32[256,128]{1,0:T(8,128)}, f32[256,128]{1,0:T(8,128)}) custom-call(f32[256,2560]{1,0:T(8,128)} %bitcast.53, bf16[256,2560]{1,0:T(8,128)(2,1)} %get-tuple-element.102.gy_ref, f32[40,256]{1,0:T(8,128)} %get-tuple-element.66.cum_ref, f32[256,40]{1,0:T(8,128)} %get-tuple-element.67.cum_t_ref, ...), custom_call_target="tpu_custom_call" | custom-call | bytes 21000000 | tf_op jit(solution)/shard_map/within/pallas_call | solution.py:387
  192.4 8.6 %across.1 = (f32[256,2560]{1,0:T(8,128)}, f32[40,256]{1,0:T(8,128)}, f32[256,128]{1,0:T(8,128)}, f32[256,128]{1,0:T(8,128)}) custom-call(f32[256,2560]{1,0:T(8,128)} %bitcast.54, bf16[256,2560]{1,0:T(8,128)(2,1)} %get-tuple-element.102.gy_ref, bf16[256,2560]{1,0:T(8,128)(2,1)} %get-tuple-element.71.grow_ref, bf16[256,2560]{1,0:T(8,128)(2,1)} %get-tuple-element.103.tail_ref, ...), custom_call_target="tpu_custom_call" | custom-call | bytes 24000000 | tf_op jit(solution)/shard_map/across/pallas_call | solution.py:462
  204.0 6.6 %all-to-all-start.5 = ((bf16[8,13,16,128]{3,2,1,0:T(8,128)(2,1)}), bf16[8,13,16,128]{3,2,1,0:T(8,128)(2,1)S(1)}, u32[]{:S(2)}, u32[]{:S(2)}) async-start(bf16[8,13,16,128]{3,2,1,0:T(8,128)(2,1)} %get-tuple-element.120), calls=%async_computation.6 | async-start | bytes 851968 | tf_op jit(solution)/shard_map/all_to_all | solution.py:236
  210.6 3.4 %collective-permute-start.15 = (f32[1,128]{1,0:T(1,128)}, f32[1,128]{1,0:T(1,128)S(1)}, u32[]{:S(2)}, u32[]{:S(2)}) collective-permute-start(f32[1,128]{1,0:T(1,128)} %get-tuple-element.121), channel_id=1, source_target_pairs={{0,48},{16,32},{32,16},{48,0},{64,112},{80,96},{96,80},{112,64},{1... | collective-permute-start | bytes 1544 | tf_op jit(solution)/shard_map/ppermute | solution.py:636
  225.1 5.8 %collective-permute-start.22 = (f32[1,128]{1,0:T(1,128)S(1)}, f32[1,128]{1,0:T(1,128)S(1)}, u32[]{:S(2)}, u32[]{:S(2)}) collective-permute-start(f32[1,128]{1,0:T(1,128)S(1)} %add_add_fusion.2), channel_id=1, source_target_pairs={{0,3},{1,2},{2,1},{3,0},{4,7},{5,6},{6,5},{7,4},{8,11},{9,10},{10,... | collective-permute-start | bytes 1544 | tf_op jit(solution)/shard_map/ppermute | solution.py:636
  235.8 3.0 %collective-permute-start.24 = (f32[1,128]{1,0:T(1,128)S(1)}, f32[1,128]{1,0:T(1,128)S(1)}, u32[]{:S(2)}, u32[]{:S(2)}) collective-permute-start(f32[1,128]{1,0:T(1,128)S(1)} %add_add_fusion.1), channel_id=1, source_target_pairs={{0,8},{1,9},{2,10},{3,11},{4,12},{5,13},{6,14},{7,15},{8,0},{9,1},... | collective-permute-start | bytes 1544 | tf_op jit(solution)/shard_map/ppermute | solution.py:636
  239.0 3.0 %collective-permute-done.24 = f32[1,128]{1,0:T(1,128)S(1)} collective-permute-done((f32[1,128]{1,0:T(1,128)S(1)}, f32[1,128]{1,0:T(1,128)S(1)}, u32[]{:S(2)}, u32[]{:S(2)}) %collective-permute-start.24) | collective-permute-done | bytes 544 | tf_op jit(solution)/shard_map/ppermute | solution.py:636
  (112 shorter events, 71.4 us)
Async XLA Ops:
  8.0 87.3 %all-gather.2.cloned.1.call-start = ((), (), s32[]{:S(2)}) async-start(), calls=%async_computation.7 | async-start | bytes 6963200 | tf_op jit(solution)/shard_map/all_gather | solution.py:665
  14.7 31.3 %all-to-all-start = ((bf16[16,176,128]{2,1,0:T(8,128)(2,1)}), bf16[16,176,128]{2,1,0:T(8,128)(2,1)S(1)}, u32[]{:S(2)}, u32[]{:S(2)}) async-start(bf16[16,176,128]{2,1,0:T(8,128)(2,1)} %get-tuple-element.73), calls=%async_computation | async-start | bytes 1441792 | tf_op jit(solution)/shard_map/all_to_all | solution.py:236
  49.6 23.2 %all-to-all-start.1 = ((bf16[16,160,128]{2,1,0:T(8,128)(2,1)}), bf16[16,160,128]{2,1,0:T(8,128)(2,1)S(1)}, u32[]{:S(2)}, u32[]{:S(2)}) async-start(bf16[16,160,128]{2,1,0:T(8,128)(2,1)} %chain.2), calls=%async_computation.1 | async-start | bytes 1310720 | tf_op jit(solution)/shard_map/all_to_all | solution.py:236
  53.1 106.3 %reduce-scatter.2.cloned.1.call-start = ((), (), s32[]{:S(2)}) async-start(), calls=%async_computation.8 | async-start | bytes 4096000 | tf_op jit(solution)/shard_map/reduce_scatter | solution.py:674
  54.1 9.9 %collective-permute-start = (bf16[256,1280]{1,0:T(8,128)(2,1)}, bf16[256,1280]{1,0:T(8,128)(2,1)S(1)}, u32[]{:S(2)}, u32[]{:S(2)}) collective-permute-start(bf16[256,1280]{1,0:T(8,128)(2,1)} %get-tuple-element.133), channel_id=1, source_target_pairs={{0,1},{1,0},{2,3},{3,2},{4,5},{5,4},{6,7},{7,6},{8,9},{9,8},{10,11... | collective-permute-start | bytes 1966088 | tf_op jit(solution)/shard_map/ppermute | solution.py:630
  92.5 11.4 %collective-permute-start.3 = (bf16[2,160,640]{2,1,0:T(8,128)(2,1)S(1)}, bf16[2,160,640]{2,1,0:T(8,128)(2,1)S(1)}, u32[]{:S(2)}, u32[]{:S(2)}) collective-permute-start(bf16[2,160,640]{2,1,0:T(8,128)(2,1)S(1)} %get-tuple-element.128), channel_id=1, source_target_pairs={{0,192},{64,0},{128,64},{192,128},{1,193},{65,1},{129,65},{193,129... | collective-permute-start | bytes 1228808 | tf_op jit(solution)/shard_map/ppermute | solution.py:601
  95.3 11.9 %collective-permute-start.2 = (bf16[2,160,640]{2,1,0:T(8,128)(2,1)S(1)}, bf16[2,160,640]{2,1,0:T(8,128)(2,1)S(1)}, u32[]{:S(2)}, u32[]{:S(2)}) collective-permute-start(bf16[2,160,640]{2,1,0:T(8,128)(2,1)S(1)} %get-tuple-element.129), channel_id=1, source_target_pairs={{0,64},{64,128},{128,192},{192,0},{1,65},{65,129},{129,193},{193,1... | collective-permute-start | bytes 1228808 | tf_op jit(solution)/shard_map/ppermute | solution.py:601
  118.2 25.2 %all-to-all-start.2 = ((bf16[16,176,128]{2,1,0:T(8,128)(2,1)}), bf16[16,176,128]{2,1,0:T(8,128)(2,1)S(1)}, u32[]{:S(2)}, u32[]{:S(2)}) async-start(bf16[16,176,128]{2,1,0:T(8,128)(2,1)} %get-tuple-element.87), calls=%async_computation.2 | async-start | bytes 1441792 | tf_op jit(solution)/shard_map/all_to_all | solution.py:236
  122.0 35.4 %collective-permute-start.5 = (bf16[4,160,640]{2,1,0:T(8,128)(2,1)}, bf16[4,160,640]{2,1,0:T(8,128)(2,1)}, u32[]{:S(2)}, u32[]{:S(2)}) collective-permute-start(bf16[4,160,640]{2,1,0:T(8,128)(2,1)} %get-tuple-element.89), channel_id=1, source_target_pairs={{0,64},{64,128},{128,192},{192,0},{1,65},{65,129},{129,193},{193,1... | collective-permute-start | bytes 2457608 | tf_op jit(solution)/shard_map/ppermute | solution.py:601
  122.0 35.4 %collective-permute-start.6 = (bf16[4,160,640]{2,1,0:T(8,128)(2,1)S(1)}, bf16[4,160,640]{2,1,0:T(8,128)(2,1)}, u32[]{:S(2)}, u32[]{:S(2)}) collective-permute-start(bf16[4,160,640]{2,1,0:T(8,128)(2,1)S(1)} %get-tuple-element.90), channel_id=1, source_target_pairs={{0,192},{64,0},{128,64},{192,128},{1,193},{65,1},{129,65},{193,129... | collective-permute-start | bytes 2457608 | tf_op jit(solution)/shard_map/ppermute | solution.py:601
  146.9 33.7 %all-to-all-start.3 = ((bf16[16,160,128]{2,1,0:T(8,128)(2,1)}), bf16[16,160,128]{2,1,0:T(8,128)(2,1)S(1)}, u32[]{:S(2)}, u32[]{:S(2)}) async-start(bf16[16,160,128]{2,1,0:T(8,128)(2,1)} %chain.3), calls=%async_computation.3 | async-start | bytes 1310720 | tf_op jit(solution)/shard_map/all_to_all | solution.py:236
  161.4 8.6 %collective-permute-start.9 = (bf16[160,640]{1,0:T(8,128)(2,1)S(1)}, bf16[160,640]{1,0:T(8,128)(2,1)S(1)}, u32[]{:S(2)}, u32[]{:S(2)}) collective-permute-start(bf16[160,640]{1,0:T(8,128)(2,1)S(1)} %get-tuple-element.138), channel_id=1, source_target_pairs={{0,128},{64,192},{128,0},{192,64},{1,129},{65,193},{129,1},{193,65... | collective-permute-start | bytes 614408 | tf_op jit(solution)/shard_map/ppermute | solution.py:601
  161.4 10.7 %collective-permute-start.8 = (bf16[160,640]{1,0:T(8,128)(2,1)S(1)}, bf16[160,640]{1,0:T(8,128)(2,1)S(1)}, u32[]{:S(2)}, u32[]{:S(2)}) collective-permute-start(bf16[160,640]{1,0:T(8,128)(2,1)S(1)} %get-tuple-element.139), channel_id=1, source_target_pairs={{0,192},{64,0},{128,64},{192,128},{1,193},{65,1},{129,65},{193,129... | collective-permute-start | bytes 614408 | tf_op jit(solution)/shard_map/ppermute | solution.py:601
  162.6 11.7 %collective-permute-start.7 = (bf16[160,640]{1,0:T(8,128)(2,1)S(1)}, bf16[160,640]{1,0:T(8,128)(2,1)S(1)}, u32[]{:S(2)}, u32[]{:S(2)}) collective-permute-start(bf16[160,640]{1,0:T(8,128)(2,1)S(1)} %get-tuple-element.140), channel_id=1, source_target_pairs={{0,64},{64,128},{128,192},{192,0},{1,65},{65,129},{129,193},{193,1... | collective-permute-start | bytes 614408 | tf_op jit(solution)/shard_map/ppermute | solution.py:601
  163.6 10.7 %collective-permute-start.12 = (bf16[160,640]{1,0:T(8,128)(2,1)S(1)}, bf16[160,640]{1,0:T(8,128)(2,1)S(1)}, u32[]{:S(2)}, u32[]{:S(2)}) collective-permute-start(bf16[160,640]{1,0:T(8,128)(2,1)S(1)} %get-tuple-element.134), channel_id=1, source_target_pairs={{0,32},{16,48},{32,0},{48,16},{1,33},{17,49},{33,1},{49,17},{2,34}... | collective-permute-start | bytes 614408 | tf_op jit(solution)/shard_map/ppermute | solution.py:601
  166.5 9.9 %collective-permute-start.11 = (bf16[160,640]{1,0:T(8,128)(2,1)S(1)}, bf16[160,640]{1,0:T(8,128)(2,1)S(1)}, u32[]{:S(2)}, u32[]{:S(2)}) collective-permute-start(bf16[160,640]{1,0:T(8,128)(2,1)S(1)} %get-tuple-element.135), channel_id=1, source_target_pairs={{0,48},{16,0},{32,16},{48,32},{1,49},{17,1},{33,17},{49,33},{2,50}... | collective-permute-start | bytes 614408 | tf_op jit(solution)/shard_map/ppermute | solution.py:601
  170.1 7.4 %collective-permute-start.10 = (bf16[160,640]{1,0:T(8,128)(2,1)S(1)}, bf16[160,640]{1,0:T(8,128)(2,1)S(1)}, u32[]{:S(2)}, u32[]{:S(2)}) collective-permute-start(bf16[160,640]{1,0:T(8,128)(2,1)S(1)} %get-tuple-element.136), channel_id=1, source_target_pairs={{0,16},{16,32},{32,48},{48,0},{1,17},{17,33},{33,49},{49,1},{2,18}... | collective-permute-start | bytes 614408 | tf_op jit(solution)/shard_map/ppermute | solution.py:601
  180.6 20.5 %all-to-all-start.4 = ((bf16[8,13,16,128]{3,2,1,0:T(8,128)(2,1)}), bf16[8,13,16,128]{3,2,1,0:T(8,128)(2,1)S(1)}, u32[]{:S(2)}, u32[]{:S(2)}) async-start(bf16[8,13,16,128]{3,2,1,0:T(8,128)(2,1)} %fold.1), calls=%async_computation.5 | async-start | bytes 851968 | tf_op jit(solution)/shard_map/all_to_all | solution.py:236
  204.0 21.1 %all-to-all-start.5 = ((bf16[8,13,16,128]{3,2,1,0:T(8,128)(2,1)}), bf16[8,13,16,128]{3,2,1,0:T(8,128)(2,1)S(1)}, u32[]{:S(2)}, u32[]{:S(2)}) async-start(bf16[8,13,16,128]{3,2,1,0:T(8,128)(2,1)} %get-tuple-element.120), calls=%async_computation.6 | async-start | bytes 851968 | tf_op jit(solution)/shard_map/all_to_all | solution.py:236
  210.6 4.5 %collective-permute-start.15 = (f32[1,128]{1,0:T(1,128)}, f32[1,128]{1,0:T(1,128)S(1)}, u32[]{:S(2)}, u32[]{:S(2)}) collective-permute-start(f32[1,128]{1,0:T(1,128)} %get-tuple-element.121), channel_id=1, source_target_pairs={{0,48},{16,32},{32,16},{48,0},{64,112},{80,96},{96,80},{112,64},{1... | collective-permute-start | bytes 1544 | tf_op jit(solution)/shard_map/ppermute | solution.py:636
  225.1 7.0 %collective-permute-start.22 = (f32[1,128]{1,0:T(1,128)S(1)}, f32[1,128]{1,0:T(1,128)S(1)}, u32[]{:S(2)}, u32[]{:S(2)}) collective-permute-start(f32[1,128]{1,0:T(1,128)S(1)} %add_add_fusion.2), channel_id=1, source_target_pairs={{0,3},{1,2},{2,1},{3,0},{4,7},{5,6},{6,5},{7,4},{8,11},{9,10},{10,... | collective-permute-start | bytes 1544 | tf_op jit(solution)/shard_map/ppermute | solution.py:636
  231.4 11.3 %collective-permute-start.19 = (bf16[8,13,16,128]{3,2,1,0:T(8,128)(2,1)S(1)}, bf16[8,13,16,128]{3,2,1,0:T(8,128)(2,1)S(1)}, u32[]{:S(2)}, u32[]{:S(2)}) collective-permute-start(bf16[8,13,16,128]{3,2,1,0:T(8,128)(2,1)S(1)} %all-to-all-done.5.own_ref), channel_id=1, source_target_pairs={{0,1},{1,0},{2,3},{3,2},{4,5},{5,4},{6,7},{7,6},{8,9},{9,8},{10,11... | collective-permute-start | bytes 1277960 | tf_op jit(solution)/shard_map/ppermute | solution.py:630
  233.3 5.7 %collective-permute-start.25 = (f32[1,128]{1,0:T(1,128)S(1)}, f32[1,128]{1,0:T(1,128)S(1)}, u32[]{:S(2)}, u32[]{:S(2)}) collective-permute-start(f32[1,128]{1,0:T(1,128)S(1)} %add_add_fusion.1), channel_id=1, source_target_pairs={{0,12},{1,13},{2,14},{3,15},{4,8},{5,9},{6,10},{7,11},{8,4},{9,5},... | collective-permute-start | bytes 1544 | tf_op jit(solution)/shard_map/ppermute | solution.py:636
  235.8 6.3 %collective-permute-start.24 = (f32[1,128]{1,0:T(1,128)S(1)}, f32[1,128]{1,0:T(1,128)S(1)}, u32[]{:S(2)}, u32[]{:S(2)}) collective-permute-start(f32[1,128]{1,0:T(1,128)S(1)} %add_add_fusion.1), channel_id=1, source_target_pairs={{0,8},{1,9},{2,10},{3,11},{4,12},{5,13},{6,14},{7,15},{8,0},{9,1},... | collective-permute-start | bytes 1544 | tf_op jit(solution)/shard_map/ppermute | solution.py:636
  (28 other events, 123.9 us)
Sparse Core Ops, SparseCore 0:
  14.8 71.4 all-gather.1
Sparse Core Ops, SparseCore 1:
  91.1 38.4 reduce-scatter.1

commit v10 on v7

--- a/solution.py
+++ b/solution.py
@@ -524,8 +524,7 @@
     total = parts_ref[0].astype(F32)
     for z in range(1, 8):
         total += parts_ref[z].astype(F32)
-    for s in range(8):
-        out_ref[s] = total.astype(BF)
+    out_ref[...] = total.astype(BF)
     found = jnp.zeros((16, N), F32)
     for i in range(TILES):
         row = row0_ref[0] + 16 * ((z_ref[0] * TILES + i) // 10)
@@ -545,7 +544,7 @@
         in_specs=[smem(), smem()] + [vmem()] * 3,
         out_specs=[vmem(), vmem()],
         out_shape=[
-            jax.ShapeDtypeStruct((8, TILES, 16, 128), BF),
+            jax.ShapeDtypeStruct((TILES, 16, 128), BF),
             jax.ShapeDtypeStruct((1, N), F32),
         ],
         compiler_params=params(),
@@ -554,15 +553,46 @@
     )(row0, z, ids, got, parts)
 
 
+def pack_kernel(tiles_ref, note_ref, out_ref):
+    note = note_ref[...]
+    hi = note.astype(BF).astype(F32)
+    mid = (note - hi).astype(BF).astype(F32)
+    at = iota((16, N), 0)
+    rows = jnp.where(at == 0, hi, jnp.where(at == 1, mid, jnp.where(at == 2, note - hi - mid, 0.0)))
+    for z in range(8):
+        out_ref[z, :TILES] = tiles_ref[...]
+        out_ref[z, TILES] = rows.astype(BF)
+
+
+def pack(tiles, note):
+    return pl.pallas_call(
+        pack_kernel,
+        in_specs=[vmem(), vmem()],
+        out_specs=vmem(),
+        out_shape=jax.ShapeDtypeStruct((8, TILES + 1, 16, 128), BF),
+        compiler_params=params(),
+        cost_estimate=cost(2),
+        name="pack",
+    )(tiles, note)
+
+
+def note_of(ref):
+    total = jnp.zeros((1, N), F32)
+    for z in range(8):
+        rows = ref[z, TILES].astype(F32)
+        total += rows[0:1, :] + rows[1:2, :] + rows[2:3, :]
+    return total
+
+
 def tile_of(ref, r, c):
     z, i = divmod(10 * r + c, TILES)
     return ref[z, i].astype(F32)
 
 
-def clip_kernel(tokens_all, row0_ref, core_ref, ids_ref, own_ref, other_ref, note_ref, w_ref, d_ref):
+def clip_kernel(tokens_all, row0_ref, core_ref, ids_ref, own_ref, other_ref, w_ref, d_ref):
     ids = ids_ref[...]
     lane = iota((1, N), 1)
-    note = note_ref[...]
+    note = note_of(own_ref) + note_of(other_ref)
     grad_d = jnp.where(lane < H, note, 0.0)
     groups = groups_of(row0_ref[0], OWN, ids_ref)
     w_factor = jnp.zeros((OWN, 1), F32)
@@ -576,7 +606,7 @@
         factor = jnp.minimum(1.0, bound / jnp.sqrt(sumsq + 1e-06))
         w_factor += jnp.where(groups == float(g), factor, 0.0)
         d_factor += jnp.where(here, factor, 0.0)
-    d_ref[...] = grad_d * d_factor
+    d_ref[...] = (grad_d * d_factor)[:, :H]
     for r in range(10):
         scale = w_factor[16 * r : 16 * r + 16, :]
         for ref, core in ((own_ref, core_ref[0]), (other_ref, 1 - core_ref[0])):
@@ -585,16 +615,16 @@
                 w_ref[16 * r : 16 * r + 16, pl.ds(col, 128)] = tile_of(ref, r, c) * scale
 
 
-def clip(tokens_all, row0, core, ids, own, other, note):
+def clip(tokens_all, row0, core, ids, own, other):
     return pl.pallas_call(
         functools.partial(clip_kernel, tokens_all),
-        in_specs=[smem(), smem()] + [vmem()] * 4,
+        in_specs=[smem(), smem()] + [vmem()] * 3,
         out_specs=[vmem(), vmem()],
-        out_shape=[jax.ShapeDtypeStruct((OWN, D), F32), jax.ShapeDtypeStruct((1, N), F32)],
+        out_shape=[jax.ShapeDtypeStruct((OWN, D), F32), jax.ShapeDtypeStruct((1, H), F32)],
         compiler_params=params(),
         cost_estimate=cost(3),
         name="clip",
-    )(row0, core, ids, own, other, note)
+    )(row0, core, ids, own, other)
 
 
 def shifted(v, axis, d):
@@ -665,6 +695,7 @@
     w_half = lax.all_gather(w_mine, ("y", "x"), axis=0, tiled=True)
     got = swap(sent, SEQ)
     y_part, grow = intra(x, cum, cum_t, b, c, d_skip)
+    y_part, g_both, at = tie(y_part, g_both, at)
     start = swap(chain(got, got, mine, False), SEQ).reshape(H * P_SIZE, N)
     y_own = inter(y_part, grow, c, start)
     y_other = other_core(y_own)
@@ -695,16 +726,17 @@
     tiles, note = zsum(row0, at_z, ids, tiles, got_back)
     note, states = tie(note, states)
     last = swap(states, SEQ).reshape(H * P_SIZE, N)
+    note = sum_over(note, ("y", "x"))
+    tiles, note, last = tie(tiles, note, last)
+    tiles = pack(tiles, note)
     tiles, last = tie(tiles, last)
     tiles = swap(tiles, "z")
-    note = sum_over(sum_over(note, ("y", "x")), SEQ)
-    last, note = tie(last, note)
     gx, ga, gb, gc = across(x, gy, grow, tail, gx1, gx2, cum, b, c, start, last, *sums)
     tiles, ga = tie(tiles, ga)
     tiles_other = other_core(tiles)
     core = core.reshape(1).astype(jnp.int32)
-    clipped_w, clipped_d = clip(tokens_all, row0, core, ids, tiles, tiles_other, note)
-    return (gx[None], ga[None], gb[None], gc[None], clipped_w, clipped_d[0, :H])
+    clipped_w, clipped_d = clip(tokens_all, row0, core, ids, tiles, tiles_other)
+    return (gx[None], ga[None], gb[None], gc[None], clipped_w, clipped_d[0])
 
 
 def solution(mesh):

time: 253 us -> 238 us (0.941)
  starting transfers between devices: 68 us -> 56.2 us
  waiting for transfers between devices: 73.7 us -> 67.6 us
    ppermute x12 -> x6, starting transfers between devices: 16.1 us -> 6.86 us  [sum_over(): lax.ppermute(v, axes, [(i, i ^ unit * k) for i in range(16)])]
    all_to_all x6, waiting for transfers between devices: 49.9 us -> 44.2 us  [swap(): return lax.all_to_all(v, axis, 0, 0, tiled=True)]
    ppermute x12 -> x6, waiting for transfers between devices: 7.42 us -> 6.48 us  [sum_over(): lax.ppermute(v, axes, [(i, i ^ unit * k) for i in range(16)])]
  transfers between devices with their start and end apart: 34 -> 28, of which waited for: 17 -> 18; matrix products, arithmetic and copies ran while one was open for 4% -> 5% of each run, Pallas kernels for 27% -> 28%
where the time goes in v10:
time: 238 us; the launch traced here: 237 us
  Pallas kernels  79.2 us (33%)
  waiting for transfers between devices  67.6 us (28%)
  starting transfers between devices  56.2 us (24%)
  between operations  15.7 us (7%)
  local copies, waits for them, and re-layouts  11.6 us (5%)
  other arithmetic  6.37 us (3%)
    all_to_all x6, waiting for transfers between devices, swap(): return lax.all_to_all(v, axis, 0, 0, tiled=True)  44.2 us
    all_to_all x6, starting transfers between devices, swap(): return lax.all_to_all(v, axis, 0, 0, tiled=True)  34.8 us
    pallas_call x2, Pallas kernels, within(): pl.pallas_call(functools.partial(within_kernel, first, steps), grid=(step...  13.9 us
    ppermute x10, starting transfers between devices, shifted(): return lax.ppermute(v, axis, [(i, (i + d) % 4) for i in range(4)])  12.8 us
    ppermute x10, waiting for transfers between devices, shifted(): return lax.ppermute(v, axis, [(i, (i + d) % 4) for i in range(4)])  10.8 us
    pallas_call x1, Pallas kernels, intra(): pl.pallas_call(intra_kernel, grid=(PAIRS // STEP,), in_specs=[wide(T, STE...  9.3 us
    pallas_call x1, Pallas kernels, across(): pl.pallas_call(across_kernel, grid=(PAIRS // WIDE,), in_specs=[wide(T, WI...  8.56 us
    pallas_call x1, Pallas kernels, gy_parts(): pl.pallas_call(gy_kernel, grid=(4,), in_specs=[whole(g.shape), pl.BlockSp...  8.46 us
  transfers between devices with their start and end apart: 28, of which 18 were waited for; matrix products, arithmetic and copies ran while one was open for 5% of the time, Pallas kernels for 28%

profile of v10, /device:TPU:1, one launch (start us, length us, event | category | flops | bytes accessed | tf_op | source)
XLA Modules:
  0.0 236.6 jit_solution(9261048933767967493)
XLA Ops:
  8.1 5.8 %ends.1 = (f32[40,256]{1,0:T(8,128)}, f32[256,40]{1,0:T(8,128)}, bf16[256,2560]{1,0:T(8,128)(2,1)}, bf16[16,176,128]{2,1,0:T(8,128)(2,1)}) custom-call(f32[256,2560]{1,0:T(8,128)} %bitcast.49, f32[40,256]{1,0:T(8,128)} %bitcast.70, f32[256,128]{1,0:T(8,128)} %bitcast.63), custom_call_target="tpu_custom_call" | custom-call | bytes 18000000 | tf_op jit(solution)/shard_map/ends/pallas_call | solution.py:134
  14.7 10.0 %all-to-all-start = ((bf16[16,176,128]{2,1,0:T(8,128)(2,1)}), bf16[16,176,128]{2,1,0:T(8,128)(2,1)S(1)}, u32[]{:S(2)}, u32[]{:S(2)}) async-start(bf16[16,176,128]{2,1,0:T(8,128)(2,1)} %get-tuple-element.73), calls=%async_computation | async-start | bytes 1441792 | tf_op jit(solution)/shard_map/all_to_all | solution.py:236
  24.7 21.3 %all-to-all-done.parts_ref.totals_ref = bf16[16,176,128]{2,1,0:T(8,128)(2,1)S(1)} async-done(((bf16[16,176,128]{2,1,0:T(8,128)(2,1)}), bf16[16,176,128]{2,1,0:T(8,128)(2,1)S(1)}, u32[]{:S(2)}, u32[]{:S(2)}) %all-to-all-start) | async-done | bytes 720928 | tf_op jit(solution)/shard_map/all_to_all | solution.py:236
  49.6 3.5 %all-to-all-start.1 = ((bf16[16,160,128]{2,1,0:T(8,128)(2,1)}), bf16[16,160,128]{2,1,0:T(8,128)(2,1)S(1)}, u32[]{:S(2)}, u32[]{:S(2)}) async-start(bf16[16,160,128]{2,1,0:T(8,128)(2,1)} %chain.2), calls=%async_computation.1 | async-start | bytes 1310720 | tf_op jit(solution)/shard_map/all_to_all | solution.py:236
  54.1 9.3 %intra.1 = (f32[256,2560]{1,0:T(8,128)}, bf16[256,2560]{1,0:T(8,128)(2,1)}) custom-call(f32[256,2560]{1,0:T(8,128)} %bitcast.50, f32[40,256]{1,0:T(8,128)} %get-tuple-element.66.cum_ref, f32[256,40]{1,0:T(8,128)} %get-tuple-element.67.cum_t_ref, f32[256,128]{1,0:T(8,128)} %bitcast.64, f32[256,128]{1,0:T(8,128)} %bitcast.57, f32[40]{0:T(128)} %skip_ref.5), custom_call_target="tpu_custom_call" | custom-call | bytes 27000000 | tf_op jit(solution)/shard_map/intra/pallas_call | solution.py:179
  65.1 7.6 %all-to-all-done.1 = bf16[16,160,128]{2,1,0:T(8,128)(2,1)S(1)} async-done(((bf16[16,160,128]{2,1,0:T(8,128)(2,1)}), bf16[16,160,128]{2,1,0:T(8,128)(2,1)S(1)}, u32[]{:S(2)}, u32[]{:S(2)}) %all-to-all-start.1) | async-done | bytes 655392 | tf_op jit(solution)/shard_map/all_to_all | solution.py:236
  73.6 4.7 %inter.1.yo_ref = bf16[256,2560]{1,0:T(8,128)(2,1)} custom-call(f32[256,2560]{1,0:T(8,128)} %get-tuple-element.70.part_ref, bf16[256,2560]{1,0:T(8,128)(2,1)} %get-tuple-element.71.grow_ref, f32[256,128]{1,0:T(8,128)} %bitcast.58, bf16[2560,128]{1,0:T(8,128)(2,1)} %bitcast.55), custom_call_target="tpu_custom_call" | custom-call | bytes 15000000 | tf_op jit(solution)/shard_map/inter/pallas_call | solution.py:200
  78.3 3.2 %collective-permute-done.1.yx_ref = bf16[256,2560]{1,0:T(8,128)(2,1)S(1)} collective-permute-done((bf16[256,2560]{1,0:T(8,128)(2,1)}, bf16[256,2560]{1,0:T(8,128)(2,1)S(1)}, u32[]{:S(2)}, u32[]{:S(2)}) %collective-permute-start.1) | collective-permute-done | bytes 1310752 | tf_op jit(solution)/shard_map/ppermute | solution.py:660
  82.6 8.4 %terms.1 = (bf16[4,4,160,640]{3,2,1,0:T(8,128)(2,1)}, bf16[4,4,160,640]{3,2,1,0:T(8,128)(2,1)}) custom-call(s32[2]{0:T(128)} %pad_add_fusion.at_ref, bf16[256,2560]{1,0:T(8,128)(2,1)} %inter.1.yo_ref, bf16[256,2560]{1,0:T(8,128)(2,1)} %copy-done.8, bf16[512,1280]{1,0:T(8,128)(2,1)} %pad_maximum_fusion.g_ref), custom_call_target="tpu_custom_call" | custom-call | bytes 24000000 | tf_op jit(solution)/shard_map/terms/pallas_call | solution.py:251
  95.3 8.5 %gy_parts.1 = (f32[256,2560]{1,0:T(8,128)}, bf16[256,2560]{1,0:T(8,128)(2,1)}) custom-call(bf16[512,1280]{1,0:T(8,128)(2,1)} %pad_maximum_fusion.g_ref, bf16[2560,1280]{1,0:T(8,128)(2,1)} %all-gather.2.cloned.1.call-done.w_ref), custom_call_target="tpu_custom_call" | custom-call | bytes 24000000 | tf_op jit(solution)/shard_map/gy_parts/pallas_call | solution.py:277
  104.0 3.2 %collective-permute-done.2 = bf16[2,160,640]{2,1,0:T(8,128)(2,1)S(1)} collective-permute-done((bf16[2,160,640]{2,1,0:T(8,128)(2,1)S(1)}, bf16[2,160,640]{2,1,0:T(8,128)(2,1)S(1)}, u32[]{:S(2)}, u32[]{:S(2)}) %collective-permute-start.2) | collective-permute-done | bytes 409632 | tf_op jit(solution)/shard_map/ppermute | solution.py:631
  114.0 6.0 %entries.1 = (bf16[256,2560]{1,0:T(8,128)(2,1)}, bf16[16,176,128]{2,1,0:T(8,128)(2,1)}) custom-call(f32[256,2560]{1,0:T(8,128)} %get-tuple-element.84.own_ref, bf16[256,2560]{1,0:T(8,128)(2,1)} %copy-done.9, f32[256,2560]{1,0:T(8,128)} %bitcast.51, bf16[256,2560]{1,0:T(8,128)(2,1)} %get-tuple-element.71.grow_ref, f32[256,128]{1,0:T(8,128)} %bitcast.59), custom_call_target="tpu_custom_call" | custom-call | bytes 18000000 | tf_op jit(solution)/shard_map/entries/pallas_call | solution.py:317
  120.0 4.3 %all-to-all-start.3 = ((bf16[16,176,128]{2,1,0:T(8,128)(2,1)}), bf16[16,176,128]{2,1,0:T(8,128)(2,1)S(1)}, u32[]{:S(2)}, u32[]{:S(2)}) async-start(bf16[16,176,128]{2,1,0:T(8,128)(2,1)} %get-tuple-element.102), calls=%async_computation.4 | async-start | bytes 1441792 | tf_op jit(solution)/shard_map/all_to_all | solution.py:236
  124.3 6.9 %within.2 = (f32[256,1280]{1,0:T(8,128)}, f32[40,256]{1,0:T(8,128)}, f32[256,128]{1,0:T(8,128)}, f32[256,128]{1,0:T(8,128)}) custom-call(f32[256,2560]{1,0:T(8,128)} %bitcast.52, bf16[256,2560]{1,0:T(8,128)(2,1)} %get-tuple-element.93.gy_ref, f32[40,256]{1,0:T(8,128)} %get-tuple-element.66.cum_ref, f32[256,40]{1,0:T(8,128)} %get-tuple-element.67.cum_t_ref, ...), custom_call_target="tpu_custom_call" | custom-call | bytes 21000000 | tf_op jit(solution)/shard_map/within/pallas_call | solution.py:387
  144.1 3.1 %collective-permute-done.8.a2 = bf16[160,640]{1,0:T(8,128)(2,1)S(1)} collective-permute-done((bf16[160,640]{1,0:T(8,128)(2,1)S(1)}, bf16[160,640]{1,0:T(8,128)(2,1)S(1)}, u32[]{:S(2)}, u32[]{:S(2)}) %collective-permute-start.8) | collective-permute-done | bytes 204832 | tf_op jit(solution)/shard_map/ppermute | solution.py:631
  153.8 5.4 %all-to-all-start.2 = ((bf16[8,13,16,128]{3,2,1,0:T(8,128)(2,1)}), bf16[8,13,16,128]{3,2,1,0:T(8,128)(2,1)S(1)}, u32[]{:S(2)}, u32[]{:S(2)}) async-start(bf16[8,13,16,128]{3,2,1,0:T(8,128)(2,1)} %fold.1), calls=%async_computation.3 | async-start | bytes 851968 | tf_op jit(solution)/shard_map/all_to_all | solution.py:236
  159.8 7.0 %within.3 = (f32[256,1280]{1,0:T(8,128)}, f32[40,256]{1,0:T(8,128)}, f32[256,128]{1,0:T(8,128)}, f32[256,128]{1,0:T(8,128)}) custom-call(f32[256,2560]{1,0:T(8,128)} %bitcast.53, bf16[256,2560]{1,0:T(8,128)(2,1)} %get-tuple-element.93.gy_ref, f32[40,256]{1,0:T(8,128)} %get-tuple-element.66.cum_ref, f32[256,40]{1,0:T(8,128)} %get-tuple-element.67.cum_t_ref, ...), custom_call_target="tpu_custom_call" | custom-call | bytes 21000000 | tf_op jit(solution)/shard_map/within/pallas_call | solution.py:387
  174.1 8.1 %all-to-all-start.4 = ((bf16[16,160,128]{2,1,0:T(8,128)(2,1)}), bf16[16,160,128]{2,1,0:T(8,128)(2,1)S(1)}, u32[]{:S(2)}, u32[]{:S(2)}) async-start(bf16[16,160,128]{2,1,0:T(8,128)(2,1)} %chain.3), calls=%async_computation.5 | async-start | bytes 1310720 | tf_op jit(solution)/shard_map/all_to_all | solution.py:236
  182.2 2.9 %collective-permute-start.15 = (f32[1,128]{1,0:T(1,128)}, f32[1,128]{1,0:T(1,128)S(1)}, u32[]{:S(2)}, u32[]{:S(2)}) collective-permute-start(f32[1,128]{1,0:T(1,128)} %get-tuple-element.108), channel_id=1, source_target_pairs={{0,48},{16,32},{32,16},{48,0},{64,112},{80,96},{96,80},{112,64},{1... | collective-permute-start | bytes 1544 | tf_op jit(solution)/shard_map/ppermute | solution.py:666
  186.2 3.3 %collective-permute-done.14 = f32[1,128]{1,0:T(1,128)S(1)} collective-permute-done((f32[1,128]{1,0:T(1,128)}, f32[1,128]{1,0:T(1,128)S(1)}, u32[]{:S(2)}, u32[]{:S(2)}) %collective-permute-start.14) | collective-permute-done | bytes 544 | tf_op jit(solution)/shard_map/ppermute | solution.py:666
  196.7 5.5 %all-to-all-done.4 = bf16[16,160,128]{2,1,0:T(8,128)(2,1)S(1)} async-done(((bf16[16,160,128]{2,1,0:T(8,128)(2,1)}), bf16[16,160,128]{2,1,0:T(8,128)(2,1)S(1)}, u32[]{:S(2)}, u32[]{:S(2)}) %all-to-all-start.4) | async-done | bytes 655392 | tf_op jit(solution)/shard_map/all_to_all | solution.py:236
  203.9 3.5 %all-to-all-start.5 = ((bf16[8,14,16,128]{3,2,1,0:T(8,128)(2,1)}), bf16[8,14,16,128]{3,2,1,0:T(8,128)(2,1)S(1)}, u32[]{:S(2)}, u32[]{:S(2)}) async-start(bf16[8,14,16,128]{3,2,1,0:T(8,128)(2,1)} %pack.1), calls=%async_computation.6 | async-start | bytes 917504 | tf_op jit(solution)/shard_map/all_to_all | solution.py:236
  207.3 8.6 %across.1 = (f32[256,2560]{1,0:T(8,128)}, f32[40,256]{1,0:T(8,128)}, f32[256,128]{1,0:T(8,128)}, f32[256,128]{1,0:T(8,128)}) custom-call(f32[256,2560]{1,0:T(8,128)} %bitcast.54, bf16[256,2560]{1,0:T(8,128)(2,1)} %get-tuple-element.93.gy_ref, bf16[256,2560]{1,0:T(8,128)(2,1)} %get-tuple-element.71.grow_ref, bf16[256,2560]{1,0:T(8,128)(2,1)} %get-tuple-element.94.tail_ref, ...), custom_call_target="tpu_custom_call" | custom-call | bytes 24000000 | tf_op jit(solution)/shard_map/across/pallas_call | solution.py:462
  215.9 7.9 %all-to-all-done.5.own_ref = bf16[8,14,16,128]{3,2,1,0:T(8,128)(2,1)S(1)} async-done(((bf16[8,14,16,128]{3,2,1,0:T(8,128)(2,1)}), bf16[8,14,16,128]{3,2,1,0:T(8,128)(2,1)S(1)}, u32[]{:S(2)}, u32[]{:S(2)}) %all-to-all-start.5) | async-done | bytes 458784 | tf_op jit(solution)/shard_map/all_to_all | solution.py:236
  (99 shorter events, 63.0 us)
Async XLA Ops:
  8.0 87.3 %all-gather.2.cloned.1.call-start = ((), (), s32[]{:S(2)}) async-start(), calls=%async_computation.7 | async-start | bytes 6963200 | tf_op jit(solution)/shard_map/all_gather | solution.py:695
  14.7 31.3 %all-to-all-start = ((bf16[16,176,128]{2,1,0:T(8,128)(2,1)}), bf16[16,176,128]{2,1,0:T(8,128)(2,1)S(1)}, u32[]{:S(2)}, u32[]{:S(2)}) async-start(bf16[16,176,128]{2,1,0:T(8,128)(2,1)} %get-tuple-element.73), calls=%async_computation | async-start | bytes 1441792 | tf_op jit(solution)/shard_map/all_to_all | solution.py:236
  49.6 23.2 %all-to-all-start.1 = ((bf16[16,160,128]{2,1,0:T(8,128)(2,1)}), bf16[16,160,128]{2,1,0:T(8,128)(2,1)S(1)}, u32[]{:S(2)}, u32[]{:S(2)}) async-start(bf16[16,160,128]{2,1,0:T(8,128)(2,1)} %chain.2), calls=%async_computation.1 | async-start | bytes 1310720 | tf_op jit(solution)/shard_map/all_to_all | solution.py:236
  53.1 80.9 %reduce-scatter.2.cloned.1.call-start = ((), (), s32[]{:S(2)}) async-start(), calls=%async_computation.8 | async-start | bytes 4096000 | tf_op jit(solution)/shard_map/reduce_scatter | solution.py:704
  54.1 9.9 %collective-permute-start = (bf16[256,1280]{1,0:T(8,128)(2,1)}, bf16[256,1280]{1,0:T(8,128)(2,1)S(1)}, u32[]{:S(2)}, u32[]{:S(2)}) collective-permute-start(bf16[256,1280]{1,0:T(8,128)(2,1)} %get-tuple-element.133), channel_id=1, source_target_pairs={{0,1},{1,0},{2,3},{3,2},{4,5},{5,4},{6,7},{7,6},{8,9},{9,8},{10,11... | collective-permute-start | bytes 1966088 | tf_op jit(solution)/shard_map/ppermute | solution.py:660
  92.5 11.5 %collective-permute-start.3 = (bf16[2,160,640]{2,1,0:T(8,128)(2,1)S(1)}, bf16[2,160,640]{2,1,0:T(8,128)(2,1)S(1)}, u32[]{:S(2)}, u32[]{:S(2)}) collective-permute-start(bf16[2,160,640]{2,1,0:T(8,128)(2,1)S(1)} %get-tuple-element.128), channel_id=1, source_target_pairs={{0,192},{64,0},{128,64},{192,128},{1,193},{65,1},{129,65},{193,129... | collective-permute-start | bytes 1228808 | tf_op jit(solution)/shard_map/ppermute | solution.py:631
  95.3 11.9 %collective-permute-start.2 = (bf16[2,160,640]{2,1,0:T(8,128)(2,1)S(1)}, bf16[2,160,640]{2,1,0:T(8,128)(2,1)S(1)}, u32[]{:S(2)}, u32[]{:S(2)}) collective-permute-start(bf16[2,160,640]{2,1,0:T(8,128)(2,1)S(1)} %get-tuple-element.129), channel_id=1, source_target_pairs={{0,64},{64,128},{128,192},{192,0},{1,65},{65,129},{129,193},{193,1... | collective-permute-start | bytes 1228808 | tf_op jit(solution)/shard_map/ppermute | solution.py:631
  107.2 4.0 %collective-permute-start.4 = (bf16[256,2560]{1,0:T(8,128)(2,1)}, bf16[256,2560]{1,0:T(8,128)(2,1)S(1)}, u32[]{:S(2)}, u32[]{:S(2)}) collective-permute-start(bf16[256,2560]{1,0:T(8,128)(2,1)} %get-tuple-element.83), channel_id=1, source_target_pairs={{0,1},{1,0},{2,3},{3,2},{4,5},{5,4},{6,7},{7,6},{8,9},{9,8},{10,11... | collective-permute-start | bytes 3932168 | tf_op jit(solution)/shard_map/ppermute | solution.py:660
  111.3 20.8 %collective-permute-start.5 = (bf16[4,160,640]{2,1,0:T(8,128)(2,1)S(1)}, bf16[4,160,640]{2,1,0:T(8,128)(2,1)}, u32[]{:S(2)}, u32[]{:S(2)}) collective-permute-start(bf16[4,160,640]{2,1,0:T(8,128)(2,1)S(1)} %get-tuple-element.88), channel_id=1, source_target_pairs={{0,64},{64,128},{128,192},{192,0},{1,65},{65,129},{129,193},{193,1... | collective-permute-start | bytes 2457608 | tf_op jit(solution)/shard_map/ppermute | solution.py:631
  111.3 20.8 %collective-permute-start.6 = (bf16[4,160,640]{2,1,0:T(8,128)(2,1)S(1)}, bf16[4,160,640]{2,1,0:T(8,128)(2,1)}, u32[]{:S(2)}, u32[]{:S(2)}) collective-permute-start(bf16[4,160,640]{2,1,0:T(8,128)(2,1)S(1)} %get-tuple-element.89), channel_id=1, source_target_pairs={{0,192},{64,0},{128,64},{192,128},{1,193},{65,1},{129,65},{193,129... | collective-permute-start | bytes 2457608 | tf_op jit(solution)/shard_map/ppermute | solution.py:631
  120.0 33.9 %all-to-all-start.3 = ((bf16[16,176,128]{2,1,0:T(8,128)(2,1)}), bf16[16,176,128]{2,1,0:T(8,128)(2,1)S(1)}, u32[]{:S(2)}, u32[]{:S(2)}) async-start(bf16[16,176,128]{2,1,0:T(8,128)(2,1)} %get-tuple-element.102), calls=%async_computation.4 | async-start | bytes 1441792 | tf_op jit(solution)/shard_map/all_to_all | solution.py:236
  136.0 7.3 %collective-permute-start.9 = (bf16[160,640]{1,0:T(8,128)(2,1)S(1)}, bf16[160,640]{1,0:T(8,128)(2,1)S(1)}, u32[]{:S(2)}, u32[]{:S(2)}) collective-permute-start(bf16[160,640]{1,0:T(8,128)(2,1)S(1)} %get-tuple-element.138), channel_id=1, source_target_pairs={{0,128},{64,192},{128,0},{192,64},{1,129},{65,193},{129,1},{193,65... | collective-permute-start | bytes 614408 | tf_op jit(solution)/shard_map/ppermute | solution.py:631
  137.2 10.0 %collective-permute-start.8 = (bf16[160,640]{1,0:T(8,128)(2,1)S(1)}, bf16[160,640]{1,0:T(8,128)(2,1)S(1)}, u32[]{:S(2)}, u32[]{:S(2)}) collective-permute-start(bf16[160,640]{1,0:T(8,128)(2,1)S(1)} %get-tuple-element.139), channel_id=1, source_target_pairs={{0,192},{64,0},{128,64},{192,128},{1,193},{65,1},{129,65},{193,129... | collective-permute-start | bytes 614408 | tf_op jit(solution)/shard_map/ppermute | solution.py:631
  138.4 9.7 %collective-permute-start.7 = (bf16[160,640]{1,0:T(8,128)(2,1)S(1)}, bf16[160,640]{1,0:T(8,128)(2,1)S(1)}, u32[]{:S(2)}, u32[]{:S(2)}) collective-permute-start(bf16[160,640]{1,0:T(8,128)(2,1)S(1)} %get-tuple-element.140), channel_id=1, source_target_pairs={{0,64},{64,128},{128,192},{192,0},{1,65},{65,129},{129,193},{193,1... | collective-permute-start | bytes 614408 | tf_op jit(solution)/shard_map/ppermute | solution.py:631
  139.7 8.4 %collective-permute-start.12 = (bf16[160,640]{1,0:T(8,128)(2,1)S(1)}, bf16[160,640]{1,0:T(8,128)(2,1)S(1)}, u32[]{:S(2)}, u32[]{:S(2)}) collective-permute-start(bf16[160,640]{1,0:T(8,128)(2,1)S(1)} %get-tuple-element.134), channel_id=1, source_target_pairs={{0,32},{16,48},{32,0},{48,16},{1,33},{17,49},{33,1},{49,17},{2,34}... | collective-permute-start | bytes 614408 | tf_op jit(solution)/shard_map/ppermute | solution.py:631
  142.5 8.1 %collective-permute-start.11 = (bf16[160,640]{1,0:T(8,128)(2,1)S(1)}, bf16[160,640]{1,0:T(8,128)(2,1)S(1)}, u32[]{:S(2)}, u32[]{:S(2)}) collective-permute-start(bf16[160,640]{1,0:T(8,128)(2,1)S(1)} %get-tuple-element.135), channel_id=1, source_target_pairs={{0,48},{16,0},{32,16},{48,32},{1,49},{17,1},{33,17},{49,33},{2,50}... | collective-permute-start | bytes 614408 | tf_op jit(solution)/shard_map/ppermute | solution.py:631
  143.4 7.3 %collective-permute-start.10 = (bf16[160,640]{1,0:T(8,128)(2,1)S(1)}, bf16[160,640]{1,0:T(8,128)(2,1)S(1)}, u32[]{:S(2)}, u32[]{:S(2)}) collective-permute-start(bf16[160,640]{1,0:T(8,128)(2,1)S(1)} %get-tuple-element.136), channel_id=1, source_target_pairs={{0,16},{16,32},{32,48},{48,0},{1,17},{17,33},{33,49},{49,1},{2,18}... | collective-permute-start | bytes 614408 | tf_op jit(solution)/shard_map/ppermute | solution.py:631
  153.8 17.5 %all-to-all-start.2 = ((bf16[8,13,16,128]{3,2,1,0:T(8,128)(2,1)}), bf16[8,13,16,128]{3,2,1,0:T(8,128)(2,1)S(1)}, u32[]{:S(2)}, u32[]{:S(2)}) async-start(bf16[8,13,16,128]{3,2,1,0:T(8,128)(2,1)} %fold.1), calls=%async_computation.3 | async-start | bytes 851968 | tf_op jit(solution)/shard_map/all_to_all | solution.py:236
  174.1 28.1 %all-to-all-start.4 = ((bf16[16,160,128]{2,1,0:T(8,128)(2,1)}), bf16[16,160,128]{2,1,0:T(8,128)(2,1)S(1)}, u32[]{:S(2)}, u32[]{:S(2)}) async-start(bf16[16,160,128]{2,1,0:T(8,128)(2,1)} %chain.3), calls=%async_computation.5 | async-start | bytes 1310720 | tf_op jit(solution)/shard_map/all_to_all | solution.py:236
  182.2 4.0 %collective-permute-start.15 = (f32[1,128]{1,0:T(1,128)}, f32[1,128]{1,0:T(1,128)S(1)}, u32[]{:S(2)}, u32[]{:S(2)}) collective-permute-start(f32[1,128]{1,0:T(1,128)} %get-tuple-element.108), channel_id=1, source_target_pairs={{0,48},{16,32},{32,16},{48,0},{64,112},{80,96},{96,80},{112,64},{1... | collective-permute-start | bytes 1544 | tf_op jit(solution)/shard_map/ppermute | solution.py:666
  185.1 4.3 %collective-permute-start.14 = (f32[1,128]{1,0:T(1,128)}, f32[1,128]{1,0:T(1,128)S(1)}, u32[]{:S(2)}, u32[]{:S(2)}) collective-permute-start(f32[1,128]{1,0:T(1,128)} %get-tuple-element.108), channel_id=1, source_target_pairs={{0,32},{16,48},{32,0},{48,16},{64,96},{80,112},{96,64},{112,80},{1... | collective-permute-start | bytes 1544 | tf_op jit(solution)/shard_map/ppermute | solution.py:666
  190.1 3.9 %collective-permute-start.18 = (f32[1,128]{1,0:T(1,128)S(1)}, f32[1,128]{1,0:T(1,128)S(1)}, u32[]{:S(2)}, u32[]{:S(2)}) collective-permute-start(f32[1,128]{1,0:T(1,128)S(1)} %add_add_fusion.1), channel_id=1, source_target_pairs={{0,192},{16,208},{32,224},{48,240},{64,128},{80,144},{96,160},{112... | collective-permute-start | bytes 1544 | tf_op jit(solution)/shard_map/ppermute | solution.py:666
  192.0 4.2 %collective-permute-start.17 = (f32[1,128]{1,0:T(1,128)S(1)}, f32[1,128]{1,0:T(1,128)S(1)}, u32[]{:S(2)}, u32[]{:S(2)}) collective-permute-start(f32[1,128]{1,0:T(1,128)S(1)} %add_add_fusion.1), channel_id=1, source_target_pairs={{0,128},{16,144},{32,160},{48,176},{64,192},{80,208},{96,224},{112... | collective-permute-start | bytes 1544 | tf_op jit(solution)/shard_map/ppermute | solution.py:666
  203.9 19.9 %all-to-all-start.5 = ((bf16[8,14,16,128]{3,2,1,0:T(8,128)(2,1)}), bf16[8,14,16,128]{3,2,1,0:T(8,128)(2,1)S(1)}, u32[]{:S(2)}, u32[]{:S(2)}) async-start(bf16[8,14,16,128]{3,2,1,0:T(8,128)(2,1)} %pack.1), calls=%async_computation.6 | async-start | bytes 917504 | tf_op jit(solution)/shard_map/all_to_all | solution.py:236
  (22 other events, 88.2 us)
Sparse Core Ops, SparseCore 0:
  14.8 71.2 all-gather.1
Sparse Core Ops, SparseCore 1:
  91.1 38.5 reduce-scatter.1

commit v11 on v10

--- a/solution.py
+++ b/solution.py
@@ -193,7 +193,7 @@
 
 def inter_kernel(part_ref, grow_ref, c_ref, start_ref, y_ref):
     read = nt(c_ref[...].astype(BF), start_ref[...])
-    y_ref[...] = (part_ref[...] + grow_ref[...].astype(F32) * read).astype(BF)
+    y_ref[...] = (part_ref[...] + grow_ref[...].astype(F32) * read).T.astype(BF)
 
 
 def inter(part, grow, c, start):
@@ -201,8 +201,8 @@
         inter_kernel,
         grid=(PAIRS // WIDE,),
         in_specs=[wide(T, WIDE), wide(T, WIDE), whole((T, N)), state_block(WIDE)],
-        out_specs=wide(T, WIDE),
-        out_shape=jax.ShapeDtypeStruct((T, D), BF),
+        out_specs=pl.BlockSpec((WIDE * 2 * P_SIZE, T), lambda p: (p, 0)),
+        out_shape=jax.ShapeDtypeStruct((D, T), BF),
         compiler_params=params(),
         cost_estimate=cost(5),
         name="inter",
@@ -236,18 +236,32 @@
     return lax.all_to_all(v, axis, 0, 0, tiled=True)
 
 
-def term_kernel(at_ref, yo_ref, yx_ref, g_ref, first_ref, second_ref):
+def term_kernel(at_ref, yo_ref, yx_ref, g_ref, first_ref, near_ref, far_up_ref, far_down_ref):
+    step = pl.program_id(0)
     half = g_ref.shape[1] // 2
-    term = tn(jnp.concatenate([yo_ref[...], yx_ref[...]], axis=0), g_ref[...]).astype(BF)
+    term = nn(jnp.concatenate([yo_ref[...], yx_ref[...]], axis=1), g_ref[...]).astype(BF)
     for k in range(4):
         rows = slice(k * OWN, (k + 1) * OWN)
         first_ref[k, 0] = term[rows, :half]
-        second_ref[0, (k + 4 - at_ref[1]) % 4] = term[rows, half:]
+        rel = (k + 4 - at_ref[1]) % 4
+
+        @pl.when(step != 2)
+        def _():
+            near_ref[0, rel] = term[rows, half:]
+
+        @pl.when((step == 2) & (rel < 2))
+        def _():
+            far_up_ref[rel] = term[rows, half:]
+
+        @pl.when((step == 2) & (rel >= 2))
+        def _():
+            far_down_ref[rel - 2] = term[rows, half:]
 
 
 def terms(at, y_own, y_other, g):
-    rows = pl.BlockSpec((T, 4 * OWN), lambda i, at: (0, (at[0] + i) % 4))
+    rows = pl.BlockSpec((4 * OWN, T), lambda i, at: ((at[0] + i) % 4, 0))
     half = g.shape[1] // 2
+    part = jax.ShapeDtypeStruct((2, OWN, half), BF)
     return pl.pallas_call(
         term_kernel,
         grid_spec=pltpu.PrefetchScalarGridSpec(
@@ -256,10 +270,17 @@
             in_specs=[rows, rows, whole(g.shape)],
             out_specs=[
                 pl.BlockSpec((4, 1, OWN, half), lambda i, at: (0, i, 0, 0)),
-                pl.BlockSpec((1, 4, OWN, half), lambda i, at: (i, 0, 0, 0)),
+                pl.BlockSpec((1, 4, OWN, half), lambda i, at: (i - i // 2, 0, 0, 0)),
+                whole(part.shape),
+                whole(part.shape),
             ],
         ),
-        out_shape=[jax.ShapeDtypeStruct((4, 4, OWN, half), BF)] * 2,
+        out_shape=[
+            jax.ShapeDtypeStruct((4, 4, OWN, half), BF),
+            jax.ShapeDtypeStruct((3, 4, OWN, half), BF),
+            part,
+            part,
+        ],
         compiler_params=params(),
         cost_estimate=cost(8),
         name="terms",
@@ -635,15 +656,10 @@
     return (a.astype(F32) + b.astype(F32)).astype(BF)
 
 
-def far(t, axis):
-    m = t.shape[1] // 2
-    return shifted(t[2, :m], axis, 1), shifted(t[2, m:], axis, -1)
-
-
 def passed(t, ra, rb):
     m = t.shape[1] // 2
     up = jnp.concatenate([plus(t[1, :m], ra), t[1, m:]], axis=0)
-    down = jnp.concatenate([t[3, :m], plus(t[3, m:], rb)], axis=0)
+    down = jnp.concatenate([t[2, :m], plus(t[2, m:], rb)], axis=0)
     return up, down
 
 
@@ -699,10 +715,10 @@
     start = swap(chain(got, got, mine, False), SEQ).reshape(H * P_SIZE, N)
     y_own = inter(y_part, grow, c, start)
     y_other = other_core(y_own)
-    first, second = terms(at, y_own, y_other, g_both)
+    first, second, far_up, far_down = terms(at, y_own, y_other, g_both)
 
     first = lax.psum_scatter(first.reshape(-1, half // 2), "x", scatter_dimension=0, tiled=True)
-    far_y = far(second, "y")
+    far_y = (shifted(far_up, "y", 1), shifted(far_down, "y", -1))
     w_half, _ = tie(w_half, second)
     gy_own, gy_other = gy_parts(g_both, w_half)
     *far_y, gy_own, gy_other = tie(*far_y, gy_own, gy_other)
@@ -714,7 +730,7 @@
     got_back = swap(sent_back, SEQ)
     steps = PAIRS // STEP // 2
     gx1, *sums = within(0, steps, x, gy, cum, cum_t, b, c, d_skip)
-    first, second, gx1 = tie(first, second, gx1)
+    first, gx1 = tie(first, gx1)
     first = direct(first.reshape(4, OWN, half // 2), "y")
     second = direct(second, "x")
     tiles = fold(first + second)

time: 238 us -> 240 us (level)
  waiting for transfers between devices: 67.6 us -> 71.1 us
    all_to_all x6, waiting for transfers between devices: 44.2 us -> 47.3 us  [swap(): return lax.all_to_all(v, axis, 0, 0, tiled=True)]
    unnamed x36 -> x42, local copies, waits for them, and re-layouts: 5.08 us -> 5.96 us
  transfers between devices with their start and end apart: 28 -> 28, of which waited for: 18 -> 19; matrix products, arithmetic and copies ran while one was open for 5% -> 4% of each run, Pallas kernels for 28% -> 29%
where the time goes in v11:
time: 240 us; the launch traced here: 238 us
  Pallas kernels  80.1 us (33%)
  waiting for transfers between devices  71.1 us (30%)
  starting transfers between devices  54.8 us (23%)
  between operations  15.7 us (7%)
  local copies, waits for them, and re-layouts  11.1 us (5%)
  other arithmetic  5.22 us (2%)
    all_to_all x6, waiting for transfers between devices, swap(): return lax.all_to_all(v, axis, 0, 0, tiled=True)  47.3 us
    all_to_all x6, starting transfers between devices, swap(): return lax.all_to_all(v, axis, 0, 0, tiled=True)  34.5 us
    pallas_call x2, Pallas kernels, within(): pl.pallas_call(functools.partial(within_kernel, first, steps), grid=(step...  13.9 us
    ppermute x10, starting transfers between devices, shifted(): return lax.ppermute(v, axis, [(i, (i + d) % 4) for i in range(4)])  12.4 us
    ppermute x10, waiting for transfers between devices, shifted(): return lax.ppermute(v, axis, [(i, (i + d) % 4) for i in range(4)])  10 us
    pallas_call x1, Pallas kernels, intra(): pl.pallas_call(intra_kernel, grid=(PAIRS // STEP,), in_specs=[wide(T, STE...  9.31 us
    pallas_call x1, Pallas kernels, terms(): pl.pallas_call(term_kernel, grid_spec=pltpu.PrefetchScalarGridSpec(num_sc...  9.03 us
    pallas_call x1, Pallas kernels, across(): pl.pallas_call(across_kernel, grid=(PAIRS // WIDE,), in_specs=[wide(T, WI...  8.56 us
  transfers between devices with their start and end apart: 28, of which 19 were waited for; matrix products, arithmetic and copies ran while one was open for 4% of the time, Pallas kernels for 29%

profile of v11, /device:TPU:1, one launch (start us, length us, event | category | flops | bytes accessed | tf_op | source)
XLA Modules:
  0.0 238.0 jit_solution(2159666346407040733)
XLA Ops:
  8.1 5.8 %ends.1 = (f32[40,256]{1,0:T(8,128)}, f32[256,40]{1,0:T(8,128)}, bf16[256,2560]{1,0:T(8,128)(2,1)}, bf16[16,176,128]{2,1,0:T(8,128)(2,1)}) custom-call(f32[256,2560]{1,0:T(8,128)} %bitcast.45, f32[40,256]{1,0:T(8,128)} %bitcast.66, f32[256,128]{1,0:T(8,128)} %bitcast.59), custom_call_target="tpu_custom_call" | custom-call | bytes 18000000 | tf_op jit(solution)/shard_map/ends/pallas_call | solution.py:134
  14.7 10.0 %all-to-all-start = ((bf16[16,176,128]{2,1,0:T(8,128)(2,1)}), bf16[16,176,128]{2,1,0:T(8,128)(2,1)S(1)}, u32[]{:S(2)}, u32[]{:S(2)}) async-start(bf16[16,176,128]{2,1,0:T(8,128)(2,1)} %get-tuple-element.74), calls=%async_computation | async-start | bytes 1441792 | tf_op jit(solution)/shard_map/all_to_all | solution.py:236
  24.7 21.3 %all-to-all-done.parts_ref.totals_ref = bf16[16,176,128]{2,1,0:T(8,128)(2,1)S(1)} async-done(((bf16[16,176,128]{2,1,0:T(8,128)(2,1)}), bf16[16,176,128]{2,1,0:T(8,128)(2,1)S(1)}, u32[]{:S(2)}, u32[]{:S(2)}) %all-to-all-start) | async-done | bytes 720928 | tf_op jit(solution)/shard_map/all_to_all | solution.py:236
  46.9 2.7 %chain.2 = bf16[16,160,128]{2,1,0:T(8,128)(2,1)} custom-call(s32[1]{0:T(128)} %bitcast.8.mine_ref, bf16[16,176,128]{2,1,0:T(8,128)(2,1)} %copy-done.1, bf16[16,176,128]{2,1,0:T(8,128)(2,1)} %copy-done.1), custom_call_target="tpu_custom_call" | custom-call | bytes 9000000 | tf_op jit(solution)/shard_map/chain/pallas_call | solution.py:224
  49.6 3.5 %all-to-all-start.1 = ((bf16[16,160,128]{2,1,0:T(8,128)(2,1)}), bf16[16,160,128]{2,1,0:T(8,128)(2,1)S(1)}, u32[]{:S(2)}, u32[]{:S(2)}) async-start(bf16[16,160,128]{2,1,0:T(8,128)(2,1)} %chain.2), calls=%async_computation.1 | async-start | bytes 1310720 | tf_op jit(solution)/shard_map/all_to_all | solution.py:236
  54.1 9.3 %intra.1 = (f32[256,2560]{1,0:T(8,128)}, bf16[256,2560]{1,0:T(8,128)(2,1)}) custom-call(f32[256,2560]{1,0:T(8,128)} %bitcast.46, f32[40,256]{1,0:T(8,128)} %get-tuple-element.67.cum_ref, f32[256,40]{1,0:T(8,128)} %get-tuple-element.68.cum_t_ref, f32[256,128]{1,0:T(8,128)} %bitcast.60, f32[256,128]{1,0:T(8,128)} %bitcast.53, f32[40]{0:T(128)} %skip_ref.5), custom_call_target="tpu_custom_call" | custom-call | bytes 27000000 | tf_op jit(solution)/shard_map/intra/pallas_call | solution.py:179
  65.1 7.6 %all-to-all-done.1 = bf16[16,160,128]{2,1,0:T(8,128)(2,1)S(1)} async-done(((bf16[16,160,128]{2,1,0:T(8,128)(2,1)}), bf16[16,160,128]{2,1,0:T(8,128)(2,1)S(1)}, u32[]{:S(2)}, u32[]{:S(2)}) %all-to-all-start.1) | async-done | bytes 655392 | tf_op jit(solution)/shard_map/all_to_all | solution.py:236
  73.6 4.9 %inter.1.yo_ref = bf16[2560,256]{1,0:T(8,128)(2,1)} custom-call(f32[256,2560]{1,0:T(8,128)} %get-tuple-element.71.part_ref, bf16[256,2560]{1,0:T(8,128)(2,1)} %get-tuple-element.72.grow_ref, f32[256,128]{1,0:T(8,128)} %bitcast.54, bf16[2560,128]{1,0:T(8,128)(2,1)} %bitcast.51), custom_call_target="tpu_custom_call" | custom-call | bytes 15000000 | tf_op jit(solution)/shard_map/inter/pallas_call | solution.py:200
  78.5 3.2 %collective-permute-done.1.yx_ref = bf16[2560,256]{1,0:T(8,128)(2,1)S(1)} collective-permute-done((bf16[2560,256]{1,0:T(8,128)(2,1)}, bf16[2560,256]{1,0:T(8,128)(2,1)S(1)}, u32[]{:S(2)}, u32[]{:S(2)}) %collective-permute-start.1) | collective-permute-done | bytes 1310752 | tf_op jit(solution)/shard_map/ppermute | solution.py:676
  82.8 9.0 %terms.1 = (bf16[4,4,160,640]{3,2,1,0:T(8,128)(2,1)}, bf16[3,4,160,640]{3,2,1,0:T(8,128)(2,1)}, bf16[2,160,640]{2,1,0:T(8,128)(2,1)}, bf16[2,160,640]{2,1,0:T(8,128)(2,1)}) custom-call(s32[2]{0:T(128)} %pad_add_fusion.at_ref, bf16[2560,256]{1,0:T(8,128)(2,1)} %inter.1.yo_ref, bf16[2560,256]{1,0:T(8,128)(2,1)} %copy-done.9, ...), custom_call_target="tpu_custom_call" | custom-call | bytes 24000000 | tf_op jit(solution)/shard_map/terms/pallas_call | solution.py:265
  95.7 8.5 %gy_parts.1 = (f32[256,2560]{1,0:T(8,128)}, bf16[256,2560]{1,0:T(8,128)(2,1)}) custom-call(bf16[512,1280]{1,0:T(8,128)(2,1)} %pad_maximum_fusion.g_ref, bf16[2560,1280]{1,0:T(8,128)(2,1)} %all-gather.2.cloned.1.call-done.w_ref), custom_call_target="tpu_custom_call" | custom-call | bytes 24000000 | tf_op jit(solution)/shard_map/gy_parts/pallas_call | solution.py:298
  111.6 6.0 %entries.1 = (bf16[256,2560]{1,0:T(8,128)(2,1)}, bf16[16,176,128]{2,1,0:T(8,128)(2,1)}) custom-call(f32[256,2560]{1,0:T(8,128)} %get-tuple-element.87.own_ref, bf16[256,2560]{1,0:T(8,128)(2,1)} %copy-done.10, f32[256,2560]{1,0:T(8,128)} %bitcast.47, bf16[256,2560]{1,0:T(8,128)(2,1)} %get-tuple-element.72.grow_ref, f32[256,128]{1,0:T(8,128)} %bitcast.55), custom_call_target="tpu_custom_call" | custom-call | bytes 18000000 | tf_op jit(solution)/shard_map/entries/pallas_call | solution.py:338
  117.6 4.2 %all-to-all-start.3 = ((bf16[16,176,128]{2,1,0:T(8,128)(2,1)}), bf16[16,176,128]{2,1,0:T(8,128)(2,1)S(1)}, u32[]{:S(2)}, u32[]{:S(2)}) async-start(bf16[16,176,128]{2,1,0:T(8,128)(2,1)} %get-tuple-element.104), calls=%async_computation.4 | async-start | bytes 1441792 | tf_op jit(solution)/shard_map/all_to_all | solution.py:236
  121.8 6.9 %within.2 = (f32[256,1280]{1,0:T(8,128)}, f32[40,256]{1,0:T(8,128)}, f32[256,128]{1,0:T(8,128)}, f32[256,128]{1,0:T(8,128)}) custom-call(f32[256,2560]{1,0:T(8,128)} %bitcast.48, bf16[256,2560]{1,0:T(8,128)(2,1)} %get-tuple-element.95.gy_ref, f32[40,256]{1,0:T(8,128)} %get-tuple-element.67.cum_ref, f32[256,40]{1,0:T(8,128)} %get-tuple-element.68.cum_t_ref, ...), custom_call_target="tpu_custom_call" | custom-call | bytes 21000000 | tf_op jit(solution)/shard_map/within/pallas_call | solution.py:408
  132.5 2.7 %collective-permute-start.7 = (bf16[160,640]{1,0:T(8,128)(2,1)S(1)}, bf16[160,640]{1,0:T(8,128)(2,1)S(1)}, u32[]{:S(2)}, u32[]{:S(2)}) collective-permute-start(bf16[160,640]{1,0:T(8,128)(2,1)S(1)} %get-tuple-element.138), channel_id=1, source_target_pairs={{0,128},{64,192},{128,0},{192,64},{1,129},{65,193},{129,1},{193,65... | collective-permute-start | bytes 614408 | tf_op jit(solution)/shard_map/ppermute | solution.py:652
  146.0 2.8 %collective-permute-done.11.b2 = bf16[160,640]{1,0:T(8,128)(2,1)S(1)} collective-permute-done((bf16[160,640]{1,0:T(8,128)(2,1)S(1)}, bf16[160,640]{1,0:T(8,128)(2,1)S(1)}, u32[]{:S(2)}, u32[]{:S(2)}) %collective-permute-start.11) | collective-permute-done | bytes 204832 | tf_op jit(solution)/shard_map/ppermute | solution.py:652
  154.4 6.7 %all-to-all-start.2 = ((bf16[8,13,16,128]{3,2,1,0:T(8,128)(2,1)}), bf16[8,13,16,128]{3,2,1,0:T(8,128)(2,1)S(1)}, u32[]{:S(2)}, u32[]{:S(2)}) async-start(bf16[8,13,16,128]{3,2,1,0:T(8,128)(2,1)} %fold.1), calls=%async_computation.3 | async-start | bytes 851968 | tf_op jit(solution)/shard_map/all_to_all | solution.py:236
  161.6 7.1 %within.3 = (f32[256,1280]{1,0:T(8,128)}, f32[40,256]{1,0:T(8,128)}, f32[256,128]{1,0:T(8,128)}, f32[256,128]{1,0:T(8,128)}) custom-call(f32[256,2560]{1,0:T(8,128)} %bitcast.49, bf16[256,2560]{1,0:T(8,128)(2,1)} %get-tuple-element.95.gy_ref, f32[40,256]{1,0:T(8,128)} %get-tuple-element.67.cum_ref, f32[256,40]{1,0:T(8,128)} %get-tuple-element.68.cum_t_ref, ...), custom_call_target="tpu_custom_call" | custom-call | bytes 21000000 | tf_op jit(solution)/shard_map/within/pallas_call | solution.py:408
  171.3 2.8 %all-to-all-done.2.parts_ref = bf16[8,13,16,128]{3,2,1,0:T(8,128)(2,1)S(1)} async-done(((bf16[8,13,16,128]{3,2,1,0:T(8,128)(2,1)}), bf16[8,13,16,128]{3,2,1,0:T(8,128)(2,1)S(1)}, u32[]{:S(2)}, u32[]{:S(2)}) %all-to-all-start.2) | async-done | bytes 426016 | tf_op jit(solution)/shard_map/all_to_all | solution.py:236
  176.9 6.6 %all-to-all-start.4 = ((bf16[16,160,128]{2,1,0:T(8,128)(2,1)}), bf16[16,160,128]{2,1,0:T(8,128)(2,1)S(1)}, u32[]{:S(2)}, u32[]{:S(2)}) async-start(bf16[16,160,128]{2,1,0:T(8,128)(2,1)} %chain.3), calls=%async_computation.5 | async-start | bytes 1310720 | tf_op jit(solution)/shard_map/all_to_all | solution.py:236
  196.1 7.5 %all-to-all-done.4 = bf16[16,160,128]{2,1,0:T(8,128)(2,1)S(1)} async-done(((bf16[16,160,128]{2,1,0:T(8,128)(2,1)}), bf16[16,160,128]{2,1,0:T(8,128)(2,1)S(1)}, u32[]{:S(2)}, u32[]{:S(2)}) %all-to-all-start.4) | async-done | bytes 655392 | tf_op jit(solution)/shard_map/all_to_all | solution.py:236
  205.3 3.5 %all-to-all-start.5 = ((bf16[8,14,16,128]{3,2,1,0:T(8,128)(2,1)}), bf16[8,14,16,128]{3,2,1,0:T(8,128)(2,1)S(1)}, u32[]{:S(2)}, u32[]{:S(2)}) async-start(bf16[8,14,16,128]{3,2,1,0:T(8,128)(2,1)} %pack.1), calls=%async_computation.6 | async-start | bytes 917504 | tf_op jit(solution)/shard_map/all_to_all | solution.py:236
  208.7 8.6 %across.1 = (f32[256,2560]{1,0:T(8,128)}, f32[40,256]{1,0:T(8,128)}, f32[256,128]{1,0:T(8,128)}, f32[256,128]{1,0:T(8,128)}) custom-call(f32[256,2560]{1,0:T(8,128)} %bitcast.50, bf16[256,2560]{1,0:T(8,128)(2,1)} %get-tuple-element.95.gy_ref, bf16[256,2560]{1,0:T(8,128)(2,1)} %get-tuple-element.72.grow_ref, bf16[256,2560]{1,0:T(8,128)(2,1)} %get-tuple-element.96.tail_ref, ...), custom_call_target="tpu_custom_call" | custom-call | bytes 24000000 | tf_op jit(solution)/shard_map/across/pallas_call | solution.py:483
  217.3 8.0 %all-to-all-done.5.own_ref = bf16[8,14,16,128]{3,2,1,0:T(8,128)(2,1)S(1)} async-done(((bf16[8,14,16,128]{3,2,1,0:T(8,128)(2,1)}), bf16[8,14,16,128]{3,2,1,0:T(8,128)(2,1)S(1)}, u32[]{:S(2)}, u32[]{:S(2)}) %all-to-all-start.5) | async-done | bytes 458784 | tf_op jit(solution)/shard_map/all_to_all | solution.py:236
  (105 shorter events, 63.0 us)
Async XLA Ops:
  8.0 87.7 %all-gather.2.cloned.1.call-start = ((), (), s32[]{:S(2)}) async-start(), calls=%async_computation.7 | async-start | bytes 6963200 | tf_op jit(solution)/shard_map/all_gather | solution.py:711
  14.7 31.3 %all-to-all-start = ((bf16[16,176,128]{2,1,0:T(8,128)(2,1)}), bf16[16,176,128]{2,1,0:T(8,128)(2,1)S(1)}, u32[]{:S(2)}, u32[]{:S(2)}) async-start(bf16[16,176,128]{2,1,0:T(8,128)(2,1)} %get-tuple-element.74), calls=%async_computation | async-start | bytes 1441792 | tf_op jit(solution)/shard_map/all_to_all | solution.py:236
  49.6 23.2 %all-to-all-start.1 = ((bf16[16,160,128]{2,1,0:T(8,128)(2,1)}), bf16[16,160,128]{2,1,0:T(8,128)(2,1)S(1)}, u32[]{:S(2)}, u32[]{:S(2)}) async-start(bf16[16,160,128]{2,1,0:T(8,128)(2,1)} %chain.2), calls=%async_computation.1 | async-start | bytes 1310720 | tf_op jit(solution)/shard_map/all_to_all | solution.py:236
  53.1 77.4 %reduce-scatter.2.cloned.1.call-start = ((), (), s32[]{:S(2)}) async-start(), calls=%async_computation.8 | async-start | bytes 4096000 | tf_op jit(solution)/shard_map/reduce_scatter | solution.py:720
  54.1 9.9 %collective-permute-start = (bf16[256,1280]{1,0:T(8,128)(2,1)}, bf16[256,1280]{1,0:T(8,128)(2,1)S(1)}, u32[]{:S(2)}, u32[]{:S(2)}) collective-permute-start(bf16[256,1280]{1,0:T(8,128)(2,1)} %get-tuple-element.133), channel_id=1, source_target_pairs={{0,1},{1,0},{2,3},{3,2},{4,5},{5,4},{6,7},{7,6},{8,9},{9,8},{10,11... | collective-permute-start | bytes 1966088 | tf_op jit(solution)/shard_map/ppermute | solution.py:676
  92.9 12.3 %collective-permute-start.2 = (bf16[2,160,640]{2,1,0:T(8,128)(2,1)S(1)}, bf16[2,160,640]{2,1,0:T(8,128)(2,1)S(1)}, u32[]{:S(2)}, u32[]{:S(2)}) collective-permute-start(bf16[2,160,640]{2,1,0:T(8,128)(2,1)S(1)} %copy-done.19), channel_id=1, source_target_pairs={{0,64},{64,128},{128,192},{192,0},{1,65},{65,129},{129,193},{193,1... | collective-permute-start | bytes 1228808 | tf_op jit(solution)/shard_map/ppermute | solution.py:652
  94.1 11.0 %collective-permute-start.3 = (bf16[2,160,640]{2,1,0:T(8,128)(2,1)S(1)}, bf16[2,160,640]{2,1,0:T(8,128)(2,1)S(1)}, u32[]{:S(2)}, u32[]{:S(2)}) collective-permute-start(bf16[2,160,640]{2,1,0:T(8,128)(2,1)S(1)} %copy-done.18), channel_id=1, source_target_pairs={{0,192},{64,0},{128,64},{192,128},{1,193},{65,1},{129,65},{193,129... | collective-permute-start | bytes 1228808 | tf_op jit(solution)/shard_map/ppermute | solution.py:652
  105.1 3.8 %collective-permute-start.4 = (bf16[256,2560]{1,0:T(8,128)(2,1)}, bf16[256,2560]{1,0:T(8,128)(2,1)S(1)}, u32[]{:S(2)}, u32[]{:S(2)}) collective-permute-start(bf16[256,2560]{1,0:T(8,128)(2,1)} %get-tuple-element.86), channel_id=1, source_target_pairs={{0,1},{1,0},{2,3},{3,2},{4,5},{5,4},{6,7},{7,6},{8,9},{9,8},{10,11... | collective-permute-start | bytes 3932168 | tf_op jit(solution)/shard_map/ppermute | solution.py:676
  108.9 27.9 %collective-permute-start.8 = (bf16[4,160,640]{2,1,0:T(8,128)(2,1)S(1)}, bf16[4,160,640]{2,1,0:T(8,128)(2,1)}, u32[]{:S(2)}, u32[]{:S(2)}) collective-permute-start(bf16[4,160,640]{2,1,0:T(8,128)(2,1)S(1)} %get-tuple-element.93), channel_id=1, source_target_pairs={{0,64},{64,128},{128,192},{192,0},{1,65},{65,129},{129,193},{193,1... | collective-permute-start | bytes 2457608 | tf_op jit(solution)/shard_map/ppermute | solution.py:652
  110.2 26.6 %collective-permute-start.9 = (bf16[4,160,640]{2,1,0:T(8,128)(2,1)S(1)}, bf16[4,160,640]{2,1,0:T(8,128)(2,1)}, u32[]{:S(2)}, u32[]{:S(2)}) collective-permute-start(bf16[4,160,640]{2,1,0:T(8,128)(2,1)S(1)} %get-tuple-element.94), channel_id=1, source_target_pairs={{0,192},{64,0},{128,64},{192,128},{1,193},{65,1},{129,65},{193,129... | collective-permute-start | bytes 2457608 | tf_op jit(solution)/shard_map/ppermute | solution.py:652
  117.6 36.7 %all-to-all-start.3 = ((bf16[16,176,128]{2,1,0:T(8,128)(2,1)}), bf16[16,176,128]{2,1,0:T(8,128)(2,1)S(1)}, u32[]{:S(2)}, u32[]{:S(2)}) async-start(bf16[16,176,128]{2,1,0:T(8,128)(2,1)} %get-tuple-element.104), calls=%async_computation.4 | async-start | bytes 1441792 | tf_op jit(solution)/shard_map/all_to_all | solution.py:236
  132.5 9.3 %collective-permute-start.7 = (bf16[160,640]{1,0:T(8,128)(2,1)S(1)}, bf16[160,640]{1,0:T(8,128)(2,1)S(1)}, u32[]{:S(2)}, u32[]{:S(2)}) collective-permute-start(bf16[160,640]{1,0:T(8,128)(2,1)S(1)} %get-tuple-element.138), channel_id=1, source_target_pairs={{0,128},{64,192},{128,0},{192,64},{1,129},{65,193},{129,1},{193,65... | collective-permute-start | bytes 614408 | tf_op jit(solution)/shard_map/ppermute | solution.py:652
  135.3 9.2 %collective-permute-start.6 = (bf16[160,640]{1,0:T(8,128)(2,1)S(1)}, bf16[160,640]{1,0:T(8,128)(2,1)S(1)}, u32[]{:S(2)}, u32[]{:S(2)}) collective-permute-start(bf16[160,640]{1,0:T(8,128)(2,1)S(1)} %get-tuple-element.139), channel_id=1, source_target_pairs={{0,192},{64,0},{128,64},{192,128},{1,193},{65,1},{129,65},{193,129... | collective-permute-start | bytes 614408 | tf_op jit(solution)/shard_map/ppermute | solution.py:652
  136.1 8.5 %collective-permute-start.5 = (bf16[160,640]{1,0:T(8,128)(2,1)S(1)}, bf16[160,640]{1,0:T(8,128)(2,1)S(1)}, u32[]{:S(2)}, u32[]{:S(2)}) collective-permute-start(bf16[160,640]{1,0:T(8,128)(2,1)S(1)} %get-tuple-element.140), channel_id=1, source_target_pairs={{0,64},{64,128},{128,192},{192,0},{1,65},{65,129},{129,193},{193,1... | collective-permute-start | bytes 614408 | tf_op jit(solution)/shard_map/ppermute | solution.py:652
  139.5 6.5 %collective-permute-start.12 = (bf16[160,640]{1,0:T(8,128)(2,1)S(1)}, bf16[160,640]{1,0:T(8,128)(2,1)S(1)}, u32[]{:S(2)}, u32[]{:S(2)}) collective-permute-start(bf16[160,640]{1,0:T(8,128)(2,1)S(1)} %get-tuple-element.134), channel_id=1, source_target_pairs={{0,32},{16,48},{32,0},{48,16},{1,33},{17,49},{33,1},{49,17},{2,34}... | collective-permute-start | bytes 614408 | tf_op jit(solution)/shard_map/ppermute | solution.py:652
  140.6 8.1 %collective-permute-start.11 = (bf16[160,640]{1,0:T(8,128)(2,1)S(1)}, bf16[160,640]{1,0:T(8,128)(2,1)S(1)}, u32[]{:S(2)}, u32[]{:S(2)}) collective-permute-start(bf16[160,640]{1,0:T(8,128)(2,1)S(1)} %get-tuple-element.135), channel_id=1, source_target_pairs={{0,48},{16,0},{32,16},{48,32},{1,49},{17,1},{33,17},{49,33},{2,50}... | collective-permute-start | bytes 614408 | tf_op jit(solution)/shard_map/ppermute | solution.py:652
  141.8 9.4 %collective-permute-start.10 = (bf16[160,640]{1,0:T(8,128)(2,1)S(1)}, bf16[160,640]{1,0:T(8,128)(2,1)S(1)}, u32[]{:S(2)}, u32[]{:S(2)}) collective-permute-start(bf16[160,640]{1,0:T(8,128)(2,1)S(1)} %get-tuple-element.136), channel_id=1, source_target_pairs={{0,16},{16,32},{32,48},{48,0},{1,17},{17,33},{33,49},{49,1},{2,18}... | collective-permute-start | bytes 614408 | tf_op jit(solution)/shard_map/ppermute | solution.py:652
  154.4 19.8 %all-to-all-start.2 = ((bf16[8,13,16,128]{3,2,1,0:T(8,128)(2,1)}), bf16[8,13,16,128]{3,2,1,0:T(8,128)(2,1)S(1)}, u32[]{:S(2)}, u32[]{:S(2)}) async-start(bf16[8,13,16,128]{3,2,1,0:T(8,128)(2,1)} %fold.1), calls=%async_computation.3 | async-start | bytes 851968 | tf_op jit(solution)/shard_map/all_to_all | solution.py:236
  176.9 26.7 %all-to-all-start.4 = ((bf16[16,160,128]{2,1,0:T(8,128)(2,1)}), bf16[16,160,128]{2,1,0:T(8,128)(2,1)S(1)}, u32[]{:S(2)}, u32[]{:S(2)}) async-start(bf16[16,160,128]{2,1,0:T(8,128)(2,1)} %chain.3), calls=%async_computation.5 | async-start | bytes 1310720 | tf_op jit(solution)/shard_map/all_to_all | solution.py:236
  184.6 4.0 %collective-permute-start.14 = (f32[1,128]{1,0:T(1,128)}, f32[1,128]{1,0:T(1,128)S(1)}, u32[]{:S(2)}, u32[]{:S(2)}) collective-permute-start(f32[1,128]{1,0:T(1,128)} %get-tuple-element.110), channel_id=1, source_target_pairs={{0,32},{16,48},{32,0},{48,16},{64,96},{80,112},{96,64},{112,80},{1... | collective-permute-start | bytes 1544 | tf_op jit(solution)/shard_map/ppermute | solution.py:682
  189.3 3.9 %collective-permute-start.18 = (f32[1,128]{1,0:T(1,128)S(1)}, f32[1,128]{1,0:T(1,128)S(1)}, u32[]{:S(2)}, u32[]{:S(2)}) collective-permute-start(f32[1,128]{1,0:T(1,128)S(1)} %add_add_fusion.1), channel_id=1, source_target_pairs={{0,192},{16,208},{32,224},{48,240},{64,128},{80,144},{96,160},{112... | collective-permute-start | bytes 1544 | tf_op jit(solution)/shard_map/ppermute | solution.py:682
  191.4 4.2 %collective-permute-start.17 = (f32[1,128]{1,0:T(1,128)S(1)}, f32[1,128]{1,0:T(1,128)S(1)}, u32[]{:S(2)}, u32[]{:S(2)}) collective-permute-start(f32[1,128]{1,0:T(1,128)S(1)} %add_add_fusion.1), channel_id=1, source_target_pairs={{0,128},{16,144},{32,160},{48,176},{64,192},{80,208},{96,224},{112... | collective-permute-start | bytes 1544 | tf_op jit(solution)/shard_map/ppermute | solution.py:682
  191.5 4.1 %collective-permute-start.16 = (f32[1,128]{1,0:T(1,128)S(1)}, f32[1,128]{1,0:T(1,128)S(1)}, u32[]{:S(2)}, u32[]{:S(2)}) collective-permute-start(f32[1,128]{1,0:T(1,128)S(1)} %add_add_fusion.1), channel_id=1, source_target_pairs={{0,64},{16,80},{32,96},{48,112},{64,0},{80,16},{96,32},{112,48},{1... | collective-permute-start | bytes 1544 | tf_op jit(solution)/shard_map/ppermute | solution.py:682
  205.3 20.1 %all-to-all-start.5 = ((bf16[8,14,16,128]{3,2,1,0:T(8,128)(2,1)}), bf16[8,14,16,128]{3,2,1,0:T(8,128)(2,1)S(1)}, u32[]{:S(2)}, u32[]{:S(2)}) async-start(bf16[8,14,16,128]{3,2,1,0:T(8,128)(2,1)} %pack.1), calls=%async_computation.6 | async-start | bytes 917504 | tf_op jit(solution)/shard_map/all_to_all | solution.py:236
  (25 other events, 118.6 us)
Sparse Core Ops, SparseCore 0:
  14.8 71.2 all-gather.1
Sparse Core Ops, SparseCore 1:
  92.0 38.5 reduce-scatter.1

commit v12 on v11

--- a/solution.py
+++ b/solution.py
@@ -21,7 +21,7 @@
 HIGH = lax.Precision.HIGHEST
 BF = jnp.bfloat16
 F32 = jnp.float32
-VMEM = 56 * 1024 * 1024
+VMEM = 62 * 1024 * 1024
 WIDE = 5
 STEP = 2
 ROWS = OWN + 16

time: 240 us -> 239 us (level)
  other arithmetic: 5.22 us -> 8.85 us
  waiting for transfers between devices: 71.1 us -> 67.7 us
    unnamed x42 -> x32, local copies, waits for them, and re-layouts: 5.96 us -> 3.95 us
  transfers between devices with their start and end apart: 28 -> 28, of which waited for: 19 -> 18; matrix products, arithmetic and copies ran while one was open for 4% -> 6% of each run, Pallas kernels for 29% -> 29%
where the time goes in v12:
time: 239 us; the launch traced here: 237 us
  Pallas kernels  80 us (33%)
  waiting for transfers between devices  67.7 us (28%)
  starting transfers between devices  54.6 us (23%)
  between operations  15.6 us (7%)
  local copies, waits for them, and re-layouts  10.3 us (4%)
  other arithmetic  8.85 us (4%)
    all_to_all x6, waiting for transfers between devices, swap(): return lax.all_to_all(v, axis, 0, 0, tiled=True)  45.8 us
    all_to_all x6, starting transfers between devices, swap(): return lax.all_to_all(v, axis, 0, 0, tiled=True)  34.3 us
    pallas_call x2, Pallas kernels, within(): pl.pallas_call(functools.partial(within_kernel, first, steps), grid=(step...  13.9 us
    ppermute x10, starting transfers between devices, shifted(): return lax.ppermute(v, axis, [(i, (i + d) % 4) for i in range(4)])  12.4 us
    ppermute x10, waiting for transfers between devices, shifted(): return lax.ppermute(v, axis, [(i, (i + d) % 4) for i in range(4)])  10.2 us
    pallas_call x1, Pallas kernels, intra(): pl.pallas_call(intra_kernel, grid=(PAIRS // STEP,), in_specs=[wide(T, STE...  9.28 us
    pallas_call x1, Pallas kernels, terms(): pl.pallas_call(term_kernel, grid_spec=pltpu.PrefetchScalarGridSpec(num_sc...  9 us
    pallas_call x1, Pallas kernels, across(): pl.pallas_call(across_kernel, grid=(PAIRS // WIDE,), in_specs=[wide(T, WI...  8.56 us
  transfers between devices with their start and end apart: 28, of which 18 were waited for; matrix products, arithmetic and copies ran while one was open for 6% of the time, Pallas kernels for 29%

profile of v12, /device:TPU:1, one launch (start us, length us, event | category | flops | bytes accessed | tf_op | source)
XLA Modules:
  0.0 237.0 jit_solution(3521737382403981904)
XLA Ops:
  8.1 5.8 %ends.1 = (f32[40,256]{1,0:T(8,128)}, f32[256,40]{1,0:T(8,128)}, bf16[256,2560]{1,0:T(8,128)(2,1)}, bf16[16,176,128]{2,1,0:T(8,128)(2,1)}) custom-call(f32[256,2560]{1,0:T(8,128)} %bitcast.45, f32[40,256]{1,0:T(8,128)} %bitcast.66, f32[256,128]{1,0:T(8,128)} %bitcast.59), custom_call_target="tpu_custom_call" | custom-call | bytes 18000000 | tf_op jit(solution)/shard_map/ends/pallas_call | solution.py:134
  14.6 10.0 %all-to-all-start = ((bf16[16,176,128]{2,1,0:T(8,128)(2,1)}), bf16[16,176,128]{2,1,0:T(8,128)(2,1)S(1)}, u32[]{:S(2)}, u32[]{:S(2)}) async-start(bf16[16,176,128]{2,1,0:T(8,128)(2,1)} %get-tuple-element.74), calls=%async_computation | async-start | bytes 1441792 | tf_op jit(solution)/shard_map/all_to_all | solution.py:236
  24.7 21.3 %all-to-all-done.parts_ref.totals_ref = bf16[16,176,128]{2,1,0:T(8,128)(2,1)S(1)} async-done(((bf16[16,176,128]{2,1,0:T(8,128)(2,1)}), bf16[16,176,128]{2,1,0:T(8,128)(2,1)S(1)}, u32[]{:S(2)}, u32[]{:S(2)}) %all-to-all-start) | async-done | bytes 720928 | tf_op jit(solution)/shard_map/all_to_all | solution.py:236
  49.5 3.6 %all-to-all-start.1 = ((bf16[16,160,128]{2,1,0:T(8,128)(2,1)}), bf16[16,160,128]{2,1,0:T(8,128)(2,1)S(1)}, u32[]{:S(2)}, u32[]{:S(2)}) async-start(bf16[16,160,128]{2,1,0:T(8,128)(2,1)} %chain.2), calls=%async_computation.1 | async-start | bytes 1310720 | tf_op jit(solution)/shard_map/all_to_all | solution.py:236
  54.3 9.3 %intra.1 = (f32[256,2560]{1,0:T(8,128)}, bf16[256,2560]{1,0:T(8,128)(2,1)}) custom-call(f32[256,2560]{1,0:T(8,128)} %bitcast.46, f32[40,256]{1,0:T(8,128)} %get-tuple-element.67.cum_ref, f32[256,40]{1,0:T(8,128)} %get-tuple-element.68.cum_t_ref, f32[256,128]{1,0:T(8,128)} %bitcast.60, f32[256,128]{1,0:T(8,128)} %bitcast.53, f32[40]{0:T(128)} %skip_ref.5), custom_call_target="tpu_custom_call" | custom-call | bytes 27000000 | tf_op jit(solution)/shard_map/intra/pallas_call | solution.py:179
  66.7 6.1 %all-to-all-done.1 = bf16[16,160,128]{2,1,0:T(8,128)(2,1)S(1)} async-done(((bf16[16,160,128]{2,1,0:T(8,128)(2,1)}), bf16[16,160,128]{2,1,0:T(8,128)(2,1)S(1)}, u32[]{:S(2)}, u32[]{:S(2)}) %all-to-all-start.1) | async-done | bytes 655392 | tf_op jit(solution)/shard_map/all_to_all | solution.py:236
  73.6 4.9 %inter.1.yo_ref = bf16[2560,256]{1,0:T(8,128)(2,1)} custom-call(f32[256,2560]{1,0:T(8,128)} %get-tuple-element.71.part_ref, bf16[256,2560]{1,0:T(8,128)(2,1)} %get-tuple-element.72.grow_ref, f32[256,128]{1,0:T(8,128)} %bitcast.54, bf16[2560,128]{1,0:T(8,128)(2,1)} %bitcast.51), custom_call_target="tpu_custom_call" | custom-call | bytes 15000000 | tf_op jit(solution)/shard_map/inter/pallas_call | solution.py:200
  78.5 3.4 %collective-permute-done.1.yx_ref = bf16[2560,256]{1,0:T(8,128)(2,1)} collective-permute-done((bf16[2560,256]{1,0:T(8,128)(2,1)}, bf16[2560,256]{1,0:T(8,128)(2,1)}, u32[]{:S(2)}, u32[]{:S(2)}) %collective-permute-start.1) | collective-permute-done | bytes 1310752 | tf_op jit(solution)/shard_map/ppermute | solution.py:676
  81.9 9.0 %terms.1 = (bf16[4,4,160,640]{3,2,1,0:T(8,128)(2,1)}, bf16[3,4,160,640]{3,2,1,0:T(8,128)(2,1)}, bf16[2,160,640]{2,1,0:T(8,128)(2,1)}, bf16[2,160,640]{2,1,0:T(8,128)(2,1)}) custom-call(s32[2]{0:T(128)} %pad_add_fusion.at_ref, bf16[2560,256]{1,0:T(8,128)(2,1)} %inter.1.yo_ref, bf16[2560,256]{1,0:T(8,128)(2,1)} %collective-permute-done.1.yx_ref, ...), custom_call_target="tpu_custom_call" | custom-call | bytes 24000000 | tf_op jit(solution)/shard_map/terms/pallas_call | solution.py:265
  93.8 8.6 %gy_parts.1 = (f32[256,2560]{1,0:T(8,128)}, bf16[256,2560]{1,0:T(8,128)(2,1)}) custom-call(bf16[512,1280]{1,0:T(8,128)(2,1)} %pad_maximum_fusion.g_ref, bf16[2560,1280]{1,0:T(8,128)(2,1)} %all-gather.2.cloned.1.call-done.w_ref), custom_call_target="tpu_custom_call" | custom-call | bytes 24000000 | tf_op jit(solution)/shard_map/gy_parts/pallas_call | solution.py:298
  111.0 6.0 %entries.1 = (bf16[256,2560]{1,0:T(8,128)(2,1)}, bf16[16,176,128]{2,1,0:T(8,128)(2,1)}) custom-call(f32[256,2560]{1,0:T(8,128)} %get-tuple-element.87.own_ref, bf16[256,2560]{1,0:T(8,128)(2,1)} %collective-permute-done.4.other_ref, f32[256,2560]{1,0:T(8,128)} %bitcast.47, bf16[256,2560]{1,0:T(8,128)(2,1)} %get-tuple-element.72.grow_ref, f32[256,128]{1,0:T(8,128)} %bitcast.55), custom_call_target="tpu_custom_call" | custom-call | bytes 18000000 | tf_op jit(solution)/shard_map/entries/pallas_call | solution.py:338
  116.9 3.8 %all-to-all-start.3 = ((bf16[16,176,128]{2,1,0:T(8,128)(2,1)}), bf16[16,176,128]{2,1,0:T(8,128)(2,1)S(1)}, u32[]{:S(2)}, u32[]{:S(2)}) async-start(bf16[16,176,128]{2,1,0:T(8,128)(2,1)} %get-tuple-element.104), calls=%async_computation.4 | async-start | bytes 1441792 | tf_op jit(solution)/shard_map/all_to_all | solution.py:236
  120.7 6.9 %within.2 = (f32[256,1280]{1,0:T(8,128)}, f32[40,256]{1,0:T(8,128)}, f32[256,128]{1,0:T(8,128)}, f32[256,128]{1,0:T(8,128)}) custom-call(f32[256,2560]{1,0:T(8,128)} %bitcast.48, bf16[256,2560]{1,0:T(8,128)(2,1)} %get-tuple-element.95.gy_ref, f32[40,256]{1,0:T(8,128)} %get-tuple-element.67.cum_ref, f32[256,40]{1,0:T(8,128)} %get-tuple-element.68.cum_t_ref, ...), custom_call_target="tpu_custom_call" | custom-call | bytes 21000000 | tf_op jit(solution)/shard_map/within/pallas_call | solution.py:408
  131.6 2.7 %collective-permute-start.7 = (bf16[160,640]{1,0:T(8,128)(2,1)S(1)}, bf16[160,640]{1,0:T(8,128)(2,1)S(1)}, u32[]{:S(2)}, u32[]{:S(2)}) collective-permute-start(bf16[160,640]{1,0:T(8,128)(2,1)S(1)} %get-tuple-element.138), channel_id=1, source_target_pairs={{0,128},{64,192},{128,0},{192,64},{1,129},{65,193},{129,1},{193,65... | collective-permute-start | bytes 614408 | tf_op jit(solution)/shard_map/ppermute | solution.py:652
  145.0 2.9 %collective-permute-done.11.b2 = bf16[160,640]{1,0:T(8,128)(2,1)S(1)} collective-permute-done((bf16[160,640]{1,0:T(8,128)(2,1)S(1)}, bf16[160,640]{1,0:T(8,128)(2,1)S(1)}, u32[]{:S(2)}, u32[]{:S(2)}) %collective-permute-start.11) | collective-permute-done | bytes 204832 | tf_op jit(solution)/shard_map/ppermute | solution.py:652
  153.3 6.7 %all-to-all-start.2 = ((bf16[8,13,16,128]{3,2,1,0:T(8,128)(2,1)}), bf16[8,13,16,128]{3,2,1,0:T(8,128)(2,1)S(1)}, u32[]{:S(2)}, u32[]{:S(2)}) async-start(bf16[8,13,16,128]{3,2,1,0:T(8,128)(2,1)} %fold.1), calls=%async_computation.3 | async-start | bytes 851968 | tf_op jit(solution)/shard_map/all_to_all | solution.py:236
  160.6 7.0 %within.3 = (f32[256,1280]{1,0:T(8,128)}, f32[40,256]{1,0:T(8,128)}, f32[256,128]{1,0:T(8,128)}, f32[256,128]{1,0:T(8,128)}) custom-call(f32[256,2560]{1,0:T(8,128)} %bitcast.49, bf16[256,2560]{1,0:T(8,128)(2,1)} %get-tuple-element.95.gy_ref, f32[40,256]{1,0:T(8,128)} %get-tuple-element.67.cum_ref, f32[256,40]{1,0:T(8,128)} %get-tuple-element.68.cum_t_ref, ...), custom_call_target="tpu_custom_call" | custom-call | bytes 21000000 | tf_op jit(solution)/shard_map/within/pallas_call | solution.py:408
  167.7 2.6 %chain.3 = bf16[16,160,128]{2,1,0:T(8,128)(2,1)} custom-call(s32[1]{0:T(128)} %bitcast.8.mine_ref, bf16[16,176,128]{2,1,0:T(8,128)(2,1)} %copy-done.2, bf16[16,176,128]{2,1,0:T(8,128)(2,1)} %copy-done.1), custom_call_target="tpu_custom_call" | custom-call | bytes 9000000 | tf_op jit(solution)/shard_map/chain/pallas_call | solution.py:224
  170.3 2.9 %all-to-all-done.2.parts_ref = bf16[8,13,16,128]{3,2,1,0:T(8,128)(2,1)S(1)} async-done(((bf16[8,13,16,128]{3,2,1,0:T(8,128)(2,1)}), bf16[8,13,16,128]{3,2,1,0:T(8,128)(2,1)S(1)}, u32[]{:S(2)}, u32[]{:S(2)}) %all-to-all-start.2) | async-done | bytes 426016 | tf_op jit(solution)/shard_map/all_to_all | solution.py:236
  175.9 6.6 %all-to-all-start.4 = ((bf16[16,160,128]{2,1,0:T(8,128)(2,1)}), bf16[16,160,128]{2,1,0:T(8,128)(2,1)S(1)}, u32[]{:S(2)}, u32[]{:S(2)}) async-start(bf16[16,160,128]{2,1,0:T(8,128)(2,1)} %chain.3), calls=%async_computation.5 | async-start | bytes 1310720 | tf_op jit(solution)/shard_map/all_to_all | solution.py:236
  195.2 7.4 %all-to-all-done.4 = bf16[16,160,128]{2,1,0:T(8,128)(2,1)S(1)} async-done(((bf16[16,160,128]{2,1,0:T(8,128)(2,1)}), bf16[16,160,128]{2,1,0:T(8,128)(2,1)S(1)}, u32[]{:S(2)}, u32[]{:S(2)}) %all-to-all-start.4) | async-done | bytes 655392 | tf_op jit(solution)/shard_map/all_to_all | solution.py:236
  204.3 3.5 %all-to-all-start.5 = ((bf16[8,14,16,128]{3,2,1,0:T(8,128)(2,1)}), bf16[8,14,16,128]{3,2,1,0:T(8,128)(2,1)S(1)}, u32[]{:S(2)}, u32[]{:S(2)}) async-start(bf16[8,14,16,128]{3,2,1,0:T(8,128)(2,1)} %pack.1), calls=%async_computation.6 | async-start | bytes 917504 | tf_op jit(solution)/shard_map/all_to_all | solution.py:236
  207.7 8.6 %across.1 = (f32[256,2560]{1,0:T(8,128)}, f32[40,256]{1,0:T(8,128)}, f32[256,128]{1,0:T(8,128)}, f32[256,128]{1,0:T(8,128)}) custom-call(f32[256,2560]{1,0:T(8,128)} %bitcast.50, bf16[256,2560]{1,0:T(8,128)(2,1)} %get-tuple-element.95.gy_ref, bf16[256,2560]{1,0:T(8,128)(2,1)} %get-tuple-element.72.grow_ref, bf16[256,2560]{1,0:T(8,128)(2,1)} %get-tuple-element.96.tail_ref, ...), custom_call_target="tpu_custom_call" | custom-call | bytes 24000000 | tf_op jit(solution)/shard_map/across/pallas_call | solution.py:483
  216.3 8.0 %all-to-all-done.5.own_ref = bf16[8,14,16,128]{3,2,1,0:T(8,128)(2,1)S(1)} async-done(((bf16[8,14,16,128]{3,2,1,0:T(8,128)(2,1)}), bf16[8,14,16,128]{3,2,1,0:T(8,128)(2,1)S(1)}, u32[]{:S(2)}, u32[]{:S(2)}) %all-to-all-start.5) | async-done | bytes 458784 | tf_op jit(solution)/shard_map/all_to_all | solution.py:236
  (95 shorter events, 63.8 us)
Async XLA Ops:
  8.0 85.7 %all-gather.2.cloned.1.call-start = ((), (), s32[]{:S(2)}) async-start(), calls=%async_computation.7 | async-start | bytes 6963200 | tf_op jit(solution)/shard_map/all_gather | solution.py:711
  14.6 31.3 %all-to-all-start = ((bf16[16,176,128]{2,1,0:T(8,128)(2,1)}), bf16[16,176,128]{2,1,0:T(8,128)(2,1)S(1)}, u32[]{:S(2)}, u32[]{:S(2)}) async-start(bf16[16,176,128]{2,1,0:T(8,128)(2,1)} %get-tuple-element.74), calls=%async_computation | async-start | bytes 1441792 | tf_op jit(solution)/shard_map/all_to_all | solution.py:236
  49.5 23.3 %all-to-all-start.1 = ((bf16[16,160,128]{2,1,0:T(8,128)(2,1)}), bf16[16,160,128]{2,1,0:T(8,128)(2,1)S(1)}, u32[]{:S(2)}, u32[]{:S(2)}) async-start(bf16[16,160,128]{2,1,0:T(8,128)(2,1)} %chain.2), calls=%async_computation.1 | async-start | bytes 1310720 | tf_op jit(solution)/shard_map/all_to_all | solution.py:236
  53.1 76.5 %reduce-scatter.2.cloned.1.call-start = ((), (), s32[]{:S(2)}) async-start(), calls=%async_computation.8 | async-start | bytes 4096000 | tf_op jit(solution)/shard_map/reduce_scatter | solution.py:720
  54.3 9.9 %collective-permute-start = (bf16[256,1280]{1,0:T(8,128)(2,1)}, bf16[256,1280]{1,0:T(8,128)(2,1)}, u32[]{:S(2)}, u32[]{:S(2)}) collective-permute-start(bf16[256,1280]{1,0:T(8,128)(2,1)} %get-tuple-element.133), channel_id=1, source_target_pairs={{0,1},{1,0},{2,3},{3,2},{4,5},{5,4},{6,7},{7,6},{8,9},{9,8},{10,11... | collective-permute-start | bytes 1966088 | tf_op jit(solution)/shard_map/ppermute | solution.py:676
  90.9 12.5 %collective-permute-start.2 = (bf16[2,160,640]{2,1,0:T(8,128)(2,1)}, bf16[2,160,640]{2,1,0:T(8,128)(2,1)S(1)}, u32[]{:S(2)}, u32[]{:S(2)}) collective-permute-start(bf16[2,160,640]{2,1,0:T(8,128)(2,1)} %get-tuple-element.77), channel_id=1, source_target_pairs={{0,64},{64,128},{128,192},{192,0},{1,65},{65,129},{129,193},{193,1... | collective-permute-start | bytes 1228808 | tf_op jit(solution)/shard_map/ppermute | solution.py:652
  92.2 11.2 %collective-permute-start.3 = (bf16[2,160,640]{2,1,0:T(8,128)(2,1)}, bf16[2,160,640]{2,1,0:T(8,128)(2,1)S(1)}, u32[]{:S(2)}, u32[]{:S(2)}) collective-permute-start(bf16[2,160,640]{2,1,0:T(8,128)(2,1)} %get-tuple-element.78), channel_id=1, source_target_pairs={{0,192},{64,0},{128,64},{192,128},{1,193},{65,1},{129,65},{193,129... | collective-permute-start | bytes 1228808 | tf_op jit(solution)/shard_map/ppermute | solution.py:652
  103.5 4.7 %collective-permute-start.4 = (bf16[256,2560]{1,0:T(8,128)(2,1)}, bf16[256,2560]{1,0:T(8,128)(2,1)}, u32[]{:S(2)}, u32[]{:S(2)}) collective-permute-start(bf16[256,2560]{1,0:T(8,128)(2,1)} %get-tuple-element.86), channel_id=1, source_target_pairs={{0,1},{1,0},{2,3},{3,2},{4,5},{5,4},{6,7},{7,6},{8,9},{9,8},{10,11... | collective-permute-start | bytes 3932168 | tf_op jit(solution)/shard_map/ppermute | solution.py:676
  108.2 27.5 %collective-permute-start.8 = (bf16[4,160,640]{2,1,0:T(8,128)(2,1)}, bf16[4,160,640]{2,1,0:T(8,128)(2,1)}, u32[]{:S(2)}, u32[]{:S(2)}) collective-permute-start(bf16[4,160,640]{2,1,0:T(8,128)(2,1)} %get-tuple-element.93), channel_id=1, source_target_pairs={{0,64},{64,128},{128,192},{192,0},{1,65},{65,129},{129,193},{193,1... | collective-permute-start | bytes 2457608 | tf_op jit(solution)/shard_map/ppermute | solution.py:652
  109.5 26.2 %collective-permute-start.9 = (bf16[4,160,640]{2,1,0:T(8,128)(2,1)}, bf16[4,160,640]{2,1,0:T(8,128)(2,1)}, u32[]{:S(2)}, u32[]{:S(2)}) collective-permute-start(bf16[4,160,640]{2,1,0:T(8,128)(2,1)} %get-tuple-element.94), channel_id=1, source_target_pairs={{0,192},{64,0},{128,64},{192,128},{1,193},{65,1},{129,65},{193,129... | collective-permute-start | bytes 2457608 | tf_op jit(solution)/shard_map/ppermute | solution.py:652
  116.9 36.4 %all-to-all-start.3 = ((bf16[16,176,128]{2,1,0:T(8,128)(2,1)}), bf16[16,176,128]{2,1,0:T(8,128)(2,1)S(1)}, u32[]{:S(2)}, u32[]{:S(2)}) async-start(bf16[16,176,128]{2,1,0:T(8,128)(2,1)} %get-tuple-element.104), calls=%async_computation.4 | async-start | bytes 1441792 | tf_op jit(solution)/shard_map/all_to_all | solution.py:236
  131.6 9.2 %collective-permute-start.7 = (bf16[160,640]{1,0:T(8,128)(2,1)S(1)}, bf16[160,640]{1,0:T(8,128)(2,1)S(1)}, u32[]{:S(2)}, u32[]{:S(2)}) collective-permute-start(bf16[160,640]{1,0:T(8,128)(2,1)S(1)} %get-tuple-element.138), channel_id=1, source_target_pairs={{0,128},{64,192},{128,0},{192,64},{1,129},{65,193},{129,1},{193,65... | collective-permute-start | bytes 614408 | tf_op jit(solution)/shard_map/ppermute | solution.py:652
  134.3 9.2 %collective-permute-start.6 = (bf16[160,640]{1,0:T(8,128)(2,1)S(1)}, bf16[160,640]{1,0:T(8,128)(2,1)S(1)}, u32[]{:S(2)}, u32[]{:S(2)}) collective-permute-start(bf16[160,640]{1,0:T(8,128)(2,1)S(1)} %get-tuple-element.139), channel_id=1, source_target_pairs={{0,192},{64,0},{128,64},{192,128},{1,193},{65,1},{129,65},{193,129... | collective-permute-start | bytes 614408 | tf_op jit(solution)/shard_map/ppermute | solution.py:652
  135.2 8.5 %collective-permute-start.5 = (bf16[160,640]{1,0:T(8,128)(2,1)S(1)}, bf16[160,640]{1,0:T(8,128)(2,1)S(1)}, u32[]{:S(2)}, u32[]{:S(2)}) collective-permute-start(bf16[160,640]{1,0:T(8,128)(2,1)S(1)} %get-tuple-element.140), channel_id=1, source_target_pairs={{0,64},{64,128},{128,192},{192,0},{1,65},{65,129},{129,193},{193,1... | collective-permute-start | bytes 614408 | tf_op jit(solution)/shard_map/ppermute | solution.py:652
  138.4 6.5 %collective-permute-start.12 = (bf16[160,640]{1,0:T(8,128)(2,1)S(1)}, bf16[160,640]{1,0:T(8,128)(2,1)S(1)}, u32[]{:S(2)}, u32[]{:S(2)}) collective-permute-start(bf16[160,640]{1,0:T(8,128)(2,1)S(1)} %get-tuple-element.134), channel_id=1, source_target_pairs={{0,32},{16,48},{32,0},{48,16},{1,33},{17,49},{33,1},{49,17},{2,34}... | collective-permute-start | bytes 614408 | tf_op jit(solution)/shard_map/ppermute | solution.py:652
  139.6 8.2 %collective-permute-start.11 = (bf16[160,640]{1,0:T(8,128)(2,1)S(1)}, bf16[160,640]{1,0:T(8,128)(2,1)S(1)}, u32[]{:S(2)}, u32[]{:S(2)}) collective-permute-start(bf16[160,640]{1,0:T(8,128)(2,1)S(1)} %get-tuple-element.135), channel_id=1, source_target_pairs={{0,48},{16,0},{32,16},{48,32},{1,49},{17,1},{33,17},{49,33},{2,50}... | collective-permute-start | bytes 614408 | tf_op jit(solution)/shard_map/ppermute | solution.py:652
  140.8 9.4 %collective-permute-start.10 = (bf16[160,640]{1,0:T(8,128)(2,1)S(1)}, bf16[160,640]{1,0:T(8,128)(2,1)S(1)}, u32[]{:S(2)}, u32[]{:S(2)}) collective-permute-start(bf16[160,640]{1,0:T(8,128)(2,1)S(1)} %get-tuple-element.136), channel_id=1, source_target_pairs={{0,16},{16,32},{32,48},{48,0},{1,17},{17,33},{33,49},{49,1},{2,18}... | collective-permute-start | bytes 614408 | tf_op jit(solution)/shard_map/ppermute | solution.py:652
  153.3 19.8 %all-to-all-start.2 = ((bf16[8,13,16,128]{3,2,1,0:T(8,128)(2,1)}), bf16[8,13,16,128]{3,2,1,0:T(8,128)(2,1)S(1)}, u32[]{:S(2)}, u32[]{:S(2)}) async-start(bf16[8,13,16,128]{3,2,1,0:T(8,128)(2,1)} %fold.1), calls=%async_computation.3 | async-start | bytes 851968 | tf_op jit(solution)/shard_map/all_to_all | solution.py:236
  175.9 26.7 %all-to-all-start.4 = ((bf16[16,160,128]{2,1,0:T(8,128)(2,1)}), bf16[16,160,128]{2,1,0:T(8,128)(2,1)S(1)}, u32[]{:S(2)}, u32[]{:S(2)}) async-start(bf16[16,160,128]{2,1,0:T(8,128)(2,1)} %chain.3), calls=%async_computation.5 | async-start | bytes 1310720 | tf_op jit(solution)/shard_map/all_to_all | solution.py:236
  183.6 4.0 %collective-permute-start.14 = (f32[1,128]{1,0:T(1,128)}, f32[1,128]{1,0:T(1,128)S(1)}, u32[]{:S(2)}, u32[]{:S(2)}) collective-permute-start(f32[1,128]{1,0:T(1,128)} %get-tuple-element.110), channel_id=1, source_target_pairs={{0,32},{16,48},{32,0},{48,16},{64,96},{80,112},{96,64},{112,80},{1... | collective-permute-start | bytes 1544 | tf_op jit(solution)/shard_map/ppermute | solution.py:682
  188.3 3.9 %collective-permute-start.18 = (f32[1,128]{1,0:T(1,128)S(1)}, f32[1,128]{1,0:T(1,128)S(1)}, u32[]{:S(2)}, u32[]{:S(2)}) collective-permute-start(f32[1,128]{1,0:T(1,128)S(1)} %add_add_fusion.1), channel_id=1, source_target_pairs={{0,192},{16,208},{32,224},{48,240},{64,128},{80,144},{96,160},{112... | collective-permute-start | bytes 1544 | tf_op jit(solution)/shard_map/ppermute | solution.py:682
  190.4 4.2 %collective-permute-start.17 = (f32[1,128]{1,0:T(1,128)S(1)}, f32[1,128]{1,0:T(1,128)S(1)}, u32[]{:S(2)}, u32[]{:S(2)}) collective-permute-start(f32[1,128]{1,0:T(1,128)S(1)} %add_add_fusion.1), channel_id=1, source_target_pairs={{0,128},{16,144},{32,160},{48,176},{64,192},{80,208},{96,224},{112... | collective-permute-start | bytes 1544 | tf_op jit(solution)/shard_map/ppermute | solution.py:682
  190.4 4.2 %collective-permute-start.16 = (f32[1,128]{1,0:T(1,128)S(1)}, f32[1,128]{1,0:T(1,128)S(1)}, u32[]{:S(2)}, u32[]{:S(2)}) collective-permute-start(f32[1,128]{1,0:T(1,128)S(1)} %add_add_fusion.1), channel_id=1, source_target_pairs={{0,64},{16,80},{32,96},{48,112},{64,0},{80,16},{96,32},{112,48},{1... | collective-permute-start | bytes 1544 | tf_op jit(solution)/shard_map/ppermute | solution.py:682
  204.3 20.1 %all-to-all-start.5 = ((bf16[8,14,16,128]{3,2,1,0:T(8,128)(2,1)}), bf16[8,14,16,128]{3,2,1,0:T(8,128)(2,1)S(1)}, u32[]{:S(2)}, u32[]{:S(2)}) async-start(bf16[8,14,16,128]{3,2,1,0:T(8,128)(2,1)} %pack.1), calls=%async_computation.6 | async-start | bytes 917504 | tf_op jit(solution)/shard_map/all_to_all | solution.py:236
  (20 other events, 99.8 us)
Sparse Core Ops, SparseCore 0:
  14.8 71.3 all-gather.1
Sparse Core Ops, SparseCore 1:
  91.0 38.5 reduce-scatter.1

commit v13 on v10

--- a/solution.py
+++ b/solution.py
@@ -21,7 +21,7 @@
 HIGH = lax.Precision.HIGHEST
 BF = jnp.bfloat16
 F32 = jnp.float32
-VMEM = 56 * 1024 * 1024
+VMEM = 62 * 1024 * 1024
 WIDE = 5
 STEP = 2
 ROWS = OWN + 16

time: 238 us -> 239 us (level)
  other arithmetic: 6.37 us -> 9.17 us
    unnamed x36 -> x32, local copies, waits for them, and re-layouts: 5.08 us -> 4.01 us
  transfers between devices with their start and end apart: 28 -> 28, of which waited for: 18 -> 17; matrix products, arithmetic and copies ran while one was open for 5% -> 7% of each run, Pallas kernels for 28% -> 28%
where the time goes in v13:
time: 239 us; the launch traced here: 237 us
  Pallas kernels  78.8 us (33%)
  waiting for transfers between devices  65.6 us (27%)
  starting transfers between devices  56.1 us (23%)
  between operations  15.6 us (7%)
  local copies, waits for them, and re-layouts  11.7 us (5%)
  other arithmetic  9.17 us (4%)
    all_to_all x6, waiting for transfers between devices, swap(): return lax.all_to_all(v, axis, 0, 0, tiled=True)  42.5 us
    all_to_all x6, starting transfers between devices, swap(): return lax.all_to_all(v, axis, 0, 0, tiled=True)  34.8 us
    pallas_call x2, Pallas kernels, within(): pl.pallas_call(functools.partial(within_kernel, first, steps), grid=(step...  13.9 us
    ppermute x10, starting transfers between devices, shifted(): return lax.ppermute(v, axis, [(i, (i + d) % 4) for i in range(4)])  12.7 us
    ppermute x10, waiting for transfers between devices, shifted(): return lax.ppermute(v, axis, [(i, (i + d) % 4) for i in range(4)])  11.5 us
    pallas_call x1, Pallas kernels, intra(): pl.pallas_call(intra_kernel, grid=(PAIRS // STEP,), in_specs=[wide(T, STE...  9.28 us
    pallas_call x1, Pallas kernels, across(): pl.pallas_call(across_kernel, grid=(PAIRS // WIDE,), in_specs=[wide(T, WI...  8.56 us
    pallas_call x1, Pallas kernels, terms(): pl.pallas_call(term_kernel, grid_spec=pltpu.PrefetchScalarGridSpec(num_sc...  8.37 us
  transfers between devices with their start and end apart: 28, of which 17 were waited for; matrix products, arithmetic and copies ran while one was open for 7% of the time, Pallas kernels for 28%

profile of v13, /device:TPU:1, one launch (start us, length us, event | category | flops | bytes accessed | tf_op | source)
XLA Modules:
  0.0 237.0 jit_solution(9087489713908684436)
XLA Ops:
  8.1 5.8 %ends.1 = (f32[40,256]{1,0:T(8,128)}, f32[256,40]{1,0:T(8,128)}, bf16[256,2560]{1,0:T(8,128)(2,1)}, bf16[16,176,128]{2,1,0:T(8,128)(2,1)}) custom-call(f32[256,2560]{1,0:T(8,128)} %bitcast.49, f32[40,256]{1,0:T(8,128)} %bitcast.70, f32[256,128]{1,0:T(8,128)} %bitcast.63), custom_call_target="tpu_custom_call" | custom-call | bytes 18000000 | tf_op jit(solution)/shard_map/ends/pallas_call | solution.py:134
  14.7 10.0 %all-to-all-start = ((bf16[16,176,128]{2,1,0:T(8,128)(2,1)}), bf16[16,176,128]{2,1,0:T(8,128)(2,1)S(1)}, u32[]{:S(2)}, u32[]{:S(2)}) async-start(bf16[16,176,128]{2,1,0:T(8,128)(2,1)} %get-tuple-element.73), calls=%async_computation | async-start | bytes 1441792 | tf_op jit(solution)/shard_map/all_to_all | solution.py:236
  24.7 21.3 %all-to-all-done.parts_ref.totals_ref = bf16[16,176,128]{2,1,0:T(8,128)(2,1)S(1)} async-done(((bf16[16,176,128]{2,1,0:T(8,128)(2,1)}), bf16[16,176,128]{2,1,0:T(8,128)(2,1)S(1)}, u32[]{:S(2)}, u32[]{:S(2)}) %all-to-all-start) | async-done | bytes 720928 | tf_op jit(solution)/shard_map/all_to_all | solution.py:236
  49.6 3.6 %all-to-all-start.1 = ((bf16[16,160,128]{2,1,0:T(8,128)(2,1)}), bf16[16,160,128]{2,1,0:T(8,128)(2,1)S(1)}, u32[]{:S(2)}, u32[]{:S(2)}) async-start(bf16[16,160,128]{2,1,0:T(8,128)(2,1)} %chain.2), calls=%async_computation.1 | async-start | bytes 1310720 | tf_op jit(solution)/shard_map/all_to_all | solution.py:236
  54.4 9.3 %intra.1 = (f32[256,2560]{1,0:T(8,128)}, bf16[256,2560]{1,0:T(8,128)(2,1)}) custom-call(f32[256,2560]{1,0:T(8,128)} %bitcast.50, f32[40,256]{1,0:T(8,128)} %get-tuple-element.66.cum_ref, f32[256,40]{1,0:T(8,128)} %get-tuple-element.67.cum_t_ref, f32[256,128]{1,0:T(8,128)} %bitcast.64, f32[256,128]{1,0:T(8,128)} %bitcast.57, f32[40]{0:T(128)} %skip_ref.5), custom_call_target="tpu_custom_call" | custom-call | bytes 27000000 | tf_op jit(solution)/shard_map/intra/pallas_call | solution.py:179
  66.8 6.1 %all-to-all-done.1 = bf16[16,160,128]{2,1,0:T(8,128)(2,1)S(1)} async-done(((bf16[16,160,128]{2,1,0:T(8,128)(2,1)}), bf16[16,160,128]{2,1,0:T(8,128)(2,1)S(1)}, u32[]{:S(2)}, u32[]{:S(2)}) %all-to-all-start.1) | async-done | bytes 655392 | tf_op jit(solution)/shard_map/all_to_all | solution.py:236
  73.7 4.7 %inter.1.yo_ref = bf16[256,2560]{1,0:T(8,128)(2,1)} custom-call(f32[256,2560]{1,0:T(8,128)} %get-tuple-element.70.part_ref, bf16[256,2560]{1,0:T(8,128)(2,1)} %get-tuple-element.71.grow_ref, f32[256,128]{1,0:T(8,128)} %bitcast.58, bf16[2560,128]{1,0:T(8,128)(2,1)} %bitcast.55), custom_call_target="tpu_custom_call" | custom-call | bytes 15000000 | tf_op jit(solution)/shard_map/inter/pallas_call | solution.py:200
  78.4 3.4 %collective-permute-done.1.yx_ref = bf16[256,2560]{1,0:T(8,128)(2,1)} collective-permute-done((bf16[256,2560]{1,0:T(8,128)(2,1)}, bf16[256,2560]{1,0:T(8,128)(2,1)}, u32[]{:S(2)}, u32[]{:S(2)}) %collective-permute-start.1) | collective-permute-done | bytes 1310752 | tf_op jit(solution)/shard_map/ppermute | solution.py:660
  81.8 8.4 %terms.1 = (bf16[4,4,160,640]{3,2,1,0:T(8,128)(2,1)}, bf16[4,4,160,640]{3,2,1,0:T(8,128)(2,1)}) custom-call(s32[2]{0:T(128)} %pad_add_fusion.at_ref, bf16[256,2560]{1,0:T(8,128)(2,1)} %inter.1.yo_ref, bf16[256,2560]{1,0:T(8,128)(2,1)} %collective-permute-done.1.yx_ref, bf16[512,1280]{1,0:T(8,128)(2,1)} %pad_maximum_fusion.g_ref), custom_call_target="tpu_custom_call" | custom-call | bytes 24000000 | tf_op jit(solution)/shard_map/terms/pallas_call | solution.py:251
  95.3 8.3 %gy_parts.1 = (f32[256,2560]{1,0:T(8,128)}, bf16[256,2560]{1,0:T(8,128)(2,1)}) custom-call(bf16[512,1280]{1,0:T(8,128)(2,1)} %pad_maximum_fusion.g_ref, bf16[2560,1280]{1,0:T(8,128)(2,1)} %all-gather.2.cloned.1.call-done.w_ref), custom_call_target="tpu_custom_call" | custom-call | bytes 24000000 | tf_op jit(solution)/shard_map/gy_parts/pallas_call | solution.py:277
  104.4 3.1 %collective-permute-done.2 = bf16[2,160,640]{2,1,0:T(8,128)(2,1)} collective-permute-done((bf16[2,160,640]{2,1,0:T(8,128)(2,1)}, bf16[2,160,640]{2,1,0:T(8,128)(2,1)}, u32[]{:S(2)}, u32[]{:S(2)}) %collective-permute-start.2) | collective-permute-done | bytes 409632 | tf_op jit(solution)/shard_map/ppermute | solution.py:631
  114.4 6.0 %entries.1 = (bf16[256,2560]{1,0:T(8,128)(2,1)}, bf16[16,176,128]{2,1,0:T(8,128)(2,1)}) custom-call(f32[256,2560]{1,0:T(8,128)} %get-tuple-element.84.own_ref, bf16[256,2560]{1,0:T(8,128)(2,1)} %collective-permute-done.4.other_ref, f32[256,2560]{1,0:T(8,128)} %bitcast.51, bf16[256,2560]{1,0:T(8,128)(2,1)} %get-tuple-element.71.grow_ref, f32[256,128]{1,0:T(8,128)} %bitcast.59), custom_call_target="tpu_custom_call" | custom-call | bytes 18000000 | tf_op jit(solution)/shard_map/entries/pallas_call | solution.py:317
  120.3 4.3 %all-to-all-start.3 = ((bf16[16,176,128]{2,1,0:T(8,128)(2,1)}), bf16[16,176,128]{2,1,0:T(8,128)(2,1)S(1)}, u32[]{:S(2)}, u32[]{:S(2)}) async-start(bf16[16,176,128]{2,1,0:T(8,128)(2,1)} %get-tuple-element.102), calls=%async_computation.4 | async-start | bytes 1441792 | tf_op jit(solution)/shard_map/all_to_all | solution.py:236
  124.7 6.9 %within.2 = (f32[256,1280]{1,0:T(8,128)}, f32[40,256]{1,0:T(8,128)}, f32[256,128]{1,0:T(8,128)}, f32[256,128]{1,0:T(8,128)}) custom-call(f32[256,2560]{1,0:T(8,128)} %bitcast.52, bf16[256,2560]{1,0:T(8,128)(2,1)} %get-tuple-element.93.gy_ref, f32[40,256]{1,0:T(8,128)} %get-tuple-element.66.cum_ref, f32[256,40]{1,0:T(8,128)} %get-tuple-element.67.cum_t_ref, ...), custom_call_target="tpu_custom_call" | custom-call | bytes 21000000 | tf_op jit(solution)/shard_map/within/pallas_call | solution.py:387
  140.4 2.8 %collective-permute-start.12 = (bf16[160,640]{1,0:T(8,128)(2,1)S(1)}, bf16[160,640]{1,0:T(8,128)(2,1)S(1)}, u32[]{:S(2)}, u32[]{:S(2)}) collective-permute-start(bf16[160,640]{1,0:T(8,128)(2,1)S(1)} %get-tuple-element.134), channel_id=1, source_target_pairs={{0,32},{16,48},{32,0},{48,16},{1,33},{17,49},{33,1},{49,17},{2,34}... | collective-permute-start | bytes 614408 | tf_op jit(solution)/shard_map/ppermute | solution.py:631
  144.8 3.1 %collective-permute-done.8.a2 = bf16[160,640]{1,0:T(8,128)(2,1)S(1)} collective-permute-done((bf16[160,640]{1,0:T(8,128)(2,1)S(1)}, bf16[160,640]{1,0:T(8,128)(2,1)S(1)}, u32[]{:S(2)}, u32[]{:S(2)}) %collective-permute-start.8) | collective-permute-done | bytes 204832 | tf_op jit(solution)/shard_map/ppermute | solution.py:631
  154.5 5.0 %all-to-all-start.2 = ((bf16[8,13,16,128]{3,2,1,0:T(8,128)(2,1)}), bf16[8,13,16,128]{3,2,1,0:T(8,128)(2,1)S(1)}, u32[]{:S(2)}, u32[]{:S(2)}) async-start(bf16[8,13,16,128]{3,2,1,0:T(8,128)(2,1)} %fold.1), calls=%async_computation.3 | async-start | bytes 851968 | tf_op jit(solution)/shard_map/all_to_all | solution.py:236
  160.1 7.0 %within.3 = (f32[256,1280]{1,0:T(8,128)}, f32[40,256]{1,0:T(8,128)}, f32[256,128]{1,0:T(8,128)}, f32[256,128]{1,0:T(8,128)}) custom-call(f32[256,2560]{1,0:T(8,128)} %bitcast.53, bf16[256,2560]{1,0:T(8,128)(2,1)} %get-tuple-element.93.gy_ref, f32[40,256]{1,0:T(8,128)} %get-tuple-element.66.cum_ref, f32[256,40]{1,0:T(8,128)} %get-tuple-element.67.cum_t_ref, ...), custom_call_target="tpu_custom_call" | custom-call | bytes 21000000 | tf_op jit(solution)/shard_map/within/pallas_call | solution.py:387
  174.2 8.4 %all-to-all-start.4 = ((bf16[16,160,128]{2,1,0:T(8,128)(2,1)}), bf16[16,160,128]{2,1,0:T(8,128)(2,1)S(1)}, u32[]{:S(2)}, u32[]{:S(2)}) async-start(bf16[16,160,128]{2,1,0:T(8,128)(2,1)} %chain.3), calls=%async_computation.5 | async-start | bytes 1310720 | tf_op jit(solution)/shard_map/all_to_all | solution.py:236
  186.4 3.3 %collective-permute-done.14 = f32[1,128]{1,0:T(1,128)S(1)} collective-permute-done((f32[1,128]{1,0:T(1,128)}, f32[1,128]{1,0:T(1,128)S(1)}, u32[]{:S(2)}, u32[]{:S(2)}) %collective-permute-start.14) | collective-permute-done | bytes 544 | tf_op jit(solution)/shard_map/ppermute | solution.py:666
  197.2 5.5 %all-to-all-done.4 = bf16[16,160,128]{2,1,0:T(8,128)(2,1)S(1)} async-done(((bf16[16,160,128]{2,1,0:T(8,128)(2,1)}), bf16[16,160,128]{2,1,0:T(8,128)(2,1)S(1)}, u32[]{:S(2)}, u32[]{:S(2)}) %all-to-all-start.4) | async-done | bytes 655392 | tf_op jit(solution)/shard_map/all_to_all | solution.py:236
  204.3 3.5 %all-to-all-start.5 = ((bf16[8,14,16,128]{3,2,1,0:T(8,128)(2,1)}), bf16[8,14,16,128]{3,2,1,0:T(8,128)(2,1)S(1)}, u32[]{:S(2)}, u32[]{:S(2)}) async-start(bf16[8,14,16,128]{3,2,1,0:T(8,128)(2,1)} %pack.1), calls=%async_computation.6 | async-start | bytes 917504 | tf_op jit(solution)/shard_map/all_to_all | solution.py:236
  207.8 8.6 %across.1 = (f32[256,2560]{1,0:T(8,128)}, f32[40,256]{1,0:T(8,128)}, f32[256,128]{1,0:T(8,128)}, f32[256,128]{1,0:T(8,128)}) custom-call(f32[256,2560]{1,0:T(8,128)} %bitcast.54, bf16[256,2560]{1,0:T(8,128)(2,1)} %get-tuple-element.93.gy_ref, bf16[256,2560]{1,0:T(8,128)(2,1)} %get-tuple-element.71.grow_ref, bf16[256,2560]{1,0:T(8,128)(2,1)} %get-tuple-element.94.tail_ref, ...), custom_call_target="tpu_custom_call" | custom-call | bytes 24000000 | tf_op jit(solution)/shard_map/across/pallas_call | solution.py:462
  216.4 7.9 %all-to-all-done.5.own_ref = bf16[8,14,16,128]{3,2,1,0:T(8,128)(2,1)S(1)} async-done(((bf16[8,14,16,128]{3,2,1,0:T(8,128)(2,1)}), bf16[8,14,16,128]{3,2,1,0:T(8,128)(2,1)S(1)}, u32[]{:S(2)}, u32[]{:S(2)}) %all-to-all-start.5) | async-done | bytes 458784 | tf_op jit(solution)/shard_map/all_to_all | solution.py:236
  (95 shorter events, 65.3 us)
Async XLA Ops:
  8.0 87.3 %all-gather.2.cloned.1.call-start = ((), (), s32[]{:S(2)}) async-start(), calls=%async_computation.7 | async-start | bytes 6963200 | tf_op jit(solution)/shard_map/all_gather | solution.py:695
  14.7 31.3 %all-to-all-start = ((bf16[16,176,128]{2,1,0:T(8,128)(2,1)}), bf16[16,176,128]{2,1,0:T(8,128)(2,1)S(1)}, u32[]{:S(2)}, u32[]{:S(2)}) async-start(bf16[16,176,128]{2,1,0:T(8,128)(2,1)} %get-tuple-element.73), calls=%async_computation | async-start | bytes 1441792 | tf_op jit(solution)/shard_map/all_to_all | solution.py:236
  49.6 23.3 %all-to-all-start.1 = ((bf16[16,160,128]{2,1,0:T(8,128)(2,1)}), bf16[16,160,128]{2,1,0:T(8,128)(2,1)S(1)}, u32[]{:S(2)}, u32[]{:S(2)}) async-start(bf16[16,160,128]{2,1,0:T(8,128)(2,1)} %chain.2), calls=%async_computation.1 | async-start | bytes 1310720 | tf_op jit(solution)/shard_map/all_to_all | solution.py:236
  53.2 81.5 %reduce-scatter.2.cloned.1.call-start = ((), (), s32[]{:S(2)}) async-start(), calls=%async_computation.8 | async-start | bytes 4096000 | tf_op jit(solution)/shard_map/reduce_scatter | solution.py:704
  54.4 9.9 %collective-permute-start = (bf16[256,1280]{1,0:T(8,128)(2,1)}, bf16[256,1280]{1,0:T(8,128)(2,1)}, u32[]{:S(2)}, u32[]{:S(2)}) collective-permute-start(bf16[256,1280]{1,0:T(8,128)(2,1)} %get-tuple-element.133), channel_id=1, source_target_pairs={{0,1},{1,0},{2,3},{3,2},{4,5},{5,4},{6,7},{7,6},{8,9},{9,8},{10,11... | collective-permute-start | bytes 1966088 | tf_op jit(solution)/shard_map/ppermute | solution.py:660
  92.6 11.7 %collective-permute-start.3 = (bf16[2,160,640]{2,1,0:T(8,128)(2,1)}, bf16[2,160,640]{2,1,0:T(8,128)(2,1)}, u32[]{:S(2)}, u32[]{:S(2)}) collective-permute-start(bf16[2,160,640]{2,1,0:T(8,128)(2,1)} %get-tuple-element.128), channel_id=1, source_target_pairs={{0,192},{64,0},{128,64},{192,128},{1,193},{65,1},{129,65},{193,129... | collective-permute-start | bytes 1228808 | tf_op jit(solution)/shard_map/ppermute | solution.py:631
  95.3 12.1 %collective-permute-start.2 = (bf16[2,160,640]{2,1,0:T(8,128)(2,1)}, bf16[2,160,640]{2,1,0:T(8,128)(2,1)}, u32[]{:S(2)}, u32[]{:S(2)}) collective-permute-start(bf16[2,160,640]{2,1,0:T(8,128)(2,1)} %get-tuple-element.129), channel_id=1, source_target_pairs={{0,64},{64,128},{128,192},{192,0},{1,65},{65,129},{129,193},{193,1... | collective-permute-start | bytes 1228808 | tf_op jit(solution)/shard_map/ppermute | solution.py:631
  107.4 4.3 %collective-permute-start.4 = (bf16[256,2560]{1,0:T(8,128)(2,1)}, bf16[256,2560]{1,0:T(8,128)(2,1)}, u32[]{:S(2)}, u32[]{:S(2)}) collective-permute-start(bf16[256,2560]{1,0:T(8,128)(2,1)} %get-tuple-element.83), channel_id=1, source_target_pairs={{0,1},{1,0},{2,3},{3,2},{4,5},{5,4},{6,7},{7,6},{8,9},{9,8},{10,11... | collective-permute-start | bytes 3932168 | tf_op jit(solution)/shard_map/ppermute | solution.py:660
  111.7 21.0 %collective-permute-start.5 = (bf16[4,160,640]{2,1,0:T(8,128)(2,1)}, bf16[4,160,640]{2,1,0:T(8,128)(2,1)}, u32[]{:S(2)}, u32[]{:S(2)}) collective-permute-start(bf16[4,160,640]{2,1,0:T(8,128)(2,1)} %get-tuple-element.88), channel_id=1, source_target_pairs={{0,64},{64,128},{128,192},{192,0},{1,65},{65,129},{129,193},{193,1... | collective-permute-start | bytes 2457608 | tf_op jit(solution)/shard_map/ppermute | solution.py:631
  111.7 21.0 %collective-permute-start.6 = (bf16[4,160,640]{2,1,0:T(8,128)(2,1)}, bf16[4,160,640]{2,1,0:T(8,128)(2,1)}, u32[]{:S(2)}, u32[]{:S(2)}) collective-permute-start(bf16[4,160,640]{2,1,0:T(8,128)(2,1)} %get-tuple-element.89), channel_id=1, source_target_pairs={{0,192},{64,0},{128,64},{192,128},{1,193},{65,1},{129,65},{193,129... | collective-permute-start | bytes 2457608 | tf_op jit(solution)/shard_map/ppermute | solution.py:631
  120.3 34.2 %all-to-all-start.3 = ((bf16[16,176,128]{2,1,0:T(8,128)(2,1)}), bf16[16,176,128]{2,1,0:T(8,128)(2,1)S(1)}, u32[]{:S(2)}, u32[]{:S(2)}) async-start(bf16[16,176,128]{2,1,0:T(8,128)(2,1)} %get-tuple-element.102), calls=%async_computation.4 | async-start | bytes 1441792 | tf_op jit(solution)/shard_map/all_to_all | solution.py:236
  136.7 7.3 %collective-permute-start.9 = (bf16[160,640]{1,0:T(8,128)(2,1)S(1)}, bf16[160,640]{1,0:T(8,128)(2,1)S(1)}, u32[]{:S(2)}, u32[]{:S(2)}) collective-permute-start(bf16[160,640]{1,0:T(8,128)(2,1)S(1)} %get-tuple-element.138), channel_id=1, source_target_pairs={{0,128},{64,192},{128,0},{192,64},{1,129},{65,193},{129,1},{193,65... | collective-permute-start | bytes 614408 | tf_op jit(solution)/shard_map/ppermute | solution.py:631
  137.8 10.0 %collective-permute-start.8 = (bf16[160,640]{1,0:T(8,128)(2,1)S(1)}, bf16[160,640]{1,0:T(8,128)(2,1)S(1)}, u32[]{:S(2)}, u32[]{:S(2)}) collective-permute-start(bf16[160,640]{1,0:T(8,128)(2,1)S(1)} %get-tuple-element.139), channel_id=1, source_target_pairs={{0,192},{64,0},{128,64},{192,128},{1,193},{65,1},{129,65},{193,129... | collective-permute-start | bytes 614408 | tf_op jit(solution)/shard_map/ppermute | solution.py:631
  139.0 9.7 %collective-permute-start.7 = (bf16[160,640]{1,0:T(8,128)(2,1)S(1)}, bf16[160,640]{1,0:T(8,128)(2,1)S(1)}, u32[]{:S(2)}, u32[]{:S(2)}) collective-permute-start(bf16[160,640]{1,0:T(8,128)(2,1)S(1)} %get-tuple-element.140), channel_id=1, source_target_pairs={{0,64},{64,128},{128,192},{192,0},{1,65},{65,129},{129,193},{193,1... | collective-permute-start | bytes 614408 | tf_op jit(solution)/shard_map/ppermute | solution.py:631
  140.4 8.4 %collective-permute-start.12 = (bf16[160,640]{1,0:T(8,128)(2,1)S(1)}, bf16[160,640]{1,0:T(8,128)(2,1)S(1)}, u32[]{:S(2)}, u32[]{:S(2)}) collective-permute-start(bf16[160,640]{1,0:T(8,128)(2,1)S(1)} %get-tuple-element.134), channel_id=1, source_target_pairs={{0,32},{16,48},{32,0},{48,16},{1,33},{17,49},{33,1},{49,17},{2,34}... | collective-permute-start | bytes 614408 | tf_op jit(solution)/shard_map/ppermute | solution.py:631
  143.2 8.1 %collective-permute-start.11 = (bf16[160,640]{1,0:T(8,128)(2,1)S(1)}, bf16[160,640]{1,0:T(8,128)(2,1)S(1)}, u32[]{:S(2)}, u32[]{:S(2)}) collective-permute-start(bf16[160,640]{1,0:T(8,128)(2,1)S(1)} %get-tuple-element.135), channel_id=1, source_target_pairs={{0,48},{16,0},{32,16},{48,32},{1,49},{17,1},{33,17},{49,33},{2,50}... | collective-permute-start | bytes 614408 | tf_op jit(solution)/shard_map/ppermute | solution.py:631
  144.0 7.3 %collective-permute-start.10 = (bf16[160,640]{1,0:T(8,128)(2,1)S(1)}, bf16[160,640]{1,0:T(8,128)(2,1)S(1)}, u32[]{:S(2)}, u32[]{:S(2)}) collective-permute-start(bf16[160,640]{1,0:T(8,128)(2,1)S(1)} %get-tuple-element.136), channel_id=1, source_target_pairs={{0,16},{16,32},{32,48},{48,0},{1,17},{17,33},{33,49},{49,1},{2,18}... | collective-permute-start | bytes 614408 | tf_op jit(solution)/shard_map/ppermute | solution.py:631
  154.5 16.9 %all-to-all-start.2 = ((bf16[8,13,16,128]{3,2,1,0:T(8,128)(2,1)}), bf16[8,13,16,128]{3,2,1,0:T(8,128)(2,1)S(1)}, u32[]{:S(2)}, u32[]{:S(2)}) async-start(bf16[8,13,16,128]{3,2,1,0:T(8,128)(2,1)} %fold.1), calls=%async_computation.3 | async-start | bytes 851968 | tf_op jit(solution)/shard_map/all_to_all | solution.py:236
  174.2 28.5 %all-to-all-start.4 = ((bf16[16,160,128]{2,1,0:T(8,128)(2,1)}), bf16[16,160,128]{2,1,0:T(8,128)(2,1)S(1)}, u32[]{:S(2)}, u32[]{:S(2)}) async-start(bf16[16,160,128]{2,1,0:T(8,128)(2,1)} %chain.3), calls=%async_computation.5 | async-start | bytes 1310720 | tf_op jit(solution)/shard_map/all_to_all | solution.py:236
  182.6 3.8 %collective-permute-start.15 = (f32[1,128]{1,0:T(1,128)}, f32[1,128]{1,0:T(1,128)S(1)}, u32[]{:S(2)}, u32[]{:S(2)}) collective-permute-start(f32[1,128]{1,0:T(1,128)} %get-tuple-element.108), channel_id=1, source_target_pairs={{0,48},{16,32},{32,16},{48,0},{64,112},{80,96},{96,80},{112,64},{1... | collective-permute-start | bytes 1544 | tf_op jit(solution)/shard_map/ppermute | solution.py:666
  185.4 4.3 %collective-permute-start.14 = (f32[1,128]{1,0:T(1,128)}, f32[1,128]{1,0:T(1,128)S(1)}, u32[]{:S(2)}, u32[]{:S(2)}) collective-permute-start(f32[1,128]{1,0:T(1,128)} %get-tuple-element.108), channel_id=1, source_target_pairs={{0,32},{16,48},{32,0},{48,16},{64,96},{80,112},{96,64},{112,80},{1... | collective-permute-start | bytes 1544 | tf_op jit(solution)/shard_map/ppermute | solution.py:666
  190.4 3.9 %collective-permute-start.18 = (f32[1,128]{1,0:T(1,128)S(1)}, f32[1,128]{1,0:T(1,128)S(1)}, u32[]{:S(2)}, u32[]{:S(2)}) collective-permute-start(f32[1,128]{1,0:T(1,128)S(1)} %add_add_fusion.1), channel_id=1, source_target_pairs={{0,192},{16,208},{32,224},{48,240},{64,128},{80,144},{96,160},{112... | collective-permute-start | bytes 1544 | tf_op jit(solution)/shard_map/ppermute | solution.py:666
  192.5 4.2 %collective-permute-start.17 = (f32[1,128]{1,0:T(1,128)S(1)}, f32[1,128]{1,0:T(1,128)S(1)}, u32[]{:S(2)}, u32[]{:S(2)}) collective-permute-start(f32[1,128]{1,0:T(1,128)S(1)} %add_add_fusion.1), channel_id=1, source_target_pairs={{0,128},{16,144},{32,160},{48,176},{64,192},{80,208},{96,224},{112... | collective-permute-start | bytes 1544 | tf_op jit(solution)/shard_map/ppermute | solution.py:666
  204.3 19.9 %all-to-all-start.5 = ((bf16[8,14,16,128]{3,2,1,0:T(8,128)(2,1)}), bf16[8,14,16,128]{3,2,1,0:T(8,128)(2,1)S(1)}, u32[]{:S(2)}, u32[]{:S(2)}) async-start(bf16[8,14,16,128]{3,2,1,0:T(8,128)(2,1)} %pack.1), calls=%async_computation.6 | async-start | bytes 917504 | tf_op jit(solution)/shard_map/all_to_all | solution.py:236
  (20 other events, 82.8 us)
Sparse Core Ops, SparseCore 0:
  14.8 71.2 all-gather.1
Sparse Core Ops, SparseCore 1:
  90.2 38.5 reduce-scatter.1
